TPU v7x, 32 devices: a whole 2x2x4 slice. The times are simulated.
32 devices in a mesh: bucket: 8 (over y, x, core), span: 4 (over z).
Axes of the slice: x: 2, y: 2, z: 4, core: 2. Of those that a mesh axis runs over, the one named last changes fastest.
Arguments:
- source_table: float32 [8192, 400], P('bucket'), may hold values from -6 to 6
- target_table: float32 [8192, 400], P('bucket'), may hold values from -6 to 6
- source_state: float32 [8192], P('bucket'), may hold values from 0.001 to 0.03
- target_state: float32 [8192], P('bucket'), may hold values from 0.001 to 0.03
- relation: float32 [16, 400], replicated, may hold values from -3 to 3
- relation_state: float32 [16], replicated, may hold values from 10 to 1000
- plan: int32 [8], replicated, may hold values from 0 to 7, each once
- source_index: int32 [8, 10240], P('bucket', 'span'), may hold values from 0 to 1023
- target_index: int32 [8, 10240], P('bucket', 'span'), may hold values from 0 to 1023
- relation_index: int32 [8, 10240], P('bucket', 'span'), may hold values from 0 to 15
- edge_counts: int32 [8], P('bucket'), may hold values from 1280 to 10240, as said below
Outputs:
- new_source: float32 [8192, 400], P('bucket')
- new_target: float32 [8192, 400], P('bucket')
- new_relation: float32 [16, 400], replicated
Inputs may be any that keep to these rules, and one draw needn't show every extreme that they name: `plan`: each partition index appears once. `edge_counts`: one bucket has exactly 10240 live slots and another exactly 1280.
All inputs are finite; a program needn't handle non-finite values.
Results may differ from a plain program's by a relative error of at most 0.0028.
The roundings to bfloat16 on the way count: a program that leaves them out, or rounds other values in their place, can miss the bound.
Values may be sent and summed in bfloat16 or wider, within the bound.
No kernel may reach another device: no remote copies, remote signals or barrier semaphores. Data moves between devices by JAX's collectives and lax.ppermute only.
A program may use at most 64 MiB of HBM per device.

v0:
```python
import jax
import jax.numpy as jnp
from jax import lax
from jax.sharding import PartitionSpec as P

E_CH = 640


LEARN_RATE = 0.25
NEG_WEIGHT = 0.03125


def span_terms(head_rows, relation_rows, tail_rows, live_mask):
    half_width = head_rows.shape[1] // 2
    head_float = head_rows.astype(jnp.float32)
    head_real = head_float[:, :half_width]
    head_imag = head_float[:, half_width:]
    rel_real = relation_rows[:, :half_width]
    rel_imag = relation_rows[:, half_width:]
    query_rows = jnp.concatenate(
        [head_real * rel_real - head_imag * rel_imag, head_real * rel_imag + head_imag * rel_real],
        axis=1,
    ).astype(jnp.bfloat16)
    scores = lax.dot_general(
        query_rows, tail_rows, (((1,), (1,)), ((), ())), preferred_element_type=jnp.float32
    )
    diagonal = lax.broadcasted_iota(jnp.int32, scores.shape, 0) == lax.broadcasted_iota(
        jnp.int32, scores.shape, 1
    )
    weights = jnp.where(diagonal, -jax.nn.sigmoid(-scores), NEG_WEIGHT * jax.nn.sigmoid(scores))
    coefficients = (weights * live_mask[:, None] * live_mask[None, :]).astype(jnp.bfloat16)
    grad_query = jnp.dot(coefficients, tail_rows, preferred_element_type=jnp.float32)
    grad_tail = lax.dot_general(
        coefficients, query_rows, (((0,), (0,)), ((), ())), preferred_element_type=jnp.float32
    )
    query_real = grad_query[:, :half_width]
    query_imag = grad_query[:, half_width:]
    grad_head = jnp.concatenate(
        [
            query_real * rel_real + query_imag * rel_imag,
            query_imag * rel_real - query_real * rel_imag,
        ],
        axis=1,
    )
    grad_relation = jnp.concatenate(
        [
            query_real * head_real + query_imag * head_imag,
            query_imag * head_real - query_real * head_imag,
        ],
        axis=1,
    )
    return (grad_head, grad_relation, grad_tail)


def row_adagrad(weights, accumulated, gradient):
    summed = accumulated + jnp.mean(gradient * gradient, axis=1)
    return weights - LEARN_RATE * gradient / jnp.sqrt(summed)[:, None]


def route_blocks(row_block, selector):
    buckets = lax.axis_size("bucket")
    rows_total, feature_width = row_block.shape
    pieces = row_block.reshape(buckets, rows_total // buckets, feature_width)
    spread_out = lax.all_to_all(pieces, "bucket", split_axis=0, concat_axis=0, tiled=True)
    picker = (selector[:, None] == jnp.arange(buckets, dtype=jnp.int32)[None, :]).astype(
        jnp.float32
    )
    chosen = jnp.einsum("ij,jrd->ird", picker, spread_out, precision=lax.Precision.HIGHEST)
    arrived = lax.all_to_all(chosen, "bucket", split_axis=0, concat_axis=0, tiled=True)
    return arrived.reshape(rows_total, feature_width)


def per_device(
    source_table,
    target_table,
    source_state,
    target_state,
    relation,
    relation_state,
    plan,
    source_index,
    target_index,
    relation_index,
    edge_counts,
):
    num_buckets = lax.axis_size("bucket")
    num_lanes = lax.axis_size("span")
    lane_index = lax.axis_index("span")
    inverse = jnp.zeros_like(plan).at[plan].set(jnp.arange(num_buckets, dtype=jnp.int32))
    live_limit = edge_counts[0]
    table_rows, feature_width = source_table.shape
    spans_here = source_index.shape[1] // E_CH
    quarter = table_rows // num_lanes
    start_row = lane_index * quarter
    relation_count = relation.shape[0]
    relation_iota = jnp.arange(relation_count, dtype=jnp.int32)
    row_iota = jnp.arange(table_rows, dtype=jnp.int32)
    head_table = source_index.reshape(spans_here, E_CH)
    tail_table = target_index.reshape(spans_here, E_CH)
    kind_table = relation_index.reshape(spans_here, E_CH)
    starts = (lane_index * spans_here + jnp.arange(spans_here, dtype=jnp.int32)) * E_CH
    source_low = source_table.astype(jnp.bfloat16)
    own_rows = lax.dynamic_slice_in_dim(target_table, start_row, quarter, 0)
    target_low = lax.all_gather(
        route_blocks(own_rows, plan).astype(jnp.bfloat16), "span", axis=0, tiled=True
    )

    def add_span(position_now, carried):
        span_start = starts[position_now]

        def compute(values):
            source_grad, target_grad, rel_grad = values
            slots = span_start + jnp.arange(E_CH, dtype=jnp.int32)
            live_mask = (slots < live_limit).astype(jnp.float32)
            head_ids = lax.dynamic_index_in_dim(head_table, position_now, 0, keepdims=False)
            tail_ids = lax.dynamic_index_in_dim(tail_table, position_now, 0, keepdims=False)
            kind_ids = lax.dynamic_index_in_dim(kind_table, position_now, 0, keepdims=False)
            one_hot = (kind_ids[:, None] == relation_iota[None, :]).astype(jnp.float32)
            relation_rows = jnp.dot(one_hot, relation, precision=lax.Precision.HIGHEST)
            head_match = head_ids[:, None] == row_iota[None, :]
            tail_match = tail_ids[:, None] == row_iota[None, :]
            head_rows = jnp.dot(
                head_match.astype(jnp.bfloat16), source_low, preferred_element_type=jnp.float32
            ).astype(jnp.bfloat16)
            tail_rows = jnp.dot(
                tail_match.astype(jnp.bfloat16), target_low, preferred_element_type=jnp.float32
            ).astype(jnp.bfloat16)
            grad_head, grad_relation, grad_tail = span_terms(
                head_rows, relation_rows, tail_rows, live_mask
            )
            rel_add = lax.dot_general(
                one_hot, grad_relation, (((0,), (0,)), ((), ())), precision=lax.Precision.HIGHEST
            )
            head_add = lax.dot_general(
                head_match.astype(jnp.float32),
                grad_head,
                (((0,), (0,)), ((), ())),
                precision=lax.Precision.HIGHEST,
            )
            tail_add = lax.dot_general(
                tail_match.astype(jnp.float32),
                grad_tail,
                (((0,), (0,)), ((), ())),
                precision=lax.Precision.HIGHEST,
            )
            return (source_grad + head_add, target_grad + tail_add, rel_grad + rel_add)

        def keep_values(values):
            return values

        return lax.cond(span_start < live_limit, compute, keep_values, carried)

    start_values = (
        jnp.zeros((table_rows, feature_width), jnp.float32),
        jnp.zeros((table_rows, feature_width), jnp.float32),
        jnp.zeros((relation_count, feature_width), jnp.float32),
    )
    source_grad, target_grad, rel_grad = lax.fori_loop(0, spans_here, add_span, start_values)
    rel_total = lax.psum(rel_grad, ("bucket", "span"))
    new_relation = row_adagrad(relation, relation_state, rel_total)
    source_part, target_part = (
        lax.psum_scatter(source_grad, "span", scatter_dimension=0, tiled=True),
        lax.psum_scatter(target_grad, "span", scatter_dimension=0, tiled=True),
    )
    target_home = route_blocks(target_part, inverse)
    source_slice = lax.dynamic_slice_in_dim(source_table, start_row, quarter, 0)
    source_slice_state = lax.dynamic_slice_in_dim(source_state, start_row, quarter, 0)
    target_slice = lax.dynamic_slice_in_dim(target_table, start_row, quarter, 0)
    target_slice_state = lax.dynamic_slice_in_dim(target_state, start_row, quarter, 0)
    updated_source = row_adagrad(source_slice, source_slice_state, source_part)
    updated_target = row_adagrad(target_slice, target_slice_state, target_home)
    new_source, new_target = (
        lax.all_gather(updated_source, "span", axis=0, tiled=True),
        lax.all_gather(updated_target, "span", axis=0, tiled=True),
    )
    return (new_source, new_target, new_relation)


def solution(mesh):
    placed = (
        P("bucket", None),
        P("bucket", None),
        P("bucket"),
        P("bucket"),
        P(),
        P(),
        P(),
        P("bucket", "span"),
        P("bucket", "span"),
        P("bucket", "span"),
        P("bucket"),
    )
    return jax.shard_map(
        per_device,
        mesh=mesh,
        in_specs=placed,
        out_specs=(P("bucket", None), P("bucket", None), P()),
        check_vma=False,
    )
```

profile of v0, /device:TPU:0, one launch (start us, length us, event | category | flops | bytes accessed | tf_op | source)
XLA Modules:
  0.0 308.9 jit_solution(257258483722769685)
XLA Ops:
  7.2 1.4 copy-done
  8.9 14.8 %all_to_all.20 = f32[8,32,400]{2,1,0:T(8,128)S(1)} all-to-all(f32[8,32,400]{2,1,0:T(8,128)S(1)} %bitcast.26), channel_id=1, replica_groups=mesh['bucket'=8,'span'=4] {'bucket'}, dimensions={0} | all-to-all | bytes 819200 | tf_op jit(solution)/shard_map/all_to_all | solution.py:64
  25.2 3.4 %all-to-all-start.1 = ((bf16[8,32,400]{2,1,0:T(8,128)(2,1)}), bf16[8,32,400]{2,1,0:T(8,128)(2,1)S(1)}, u32[]{:S(2)}, u32[]{:S(2)}) async-start(bf16[8,32,400]{2,1,0:T(8,128)(2,1)} %copy.45), calls=%async_computation.1 | async-start | bytes 524288 | tf_op jit(solution)/shard_map/all_to_all | solution.py:69
  28.8 2.4 copy.42
  31.3 4.2 %all-to-all-done.1 = bf16[8,32,400]{2,1,0:T(8,128)(2,1)S(1)} async-done(((bf16[8,32,400]{2,1,0:T(8,128)(2,1)}), bf16[8,32,400]{2,1,0:T(8,128)(2,1)S(1)}, u32[]{:S(2)}, u32[]{:S(2)}) %all-to-all-start.1) | async-done | bytes 204832 | tf_op jit(solution)/shard_map/all_to_all | solution.py:69
  35.5 23.2 %all_gather.9 = bf16[1024,400]{1,0:T(8,128)(2,1)} all-gather(bf16[256,400]{1,0:T(8,128)(2,1)S(1)} %bitcast.27), channel_id=1, replica_groups=mesh['bucket'=8,'span'=4] {'span'}, dimensions={0}, use_global_device_ids=true | all-gather | bytes 1024000 | tf_op jit(solution)/shard_map/all_gather | solution.py:104
  58.9 1.4 broadcast.61
  60.3 71.6 %while.19 = (s32[]{:T(128)}, f32[1024,400]{0,1:T(8,128)}, f32[1024,400]{0,1:T(8,128)S(1)}, f32[16,400]{1,0:T(8,128)S(1)}, s32[4]{0:T(128)S(1)}, /*index=5*/s32[]...) while((s32[]{:T(128)}, f32[1024,400]{0,1:T(8,128)}, ...), condition=%wide.region_3.4_spmd.clone.clone, body=%wide.region_0.3_spmd.clone.clone.sunk | while | flops 8435658752 | bytes 31468124 | solution.py:158
  62.1 16.1 %conditional.4 = ((f32[1024,400]{0,1:T(8,128)}, f32[1024,400]{0,1:T(8,128)S(1)}, f32[16,400]{1,0:T(8,128)S(1)})) conditional(s32[]{:T(128)} %convert_element_type.60, (f32[1024,400]{0,1:T(8,128)}, f32[1024,400]{0,1:T(8,128)S(1)}, f32[16,400]{1,0:T(8,128)S(1)}) %tuple.62, (s32[]{:T(128)}, s32[4,640]{1,0:T(4,128)S(1)}, s32[1024]{0:T(1024)S(1)}, ...), branch_computations={%region_1.1_spmd, %region_2.0_spmd} | conditional | flops 8435658752 | bytes 31463662 | solution.py:151
  62.1 2.3 fusion.32
  64.5 1.0 fusion.29
  65.4 1.2 fusion.49
  67.5 0.9 multiply_convert_fusion
  70.7 2.6 fusion.15
  73.3 4.8 %fusion.12 = f32[1024,400]{0,1:T(8,128)} fusion(f32[1024,400]{0,1:T(8,128)} %get-tuple-element.256, s32[1024]{0:T(1024)S(1)} %get-tuple-element.265, s32[640]{0:T(1024)S(1)} %dynamic-slice_reduce_fusion.2, f32[640,200]{0,1:T(8,128)S(1)} %get-tuple-element.406, f32[640,200]{0,1:T(8,128)S(1)} %get-tuple-element.407), kind=kOutput, calls=%fused_computation.13 | convolution fusion | flops 3147048960 | bytes 4307456 | tf_op jit(solution)/shard_map/while/body/eval_jaxpr/cond/branch_1_fun/dot_general | solution.py:134
  80.0 16.1 %conditional.4 = ((f32[1024,400]{0,1:T(8,128)}, f32[1024,400]{0,1:T(8,128)S(1)}, f32[16,400]{1,0:T(8,128)S(1)})) conditional(s32[]{:T(128)} %convert_element_type.60, (f32[1024,400]{0,1:T(8,128)}, f32[1024,400]{0,1:T(8,128)S(1)}, f32[16,400]{1,0:T(8,128)S(1)}) %tuple.62, (s32[]{:T(128)}, s32[4,640]{1,0:T(4,128)S(1)}, s32[1024]{0:T(1024)S(1)}, ...), branch_computations={%region_1.1_spmd, %region_2.0_spmd} | conditional | flops 8435658752 | bytes 31463662 | solution.py:151
  80.0 2.3 fusion.32
  82.4 0.9 fusion.29
  83.3 1.2 fusion.49
  85.4 0.9 multiply_convert_fusion
  88.6 2.6 fusion.15
  91.2 4.8 %fusion.12 = f32[1024,400]{0,1:T(8,128)} fusion(f32[1024,400]{0,1:T(8,128)} %get-tuple-element.256, s32[1024]{0:T(1024)S(1)} %get-tuple-element.265, s32[640]{0:T(1024)S(1)} %dynamic-slice_reduce_fusion.2, f32[640,200]{0,1:T(8,128)S(1)} %get-tuple-element.406, f32[640,200]{0,1:T(8,128)S(1)} %get-tuple-element.407), kind=kOutput, calls=%fused_computation.13 | convolution fusion | flops 3147048960 | bytes 4307456 | tf_op jit(solution)/shard_map/while/body/eval_jaxpr/cond/branch_1_fun/dot_general | solution.py:134
  97.9 16.1 %conditional.4 = ((f32[1024,400]{0,1:T(8,128)}, f32[1024,400]{0,1:T(8,128)S(1)}, f32[16,400]{1,0:T(8,128)S(1)})) conditional(s32[]{:T(128)} %convert_element_type.60, (f32[1024,400]{0,1:T(8,128)}, f32[1024,400]{0,1:T(8,128)S(1)}, f32[16,400]{1,0:T(8,128)S(1)}) %tuple.62, (s32[]{:T(128)}, s32[4,640]{1,0:T(4,128)S(1)}, s32[1024]{0:T(1024)S(1)}, ...), branch_computations={%region_1.1_spmd, %region_2.0_spmd} | conditional | flops 8435658752 | bytes 31463662 | solution.py:151
  98.0 2.3 fusion.32
  100.3 0.9 fusion.29
  101.2 1.2 fusion.49
  103.3 0.9 multiply_convert_fusion
  106.5 2.6 fusion.15
  109.1 4.8 %fusion.12 = f32[1024,400]{0,1:T(8,128)} fusion(f32[1024,400]{0,1:T(8,128)} %get-tuple-element.256, s32[1024]{0:T(1024)S(1)} %get-tuple-element.265, s32[640]{0:T(1024)S(1)} %dynamic-slice_reduce_fusion.2, f32[640,200]{0,1:T(8,128)S(1)} %get-tuple-element.406, f32[640,200]{0,1:T(8,128)S(1)} %get-tuple-element.407), kind=kOutput, calls=%fused_computation.13 | convolution fusion | flops 3147048960 | bytes 4307456 | tf_op jit(solution)/shard_map/while/body/eval_jaxpr/cond/branch_1_fun/dot_general | solution.py:134
  115.8 16.1 %conditional.4 = ((f32[1024,400]{0,1:T(8,128)}, f32[1024,400]{0,1:T(8,128)S(1)}, f32[16,400]{1,0:T(8,128)S(1)})) conditional(s32[]{:T(128)} %convert_element_type.60, (f32[1024,400]{0,1:T(8,128)}, f32[1024,400]{0,1:T(8,128)S(1)}, f32[16,400]{1,0:T(8,128)S(1)}) %tuple.62, (s32[]{:T(128)}, s32[4,640]{1,0:T(4,128)S(1)}, s32[1024]{0:T(1024)S(1)}, ...), branch_computations={%region_1.1_spmd, %region_2.0_spmd} | conditional | flops 8435658752 | bytes 31463662 | solution.py:151
  115.9 2.3 fusion.32
  118.2 0.9 fusion.29
  119.1 1.2 fusion.49
  121.2 0.9 multiply_convert_fusion
  124.4 2.6 fusion.15
  127.0 4.8 %fusion.12 = f32[1024,400]{0,1:T(8,128)} fusion(f32[1024,400]{0,1:T(8,128)} %get-tuple-element.256, s32[1024]{0:T(1024)S(1)} %get-tuple-element.265, s32[640]{0:T(1024)S(1)} %dynamic-slice_reduce_fusion.2, f32[640,200]{0,1:T(8,128)S(1)} %get-tuple-element.406, f32[640,200]{0,1:T(8,128)S(1)} %get-tuple-element.407), kind=kOutput, calls=%fused_computation.13 | convolution fusion | flops 3147048960 | bytes 4307456 | tf_op jit(solution)/shard_map/while/body/eval_jaxpr/cond/branch_1_fun/dot_general | solution.py:134
  132.1 1.9 copy.46
  134.1 32.3 %reduce-scatter.3.cloned.1.call-done = f32[256,400]{0,1:T(8,128)} async-done(((f32[1024,400]{0,1:T(8,128)}), f32[256,400]{0,1:T(8,128)}) %reduce-scatter.3.cloned.1.call-update) | async-done | bytes 409616 | tf_op jit(solution)/shard_map/reduce_scatter | solution.py:162
  166.4 1.1 multiply_reduce_fusion.1
  168.2 1.9 divide_subtract_fusion
  170.2 41.5 %reduce-scatter.5.cloned.1.call-done = f32[256,400]{1,0:T(8,128)} async-done(((f32[1024,400]{1,0:T(8,128)}), f32[256,400]{1,0:T(8,128)}) %reduce-scatter.5.cloned.1.call-update) | async-done | bytes 409616 | tf_op jit(solution)/shard_map/reduce_scatter | solution.py:163
  211.7 3.6 %all-to-all-start.2 = ((f32[8,32,400]{2,1,0:T(8,128)}), f32[8,32,400]{2,1,0:T(8,128)S(1)}, u32[]{:S(2)}, u32[]{:S(2)}) async-start(f32[8,32,400]{2,1,0:T(8,128)} %bitcast.28), calls=%async_computation.4 | async-start | bytes 1048576 | tf_op jit(solution)/shard_map/all_to_all | solution.py:64
  216.0 9.1 %all-to-all-done.2 = f32[8,32,400]{2,1,0:T(8,128)S(1)} async-done(((f32[8,32,400]{2,1,0:T(8,128)}), f32[8,32,400]{2,1,0:T(8,128)S(1)}, u32[]{:S(2)}, u32[]{:S(2)}) %all-to-all-start.2) | async-done | bytes 409632 | tf_op jit(solution)/shard_map/all_to_all | solution.py:64
  226.1 12.2 %all_to_all.21 = f32[8,32,400]{2,1,0:T(8,128)S(1)} all-to-all(f32[8,32,400]{2,1,0:T(8,128)S(1)} %copy.48), channel_id=1, replica_groups=mesh['bucket'=8,'span'=4] {'bucket'}, dimensions={0} | all-to-all | bytes 819200 | tf_op jit(solution)/shard_map/all_to_all | solution.py:69
  240.2 40.4 %psum.7 = f32[16,400]{1,0:T(8,128)S(1)} all-reduce(f32[16,400]{1,0:T(8,128)S(1)} %get-tuple-element.298), channel_id=1, replica_groups=mesh['bucket'=8,'span'=4] {'bucket','span'}, use_global_device_ids=true, to_apply=%region_9.10 | all-reduce | flops 6400 | bytes 51200 | tf_op jit(solution)/shard_map/psum | solution.py:159
  281.4 17.0 %all-gather.5.cloned.1.call-done = f32[1024,400]{1,0:T(8,128)} async-done(((f32[256,400]{1,0:T(8,128)}), f32[1024,400]{1,0:T(8,128)}) %all-gather.5.cloned.1.call-update) | async-done | bytes 1638416 | tf_op jit(solution)/shard_map/all_gather | solution.py:174
  298.4 2.7 copy.51
  301.2 1.2 copy.77
  (107 shorter events, 22.7 us)
Async XLA Ops:
  7.2 1.4 copy-start
  7.2 16.6 %copy-start.9 = (s32[8]{0:T(128)S(1)}, s32[8]{0:T(128)}, u32[]{:S(2)}) copy-start(s32[8]{0:T(128)} %param.21) | copy-start | bytes 100
  8.8 22.4 %copy-start.1 = (f32[256,400]{1,0:T(8,128)}, f32[256,400]{1,0:T(8,128)S(1)}, u32[]{:S(2)}) copy-start(f32[256,400]{1,0:T(8,128)S(1)} %copy.53) | copy-start | bytes 1228804
  8.8 19.8 %copy-start.6 = (s32[1,2560]{1,0:T(1,128)S(1)}, s32[1,2560]{1,0:T(1,128)}, u32[]{:S(2)}) copy-start(s32[1,2560]{1,0:T(1,128)} %param.22) | copy-start | bytes 30724
  8.9 19.9 %copy-start.7 = (s32[1,2560]{1,0:T(1,128)S(1)}, s32[1,2560]{1,0:T(1,128)}, u32[]{:S(2)}) copy-start(s32[1,2560]{1,0:T(1,128)} %param.23) | copy-start | bytes 30724
  8.9 19.9 %copy-start.8 = (s32[1,2560]{1,0:T(1,128)S(1)}, s32[1,2560]{1,0:T(1,128)}, u32[]{:S(2)}) copy-start(s32[1,2560]{1,0:T(1,128)} %param.24) | copy-start | bytes 30724
  25.2 10.3 %all-to-all-start.1 = ((bf16[8,32,400]{2,1,0:T(8,128)(2,1)}), bf16[8,32,400]{2,1,0:T(8,128)(2,1)S(1)}, u32[]{:S(2)}, u32[]{:S(2)}) async-start(bf16[8,32,400]{2,1,0:T(8,128)(2,1)} %copy.45), calls=%async_computation.1 | async-start | bytes 524288 | tf_op jit(solution)/shard_map/all_to_all | solution.py:69
  28.6 137.8 %reduce-scatter.3.cloned.1.call-start = ((), (), s32[]{:S(2)}) async-start(), calls=%async_computation.6 | async-start | bytes 2048000 | tf_op jit(solution)/shard_map/reduce_scatter | solution.py:162
  58.7 1.6 copy-start.4
  62.1 2.3 copy-start.5
  80.0 2.3 copy-start.5
  97.9 2.3 copy-start.5
  115.8 2.3 copy-start.5
  131.9 79.8 %reduce-scatter.5.cloned.1.call-start = ((), (), s32[]{:S(2)}) async-start(), calls=%async_computation.8 | async-start | bytes 2621440 | tf_op jit(solution)/shard_map/reduce_scatter | solution.py:163
  134.0 147.4 %all-gather.3.cloned.1.call-start = ((), (), s32[]{:S(2)}) async-start(), calls=%async_computation.7 | async-start | bytes 2048000 | tf_op jit(solution)/shard_map/all_gather | solution.py:173
  211.7 13.4 %all-to-all-start.2 = ((f32[8,32,400]{2,1,0:T(8,128)}), f32[8,32,400]{2,1,0:T(8,128)S(1)}, u32[]{:S(2)}, u32[]{:S(2)}) async-start(f32[8,32,400]{2,1,0:T(8,128)} %bitcast.28), calls=%async_computation.4 | async-start | bytes 1048576 | tf_op jit(solution)/shard_map/all_to_all | solution.py:64
  215.3 83.1 %all-gather.5.cloned.1.call-start = ((), (), s32[]{:S(2)}) async-start(), calls=%async_computation.9 | async-start | bytes 2621440 | tf_op jit(solution)/shard_map/all_gather | solution.py:174
  225.7 13.5 %copy-start.2 = (f32[256,400]{1,0:T(8,128)S(1)}, f32[256,400]{1,0:T(8,128)}, u32[]{:S(2)}) copy-start(f32[256,400]{1,0:T(8,128)} %copy-done.1) | copy-start | bytes 1228804
  238.2 42.5 %copy-start.10 = (f32[16]{0:T(128)S(1)}, f32[16]{0:T(128)}, u32[]{:S(2)}) copy-start(f32[16]{0:T(128)} %param.20) | copy-start | bytes 196
  281.4 19.8 %copy-start.3 = (f32[1024,400]{0,1:T(8,128)S(1)}, f32[1024,400]{0,1:T(8,128)}, u32[]{:S(2)}) copy-start(f32[1024,400]{0,1:T(8,128)} %all-gather.3.cloned.1.call-done) | copy-start | bytes 4915204
Sparse Core Ops, SparseCore 0:
  132.0 34.3 reduce-scatter.2
  168.8 42.8 reduce-scatter.4
  213.8 37.4 all-gather.2
  253.4 45.0 all-gather.4
where the time goes:
time: 310 us; the launch traced here: 309 us
  waiting for transfers between devices  104 us (34%)
  blocking collectives  90.6 us (29%)
  matrix products  58.7 us (19%)
  local copies, waits for them, and re-layouts  15.7 us (5%)
  between operations  14 us (5%)
  other arithmetic  12.8 us (4%)
  starting transfers between devices  7.4 us (2%)
  loops' own time  5.37 us (2%)
    reduce_scatter x1, waiting for transfers between devices, per_device(): lax.psum_scatter(target_grad, 'span', scatter_dimension=0, tiled=True)  41.5 us
    psum x1, blocking collectives, per_device(): rel_total = lax.psum(rel_grad, ('bucket', 'span'))  40.4 us
    reduce_scatter x1, waiting for transfers between devices, per_device(): lax.psum_scatter(source_grad, 'span', scatter_dimension=0, tiled=True)  32.3 us
    all_gather x1, blocking collectives, per_device(): lax.all_gather(route_blocks(own_rows, plan).astype(jnp.bfloat16), 'span',...  23.2 us
    dot_general x4, matrix products, compute(): lax.dot_general(head_match.astype(jnp.float32), grad_head, (((0,), (0,)),...  19.4 us
    all_gather x1, waiting for transfers between devices, per_device(): lax.all_gather(updated_target, 'span', axis=0, tiled=True)  17 us
    all_to_all x1, blocking collectives, route_blocks(): lax.all_to_all(pieces, 'bucket', split_axis=0, concat_axis=0, tiled=True)  14.8 us
    all_to_all x1, blocking collectives, route_blocks(): lax.all_to_all(chosen, 'bucket', split_axis=0, concat_axis=0, tiled=True)  12.2 us
  transfers between devices with their start and end apart: 6, of which 5 were waited for; matrix products, arithmetic and copies ran while one was open for 4% of the time, Pallas kernels for 0%

commit v1 on v0

v1 whole, which is shorter than its diff:
```python
import functools

import jax
import jax.numpy as jnp
from jax import lax
from jax.experimental import pallas as pl
from jax.experimental.pallas import tpu as pltpu
from jax.sharding import PartitionSpec as P

E_CH = 640
LEARN_RATE = 0.25
NEG_WEIGHT = 0.03125

F32 = jnp.float32
BF16 = jnp.bfloat16
VMEM_BYTES = 56 * 1024 * 1024
SMEM_SPEC = pl.BlockSpec(memory_space=pltpu.SMEM)


def params():
    return pltpu.CompilerParams(vmem_limit_bytes=VMEM_BYTES)


def dot_nn(a, b):
    return lax.dot_general(a, b, (((1,), (0,)), ((), ())), preferred_element_type=F32)


def dot_nt(a, b):
    return lax.dot_general(a, b, (((1,), (1,)), ((), ())), preferred_element_type=F32)


def dot_tn(a, b):
    return lax.dot_general(a, b, (((0,), (0,)), ((), ())), preferred_element_type=F32)


def live_ids(ids, meta_ref, step, steps):
    width = ids.shape[1]
    start = (meta_ref[1] * steps + step) * width
    slots = start + lax.broadcasted_iota(jnp.int32, ids.shape, 1)
    return jnp.where(slots < meta_ref[0], ids, -1)


def is_live(meta_ref, step, steps, width):
    return (meta_ref[1] * steps + step) * width < meta_ref[0]


def one_hot(ids, rows):
    match = lax.broadcasted_iota(jnp.int32, (rows, ids.shape[1]), 0) == ids
    return jnp.where(match, 1.0, 0.0).astype(BF16)


def relation_columns(rel_ref, kind):
    rel = rel_ref[...]
    high = rel.astype(BF16)
    rest = rel - high.astype(F32)
    middle = rest.astype(BF16)
    low = (rest - middle.astype(F32)).astype(BF16)
    parts = jnp.concatenate([high.astype(F32), middle.astype(F32), low.astype(F32)], axis=0)
    hot = jnp.concatenate([kind, kind, kind], axis=0)
    return dot_tn(parts.astype(BF16), hot.astype(BF16))


def kind_hot(ids, count):
    match = lax.broadcasted_iota(jnp.int32, (count, ids.shape[1]), 0) == ids
    return jnp.where(match, 1.0, 0.0)


def prep_kernel(steps, meta_ref, hid_ref, rid_ref, src_ref, rel_ref, q_ref, head_ref, low_ref):
    step = pl.program_id(0)

    @pl.when(step == 0)
    def _():
        low_ref[...] = src_ref[...].astype(BF16)

    @pl.when(is_live(meta_ref, step, steps, hid_ref.shape[2]))
    def _():
        ids = live_ids(hid_ref[0], meta_ref, step, steps)
        kinds = live_ids(rid_ref[0], meta_ref, step, steps)
        head = dot_nn(low_ref[...], one_hot(ids, low_ref.shape[1]))
        rel = relation_columns(rel_ref, kind_hot(kinds, rel_ref.shape[0]))
        half = head.shape[0] // 2
        h_re, h_im, r_re, r_im = head[:half], head[half:], rel[:half], rel[half:]
        query = jnp.concatenate([h_re * r_re - h_im * r_im, h_re * r_im + h_im * r_re], axis=0)
        q_ref[0] = query.astype(BF16)
        head_ref[0] = head.astype(BF16)


def assemble(lane, parts, out_ref):
    total = len(parts)
    pieces, block, width = parts[0].shape
    for at in range(total):

        @pl.when(lane == at)
        def _():
            for k in range(total):
                row = ((at - k) % total) * block
                for b in range(pieces):
                    out_ref[row : row + block, b * width : (b + 1) * width] = parts[k][b].astype(F32)


def emit(lane, acc_ref, outs):
    total = len(outs)
    pieces, block, width = outs[0].shape
    for at in range(total):

        @pl.when(lane == at)
        def _():
            for k in range(total):
                row = ((at + k) % total) * block
                for b in range(pieces):
                    outs[k][b] = acc_ref[row : row + block, b * width : (b + 1) * width].astype(
                        outs[k].dtype
                    )


def target_kernel(steps, lanes, meta_ref, tid_ref, q_ref, *refs):
    parts = refs[:lanes]
    tail_ref, coef_ref = refs[lanes : lanes + 2]
    outs = refs[lanes + 2 : 2 * lanes + 2]
    wide_ref, table_ref, acc_ref, hot_ref = refs[2 * lanes + 2 :]
    step = pl.program_id(0)

    @pl.when(step == 0)
    def _():
        assemble(meta_ref[1], parts, wide_ref)
        table_ref[...] = wide_ref[...].astype(BF16)
        acc_ref[...] = jnp.zeros_like(acc_ref)

    @pl.when(is_live(meta_ref, step, steps, tid_ref.shape[2]))
    def _():
        ids = live_ids(tid_ref[0], meta_ref, step, steps)
        hot_ref[...] = one_hot(ids, table_ref.shape[1])
        tail = dot_nn(table_ref[...], hot_ref[...]).astype(BF16)
        tail_ref[0] = tail
        scores = dot_tn(q_ref[0], tail)
        sig = 0.5 * jnp.tanh(0.5 * scores) + 0.5
        diagonal = lax.broadcasted_iota(jnp.int32, scores.shape, 0) == lax.broadcasted_iota(
            jnp.int32, scores.shape, 1
        )
        coef_ref[0] = jnp.where(diagonal, sig - 1.0, NEG_WEIGHT * sig).astype(BF16)
        grad_tail = dot_nn(q_ref[0], coef_ref[0])
        acc_ref[...] += dot_nt(grad_tail.astype(BF16), hot_ref[...])

    @pl.when(step == steps - 1)
    def _():
        emit(meta_ref[1], acc_ref, outs)


def source_kernel(steps, lanes, meta_ref, hid_ref, rid_ref, rel_ref, head_ref, tail_ref, coef_ref, *refs):
    outs = refs[:lanes]
    rel_out_ref, acc_ref = refs[lanes:]
    step = pl.program_id(0)

    @pl.when(step == 0)
    def _():
        acc_ref[...] = jnp.zeros_like(acc_ref)
        rel_out_ref[...] = jnp.zeros_like(rel_out_ref)

    @pl.when(is_live(meta_ref, step, steps, hid_ref.shape[2]))
    def _():
        ids = live_ids(hid_ref[0], meta_ref, step, steps)
        kinds = live_ids(rid_ref[0], meta_ref, step, steps)
        kind = kind_hot(kinds, rel_ref.shape[0])
        rel = relation_columns(rel_ref, kind)
        head = head_ref[0].astype(F32)
        half = head.shape[0] // 2
        h_re, h_im, r_re, r_im = head[:half], head[half:], rel[:half], rel[half:]
        grad_query = dot_nt(tail_ref[0], coef_ref[0])
        g_re, g_im = grad_query[:half], grad_query[half:]
        grad_head = jnp.concatenate([g_re * r_re + g_im * r_im, g_im * r_re - g_re * r_im], axis=0)
        acc_ref[...] += dot_nt(grad_head.astype(BF16), one_hot(ids, acc_ref.shape[1]))
        grad_rel = jnp.concatenate([g_re * h_re + g_im * h_im, g_im * h_re - g_re * h_im], axis=0)
        high = grad_rel.astype(BF16)
        low = (grad_rel - high.astype(F32)).astype(BF16)
        kind = kind.astype(BF16)
        rel_out_ref[...] += dot_nt(kind, high) + dot_nt(kind, low)

    @pl.when(step == steps - 1)
    def _():
        emit(meta_ref[1], acc_ref, outs)


def sum_kernel(*refs):
    total = refs[0][...]
    for ref in refs[1:-1]:
        total = total + ref[...].astype(F32)
    refs[-1][...] = total.astype(BF16)


def pick_kernel(plan_ref, in_ref, out_ref):
    for b in range(in_ref.shape[0]):
        out_ref[b] = in_ref[plan_ref[b]]


def place_kernel(plan_ref, in_ref, out_ref):
    for b in range(in_ref.shape[0]):
        out_ref[plan_ref[b]] = in_ref[b]


def update_kernel(lanes, meta_ref, table_ref, state_ref, *refs):
    parts = refs[:lanes]
    out_ref, grad_ref = refs[lanes:]
    assemble(meta_ref[1], parts, grad_ref)
    grad = grad_ref[...]
    mean = jnp.sum(grad * grad, axis=0, keepdims=True) / grad.shape[0]
    scale = LEARN_RATE / jnp.sqrt(state_ref[...] + mean)
    out_ref[...] = table_ref[...] - grad * scale


def whole(shape):
    zeros = (0,) * len(shape)
    return pl.BlockSpec(tuple(shape), lambda i: zeros)


def per_span(shape):
    rest = (0,) * (len(shape) - 1)
    return pl.BlockSpec((1,) + tuple(shape[1:]), lambda i: (i,) + rest)


def shift_span(x, by):
    count = lax.axis_size("span")
    return lax.ppermute(x, "span", [(i, (i + by) % count) for i in range(count)])


def plain(kernel, out, *operands, smem=1):
    vmem = pl.BlockSpec(memory_space=pltpu.VMEM)
    return pl.pallas_call(
        kernel,
        out_shape=out,
        in_specs=[SMEM_SPEC] * smem + [vmem] * (len(operands) - smem),
        out_specs=vmem,
        compiler_params=params(),
    )(*operands)


def swap_buckets(x):
    return lax.all_to_all(x, "bucket", split_axis=0, concat_axis=0, tiled=True)


def update(meta, table, state, parts):
    lanes = len(parts)
    vmem = pl.BlockSpec(memory_space=pltpu.VMEM)
    return pl.pallas_call(
        functools.partial(update_kernel, lanes),
        out_shape=jax.ShapeDtypeStruct(table.shape, F32),
        in_specs=[SMEM_SPEC] + [vmem] * (lanes + 2),
        out_specs=vmem,
        scratch_shapes=[pltpu.VMEM(table.shape, F32)],
        compiler_params=params(),
    )(meta, table, state, *parts)


def sum_all(x):
    for axis in ("span", "bucket"):
        count = lax.axis_size(axis)
        if count & (count - 1):
            x = lax.psum(x, axis)
            continue
        bit = 1
        while bit < count:
            x = x + lax.ppermute(x, axis, [(i, i ^ bit) for i in range(count)])
            bit *= 2
    return x


def per_device(
    source_table,
    target_table,
    source_state,
    target_state,
    relation,
    relation_state,
    plan,
    source_index,
    target_index,
    relation_index,
    edge_counts,
):
    buckets = lax.axis_size("bucket")
    lanes = lax.axis_size("span")
    lane = lax.axis_index("span").astype(jnp.int32)
    rows, features = source_table.shape
    steps = source_index.shape[1] // E_CH
    kinds = relation.shape[0]
    block = features // lanes
    width = rows // buckets
    meta = jnp.stack([edge_counts[0], lane])
    hid = source_index.reshape(steps, 1, E_CH)
    tid = target_index.reshape(steps, 1, E_CH)
    rid = relation_index.reshape(steps, 1, E_CH)
    source_cols, target_cols = source_table.T, target_table.T

    own = lax.dynamic_slice_in_dim(target_cols, lane * block, block, 0).astype(BF16)
    pieces = own.reshape(block, buckets, width).transpose(1, 0, 2)
    piece_shape = jax.ShapeDtypeStruct(pieces.shape, BF16)
    spread = swap_buckets(pieces)
    chosen = plain(pick_kernel, piece_shape, plan, spread)
    fetched = swap_buckets(chosen)
    target_parts = [fetched] + [shift_span(fetched, k) for k in range(1, lanes)]

    edge_shape = (steps, features, E_CH)
    query, head = pl.pallas_call(
        functools.partial(prep_kernel, steps),
        grid=(steps,),
        out_shape=[jax.ShapeDtypeStruct(edge_shape, BF16)] * 2,
        in_specs=[
            SMEM_SPEC,
            per_span(hid.shape),
            per_span(rid.shape),
            whole(source_cols.shape),
            whole(relation.shape),
        ],
        out_specs=[per_span(edge_shape)] * 2,
        scratch_shapes=[pltpu.VMEM((features, rows), BF16)],
        compiler_params=params(),
    )(meta, hid, rid, source_cols, relation)

    out_pieces = [jax.ShapeDtypeStruct(pieces.shape, F32)] + [piece_shape] * (lanes - 1)
    coef_shape = (steps, E_CH, E_CH)
    tail, coef, *target_out = pl.pallas_call(
        functools.partial(target_kernel, steps, lanes),
        grid=(steps,),
        out_shape=[jax.ShapeDtypeStruct(edge_shape, BF16), jax.ShapeDtypeStruct(coef_shape, BF16)]
        + out_pieces,
        in_specs=[SMEM_SPEC, per_span(tid.shape), per_span(edge_shape)]
        + [whole(pieces.shape)] * lanes,
        out_specs=[per_span(edge_shape), per_span(coef_shape)] + [whole(pieces.shape)] * lanes,
        scratch_shapes=[
            pltpu.VMEM((features, rows), F32),
            pltpu.VMEM((features, rows), BF16),
            pltpu.VMEM((features, rows), F32),
            pltpu.VMEM((rows, E_CH), BF16),
        ],
        compiler_params=params(),
    )(meta, tid, query, *target_parts)

    target_in = [shift_span(target_out[k], k) for k in range(1, lanes)]
    *source_out, rel_part = pl.pallas_call(
        functools.partial(source_kernel, steps, lanes),
        grid=(steps,),
        out_shape=out_pieces + [jax.ShapeDtypeStruct(relation.shape, F32)],
        in_specs=[
            SMEM_SPEC,
            per_span(hid.shape),
            per_span(rid.shape),
            whole(relation.shape),
            per_span(edge_shape),
            per_span(edge_shape),
            per_span(coef_shape),
        ],
        out_specs=[whole(pieces.shape)] * lanes + [whole(relation.shape)],
        scratch_shapes=[pltpu.VMEM((features, rows), F32)],
        compiler_params=params(),
    )(meta, hid, rid, relation, head, tail, coef)

    target_sum = plain(sum_kernel, piece_shape, target_out[0], *target_in, smem=0)
    returned = swap_buckets(target_sum)
    sorted_out = plain(place_kernel, piece_shape, plan, returned)
    target_home = swap_buckets(sorted_out)
    source_in = [shift_span(source_out[k], k) for k in range(1, lanes)]
    source_sum = plain(sum_kernel, piece_shape, source_out[0], *source_in, smem=0)
    source_parts = [source_sum] + [shift_span(source_sum, k) for k in range(1, lanes)]
    home_parts = [target_home] + [shift_span(target_home, k) for k in range(1, lanes)]
    new_source = update(meta, source_cols, source_state.reshape(1, rows), source_parts)
    new_target = update(meta, target_cols, target_state.reshape(1, rows), home_parts)

    rel_total = sum_all(rel_part)
    rel_scale = LEARN_RATE / jnp.sqrt(relation_state + jnp.mean(rel_total * rel_total, axis=1))
    new_relation = relation - rel_total * rel_scale[:, None]
    return (new_source.T, new_target.T, new_relation)


def solution(mesh):
    placed = (
        P("bucket", None),
        P("bucket", None),
        P("bucket"),
        P("bucket"),
        P(),
        P(),
        P(),
        P("bucket", "span"),
        P("bucket", "span"),
        P("bucket", "span"),
        P("bucket"),
    )
    return jax.shard_map(
        per_device,
        mesh=mesh,
        in_specs=placed,
        out_specs=(P("bucket", None), P("bucket", None), P()),
        check_vma=False,
    )
```

time: 310 us -> 164 us (0.53)
  blocking collectives: 90.6 us -> 21.2 us
  matrix products: 58.7 us -> 0 us
  waiting for transfers between devices: 104 us -> 54.9 us
  Pallas kernels: 0 us -> 38.4 us
  starting transfers between devices: 7.4 us -> 39.1 us
  between operations: 14 us -> 1.47 us
  other arithmetic: 12.8 us -> 2.22 us
  local copies, waits for them, and re-layouts: 15.7 us -> 5.55 us
  loops' own time: 5.37 us -> 0 us
    reduce_scatter x2 -> x0, waiting for transfers between devices: 73.8 us -> none  [the longest x1 41.5 us: per_device(): lax.psum_scatter(target_grad, 'span', scatter_dimension=0, tiled=True)]
    dot_general x38 -> x0, matrix products: 58.7 us -> none  [the longest x4 19.4 us: compute(): lax.dot_general(head_match.astype(jnp.float32), grad_head, (((0,), (0,)),...]
    ppermute x0 -> x20, waiting for transfers between devices: none -> 50.2 us  [the longest x15 37.7 us: shift_span(): lax.ppermute(x, 'span', [(i, (i + by) % count) for i in range(count)])]
    psum x1 -> x0, blocking collectives: 40.4 us -> none  [per_device(): rel_total = lax.psum(rel_grad, ('bucket', 'span'))]
    pallas_call x0 -> x9, Pallas kernels: none -> 38.4 us  [the longest x1 10.2 us: per_device(): pl.pallas_call(functools.partial(target_kernel, steps, lanes), grid=(step...]
    ppermute x0 -> x20, starting transfers between devices: none -> 32.1 us  [the longest x15 21.6 us: shift_span(): lax.ppermute(x, 'span', [(i, (i + by) % count) for i in range(count)])]
    all_gather x1 -> x0, blocking collectives: 23.2 us -> none  [per_device(): lax.all_gather(route_blocks(own_rows, plan).astype(jnp.bfloat16), 'span',...]
    all_gather x2 -> x0, waiting for transfers between devices: 17 us -> none  [the longest x1 17 us: per_device(): lax.all_gather(updated_target, 'span', axis=0, tiled=True)]
  transfers between devices with their start and end apart: 6 -> 22, of which waited for: 5 -> 9; matrix products, arithmetic and copies ran while one was open for 4% -> 1% of each run, Pallas kernels for 0% -> 14%
where the time goes in v1:
time: 164 us; the launch traced here: 163 us
  waiting for transfers between devices  54.9 us (33%)
  starting transfers between devices  39.1 us (24%)
  Pallas kernels  38.4 us (23%)
  blocking collectives  21.2 us (13%)
  local copies, waits for them, and re-layouts  5.55 us (3%)
  other arithmetic  2.22 us (1%)
    ppermute x15, waiting for transfers between devices, shift_span(): lax.ppermute(x, 'span', [(i, (i + by) % count) for i in range(count)])  37.7 us
    ppermute x15, starting transfers between devices, shift_span(): lax.ppermute(x, 'span', [(i, (i + by) % count) for i in range(count)])  21.6 us
    all_to_all x2, blocking collectives, swap_buckets(): return lax.all_to_all(x, 'bucket', split_axis=0, concat_axis=0, tiled=True)  21.2 us
    ppermute x5, waiting for transfers between devices, sum_all(): x = x + lax.ppermute(x, axis, [(i, i ^ bit) for i in range(count)])  12.6 us
    ppermute x5, starting transfers between devices, sum_all(): x = x + lax.ppermute(x, axis, [(i, i ^ bit) for i in range(count)])  10.5 us
    pallas_call x1, Pallas kernels, per_device(): pl.pallas_call(functools.partial(target_kernel, steps, lanes), grid=(step...  10.2 us
    pallas_call x1, Pallas kernels, per_device(): pl.pallas_call(functools.partial(source_kernel, steps, lanes), grid=(step...  8.51 us
    pallas_call x4, Pallas kernels, plain(): pl.pallas_call(kernel, out_shape=out, in_specs=[SMEM_SPEC] * smem + [vmem...  7.31 us
  transfers between devices with their start and end apart: 22, of which 9 were waited for; matrix products, arithmetic and copies ran while one was open for 1% of the time, Pallas kernels for 14%

profile of v1, /device:TPU:0, one launch (start us, length us, event | category | flops | bytes accessed | tf_op | source)
XLA Modules:
  0.0 162.7 jit_solution(2572688709610387648)
XLA Ops:
  0.6 1.1 dynamic-slice_convert_fusion
  1.8 11.5 %all_to_all.20.in_ref = bf16[8,100,128]{2,1,0:T(8,128)(2,1)} all-to-all(bf16[8,100,128]{2,1,0:T(8,128)(2,1)S(1)} %bitcast.22), channel_id=1, replica_groups=mesh['bucket'=8,'span'=4] {'bucket'}, dimensions={0} | all-to-all | bytes 409600 | tf_op jit(solution)/shard_map/all_to_all | solution.py:237
  13.3 1.6 %shard_map.131 = bf16[8,100,128]{2,1,0:T(8,128)(2,1)} custom-call(s32[8]{0:T(128)} %plan_ref.3, bf16[8,100,128]{2,1,0:T(8,128)(2,1)} %all_to_all.20.in_ref), custom_call_target="tpu_custom_call" | custom-call | tf_op jit(solution)/shard_map/pallas_call | solution.py:227
  14.9 9.7 %all_to_all.21.refs_0_ = bf16[8,100,128]{2,1,0:T(8,128)(2,1)S(1)} all-to-all(bf16[8,100,128]{2,1,0:T(8,128)(2,1)} %shard_map.131), channel_id=1, replica_groups=mesh['bucket'=8,'span'=4] {'bucket'}, dimensions={0} | all-to-all | bytes 409600 | tf_op jit(solution)/shard_map/all_to_all | solution.py:237
  24.7 3.6 %collective-permute-start.2 = (bf16[8,100,128]{2,1,0:T(8,128)(2,1)S(1)}, bf16[8,100,128]{2,1,0:T(8,128)(2,1)S(1)}, u32[]{:S(2)}, u32[]{:S(2)}) collective-permute-start(bf16[8,100,128]{2,1,0:T(8,128)(2,1)S(1)} %all_to_all.21.refs_0_), channel_id=1, source_target_pairs={{0,3},{1,0},{2,1},{3,2},{4,7},{5,4},{6,5},{7,6},{8,11},{9,8},{10,9... | collective-permute-start | bytes 614408 | tf_op jit(solution)/shard_map/ppermute | solution.py:222
  28.2 1.0 collective-permute-start
  29.9 0.6 pad_add_fusion.meta_ref
  30.5 5.7 %shard_map.130 = (bf16[4,400,640]{2,1,0:T(8,128)(2,1)}, bf16[4,400,640]{2,1,0:T(8,128)(2,1)}) custom-call(s32[2]{0:T(128)} %pad_add_fusion.meta_ref, s32[4,1,640]{2,1,0:T(1,128)} %bitcast.25, s32[4,1,640]{2,1,0:T(1,128)} %bitcast.27, f32[400,1024]{1,0:T(8,128)} %bitcast.17, f32[16,400]{1,0:T(8,128)} %rel_ref.3), custom_call_target="tpu_custom_call" | custom-call | tf_op jit(solution)/shard_map/pallas_call | solution.py:302
  36.3 9.7 %collective-permute-done.1.refs_2_ = bf16[8,100,128]{2,1,0:T(8,128)(2,1)S(1)} collective-permute-done((bf16[8,100,128]{2,1,0:T(8,128)(2,1)S(1)}, bf16[8,100,128]{2,1,0:T(8,128)(2,1)S(1)}, u32[]{:S(2)}, u32[]{:S(2)}) %collective-permute-start.1) | collective-permute-done | bytes 204832 | tf_op jit(solution)/shard_map/ppermute | solution.py:222
  46.0 0.7 copy-done.16
  46.7 10.2 %shard_map.132 = (bf16[4,400,640]{2,1,0:T(8,128)(2,1)}, bf16[4,640,640]{2,1,0:T(8,128)(2,1)}, f32[8,100,128]{2,1,0:T(8,128)}, bf16[8,100,128]{2,1,0:T(8,128)(2,1...) custom-call(s32[2]{0:T(128)} %pad_add_fusion.meta_ref, s32[4,1,640]{2,1,0:T(1,128)} %bitcast.29, ...), custom_call_target="tpu_custom_call" | custom-call | tf_op jit(solution)/shard_map/pallas_call | solution.py:320
  57.1 3.7 %collective-permute-start.11 = (bf16[8,100,128]{2,1,0:T(8,128)(2,1)}, bf16[8,100,128]{2,1,0:T(8,128)(2,1)S(1)}, u32[]{:S(2)}, u32[]{:S(2)}) collective-permute-start(bf16[8,100,128]{2,1,0:T(8,128)(2,1)} %get-tuple-element.27), channel_id=1, source_target_pairs={{0,3},{1,0},{2,1},{3,2},{4,7},{5,4},{6,5},{7,6},{8,11},{9,8},{10,9... | collective-permute-start | bytes 614408 | tf_op jit(solution)/shard_map/ppermute | solution.py:222
  60.8 8.5 %shard_map.133 = (f32[8,100,128]{2,1,0:T(8,128)}, bf16[8,100,128]{2,1,0:T(8,128)(2,1)}, bf16[8,100,128]{2,1,0:T(8,128)(2,1)}, bf16[8,100,128]{2,1,0:T(8,128)(2,1)}, f32[16,400]{1,0:T(8,128)}) custom-call(s32[2]{0:T(128)} %pad_add_fusion.meta_ref, s32[4,1,640]{2,1,0:T(1,128)} %bitcast.26, s32[4,1,640]{2,1,0:T(1,128)} %bitcast.28, f32[16,400]{1,0:T(8,128)} %rel_ref.3, ...), custom_call_target="tpu_custom_call" | custom-call | tf_op jit(solution)/shard_map/pallas_call | solution.py:338
  69.4 5.7 %collective-permute-done.15 = f32[16,400]{1,0:T(8,128)S(1)} collective-permute-done((f32[16,400]{1,0:T(8,128)}, f32[16,400]{1,0:T(8,128)S(1)}, u32[]{:S(2)}, u32[]{:S(2)}) %collective-permute-start.15) | collective-permute-done | bytes 25632 | tf_op jit(solution)/shard_map/ppermute | solution.py:261
  75.0 0.8 add.22
  75.8 0.8 collective-permute-start.16
  76.6 4.1 %collective-permute-done.16 = f32[16,400]{1,0:T(8,128)S(1)} collective-permute-done((f32[16,400]{1,0:T(8,128)S(1)}, f32[16,400]{1,0:T(8,128)S(1)}, u32[]{:S(2)}, u32[]{:S(2)}) %collective-permute-start.16) | collective-permute-done | bytes 25632 | tf_op jit(solution)/shard_map/ppermute | solution.py:261
  80.8 3.1 %collective-permute-start.17 = (f32[16,400]{1,0:T(8,128)S(1)}, f32[16,400]{1,0:T(8,128)S(1)}, u32[]{:S(2)}, u32[]{:S(2)}) collective-permute-start(f32[16,400]{1,0:T(8,128)S(1)} %add.23), channel_id=1, source_target_pairs={{0,4},{4,0},{8,12},{12,8},{16,20},{20,16},{24,28},{28,24},{1,5},{5... | collective-permute-start | bytes 76808 | tf_op jit(solution)/shard_map/ppermute | solution.py:261
  83.9 0.9 collective-permute-done.17
  84.8 3.1 %collective-permute-start.18 = (f32[16,400]{1,0:T(8,128)S(1)}, f32[16,400]{1,0:T(8,128)S(1)}, u32[]{:S(2)}, u32[]{:S(2)}) collective-permute-start(f32[16,400]{1,0:T(8,128)S(1)} %add.24), channel_id=1, source_target_pairs={{0,8},{4,12},{8,0},{12,4},{16,24},{20,28},{24,16},{28,20},{1,9},{5... | collective-permute-start | bytes 76808 | tf_op jit(solution)/shard_map/ppermute | solution.py:261
  87.8 1.9 %collective-permute-done.18 = f32[16,400]{1,0:T(8,128)S(1)} collective-permute-done((f32[16,400]{1,0:T(8,128)S(1)}, f32[16,400]{1,0:T(8,128)S(1)}, u32[]{:S(2)}, u32[]{:S(2)}) %collective-permute-start.18) | collective-permute-done | bytes 25632 | tf_op jit(solution)/shard_map/ppermute | solution.py:261
  89.7 3.5 %collective-permute-start.19 = (f32[16,400]{1,0:T(8,128)S(1)}, f32[16,400]{1,0:T(8,128)S(1)}, u32[]{:S(2)}, u32[]{:S(2)}) collective-permute-start(f32[16,400]{1,0:T(8,128)S(1)} %add.25), channel_id=1, source_target_pairs={{0,16},{4,20},{8,24},{12,28},{16,0},{20,4},{24,8},{28,12},{1,17},{... | collective-permute-start | bytes 76808 | tf_op jit(solution)/shard_map/ppermute | solution.py:261
  93.2 0.2 collective-permute-start.3
  93.4 2.1 %collective-permute-start.4 = (bf16[8,100,128]{2,1,0:T(8,128)(2,1)}, bf16[8,100,128]{2,1,0:T(8,128)(2,1)S(1)}, u32[]{:S(2)}, u32[]{:S(2)}) collective-permute-start(bf16[8,100,128]{2,1,0:T(8,128)(2,1)} %get-tuple-element.22), channel_id=1, source_target_pairs={{0,2},{1,3},{2,0},{3,1},{4,6},{5,7},{6,4},{7,5},{8,10},{9,11},{10,... | collective-permute-start | bytes 614408 | tf_op jit(solution)/shard_map/ppermute | solution.py:222
  95.5 1.6 collective-permute-start.5
  97.1 0.7 copy-done.6
  97.8 2.0 %shard_map.136 = bf16[8,100,128]{2,1,0:T(8,128)(2,1)} custom-call(f32[8,100,128]{2,1,0:T(8,128)} %get-tuple-element.24.refs_0_, bf16[8,100,128]{2,1,0:T(8,128)(2,1)} %copy-done.4, bf16[8,100,128]{2,1,0:T(8,128)(2,1)} %copy-done.5, bf16[8,100,128]{2,1,0:T(8,128)(2,1)} %copy-done.6), custom_call_target="tpu_custom_call" | custom-call | tf_op jit(solution)/shard_map/pallas_call | solution.py:227
  99.8 3.5 %all-to-all-start.2 = ((bf16[8,100,128]{2,1,0:T(8,128)(2,1)}), bf16[8,100,128]{2,1,0:T(8,128)(2,1)S(1)}, u32[]{:S(2)}, u32[]{:S(2)}) async-start(bf16[8,100,128]{2,1,0:T(8,128)(2,1)} %shard_map.136), calls=%async_computation.2 | async-start | bytes 425984 | tf_op jit(solution)/shard_map/all_to_all | solution.py:237
  103.3 0.1 multiply_reduce_fusion
  103.5 6.9 %collective-permute-done.4.refs_2_ = bf16[8,100,128]{2,1,0:T(8,128)(2,1)S(1)} collective-permute-done((bf16[8,100,128]{2,1,0:T(8,128)(2,1)}, bf16[8,100,128]{2,1,0:T(8,128)(2,1)S(1)}, u32[]{:S(2)}, u32[]{:S(2)}) %collective-permute-start.4) | collective-permute-done | bytes 204832 | tf_op jit(solution)/shard_map/ppermute | solution.py:222
  110.4 0.7 copy-done.8
  111.2 2.0 %shard_map.134.refs_0_ = bf16[8,100,128]{2,1,0:T(8,128)(2,1)} custom-call(f32[8,100,128]{2,1,0:T(8,128)} %get-tuple-element.20.refs_0_, bf16[8,100,128]{2,1,0:T(8,128)(2,1)} %copy-done.7, bf16[8,100,128]{2,1,0:T(8,128)(2,1)} %copy-done.8, bf16[8,100,128]{2,1,0:T(8,128)(2,1)} %copy-done.9), custom_call_target="tpu_custom_call" | custom-call | tf_op jit(solution)/shard_map/pallas_call | solution.py:227
  113.2 3.9 %collective-permute-start.8 = (bf16[8,100,128]{2,1,0:T(8,128)(2,1)}, bf16[8,100,128]{2,1,0:T(8,128)(2,1)S(1)}, u32[]{:S(2)}, u32[]{:S(2)}) collective-permute-start(bf16[8,100,128]{2,1,0:T(8,128)(2,1)} %shard_map.134.refs_0_), channel_id=1, source_target_pairs={{0,3},{1,0},{2,1},{3,2},{4,7},{5,4},{6,5},{7,6},{8,11},{9,8},{10,9... | collective-permute-start | bytes 614408 | tf_op jit(solution)/shard_map/ppermute | solution.py:222
  117.2 0.7 copy-done
  117.8 1.6 %shard_map.137 = bf16[8,100,128]{2,1,0:T(8,128)(2,1)} custom-call(s32[8]{0:T(128)} %plan_ref.3, bf16[8,100,128]{2,1,0:T(8,128)(2,1)} %copy-done), custom_call_target="tpu_custom_call" | custom-call | tf_op jit(solution)/shard_map/pallas_call | solution.py:227
  119.5 3.4 %all-to-all-start.3 = ((bf16[8,100,128]{2,1,0:T(8,128)(2,1)}), bf16[8,100,128]{2,1,0:T(8,128)(2,1)S(1)}, u32[]{:S(2)}, u32[]{:S(2)}) async-start(bf16[8,100,128]{2,1,0:T(8,128)(2,1)} %shard_map.137), calls=%async_computation.3 | async-start | bytes 425984 | tf_op jit(solution)/shard_map/all_to_all | solution.py:237
  122.9 1.7 %collective-permute-start.7 = (bf16[8,100,128]{2,1,0:T(8,128)(2,1)}, bf16[8,100,128]{2,1,0:T(8,128)(2,1)S(1)}, u32[]{:S(2)}, u32[]{:S(2)}) collective-permute-start(bf16[8,100,128]{2,1,0:T(8,128)(2,1)} %shard_map.134.refs_0_), channel_id=1, source_target_pairs={{0,2},{1,3},{2,0},{3,1},{4,6},{5,7},{6,4},{7,5},{8,10},{9,11},{10,... | collective-permute-start | bytes 614408 | tf_op jit(solution)/shard_map/ppermute | solution.py:222
  124.6 4.6 %all-to-all-done.3.refs_0_ = bf16[8,100,128]{2,1,0:T(8,128)(2,1)S(1)} async-done(((bf16[8,100,128]{2,1,0:T(8,128)(2,1)}), bf16[8,100,128]{2,1,0:T(8,128)(2,1)S(1)}, u32[]{:S(2)}, u32[]{:S(2)}) %all-to-all-start.3) | async-done | bytes 204832 | tf_op jit(solution)/shard_map/all_to_all | solution.py:237
  129.2 0.7 collective-permute-start.14
  129.9 0.9 collective-permute-start.13
  130.8 2.0 %collective-permute-start.12 = (bf16[8,100,128]{2,1,0:T(8,128)(2,1)S(1)}, bf16[8,100,128]{2,1,0:T(8,128)(2,1)S(1)}, u32[]{:S(2)}, u32[]{:S(2)}) collective-permute-start(bf16[8,100,128]{2,1,0:T(8,128)(2,1)S(1)} %all-to-all-done.3.refs_0_), channel_id=1, source_target_pairs={{0,1},{1,2},{2,3},{3,0},{4,5},{5,6},{6,7},{7,4},{8,9},{9,10},{10,1... | collective-permute-start | bytes 614408 | tf_op jit(solution)/shard_map/ppermute | solution.py:222
  132.9 0.7 multiply_subtract_fusion
  133.5 7.4 %collective-permute-done.7.refs_2_ = bf16[8,100,128]{2,1,0:T(8,128)(2,1)S(1)} collective-permute-done((bf16[8,100,128]{2,1,0:T(8,128)(2,1)}, bf16[8,100,128]{2,1,0:T(8,128)(2,1)S(1)}, u32[]{:S(2)}, u32[]{:S(2)}) %collective-permute-start.7) | collective-permute-done | bytes 204832 | tf_op jit(solution)/shard_map/ppermute | solution.py:222
  141.0 0.7 copy-done.12
  141.7 3.3 %shard_map.135 = f32[400,1024]{1,0:T(8,128)} custom-call(s32[2]{0:T(128)} %pad_add_fusion.meta_ref, f32[400,1024]{1,0:T(8,128)} %bitcast.18, f32[1,1024]{1,0:T(1,128)} %bitcast.30, bf16[8,100,128]{2,1,0:T(8,128)(2,1)} %shard_map.134.refs_0_, bf16[8,100,128]{2,1,0:T(8,128)(2,1)} %copy-done.14, bf16[8,100,128]{2,1,0:T(8,128)(2,1)} %copy-done.12, ...), custom_call_target="tpu_custom_call" | custom-call | tf_op jit(solution)/shard_map/pallas_call | solution.py:243
  145.1 13.5 %collective-permute-done.13.refs_2_ = bf16[8,100,128]{2,1,0:T(8,128)(2,1)S(1)} collective-permute-done((bf16[8,100,128]{2,1,0:T(8,128)(2,1)S(1)}, bf16[8,100,128]{2,1,0:T(8,128)(2,1)S(1)}, u32[]{:S(2)}, u32[]{:S(2)}) %collective-permute-start.13) | collective-permute-done | bytes 204832 | tf_op jit(solution)/shard_map/ppermute | solution.py:222
  158.6 0.7 copy-done.13
  159.4 3.3 %shard_map.138 = f32[400,1024]{1,0:T(8,128)} custom-call(s32[2]{0:T(128)} %pad_add_fusion.meta_ref, f32[400,1024]{1,0:T(8,128)} %bitcast.19, f32[1,1024]{1,0:T(1,128)} %bitcast.31, bf16[8,100,128]{2,1,0:T(8,128)(2,1)} %copy-done.1, bf16[8,100,128]{2,1,0:T(8,128)(2,1)} %copy-done.17, bf16[8,100,128]{2,1,0:T(8,128)(2,1)} %copy-done.13, ...), custom_call_target="tpu_custom_call" | custom-call | tf_op jit(solution)/shard_map/pallas_call | solution.py:243
  (59 shorter events, 0.7 us)
Async XLA Ops:
  24.6 21.3 %copy-start.2 = (bf16[8,100,128]{2,1,0:T(8,128)(2,1)}, bf16[8,100,128]{2,1,0:T(8,128)(2,1)S(1)}, u32[]{:S(2)}) copy-start(bf16[8,100,128]{2,1,0:T(8,128)(2,1)S(1)} %all_to_all.21.refs_0_) | copy-start | bytes 614404
  24.7 11.6 %collective-permute-start.2 = (bf16[8,100,128]{2,1,0:T(8,128)(2,1)S(1)}, bf16[8,100,128]{2,1,0:T(8,128)(2,1)S(1)}, u32[]{:S(2)}, u32[]{:S(2)}) collective-permute-start(bf16[8,100,128]{2,1,0:T(8,128)(2,1)S(1)} %all_to_all.21.refs_0_), channel_id=1, source_target_pairs={{0,3},{1,0},{2,1},{3,2},{4,7},{5,4},{6,5},{7,6},{8,11},{9,8},{10,9... | collective-permute-start | bytes 614408 | tf_op jit(solution)/shard_map/ppermute | solution.py:222
  28.2 17.7 %collective-permute-start.1 = (bf16[8,100,128]{2,1,0:T(8,128)(2,1)S(1)}, bf16[8,100,128]{2,1,0:T(8,128)(2,1)S(1)}, u32[]{:S(2)}, u32[]{:S(2)}) collective-permute-start(bf16[8,100,128]{2,1,0:T(8,128)(2,1)S(1)} %all_to_all.21.refs_0_), channel_id=1, source_target_pairs={{0,2},{1,3},{2,0},{3,1},{4,6},{5,7},{6,4},{7,5},{8,10},{9,11},{10,... | collective-permute-start | bytes 614408 | tf_op jit(solution)/shard_map/ppermute | solution.py:222
  28.2 17.7 %collective-permute-start = (bf16[8,100,128]{2,1,0:T(8,128)(2,1)S(1)}, bf16[8,100,128]{2,1,0:T(8,128)(2,1)S(1)}, u32[]{:S(2)}, u32[]{:S(2)}) collective-permute-start(bf16[8,100,128]{2,1,0:T(8,128)(2,1)S(1)} %all_to_all.21.refs_0_), channel_id=1, source_target_pairs={{0,1},{1,2},{2,3},{3,0},{4,5},{5,6},{6,7},{7,4},{8,9},{9,10},{10,1... | collective-permute-start | bytes 614408 | tf_op jit(solution)/shard_map/ppermute | solution.py:222
  36.3 9.7 %copy-start.15 = (bf16[8,100,128]{2,1,0:T(8,128)(2,1)}, bf16[8,100,128]{2,1,0:T(8,128)(2,1)S(1)}, u32[]{:S(2)}) copy-start(bf16[8,100,128]{2,1,0:T(8,128)(2,1)S(1)} %collective-permute-done.2.refs_3_) | copy-start | bytes 614404
  46.0 0.7 copy-start.16
  46.0 0.8 copy-start.18
  56.9 36.5 %collective-permute-start.9 = (bf16[8,100,128]{2,1,0:T(8,128)(2,1)}, bf16[8,100,128]{2,1,0:T(8,128)(2,1)S(1)}, u32[]{:S(2)}, u32[]{:S(2)}) collective-permute-start(bf16[8,100,128]{2,1,0:T(8,128)(2,1)} %get-tuple-element.25), channel_id=1, source_target_pairs={{0,1},{1,2},{2,3},{3,0},{4,5},{5,6},{6,7},{7,4},{8,9},{9,10},{10,1... | collective-permute-start | bytes 614408 | tf_op jit(solution)/shard_map/ppermute | solution.py:222
  57.0 38.5 %collective-permute-start.10 = (bf16[8,100,128]{2,1,0:T(8,128)(2,1)}, bf16[8,100,128]{2,1,0:T(8,128)(2,1)S(1)}, u32[]{:S(2)}, u32[]{:S(2)}) collective-permute-start(bf16[8,100,128]{2,1,0:T(8,128)(2,1)} %get-tuple-element.26), channel_id=1, source_target_pairs={{0,2},{1,3},{2,0},{3,1},{4,6},{5,7},{6,4},{7,5},{8,10},{9,11},{10,... | collective-permute-start | bytes 614408 | tf_op jit(solution)/shard_map/ppermute | solution.py:222
  57.1 40.0 %collective-permute-start.11 = (bf16[8,100,128]{2,1,0:T(8,128)(2,1)}, bf16[8,100,128]{2,1,0:T(8,128)(2,1)S(1)}, u32[]{:S(2)}, u32[]{:S(2)}) collective-permute-start(bf16[8,100,128]{2,1,0:T(8,128)(2,1)} %get-tuple-element.27), channel_id=1, source_target_pairs={{0,3},{1,0},{2,1},{3,2},{4,7},{5,4},{6,5},{7,6},{8,11},{9,8},{10,9... | collective-permute-start | bytes 614408 | tf_op jit(solution)/shard_map/ppermute | solution.py:222
  69.3 5.7 %collective-permute-start.15 = (f32[16,400]{1,0:T(8,128)}, f32[16,400]{1,0:T(8,128)S(1)}, u32[]{:S(2)}, u32[]{:S(2)}) collective-permute-start(f32[16,400]{1,0:T(8,128)} %get-tuple-element.28), channel_id=1, source_target_pairs={{0,1},{1,0},{2,3},{3,2},{4,5},{5,4},{6,7},{7,6},{8,9},{9,8},{10,11... | collective-permute-start | bytes 76808 | tf_op jit(solution)/shard_map/ppermute | solution.py:261
  75.8 5.0 %collective-permute-start.16 = (f32[16,400]{1,0:T(8,128)S(1)}, f32[16,400]{1,0:T(8,128)S(1)}, u32[]{:S(2)}, u32[]{:S(2)}) collective-permute-start(f32[16,400]{1,0:T(8,128)S(1)} %add.22), channel_id=1, source_target_pairs={{0,2},{1,3},{2,0},{3,1},{4,6},{5,7},{6,4},{7,5},{8,10},{9,11},{10,... | collective-permute-start | bytes 76808 | tf_op jit(solution)/shard_map/ppermute | solution.py:261
  80.8 4.0 %collective-permute-start.17 = (f32[16,400]{1,0:T(8,128)S(1)}, f32[16,400]{1,0:T(8,128)S(1)}, u32[]{:S(2)}, u32[]{:S(2)}) collective-permute-start(f32[16,400]{1,0:T(8,128)S(1)} %add.23), channel_id=1, source_target_pairs={{0,4},{4,0},{8,12},{12,8},{16,20},{20,16},{24,28},{28,24},{1,5},{5... | collective-permute-start | bytes 76808 | tf_op jit(solution)/shard_map/ppermute | solution.py:261
  84.8 4.9 %collective-permute-start.18 = (f32[16,400]{1,0:T(8,128)S(1)}, f32[16,400]{1,0:T(8,128)S(1)}, u32[]{:S(2)}, u32[]{:S(2)}) collective-permute-start(f32[16,400]{1,0:T(8,128)S(1)} %add.24), channel_id=1, source_target_pairs={{0,8},{4,12},{8,0},{12,4},{16,24},{20,28},{24,16},{28,20},{1,9},{5... | collective-permute-start | bytes 76808 | tf_op jit(solution)/shard_map/ppermute | solution.py:261
  89.7 13.6 %collective-permute-start.19 = (f32[16,400]{1,0:T(8,128)S(1)}, f32[16,400]{1,0:T(8,128)S(1)}, u32[]{:S(2)}, u32[]{:S(2)}) collective-permute-start(f32[16,400]{1,0:T(8,128)S(1)} %add.25), channel_id=1, source_target_pairs={{0,16},{4,20},{8,24},{12,28},{16,0},{20,4},{24,8},{28,12},{1,17},{... | collective-permute-start | bytes 76808 | tf_op jit(solution)/shard_map/ppermute | solution.py:261
  93.2 10.3 %collective-permute-start.3 = (bf16[8,100,128]{2,1,0:T(8,128)(2,1)}, bf16[8,100,128]{2,1,0:T(8,128)(2,1)S(1)}, u32[]{:S(2)}, u32[]{:S(2)}) collective-permute-start(bf16[8,100,128]{2,1,0:T(8,128)(2,1)} %get-tuple-element.21), channel_id=1, source_target_pairs={{0,1},{1,2},{2,3},{3,0},{4,5},{5,6},{6,7},{7,4},{8,9},{9,10},{10,1... | collective-permute-start | bytes 614408 | tf_op jit(solution)/shard_map/ppermute | solution.py:222
  93.4 3.7 %copy-start.4 = (bf16[8,100,128]{2,1,0:T(8,128)(2,1)}, bf16[8,100,128]{2,1,0:T(8,128)(2,1)S(1)}, u32[]{:S(2)}) copy-start(bf16[8,100,128]{2,1,0:T(8,128)(2,1)S(1)} %collective-permute-done.9.refs_1_) | copy-start | bytes 614404
  93.4 17.0 %collective-permute-start.4 = (bf16[8,100,128]{2,1,0:T(8,128)(2,1)}, bf16[8,100,128]{2,1,0:T(8,128)(2,1)S(1)}, u32[]{:S(2)}, u32[]{:S(2)}) collective-permute-start(bf16[8,100,128]{2,1,0:T(8,128)(2,1)} %get-tuple-element.22), channel_id=1, source_target_pairs={{0,2},{1,3},{2,0},{3,1},{4,6},{5,7},{6,4},{7,5},{8,10},{9,11},{10,... | collective-permute-start | bytes 614408 | tf_op jit(solution)/shard_map/ppermute | solution.py:222
  95.5 1.6 copy-start.5
  95.5 14.9 %collective-permute-start.5 = (bf16[8,100,128]{2,1,0:T(8,128)(2,1)}, bf16[8,100,128]{2,1,0:T(8,128)(2,1)S(1)}, u32[]{:S(2)}, u32[]{:S(2)}) collective-permute-start(bf16[8,100,128]{2,1,0:T(8,128)(2,1)} %get-tuple-element.23), channel_id=1, source_target_pairs={{0,3},{1,0},{2,1},{3,2},{4,7},{5,4},{6,5},{7,6},{8,11},{9,8},{10,9... | collective-permute-start | bytes 614408 | tf_op jit(solution)/shard_map/ppermute | solution.py:222
  97.1 0.7 copy-start.6
  99.8 23.1 %copy-start.19 = (f32[16]{0:T(128)S(1)}, f32[16]{0:T(128)}, u32[]{:S(2)}) copy-start(f32[16]{0:T(128)} %param.16) | copy-start | bytes 196
  99.8 33.1 %copy-start.3 = (f32[16,400]{1,0:T(8,128)S(1)}, f32[16,400]{1,0:T(8,128)}, u32[]{:S(2)}) copy-start(f32[16,400]{1,0:T(8,128)} %rel_ref.3) | copy-start | bytes 76804
  99.8 17.4 %all-to-all-start.2 = ((bf16[8,100,128]{2,1,0:T(8,128)(2,1)}), bf16[8,100,128]{2,1,0:T(8,128)(2,1)S(1)}, u32[]{:S(2)}, u32[]{:S(2)}) async-start(bf16[8,100,128]{2,1,0:T(8,128)(2,1)} %shard_map.136), calls=%async_computation.2 | async-start | bytes 425984 | tf_op jit(solution)/shard_map/all_to_all | solution.py:237
  103.5 6.9 %copy-start.7 = (bf16[8,100,128]{2,1,0:T(8,128)(2,1)}, bf16[8,100,128]{2,1,0:T(8,128)(2,1)S(1)}, u32[]{:S(2)}) copy-start(bf16[8,100,128]{2,1,0:T(8,128)(2,1)S(1)} %collective-permute-done.3.refs_1_) | copy-start | bytes 614404
  110.4 0.7 copy-start.8
  110.4 0.8 copy-start.9
  113.2 17.6 %collective-permute-start.8 = (bf16[8,100,128]{2,1,0:T(8,128)(2,1)}, bf16[8,100,128]{2,1,0:T(8,128)(2,1)S(1)}, u32[]{:S(2)}, u32[]{:S(2)}) collective-permute-start(bf16[8,100,128]{2,1,0:T(8,128)(2,1)} %shard_map.134.refs_0_), channel_id=1, source_target_pairs={{0,3},{1,0},{2,1},{3,2},{4,7},{5,4},{6,5},{7,6},{8,11},{9,8},{10,9... | collective-permute-start | bytes 614408 | tf_op jit(solution)/shard_map/ppermute | solution.py:222
  117.2 0.7 copy-start
  119.5 9.7 %all-to-all-start.3 = ((bf16[8,100,128]{2,1,0:T(8,128)(2,1)}), bf16[8,100,128]{2,1,0:T(8,128)(2,1)S(1)}, u32[]{:S(2)}, u32[]{:S(2)}) async-start(bf16[8,100,128]{2,1,0:T(8,128)(2,1)} %shard_map.137), calls=%async_computation.3 | async-start | bytes 425984 | tf_op jit(solution)/shard_map/all_to_all | solution.py:237
  122.9 18.1 %collective-permute-start.7 = (bf16[8,100,128]{2,1,0:T(8,128)(2,1)}, bf16[8,100,128]{2,1,0:T(8,128)(2,1)S(1)}, u32[]{:S(2)}, u32[]{:S(2)}) collective-permute-start(bf16[8,100,128]{2,1,0:T(8,128)(2,1)} %shard_map.134.refs_0_), channel_id=1, source_target_pairs={{0,2},{1,3},{2,0},{3,1},{4,6},{5,7},{6,4},{7,5},{8,10},{9,11},{10,... | collective-permute-start | bytes 614408 | tf_op jit(solution)/shard_map/ppermute | solution.py:222
  124.6 16.4 %collective-permute-start.6 = (bf16[8,100,128]{2,1,0:T(8,128)(2,1)}, bf16[8,100,128]{2,1,0:T(8,128)(2,1)S(1)}, u32[]{:S(2)}, u32[]{:S(2)}) collective-permute-start(bf16[8,100,128]{2,1,0:T(8,128)(2,1)} %shard_map.134.refs_0_), channel_id=1, source_target_pairs={{0,1},{1,2},{2,3},{3,0},{4,5},{5,6},{6,7},{7,4},{8,9},{9,10},{10,1... | collective-permute-start | bytes 614408 | tf_op jit(solution)/shard_map/ppermute | solution.py:222
  129.2 15.9 %copy-start.1 = (bf16[8,100,128]{2,1,0:T(8,128)(2,1)}, bf16[8,100,128]{2,1,0:T(8,128)(2,1)S(1)}, u32[]{:S(2)}) copy-start(bf16[8,100,128]{2,1,0:T(8,128)(2,1)S(1)} %all-to-all-done.3.refs_0_) | copy-start | bytes 614404
  129.2 15.9 %collective-permute-start.14 = (bf16[8,100,128]{2,1,0:T(8,128)(2,1)S(1)}, bf16[8,100,128]{2,1,0:T(8,128)(2,1)S(1)}, u32[]{:S(2)}, u32[]{:S(2)}) collective-permute-start(bf16[8,100,128]{2,1,0:T(8,128)(2,1)S(1)} %all-to-all-done.3.refs_0_), channel_id=1, source_target_pairs={{0,3},{1,0},{2,1},{3,2},{4,7},{5,4},{6,5},{7,6},{8,11},{9,8},{10,9... | collective-permute-start | bytes 614408 | tf_op jit(solution)/shard_map/ppermute | solution.py:222
  129.9 28.7 %collective-permute-start.13 = (bf16[8,100,128]{2,1,0:T(8,128)(2,1)S(1)}, bf16[8,100,128]{2,1,0:T(8,128)(2,1)S(1)}, u32[]{:S(2)}, u32[]{:S(2)}) collective-permute-start(bf16[8,100,128]{2,1,0:T(8,128)(2,1)S(1)} %all-to-all-done.3.refs_0_), channel_id=1, source_target_pairs={{0,2},{1,3},{2,0},{3,1},{4,6},{5,7},{6,4},{7,5},{8,10},{9,11},{10,... | collective-permute-start | bytes 614408 | tf_op jit(solution)/shard_map/ppermute | solution.py:222
  130.8 10.2 %copy-start.10 = (bf16[8,100,128]{2,1,0:T(8,128)(2,1)}, bf16[8,100,128]{2,1,0:T(8,128)(2,1)S(1)}, u32[]{:S(2)}) copy-start(bf16[8,100,128]{2,1,0:T(8,128)(2,1)S(1)} %collective-permute-done.8.refs_3_) | copy-start | bytes 614404
  130.8 27.8 %collective-permute-start.12 = (bf16[8,100,128]{2,1,0:T(8,128)(2,1)S(1)}, bf16[8,100,128]{2,1,0:T(8,128)(2,1)S(1)}, u32[]{:S(2)}, u32[]{:S(2)}) collective-permute-start(bf16[8,100,128]{2,1,0:T(8,128)(2,1)S(1)} %all-to-all-done.3.refs_0_), channel_id=1, source_target_pairs={{0,1},{1,2},{2,3},{3,0},{4,5},{5,6},{6,7},{7,4},{8,9},{9,10},{10,1... | collective-permute-start | bytes 614408 | tf_op jit(solution)/shard_map/ppermute | solution.py:222
  141.0 0.7 copy-start.12
  141.0 0.7 copy-start.14
  145.1 13.5 %copy-start.11 = (bf16[8,100,128]{2,1,0:T(8,128)(2,1)}, bf16[8,100,128]{2,1,0:T(8,128)(2,1)S(1)}, u32[]{:S(2)}) copy-start(bf16[8,100,128]{2,1,0:T(8,128)(2,1)S(1)} %collective-permute-done.14.refs_3_) | copy-start | bytes 614404
  158.6 0.7 copy-start.13
  158.6 0.8 copy-start.17

commit v2 on v1

v2 whole, which is shorter than its diff:
```python
import functools

import jax
import jax.numpy as jnp
from jax import lax
from jax.experimental import pallas as pl
from jax.experimental.pallas import tpu as pltpu
from jax.sharding import PartitionSpec as P

E_CH = 640
LEARN_RATE = 0.25
NEG_WEIGHT = 0.03125

F32 = jnp.float32
BF16 = jnp.bfloat16
VMEM_BYTES = 56 * 1024 * 1024
SMEM_SPEC = pl.BlockSpec(memory_space=pltpu.SMEM)


def params():
    return pltpu.CompilerParams(vmem_limit_bytes=VMEM_BYTES)


def cost(flops, nbytes):
    return pl.CostEstimate(flops=int(flops), bytes_accessed=int(nbytes), transcendentals=0)


def dot_nn(a, b):
    return lax.dot_general(a, b, (((1,), (0,)), ((), ())), preferred_element_type=F32)


def dot_nt(a, b):
    return lax.dot_general(a, b, (((1,), (1,)), ((), ())), preferred_element_type=F32)


def dot_tn(a, b):
    return lax.dot_general(a, b, (((0,), (0,)), ((), ())), preferred_element_type=F32)


def live_ids(ids, meta_ref, step, steps):
    width = ids.shape[1]
    start = (meta_ref[1] * steps + step) * width
    slots = start + lax.broadcasted_iota(jnp.int32, ids.shape, 1)
    return jnp.where(slots < meta_ref[0], ids, -1)


def is_live(meta_ref, step, steps, width):
    return (meta_ref[1] * steps + step) * width < meta_ref[0]


def one_hot(ids, rows):
    match = lax.broadcasted_iota(jnp.int32, (rows, ids.shape[1]), 0) == ids
    return jnp.where(match, 1.0, 0.0).astype(BF16)


def relation_columns(rel_ref, kind):
    rel = rel_ref[...]
    high = rel.astype(BF16)
    rest = rel - high.astype(F32)
    middle = rest.astype(BF16)
    low = (rest - middle.astype(F32)).astype(BF16)
    parts = jnp.concatenate([high.astype(F32), middle.astype(F32), low.astype(F32)], axis=0)
    hot = jnp.concatenate([kind, kind, kind], axis=0)
    return dot_tn(parts.astype(BF16), hot.astype(BF16))


def kind_hot(ids, count):
    match = lax.broadcasted_iota(jnp.int32, (count, ids.shape[1]), 0) == ids
    return jnp.where(match, 1.0, 0.0)


def prep_kernel(steps, meta_ref, hid_ref, rid_ref, src_ref, rel_ref, q_ref, head_ref, low_ref):
    step = pl.program_id(0)

    @pl.when(step == 0)
    def _():
        low_ref[...] = src_ref[...].astype(BF16)

    @pl.when(is_live(meta_ref, step, steps, hid_ref.shape[2]))
    def _():
        ids = live_ids(hid_ref[0], meta_ref, step, steps)
        kinds = live_ids(rid_ref[0], meta_ref, step, steps)
        head = dot_nn(low_ref[...], one_hot(ids, low_ref.shape[1]))
        rel = relation_columns(rel_ref, kind_hot(kinds, rel_ref.shape[0]))
        half = head.shape[0] // 2
        h_re, h_im, r_re, r_im = head[:half], head[half:], rel[:half], rel[half:]
        query = jnp.concatenate([h_re * r_re - h_im * r_im, h_re * r_im + h_im * r_re], axis=0)
        q_ref[0] = query.astype(BF16)
        head_ref[0] = head.astype(BF16)


def ring_plan(lanes, pieces):
    plan = [(0, 0, pieces)]
    for k in range(1, (lanes + 1) // 2):
        plan += [(k, 0, pieces), (-k, 0, pieces)]
    if lanes % 2 == 0:
        half = pieces // 2
        plan += [(lanes // 2, 0, half), (-(lanes // 2), half, pieces - half)]
    return plan


def add_pieces(total, part, first):
    last, part = first + part.shape[0], part.astype(F32)
    if part.shape == total.shape:
        return total + part
    return jnp.concatenate([total[:first], total[first:last] + part, total[last:]], axis=0)


def ring_sum(parts, waits):
    lanes = lax.axis_size("span")
    if lanes == 1:
        return parts[0].astype(BF16)
    plan = ring_plan(lanes, parts[0].shape[0])
    blocks = {away: part for part, (away, _, _) in zip(parts, plan)}
    reach, first = lanes // 2, plan[-1][1]
    ahead, behind = blocks[reach].astype(BF16), blocks[-reach].astype(BF16)
    for away in range(reach, 0, -1):
        ahead, behind = shift_span(ahead, 1), shift_span(behind, -1)
        for wait in waits[reach - away : reach - away + 1]:
            ahead, behind = after((ahead, behind), wait)
        if away > 1:
            ahead = add_pieces(blocks[away - 1], ahead, 0).astype(BF16)
            behind = add_pieces(blocks[1 - away], behind, first).astype(BF16)
    return add_pieces(add_pieces(parts[0], ahead, 0), behind, first).astype(BF16)


def ring_shapes(shape, lanes):
    return [
        jax.ShapeDtypeStruct((count,) + tuple(shape[1:]), F32 if abs(away) < (lanes + 1) // 2 else BF16)
        for away, first, count in ring_plan(lanes, shape[0])
    ]


def gather_span(x):
    lanes = lax.axis_size("span")
    parts, ahead, behind = [x], x, x
    for _ in range(1, (lanes + 1) // 2):
        ahead, behind = shift_span(ahead, 1), shift_span(behind, -1)
        parts += [ahead, behind]
    if lanes % 2 == 0:
        half = x.shape[0] // 2
        parts += [shift_span(ahead[:half], 1), shift_span(behind[half:], -1)]
    return parts


def assemble(lanes, lane, parts, out_ref):
    width = parts[0].shape[2]
    block = out_ref.shape[0] // lanes
    plan = ring_plan(lanes, parts[0].shape[0])
    for at in range(lanes):

        @pl.when(lane == at)
        def _():
            for part, (behind, first, count) in zip(parts, plan):
                row = ((at - behind) % lanes) * block
                for b in range(count):
                    col = (first + b) * width
                    out_ref[row : row + block, col : col + width] = part[b, :block].astype(F32)


def emit(lanes, lane, acc_ref, outs):
    width = outs[0].shape[2]
    block = acc_ref.shape[0] // lanes
    plan = ring_plan(lanes, outs[0].shape[0])
    for at in range(lanes):

        @pl.when(lane == at)
        def _():
            for out, (away, first, count) in zip(outs, plan):
                row = ((at + away) % lanes) * block
                for b in range(count):
                    col = (first + b) * width
                    out[b, :block] = acc_ref[row : row + block, col : col + width].astype(out.dtype)


def main_kernel(
    steps, lanes, packed, meta_ref, tid_ref, rid_ref, rel_ref, q_ref, head_ref, parts_ref, *refs
):
    grad_ref, rel_out_ref = refs[:2]
    outs = refs[2:-4]
    table_ref, acc_ref, hot_ref, coef_ref = refs[-4:]
    step = pl.program_id(0)

    @pl.when(step == 0)
    def _():
        width = parts_ref.shape[2]
        for b in range(parts_ref.shape[0]):
            table_ref[:, b * width : (b + 1) * width] = parts_ref[b]
        acc_ref[...] = jnp.zeros_like(acc_ref)
        rel_out_ref[...] = jnp.zeros_like(rel_out_ref)

    @pl.when(is_live(meta_ref, step, steps, tid_ref.shape[2]))
    def _():
        ids = live_ids(tid_ref[0], meta_ref, step, steps)
        hot_ref[...] = one_hot(ids, table_ref.shape[1])
        tail = dot_nn(table_ref[...], hot_ref[...]).astype(BF16)
        scores = dot_tn(q_ref[0], tail)
        sig = 0.5 * jnp.tanh(0.5 * scores) + 0.5
        diagonal = lax.broadcasted_iota(jnp.int32, scores.shape, 0) == lax.broadcasted_iota(
            jnp.int32, scores.shape, 1
        )
        coef_ref[...] = jnp.where(diagonal, sig - 1.0, NEG_WEIGHT * sig).astype(BF16)
        grad_tail = dot_nn(q_ref[0], coef_ref[...])
        acc_ref[...] += dot_nt(grad_tail.astype(BF16), hot_ref[...])

        kinds = live_ids(rid_ref[0], meta_ref, step, steps)
        kind = kind_hot(kinds, rel_ref.shape[0])
        rel = relation_columns(rel_ref, kind)
        head = head_ref[0].astype(F32)
        half = head.shape[0] // 2
        h_re, h_im, r_re, r_im = head[:half], head[half:], rel[:half], rel[half:]
        grad_query = dot_nt(tail, coef_ref[...])
        g_re, g_im = grad_query[:half], grad_query[half:]
        grad_head = jnp.concatenate([g_re * r_re + g_im * r_im, g_im * r_re - g_re * r_im], axis=0)
        grad_ref[0] = grad_head.astype(BF16)
        grad_rel = jnp.concatenate([g_re * h_re + g_im * h_im, g_im * h_re - g_re * h_im], axis=0)
        rel_out_ref[...] += dot_nt(grad_rel.astype(BF16), kind.astype(BF16))

    @pl.when(step == steps - 1)
    def _():
        emit(lanes, meta_ref[1], acc_ref, outs)
        if packed:
            rel_rows = rel_out_ref[...].T
            block = rel_rows.shape[1] // lanes
            each = rel_rows.shape[0] // outs[0].shape[0]
            plan = ring_plan(lanes, outs[0].shape[0])
            for at in range(lanes):

                @pl.when(meta_ref[1] == at)
                def _():
                    for out, (away, first, count) in zip(outs, plan):
                        col = ((at + away) % lanes) * block
                        for b in range(count):
                            row = (first + b) * each
                            out[b, block:, :block] = rel_rows[
                                row : row + each, col : col + block
                            ].astype(out.dtype)


def source_kernel(steps, lanes, meta_ref, hid_ref, grad_ref, *refs):
    outs, acc_ref = refs[:-1], refs[-1]
    step = pl.program_id(0)

    @pl.when(step == 0)
    def _():
        acc_ref[...] = jnp.zeros_like(acc_ref)

    @pl.when(is_live(meta_ref, step, steps, hid_ref.shape[2]))
    def _():
        ids = live_ids(hid_ref[0], meta_ref, step, steps)
        acc_ref[...] += dot_nt(grad_ref[0], one_hot(ids, acc_ref.shape[1]))

    @pl.when(step == steps - 1)
    def _():
        emit(lanes, meta_ref[1], acc_ref, outs)


def pick_kernel(plan_ref, in_ref, out_ref):
    for b in range(in_ref.shape[0]):
        out_ref[b] = in_ref[plan_ref[b]]


def place_kernel(block, plan_ref, in_ref, out_ref):
    for b in range(in_ref.shape[0]):
        out_ref[plan_ref[b]] = in_ref[b]
    if in_ref.shape[1] > block:
        total = jnp.sum(in_ref[:, block:].astype(F32), axis=0).astype(BF16)
        for b in range(in_ref.shape[0]):
            out_ref[b, block:] = total


def adagrad(table, state, grad, axis):
    mean = jnp.sum(grad * grad, axis=axis, keepdims=True) / grad.shape[axis]
    return table - grad * (LEARN_RATE / jnp.sqrt(state + mean))


def update_kernel(lanes, meta_ref, table_ref, state_ref, *refs):
    parts, out_ref, grad_ref = refs[:-2], refs[-2], refs[-1]
    assemble(lanes, meta_ref[1], parts, grad_ref)
    out_ref[...] = adagrad(table_ref[...], state_ref[...], grad_ref[...], 0)


def update_both_kernel(lanes, meta_ref, table_ref, state_ref, rel_ref, rel_state_ref, *refs):
    parts = refs[:-4]
    out_ref, rel_out_ref, grad_ref, rel_grad_ref = refs[-4:]
    assemble(lanes, meta_ref[1], parts, grad_ref)
    out_ref[...] = adagrad(table_ref[...], state_ref[...], grad_ref[...], 0)
    block = rel_ref.shape[1] // lanes
    each = parts[0].shape[1] - block
    plan = ring_plan(lanes, parts[0].shape[0])
    for at in range(lanes):

        @pl.when(meta_ref[1] == at)
        def _():
            for part, (behind, first, count) in zip(parts, plan):
                col = ((at - behind) % lanes) * block
                for b in range(count):
                    row = (first + b) * each
                    rel_grad_ref[row : row + each, col : col + block] = part[
                        b, block:, :block
                    ].astype(F32)

    rel_out_ref[...] = adagrad(rel_ref[...], rel_state_ref[...], rel_grad_ref[...], 1)


def whole(shape):
    zeros = (0,) * len(shape)
    return pl.BlockSpec(tuple(shape), lambda i: zeros)


def per_span(shape):
    rest = (0,) * (len(shape) - 1)
    return pl.BlockSpec((1,) + tuple(shape[1:]), lambda i: (i,) + rest)


def shift_span(x, by):
    count = lax.axis_size("span")
    return lax.ppermute(x, "span", [(i, (i + by) % count) for i in range(count)])


def plain(kernel, out, *operands, smem=1):
    vmem = pl.BlockSpec(memory_space=pltpu.VMEM)
    return pl.pallas_call(
        kernel,
        out_shape=out,
        in_specs=[SMEM_SPEC] * smem + [vmem] * (len(operands) - smem),
        out_specs=vmem,
        compiler_params=params(),
    )(*operands)


def swap_buckets(x):
    return lax.all_to_all(x, "bucket", split_axis=0, concat_axis=0, tiled=True)


def after(x, y):
    return lax.optimization_barrier((x, y))[0]


def update(kernel, lanes, meta, weights, parts):
    vmem = pl.BlockSpec(memory_space=pltpu.VMEM)
    tables = weights[::2]
    return pl.pallas_call(
        functools.partial(kernel, lanes),
        out_shape=[jax.ShapeDtypeStruct(t.shape, F32) for t in tables],
        in_specs=[SMEM_SPEC] + [vmem] * (len(weights) + len(parts)),
        out_specs=[vmem] * len(tables),
        scratch_shapes=[pltpu.VMEM(t.shape, F32) for t in tables],
        compiler_params=params(),
    )(meta, *weights, *parts)


def sum_all(x):
    for axis in ("span", "bucket"):
        count = lax.axis_size(axis)
        if count & (count - 1):
            x = lax.psum(x, axis)
            continue
        bit = 1
        while bit < count:
            x = x + lax.ppermute(x, axis, [(i, i ^ bit) for i in range(count)])
            bit *= 2
    return x


def per_device(
    source_table,
    target_table,
    source_state,
    target_state,
    relation,
    relation_state,
    plan,
    source_index,
    target_index,
    relation_index,
    edge_counts,
):
    buckets = lax.axis_size("bucket")
    lanes = lax.axis_size("span")
    lane = lax.axis_index("span").astype(jnp.int32)
    rows, features = source_table.shape
    steps = source_index.shape[1] // E_CH
    kinds = relation.shape[0]
    block = features // lanes
    width = rows // buckets
    meta = jnp.stack([edge_counts[0], lane])
    hid = source_index.reshape(steps, 1, E_CH)
    tid = target_index.reshape(steps, 1, E_CH)
    rid = relation_index.reshape(steps, 1, E_CH)
    source_cols, target_cols = source_table.T, target_table.T

    owned = target_cols.astype(BF16).reshape(features, buckets, width).transpose(1, 0, 2)
    spread = swap_buckets(owned)
    chosen = plain(pick_kernel, jax.ShapeDtypeStruct(owned.shape, BF16), plan, spread)
    fetched = swap_buckets(chosen)
    packed = kinds % buckets == 0 and width >= block
    pieces = (buckets, block, width)
    piece_shape = jax.ShapeDtypeStruct(pieces, BF16)
    bundles = (buckets, block + kinds // buckets, width) if packed else pieces
    bundle_shape = jax.ShapeDtypeStruct(bundles, BF16)

    edge_shape = (steps, features, E_CH)
    query, head = pl.pallas_call(
        functools.partial(prep_kernel, steps),
        grid=(steps,),
        out_shape=[jax.ShapeDtypeStruct(edge_shape, BF16)] * 2,
        in_specs=[
            SMEM_SPEC,
            per_span(hid.shape),
            per_span(rid.shape),
            whole(source_cols.shape),
            whole(relation.shape),
        ],
        out_specs=[per_span(edge_shape)] * 2,
        scratch_shapes=[pltpu.VMEM((features, rows), BF16)],
        compiler_params=params(),
        cost_estimate=cost(4 * steps * features * rows * E_CH, 8 * features * steps * E_CH),
    )(meta, hid, rid, source_cols, relation)

    bundle_outs, piece_outs = ring_shapes(bundles, lanes), ring_shapes(pieces, lanes)
    grad_head, rel_part, *target_out = pl.pallas_call(
        functools.partial(main_kernel, steps, lanes, packed),
        grid=(steps,),
        out_shape=[
            jax.ShapeDtypeStruct(edge_shape, BF16),
            jax.ShapeDtypeStruct((features, kinds), F32),
        ]
        + bundle_outs,
        in_specs=[
            SMEM_SPEC,
            per_span(tid.shape),
            per_span(rid.shape),
            whole(relation.shape),
            per_span(edge_shape),
            per_span(edge_shape),
            whole(owned.shape),
        ],
        out_specs=[per_span(edge_shape), whole((features, kinds))]
        + [whole(out.shape) for out in bundle_outs],
        scratch_shapes=[
            pltpu.VMEM((features, rows), BF16),
            pltpu.VMEM((features, rows), F32),
            pltpu.VMEM((rows, E_CH), BF16),
            pltpu.VMEM((E_CH, E_CH), BF16),
        ],
        compiler_params=params(),
        cost_estimate=cost(12 * steps * features * rows * E_CH, 8 * features * steps * E_CH),
    )(meta, tid, rid, relation, query, head, fetched)

    source_out = pl.pallas_call(
        functools.partial(source_kernel, steps, lanes),
        grid=(steps,),
        out_shape=piece_outs,
        in_specs=[SMEM_SPEC, per_span(hid.shape), per_span(edge_shape)],
        out_specs=[whole(out.shape) for out in piece_outs],
        scratch_shapes=[pltpu.VMEM((features, rows), F32)],
        compiler_params=params(),
        cost_estimate=cost(4 * steps * features * rows * E_CH, 8 * features * steps * E_CH),
    )(meta, hid, grad_head)

    target_sum = ring_sum(target_out, [source_out])
    returned = swap_buckets(target_sum)
    placing = functools.partial(place_kernel, block)
    sorted_out = plain(placing, bundle_shape, plan, returned)
    target_home = swap_buckets(sorted_out)
    source_sum = ring_sum(source_out, [sorted_out])
    source_parts = gather_span(source_sum)
    home_parts = gather_span(target_home)
    source_weights = (source_cols, source_state.reshape(1, rows))
    target_weights = (target_cols, target_state.reshape(1, rows))
    (new_source,) = update(update_kernel, lanes, meta, source_weights, source_parts)
    if packed:
        weights = target_weights + (relation, relation_state.reshape(kinds, 1))
        new_target, new_relation = update(update_both_kernel, lanes, meta, weights, home_parts)
    else:
        (new_target,) = update(update_kernel, lanes, meta, target_weights, home_parts)
        rel_total = sum_all(rel_part).T
        mean = jnp.mean(rel_total * rel_total, axis=1)
        new_relation = relation - LEARN_RATE * rel_total / jnp.sqrt(relation_state + mean)[:, None]
    return (new_source.T, new_target.T, new_relation)


def solution(mesh):
    placed = (
        P("bucket", None),
        P("bucket", None),
        P("bucket"),
        P("bucket"),
        P(),
        P(),
        P(),
        P("bucket", "span"),
        P("bucket", "span"),
        P("bucket", "span"),
        P("bucket"),
    )
    return jax.shard_map(
        per_device,
        mesh=mesh,
        in_specs=placed,
        out_specs=(P("bucket", None), P("bucket", None), P()),
        check_vma=False,
    )
```

time: 164 us -> 140 us (0.85)
  waiting for transfers between devices: 54.9 us -> 28.5 us
  blocking collectives: 21.2 us -> 27.7 us
  starting transfers between devices: 39.1 us -> 33.3 us
  Pallas kernels: 38.4 us -> 41.6 us
  local copies, waits for them, and re-layouts: 5.55 us -> 3.7 us
    ppermute x15 -> x16, waiting for transfers between devices: 37.7 us -> 21.1 us  [shift_span(): lax.ppermute(x, 'span', [(i, (i + by) % count) for i in range(count)])]
    ppermute x5 -> x0, waiting for transfers between devices: 12.6 us -> none  [sum_all(): x = x + lax.ppermute(x, axis, [(i, i ^ bit) for i in range(count)])]
    ppermute x5 -> x0, starting transfers between devices: 10.5 us -> none  [sum_all(): x = x + lax.ppermute(x, axis, [(i, i ^ bit) for i in range(count)])]
    pallas_call x3, Pallas kernels: 16.8 us -> 25 us  [the longest x1 18.1 us: per_device(): pl.pallas_call(functools.partial(main_kernel, steps, lanes, packed), grid...]
    all_to_all x2, blocking collectives: 21.2 us -> 27.7 us  [swap_buckets(): return lax.all_to_all(x, 'bucket', split_axis=0, concat_axis=0, tiled=True)]
    pallas_call x4 -> x2, Pallas kernels: 7.31 us -> 3.74 us  [plain(): pl.pallas_call(kernel, out_shape=out, in_specs=[SMEM_SPEC] * smem + [vmem...]
    ppermute x15 -> x16, starting transfers between devices: 21.6 us -> 24.8 us  [shift_span(): lax.ppermute(x, 'span', [(i, (i + by) % count) for i in range(count)])]
    all_to_all x2, waiting for transfers between devices: 4.63 us -> 7.43 us  [swap_buckets(): return lax.all_to_all(x, 'bucket', split_axis=0, concat_axis=0, tiled=True)]
  transfers between devices with their start and end apart: 22 -> 18, of which waited for: 9 -> 10; matrix products, arithmetic and copies ran while one was open for 1% -> 1% of each run, Pallas kernels for 14% -> 13%
where the time goes in v2:
time: 140 us
  Pallas kernels  41.6 us (30%)
  starting transfers between devices  33.3 us (24%)
  waiting for transfers between devices  28.5 us (20%)
  blocking collectives  27.7 us (20%)
  local copies, waits for them, and re-layouts  3.7 us (3%)
  other arithmetic  3.2 us (2%)
  between operations  1.6 us (1%)
    all_to_all x2, blocking collectives, swap_buckets(): return lax.all_to_all(x, 'bucket', split_axis=0, concat_axis=0, tiled=True)  27.7 us
    ppermute x16, starting transfers between devices, shift_span(): lax.ppermute(x, 'span', [(i, (i + by) % count) for i in range(count)])  24.8 us
    ppermute x16, waiting for transfers between devices, shift_span(): lax.ppermute(x, 'span', [(i, (i + by) % count) for i in range(count)])  21.1 us
    pallas_call x1, Pallas kernels, per_device(): pl.pallas_call(functools.partial(main_kernel, steps, lanes, packed), grid...  18.1 us
    all_to_all x2, starting transfers between devices, swap_buckets(): return lax.all_to_all(x, 'bucket', split_axis=0, concat_axis=0, tiled=True)  8.56 us
    all_to_all x2, waiting for transfers between devices, swap_buckets(): return lax.all_to_all(x, 'bucket', split_axis=0, concat_axis=0, tiled=True)  7.43 us
    pallas_call x2, Pallas kernels, update(): pl.pallas_call(functools.partial(kernel, lanes), out_shape=[jax.ShapeDtyp...  6.85 us
    pallas_call x1, Pallas kernels, per_device(): pl.pallas_call(functools.partial(prep_kernel, steps), grid=(steps,), out_...  6.67 us
  transfers between devices with their start and end apart: 18, of which 10 were waited for; matrix products, arithmetic and copies ran while one was open for 1% of the time, Pallas kernels for 13%

profile of v2, /device:TPU:0, one launch (start us, length us, event | category | flops | bytes accessed | tf_op | source)
XLA Modules:
  0.0 139.7 jit_solution(5515519423836093294)
XLA Ops:
  0.6 1.5 %bitcast_bitcast_fusion = bf16[8,400,128]{2,1,0:T(8,128)(2,1)S(1)} fusion(f32[1024,400]{0,1:T(8,128)} %param.12), kind=kLoop, calls=%fused_computation | loop fusion | flops 409600 | bytes 2457600 | tf_op jit(solution)/shard_map/transpose | solution.py:393
  2.2 18.0 %all_to_all.20.in_ref = bf16[8,400,128]{2,1,0:T(8,128)(2,1)} all-to-all(bf16[8,400,128]{2,1,0:T(8,128)(2,1)S(1)} %bitcast_bitcast_fusion), channel_id=1, replica_groups=mesh['bucket'=8,'span'=4] {'bucket'}, dimensions={0} | all-to-all | bytes 1638400 | tf_op jit(solution)/shard_map/all_to_all | solution.py:333
  20.2 2.1 %shard_map.131 = bf16[8,400,128]{2,1,0:T(8,128)(2,1)} custom-call(s32[8]{0:T(128)} %plan_ref.3, bf16[8,400,128]{2,1,0:T(8,128)(2,1)} %all_to_all.20.in_ref), custom_call_target="tpu_custom_call" | custom-call | tf_op jit(solution)/shard_map/pallas_call | solution.py:323
  22.3 3.5 %all-to-all-start.1 = ((bf16[8,400,128]{2,1,0:T(8,128)(2,1)}), bf16[8,400,128]{2,1,0:T(8,128)(2,1)S(1)}, u32[]{:S(2)}, u32[]{:S(2)}) async-start(bf16[8,400,128]{2,1,0:T(8,128)(2,1)} %shard_map.131), calls=%async_computation.1 | async-start | bytes 1638400 | tf_op jit(solution)/shard_map/all_to_all | solution.py:333
  26.5 0.6 pad_add_fusion.meta_ref
  27.1 6.7 %shard_map.130 = (bf16[4,400,640]{2,1,0:T(8,128)(2,1)}, bf16[4,400,640]{2,1,0:T(8,128)(2,1)}) custom-call(s32[2]{0:T(128)} %pad_add_fusion.meta_ref, s32[4,1,640]{2,1,0:T(1,128)} %bitcast.31, s32[4,1,640]{2,1,0:T(1,128)} %bitcast.29, f32[400,1024]{1,0:T(8,128)} %bitcast.21, f32[16,400]{1,0:T(8,128)} %rel_ref.5), custom_call_target="tpu_custom_call" | custom-call | flops 4194304000 | bytes 8192000 | tf_op jit(solution)/shard_map/pallas_call | solution.py:404
  33.7 5.0 %all-to-all-done.1.parts_ref = bf16[8,400,128]{2,1,0:T(8,128)(2,1)S(1)} async-done(((bf16[8,400,128]{2,1,0:T(8,128)(2,1)}), bf16[8,400,128]{2,1,0:T(8,128)(2,1)S(1)}, u32[]{:S(2)}, u32[]{:S(2)}) %all-to-all-start.1) | async-done | bytes 819232 | tf_op jit(solution)/shard_map/all_to_all | solution.py:333
  38.7 0.9 copy-done.4
  39.6 18.1 %shard_map.132 = (bf16[4,400,640]{2,1,0:T(8,128)(2,1)}, f32[400,16]{1,0:T(8,128)}, f32[8,102,128]{2,1,0:T(8,128)}, f32[8,102,128]{2,1,0:T(8,128)}, f32[8,102,128...) custom-call(s32[2]{0:T(128)} %pad_add_fusion.meta_ref, s32[4,1,640]{2,1,0:T(1,128)} %bitcast.28, ...), custom_call_target="tpu_custom_call" | custom-call | flops 12582912000 | bytes 8192000 | tf_op jit(solution)/shard_map/pallas_call | solution.py:422
  57.7 1.7 %collective-permute-start.2 = (bf16[4,102,128]{2,1,0:T(8,128)(2,1)}, bf16[4,102,128]{2,1,0:T(8,128)(2,1)S(1)}, u32[]{:S(2)}, u32[]{:S(2)}) collective-permute-start(bf16[4,102,128]{2,1,0:T(8,128)(2,1)} %get-tuple-element.31), channel_id=1, source_target_pairs={{0,1},{1,2},{2,3},{3,0},{4,5},{5,6},{6,7},{7,4},{8,9},{9,10},{10,1... | collective-permute-start | bytes 313352 | tf_op jit(solution)/shard_map/ppermute | solution.py:318
  59.4 2.2 %collective-permute-start.3 = (bf16[4,102,128]{2,1,0:T(8,128)(2,1)}, bf16[4,102,128]{2,1,0:T(8,128)(2,1)S(1)}, u32[]{:S(2)}, u32[]{:S(2)}) collective-permute-start(bf16[4,102,128]{2,1,0:T(8,128)(2,1)} %get-tuple-element.32), channel_id=1, source_target_pairs={{0,3},{1,0},{2,1},{3,2},{4,7},{5,4},{6,5},{7,6},{8,11},{9,8},{10,9... | collective-permute-start | bytes 313352 | tf_op jit(solution)/shard_map/ppermute | solution.py:318
  61.6 6.2 %shard_map.133 = (f32[8,100,128]{2,1,0:T(8,128)}, f32[8,100,128]{2,1,0:T(8,128)}, f32[8,100,128]{2,1,0:T(8,128)}, bf16[4,100,128]{2,1,0:T(8,128)(2,1)}, bf16[4,100,128]{2,1,0:T(8,128)(2,1)}) custom-call(s32[2]{0:T(128)} %pad_add_fusion.meta_ref, s32[4,1,640]{2,1,0:T(1,128)} %bitcast.32, bf16[4,400,640]{2,1,0:T(8,128)(2,1)} %get-tuple-element.24.grad_ref), custom_call_target="tpu_custom_call" | custom-call | flops 4194304000 | bytes 8192000 | tf_op jit(solution)/shard_map/pallas_call | solution.py:451
  67.9 0.0 collective-permute-done.2
  68.0 0.1 collective-permute-start.4
  68.1 3.9 %collective-permute-start.5 = (bf16[8,102,128]{2,1,0:T(8,128)(2,1)S(1)}, bf16[8,102,128]{2,1,0:T(8,128)(2,1)S(1)}, u32[]{:S(2)}, u32[]{:S(2)}) collective-permute-start(bf16[8,102,128]{2,1,0:T(8,128)(2,1)S(1)} %pad_maximum_fusion.1), channel_id=1, source_target_pairs={{0,3},{1,0},{2,1},{3,2},{4,7},{5,4},{6,5},{7,6},{8,11},{9,8},{10,9... | collective-permute-start | bytes 626696 | tf_op jit(solution)/shard_map/ppermute | solution.py:318
  72.0 3.9 %collective-permute-done.4 = bf16[8,102,128]{2,1,0:T(8,128)(2,1)S(1)} collective-permute-done((bf16[8,102,128]{2,1,0:T(8,128)(2,1)S(1)}, bf16[8,102,128]{2,1,0:T(8,128)(2,1)S(1)}, u32[]{:S(2)}, u32[]{:S(2)}) %collective-permute-start.4) | collective-permute-done | bytes 208928 | tf_op jit(solution)/shard_map/ppermute | solution.py:318
  75.9 0.5 collective-permute-done.5
  76.3 0.8 add_convert_fusion.1
  77.1 5.0 %all-to-all-start.2 = ((bf16[8,102,128]{2,1,0:T(8,128)(2,1)}), bf16[8,102,128]{2,1,0:T(8,128)(2,1)S(1)}, u32[]{:S(2)}, u32[]{:S(2)}) async-start(bf16[8,102,128]{2,1,0:T(8,128)(2,1)} %add_convert_fusion.1), calls=%async_computation.2 | async-start | bytes 425984 | tf_op jit(solution)/shard_map/all_to_all | solution.py:333
  82.1 1.1 collective-permute-start
  83.2 2.8 %collective-permute-start.1 = (bf16[4,100,128]{2,1,0:T(8,128)(2,1)S(1)}, bf16[4,100,128]{2,1,0:T(8,128)(2,1)S(1)}, u32[]{:S(2)}, u32[]{:S(2)}) collective-permute-start(bf16[4,100,128]{2,1,0:T(8,128)(2,1)S(1)} %copy-done.20), channel_id=1, source_target_pairs={{0,3},{1,0},{2,1},{3,2},{4,7},{5,4},{6,5},{7,6},{8,11},{9,8},{10,9... | collective-permute-start | bytes 307208 | tf_op jit(solution)/shard_map/ppermute | solution.py:318
  86.0 2.5 %all-to-all-done.2.in_ref = bf16[8,102,128]{2,1,0:T(8,128)(2,1)S(1)} async-done(((bf16[8,102,128]{2,1,0:T(8,128)(2,1)}), bf16[8,102,128]{2,1,0:T(8,128)(2,1)S(1)}, u32[]{:S(2)}, u32[]{:S(2)}) %all-to-all-start.2) | async-done | bytes 208928 | tf_op jit(solution)/shard_map/all_to_all | solution.py:333
  88.5 0.7 copy-done.1
  89.2 1.6 %shard_map.134 = bf16[8,102,128]{2,1,0:T(8,128)(2,1)} custom-call(s32[8]{0:T(128)} %plan_ref.3, bf16[8,102,128]{2,1,0:T(8,128)(2,1)} %copy-done.1), custom_call_target="tpu_custom_call" | custom-call | tf_op jit(solution)/shard_map/pallas_call | solution.py:323
  90.9 0.0 copy-start.19
  90.9 1.3 collective-permute-start.6
  92.3 2.6 %collective-permute-start.7 = (bf16[8,100,128]{2,1,0:T(8,128)(2,1)S(1)}, bf16[8,100,128]{2,1,0:T(8,128)(2,1)S(1)}, u32[]{:S(2)}, u32[]{:S(2)}) collective-permute-start(bf16[8,100,128]{2,1,0:T(8,128)(2,1)S(1)} %pad_maximum_fusion.3), channel_id=1, source_target_pairs={{0,3},{1,0},{2,1},{3,2},{4,7},{5,4},{6,5},{7,6},{8,11},{9,8},{10,9... | collective-permute-start | bytes 614408 | tf_op jit(solution)/shard_map/ppermute | solution.py:318
  94.9 9.8 %all_to_all.21.refs_0_ = bf16[8,102,128]{2,1,0:T(8,128)(2,1)S(1)} all-to-all(bf16[8,102,128]{2,1,0:T(8,128)(2,1)S(1)} %copy-done), channel_id=1, replica_groups=mesh['bucket'=8,'span'=4] {'bucket'}, dimensions={0} | all-to-all | bytes 417792 | tf_op jit(solution)/shard_map/all_to_all | solution.py:333
  104.7 3.8 %collective-permute-start.13 = (bf16[8,102,128]{2,1,0:T(8,128)(2,1)S(1)}, bf16[8,102,128]{2,1,0:T(8,128)(2,1)S(1)}, u32[]{:S(2)}, u32[]{:S(2)}) collective-permute-start(bf16[8,102,128]{2,1,0:T(8,128)(2,1)S(1)} %all_to_all.21.refs_0_), channel_id=1, source_target_pairs={{0,3},{1,0},{2,1},{3,2},{4,7},{5,4},{6,5},{7,6},{8,11},{9,8},{10,9... | collective-permute-start | bytes 626696 | tf_op jit(solution)/shard_map/ppermute | solution.py:318
  108.5 0.1 add_convert_fusion.refs_0_
  108.6 0.1 collective-permute-start.8
  108.7 3.8 %collective-permute-start.9 = (bf16[8,100,128]{2,1,0:T(8,128)(2,1)S(1)}, bf16[8,100,128]{2,1,0:T(8,128)(2,1)S(1)}, u32[]{:S(2)}, u32[]{:S(2)}) collective-permute-start(bf16[8,100,128]{2,1,0:T(8,128)(2,1)S(1)} %add_convert_fusion.refs_0_), channel_id=1, source_target_pairs={{0,3},{1,0},{2,1},{3,2},{4,7},{5,4},{6,5},{7,6},{8,11},{9,8},{10,9... | collective-permute-start | bytes 614408 | tf_op jit(solution)/shard_map/ppermute | solution.py:318
  112.5 2.2 %collective-permute-done.12.refs_1_ = bf16[8,102,128]{2,1,0:T(8,128)(2,1)S(1)} collective-permute-done((bf16[8,102,128]{2,1,0:T(8,128)(2,1)S(1)}, bf16[8,102,128]{2,1,0:T(8,128)(2,1)S(1)}, u32[]{:S(2)}, u32[]{:S(2)}) %collective-permute-start.12) | collective-permute-done | bytes 208928 | tf_op jit(solution)/shard_map/ppermute | solution.py:318
  114.7 0.1 collective-permute-start.14
  114.8 4.0 %collective-permute-done.13.refs_2_ = bf16[8,102,128]{2,1,0:T(8,128)(2,1)S(1)} collective-permute-done((bf16[8,102,128]{2,1,0:T(8,128)(2,1)S(1)}, bf16[8,102,128]{2,1,0:T(8,128)(2,1)S(1)}, u32[]{:S(2)}, u32[]{:S(2)}) %collective-permute-start.13) | collective-permute-done | bytes 208928 | tf_op jit(solution)/shard_map/ppermute | solution.py:318
  118.7 0.6 collective-permute-start.15
  119.3 4.5 %collective-permute-done.8.refs_1_ = bf16[8,100,128]{2,1,0:T(8,128)(2,1)S(1)} collective-permute-done((bf16[8,100,128]{2,1,0:T(8,128)(2,1)S(1)}, bf16[8,100,128]{2,1,0:T(8,128)(2,1)S(1)}, u32[]{:S(2)}, u32[]{:S(2)}) %collective-permute-start.8) | collective-permute-done | bytes 204832 | tf_op jit(solution)/shard_map/ppermute | solution.py:318
  123.9 0.1 collective-permute-start.10
  123.9 3.8 %collective-permute-done.9.refs_2_ = bf16[8,100,128]{2,1,0:T(8,128)(2,1)S(1)} collective-permute-done((bf16[8,100,128]{2,1,0:T(8,128)(2,1)S(1)}, bf16[8,100,128]{2,1,0:T(8,128)(2,1)S(1)}, u32[]{:S(2)}, u32[]{:S(2)}) %collective-permute-start.9) | collective-permute-done | bytes 204832 | tf_op jit(solution)/shard_map/ppermute | solution.py:318
  127.7 0.8 collective-permute-start.11
  128.5 0.7 copy.15.rel_state_ref
  129.2 1.6 %collective-permute-done.14.refs_3_ = bf16[4,102,128]{2,1,0:T(8,128)(2,1)S(1)} collective-permute-done((bf16[4,102,128]{2,1,0:T(8,128)(2,1)S(1)}, bf16[4,102,128]{2,1,0:T(8,128)(2,1)S(1)}, u32[]{:S(2)}, u32[]{:S(2)}) %collective-permute-start.14) | collective-permute-done | bytes 104480 | tf_op jit(solution)/shard_map/ppermute | solution.py:318
  130.8 0.7 collective-permute-done.15.refs_4_
  131.5 0.6 copy-done.17
  132.1 3.5 %shard_map.136 = (f32[400,1024]{1,0:T(8,128)}, f32[16,400]{1,0:T(8,128)}) custom-call(s32[2]{0:T(128)} %pad_add_fusion.meta_ref, f32[400,1024]{1,0:T(8,128)} %bitcast.20, f32[1,1024]{1,0:T(1,128)} %bitcast.24, f32[16,400]{1,0:T(8,128)} %rel_ref.5, f32[16,1]{1,0:T(8,128)} %copy.15.rel_state_ref, bf16[8,102,128]{2,1,0:T(8,128)(2,1)} %copy-done.2, ...), custom_call_target="tpu_custom_call" | custom-call | tf_op jit(solution)/shard_map/pallas_call | solution.py:343
  135.7 0.6 copy-done.16
  136.3 0.1 copy-done.18
  136.3 3.4 %shard_map.135 = f32[400,1024]{1,0:T(8,128)} custom-call(s32[2]{0:T(128)} %pad_add_fusion.meta_ref, f32[400,1024]{1,0:T(8,128)} %bitcast.22, f32[1,1024]{1,0:T(1,128)} %bitcast.25, bf16[8,100,128]{2,1,0:T(8,128)(2,1)} %copy-done.3, bf16[8,100,128]{2,1,0:T(8,128)(2,1)} %copy-done.7, bf16[8,100,128]{2,1,0:T(8,128)(2,1)} %copy-done.8, ...), custom_call_target="tpu_custom_call" | custom-call | tf_op jit(solution)/shard_map/pallas_call | solution.py:343
  (62 shorter events, 0.4 us)
Async XLA Ops:
  22.3 16.4 %all-to-all-start.1 = ((bf16[8,400,128]{2,1,0:T(8,128)(2,1)}), bf16[8,400,128]{2,1,0:T(8,128)(2,1)S(1)}, u32[]{:S(2)}, u32[]{:S(2)}) async-start(bf16[8,400,128]{2,1,0:T(8,128)(2,1)} %shard_map.131), calls=%async_computation.1 | async-start | bytes 1638400 | tf_op jit(solution)/shard_map/all_to_all | solution.py:333
  38.7 0.9 copy-start.4
  57.7 10.2 %collective-permute-start.2 = (bf16[4,102,128]{2,1,0:T(8,128)(2,1)}, bf16[4,102,128]{2,1,0:T(8,128)(2,1)S(1)}, u32[]{:S(2)}, u32[]{:S(2)}) collective-permute-start(bf16[4,102,128]{2,1,0:T(8,128)(2,1)} %get-tuple-element.31), channel_id=1, source_target_pairs={{0,1},{1,2},{2,3},{3,0},{4,5},{5,6},{6,7},{7,4},{8,9},{9,10},{10,1... | collective-permute-start | bytes 313352 | tf_op jit(solution)/shard_map/ppermute | solution.py:318
  59.4 8.5 %collective-permute-start.3 = (bf16[4,102,128]{2,1,0:T(8,128)(2,1)}, bf16[4,102,128]{2,1,0:T(8,128)(2,1)S(1)}, u32[]{:S(2)}, u32[]{:S(2)}) collective-permute-start(bf16[4,102,128]{2,1,0:T(8,128)(2,1)} %get-tuple-element.32), channel_id=1, source_target_pairs={{0,3},{1,0},{2,1},{3,2},{4,7},{5,4},{6,5},{7,6},{8,11},{9,8},{10,9... | collective-permute-start | bytes 313352 | tf_op jit(solution)/shard_map/ppermute | solution.py:318
  61.6 6.2 %copy-start.14 = (f32[8,102,128]{2,1,0:T(8,128)S(1)}, f32[8,102,128]{2,1,0:T(8,128)}, u32[]{:S(2)}) copy-start(f32[8,102,128]{2,1,0:T(8,128)} %get-tuple-element.30) | copy-start | bytes 1253380
  61.6 6.2 %copy-start.13 = (f32[8,102,128]{2,1,0:T(8,128)S(1)}, f32[8,102,128]{2,1,0:T(8,128)}, u32[]{:S(2)}) copy-start(f32[8,102,128]{2,1,0:T(8,128)} %get-tuple-element.35) | copy-start | bytes 1253380
  67.8 8.5 %copy-start.10 = (f32[8,102,128]{2,1,0:T(8,128)S(1)}, f32[8,102,128]{2,1,0:T(8,128)}, u32[]{:S(2)}) copy-start(f32[8,102,128]{2,1,0:T(8,128)} %get-tuple-element.29) | copy-start | bytes 1253380
  67.9 14.2 %copy-start.21 = (bf16[4,100,128]{2,1,0:T(8,128)(2,1)S(1)}, bf16[4,100,128]{2,1,0:T(8,128)(2,1)}, u32[]{:S(2)}) copy-start(bf16[4,100,128]{2,1,0:T(8,128)(2,1)} %get-tuple-element.27) | copy-start | bytes 307204
  67.9 15.3 %copy-start.20 = (bf16[4,100,128]{2,1,0:T(8,128)(2,1)S(1)}, bf16[4,100,128]{2,1,0:T(8,128)(2,1)}, u32[]{:S(2)}) copy-start(bf16[4,100,128]{2,1,0:T(8,128)(2,1)} %get-tuple-element.28) | copy-start | bytes 307204
  67.9 18.1 %copy-start.12 = (f32[8,100,128]{2,1,0:T(8,128)S(1)}, f32[8,100,128]{2,1,0:T(8,128)}, u32[]{:S(2)}) copy-start(f32[8,100,128]{2,1,0:T(8,128)} %get-tuple-element.26) | copy-start | bytes 1228804
  67.9 18.1 %copy-start.11 = (f32[8,100,128]{2,1,0:T(8,128)S(1)}, f32[8,100,128]{2,1,0:T(8,128)}, u32[]{:S(2)}) copy-start(f32[8,100,128]{2,1,0:T(8,128)} %get-tuple-element.33) | copy-start | bytes 1228804
  68.0 7.9 %collective-permute-start.4 = (bf16[8,102,128]{2,1,0:T(8,128)(2,1)S(1)}, bf16[8,102,128]{2,1,0:T(8,128)(2,1)S(1)}, u32[]{:S(2)}, u32[]{:S(2)}) collective-permute-start(bf16[8,102,128]{2,1,0:T(8,128)(2,1)S(1)} %pad_maximum_fusion), channel_id=1, source_target_pairs={{0,1},{1,2},{2,3},{3,0},{4,5},{5,6},{6,7},{7,4},{8,9},{9,10},{10,1... | collective-permute-start | bytes 626696 | tf_op jit(solution)/shard_map/ppermute | solution.py:318
  68.1 8.2 %collective-permute-start.5 = (bf16[8,102,128]{2,1,0:T(8,128)(2,1)S(1)}, bf16[8,102,128]{2,1,0:T(8,128)(2,1)S(1)}, u32[]{:S(2)}, u32[]{:S(2)}) collective-permute-start(bf16[8,102,128]{2,1,0:T(8,128)(2,1)S(1)} %pad_maximum_fusion.1), channel_id=1, source_target_pairs={{0,3},{1,0},{2,1},{3,2},{4,7},{5,4},{6,5},{7,6},{8,11},{9,8},{10,9... | collective-permute-start | bytes 626696 | tf_op jit(solution)/shard_map/ppermute | solution.py:318
  77.1 31.4 %copy-start.9 = (f32[8,100,128]{2,1,0:T(8,128)S(1)}, f32[8,100,128]{2,1,0:T(8,128)}, u32[]{:S(2)}) copy-start(f32[8,100,128]{2,1,0:T(8,128)} %get-tuple-element.25) | copy-start | bytes 1228804
  77.1 11.4 %all-to-all-start.2 = ((bf16[8,102,128]{2,1,0:T(8,128)(2,1)}), bf16[8,102,128]{2,1,0:T(8,128)(2,1)S(1)}, u32[]{:S(2)}, u32[]{:S(2)}) async-start(bf16[8,102,128]{2,1,0:T(8,128)(2,1)} %add_convert_fusion.1), calls=%async_computation.2 | async-start | bytes 425984 | tf_op jit(solution)/shard_map/all_to_all | solution.py:333
  82.1 8.7 %collective-permute-start = (bf16[4,100,128]{2,1,0:T(8,128)(2,1)S(1)}, bf16[4,100,128]{2,1,0:T(8,128)(2,1)S(1)}, u32[]{:S(2)}, u32[]{:S(2)}) collective-permute-start(bf16[4,100,128]{2,1,0:T(8,128)(2,1)S(1)} %copy-done.21), channel_id=1, source_target_pairs={{0,1},{1,2},{2,3},{3,0},{4,5},{5,6},{6,7},{7,4},{8,9},{9,10},{10,1... | collective-permute-start | bytes 307208 | tf_op jit(solution)/shard_map/ppermute | solution.py:318
  83.2 7.7 %collective-permute-start.1 = (bf16[4,100,128]{2,1,0:T(8,128)(2,1)S(1)}, bf16[4,100,128]{2,1,0:T(8,128)(2,1)S(1)}, u32[]{:S(2)}, u32[]{:S(2)}) collective-permute-start(bf16[4,100,128]{2,1,0:T(8,128)(2,1)S(1)} %copy-done.20), channel_id=1, source_target_pairs={{0,3},{1,0},{2,1},{3,2},{4,7},{5,4},{6,5},{7,6},{8,11},{9,8},{10,9... | collective-permute-start | bytes 307208 | tf_op jit(solution)/shard_map/ppermute | solution.py:318
  88.5 0.7 copy-start.1
  90.8 4.1 %copy-start = (bf16[8,102,128]{2,1,0:T(8,128)(2,1)S(1)}, bf16[8,102,128]{2,1,0:T(8,128)(2,1)}, u32[]{:S(2)}) copy-start(bf16[8,102,128]{2,1,0:T(8,128)(2,1)} %shard_map.134) | copy-start | bytes 626692
  90.9 37.6 %copy-start.19 = (f32[16]{0:T(128)S(1)}, f32[16]{0:T(128)}, u32[]{:S(2)}) copy-start(f32[16]{0:T(128)} %param.16) | copy-start | bytes 196
  90.9 17.6 %collective-permute-start.6 = (bf16[8,100,128]{2,1,0:T(8,128)(2,1)S(1)}, bf16[8,100,128]{2,1,0:T(8,128)(2,1)S(1)}, u32[]{:S(2)}, u32[]{:S(2)}) collective-permute-start(bf16[8,100,128]{2,1,0:T(8,128)(2,1)S(1)} %pad_maximum_fusion.2), channel_id=1, source_target_pairs={{0,1},{1,2},{2,3},{3,0},{4,5},{5,6},{6,7},{7,4},{8,9},{9,10},{10,1... | collective-permute-start | bytes 614408 | tf_op jit(solution)/shard_map/ppermute | solution.py:318
  92.3 16.2 %collective-permute-start.7 = (bf16[8,100,128]{2,1,0:T(8,128)(2,1)S(1)}, bf16[8,100,128]{2,1,0:T(8,128)(2,1)S(1)}, u32[]{:S(2)}, u32[]{:S(2)}) collective-permute-start(bf16[8,100,128]{2,1,0:T(8,128)(2,1)S(1)} %pad_maximum_fusion.3), channel_id=1, source_target_pairs={{0,3},{1,0},{2,1},{3,2},{4,7},{5,4},{6,5},{7,6},{8,11},{9,8},{10,9... | collective-permute-start | bytes 614408 | tf_op jit(solution)/shard_map/ppermute | solution.py:318
  104.7 26.8 %copy-start.2 = (bf16[8,102,128]{2,1,0:T(8,128)(2,1)}, bf16[8,102,128]{2,1,0:T(8,128)(2,1)S(1)}, u32[]{:S(2)}) copy-start(bf16[8,102,128]{2,1,0:T(8,128)(2,1)S(1)} %all_to_all.21.refs_0_) | copy-start | bytes 626692
  104.7 10.0 %collective-permute-start.12 = (bf16[8,102,128]{2,1,0:T(8,128)(2,1)S(1)}, bf16[8,102,128]{2,1,0:T(8,128)(2,1)S(1)}, u32[]{:S(2)}, u32[]{:S(2)}) collective-permute-start(bf16[8,102,128]{2,1,0:T(8,128)(2,1)S(1)} %all_to_all.21.refs_0_), channel_id=1, source_target_pairs={{0,1},{1,2},{2,3},{3,0},{4,5},{5,6},{6,7},{7,4},{8,9},{9,10},{10,1... | collective-permute-start | bytes 626696 | tf_op jit(solution)/shard_map/ppermute | solution.py:318
  104.7 14.0 %collective-permute-start.13 = (bf16[8,102,128]{2,1,0:T(8,128)(2,1)S(1)}, bf16[8,102,128]{2,1,0:T(8,128)(2,1)S(1)}, u32[]{:S(2)}, u32[]{:S(2)}) collective-permute-start(bf16[8,102,128]{2,1,0:T(8,128)(2,1)S(1)} %all_to_all.21.refs_0_), channel_id=1, source_target_pairs={{0,3},{1,0},{2,1},{3,2},{4,7},{5,4},{6,5},{7,6},{8,11},{9,8},{10,9... | collective-permute-start | bytes 626696 | tf_op jit(solution)/shard_map/ppermute | solution.py:318
  108.6 27.0 %copy-start.3 = (bf16[8,100,128]{2,1,0:T(8,128)(2,1)}, bf16[8,100,128]{2,1,0:T(8,128)(2,1)S(1)}, u32[]{:S(2)}) copy-start(bf16[8,100,128]{2,1,0:T(8,128)(2,1)S(1)} %add_convert_fusion.refs_0_) | copy-start | bytes 614404
  108.6 15.2 %collective-permute-start.8 = (bf16[8,100,128]{2,1,0:T(8,128)(2,1)S(1)}, bf16[8,100,128]{2,1,0:T(8,128)(2,1)S(1)}, u32[]{:S(2)}, u32[]{:S(2)}) collective-permute-start(bf16[8,100,128]{2,1,0:T(8,128)(2,1)S(1)} %add_convert_fusion.refs_0_), channel_id=1, source_target_pairs={{0,1},{1,2},{2,3},{3,0},{4,5},{5,6},{6,7},{7,4},{8,9},{9,10},{10,1... | collective-permute-start | bytes 614408 | tf_op jit(solution)/shard_map/ppermute | solution.py:318
  108.7 19.0 %collective-permute-start.9 = (bf16[8,100,128]{2,1,0:T(8,128)(2,1)S(1)}, bf16[8,100,128]{2,1,0:T(8,128)(2,1)S(1)}, u32[]{:S(2)}, u32[]{:S(2)}) collective-permute-start(bf16[8,100,128]{2,1,0:T(8,128)(2,1)S(1)} %add_convert_fusion.refs_0_), channel_id=1, source_target_pairs={{0,3},{1,0},{2,1},{3,2},{4,7},{5,4},{6,5},{7,6},{8,11},{9,8},{10,9... | collective-permute-start | bytes 614408 | tf_op jit(solution)/shard_map/ppermute | solution.py:318
  114.7 16.8 %copy-start.5 = (bf16[8,102,128]{2,1,0:T(8,128)(2,1)}, bf16[8,102,128]{2,1,0:T(8,128)(2,1)S(1)}, u32[]{:S(2)}) copy-start(bf16[8,102,128]{2,1,0:T(8,128)(2,1)S(1)} %collective-permute-done.12.refs_1_) | copy-start | bytes 626692
  114.7 16.1 %collective-permute-start.14 = (bf16[4,102,128]{2,1,0:T(8,128)(2,1)S(1)}, bf16[4,102,128]{2,1,0:T(8,128)(2,1)S(1)}, u32[]{:S(2)}, u32[]{:S(2)}) collective-permute-start(bf16[4,102,128]{2,1,0:T(8,128)(2,1)S(1)} %slice.58), channel_id=1, source_target_pairs={{0,1},{1,2},{2,3},{3,0},{4,5},{5,6},{6,7},{7,4},{8,9},{9,10},{10,1... | collective-permute-start | bytes 313352 | tf_op jit(solution)/shard_map/ppermute | solution.py:318
  118.7 12.8 %copy-start.6 = (bf16[8,102,128]{2,1,0:T(8,128)(2,1)}, bf16[8,102,128]{2,1,0:T(8,128)(2,1)S(1)}, u32[]{:S(2)}) copy-start(bf16[8,102,128]{2,1,0:T(8,128)(2,1)S(1)} %collective-permute-done.13.refs_2_) | copy-start | bytes 626692
  118.7 12.7 %collective-permute-start.15 = (bf16[4,102,128]{2,1,0:T(8,128)(2,1)S(1)}, bf16[4,102,128]{2,1,0:T(8,128)(2,1)S(1)}, u32[]{:S(2)}, u32[]{:S(2)}) collective-permute-start(bf16[4,102,128]{2,1,0:T(8,128)(2,1)S(1)} %slice.59), channel_id=1, source_target_pairs={{0,3},{1,0},{2,1},{3,2},{4,7},{5,4},{6,5},{7,6},{8,11},{9,8},{10,9... | collective-permute-start | bytes 313352 | tf_op jit(solution)/shard_map/ppermute | solution.py:318
  123.8 11.8 %copy-start.7 = (bf16[8,100,128]{2,1,0:T(8,128)(2,1)}, bf16[8,100,128]{2,1,0:T(8,128)(2,1)S(1)}, u32[]{:S(2)}) copy-start(bf16[8,100,128]{2,1,0:T(8,128)(2,1)S(1)} %collective-permute-done.8.refs_1_) | copy-start | bytes 614404
  123.9 11.8 %collective-permute-start.10 = (bf16[4,100,128]{2,1,0:T(8,128)(2,1)S(1)}, bf16[4,100,128]{2,1,0:T(8,128)(2,1)S(1)}, u32[]{:S(2)}, u32[]{:S(2)}) collective-permute-start(bf16[4,100,128]{2,1,0:T(8,128)(2,1)S(1)} %slice.56), channel_id=1, source_target_pairs={{0,1},{1,2},{2,3},{3,0},{4,5},{5,6},{6,7},{7,4},{8,9},{9,10},{10,1... | collective-permute-start | bytes 307208 | tf_op jit(solution)/shard_map/ppermute | solution.py:318
  127.7 8.0 %copy-start.8 = (bf16[8,100,128]{2,1,0:T(8,128)(2,1)}, bf16[8,100,128]{2,1,0:T(8,128)(2,1)S(1)}, u32[]{:S(2)}) copy-start(bf16[8,100,128]{2,1,0:T(8,128)(2,1)S(1)} %collective-permute-done.9.refs_2_) | copy-start | bytes 614404
  127.7 7.9 %collective-permute-start.11 = (bf16[4,100,128]{2,1,0:T(8,128)(2,1)S(1)}, bf16[4,100,128]{2,1,0:T(8,128)(2,1)S(1)}, u32[]{:S(2)}, u32[]{:S(2)}) collective-permute-start(bf16[4,100,128]{2,1,0:T(8,128)(2,1)S(1)} %slice.57), channel_id=1, source_target_pairs={{0,3},{1,0},{2,1},{3,2},{4,7},{5,4},{6,5},{7,6},{8,11},{9,8},{10,9... | collective-permute-start | bytes 307208 | tf_op jit(solution)/shard_map/ppermute | solution.py:318
  130.8 0.7 copy-start.15
  131.5 0.6 copy-start.17
  135.6 0.6 copy-start.16
  135.7 0.7 copy-start.18

commit v3 on v2

--- a/solution.py
+++ b/solution.py
@@ -13,12 +13,15 @@
 
 F32 = jnp.float32
 BF16 = jnp.bfloat16
-VMEM_BYTES = 56 * 1024 * 1024
+MIB = 1024 * 1024
 SMEM_SPEC = pl.BlockSpec(memory_space=pltpu.SMEM)
 
 
-def params():
-    return pltpu.CompilerParams(vmem_limit_bytes=VMEM_BYTES)
+ANY_SPEC = pl.BlockSpec(memory_space=pl.ANY)
+
+
+def params(mib):
+    return pltpu.CompilerParams(vmem_limit_bytes=mib * MIB)
 
 
 def cost(flops, nbytes):
@@ -69,7 +72,7 @@
     return jnp.where(match, 1.0, 0.0)
 
 
-def prep_kernel(steps, meta_ref, hid_ref, rid_ref, src_ref, rel_ref, q_ref, head_ref, low_ref):
+def prep_kernel(steps, meta_ref, hid_ref, rid_ref, src_ref, rel_ref, out_ref, low_ref):
     step = pl.program_id(0)
 
     @pl.when(step == 0)
@@ -85,8 +88,8 @@
         half = head.shape[0] // 2
         h_re, h_im, r_re, r_im = head[:half], head[half:], rel[:half], rel[half:]
         query = jnp.concatenate([h_re * r_re - h_im * r_im, h_re * r_im + h_im * r_re], axis=0)
-        q_ref[0] = query.astype(BF16)
-        head_ref[0] = head.astype(BF16)
+        out_ref[0, 0] = query.astype(BF16)
+        out_ref[0, 1] = head.astype(BF16)
 
 
 def ring_plan(lanes, pieces):
@@ -106,22 +109,23 @@
     return jnp.concatenate([total[:first], total[first:last] + part, total[last:]], axis=0)
 
 
-def ring_sum(parts, waits):
-    lanes = lax.axis_size("span")
-    if lanes == 1:
-        return parts[0].astype(BF16)
-    plan = ring_plan(lanes, parts[0].shape[0])
-    blocks = {away: part for part, (away, _, _) in zip(parts, plan)}
-    reach, first = lanes // 2, plan[-1][1]
-    ahead, behind = blocks[reach].astype(BF16), blocks[-reach].astype(BF16)
-    for away in range(reach, 0, -1):
-        ahead, behind = shift_span(ahead, 1), shift_span(behind, -1)
-        for wait in waits[reach - away : reach - away + 1]:
-            ahead, behind = after((ahead, behind), wait)
-        if away > 1:
-            ahead = add_pieces(blocks[away - 1], ahead, 0).astype(BF16)
-            behind = add_pieces(blocks[1 - away], behind, first).astype(BF16)
-    return add_pieces(add_pieces(parts[0], ahead, 0), behind, first).astype(BF16)
+def ring_payload(parts, away, ahead=None, behind=None):
+    plan = ring_plan(lax.axis_size("span"), parts[0].shape[0])
+    blocks = {far: part for part, (far, _, _) in zip(parts, plan)}
+    if ahead is None:
+        return blocks[away].astype(BF16), blocks[-away].astype(BF16)
+    ahead = add_pieces(blocks[away], ahead, 0)
+    return ahead.astype(BF16), add_pieces(blocks[-away], behind, plan[-1][1]).astype(BF16)
+
+
+def ring_total(parts, ahead, behind):
+    plan = ring_plan(lax.axis_size("span"), parts[0].shape[0])
+    return add_pieces(add_pieces(parts[0], ahead, 0), behind, plan[-1][1]).astype(BF16)
+
+
+def shift_two(x, y, by):
+    both = shift_span(jnp.concatenate([x, y], axis=0), by)
+    return both[: x.shape[0]], both[x.shape[0] :]
 
 
 def ring_shapes(shape, lanes):
@@ -174,39 +178,51 @@
 
 
 def main_kernel(
-    steps, lanes, packed, meta_ref, tid_ref, rid_ref, rel_ref, q_ref, head_ref, parts_ref, *refs
+    steps, lanes, packed, meta_ref, tid_ref, rid_ref, rel_ref, edge_ref, parts_ref, *refs
 ):
     grad_ref, rel_out_ref = refs[:2]
-    outs = refs[2:-4]
-    table_ref, acc_ref, hot_ref, coef_ref = refs[-4:]
+    outs = refs[2:-6]
+    table_ref, acc_ref, hot_ref, coef_ref, stage_ref, sems = refs[-6:]
     step = pl.program_id(0)
 
     @pl.when(step == 0)
     def _():
-        width = parts_ref.shape[2]
-        for b in range(parts_ref.shape[0]):
-            table_ref[:, b * width : (b + 1) * width] = parts_ref[b]
+        pieces, _, width = parts_ref.shape
+        copies = [
+            pltpu.make_async_copy(parts_ref.at[b], there, sems.at[b])
+            for b, there in enumerate(
+                table_ref.at[:, pl.ds(b * width, width)] if width % 128 == 0 else stage_ref.at[b]
+                for b in range(pieces)
+            )
+        ]
+        for copy in copies:
+            copy.start()
         acc_ref[...] = jnp.zeros_like(acc_ref)
         rel_out_ref[...] = jnp.zeros_like(rel_out_ref)
+        for copy in copies:
+            copy.wait()
+        if width % 128:
+            for b in range(pieces):
+                table_ref[:, b * width : (b + 1) * width] = stage_ref[b]
 
     @pl.when(is_live(meta_ref, step, steps, tid_ref.shape[2]))
     def _():
         ids = live_ids(tid_ref[0], meta_ref, step, steps)
         hot_ref[...] = one_hot(ids, table_ref.shape[1])
         tail = dot_nn(table_ref[...], hot_ref[...]).astype(BF16)
-        scores = dot_tn(q_ref[0], tail)
+        scores = dot_tn(edge_ref[0, 0], tail)
         sig = 0.5 * jnp.tanh(0.5 * scores) + 0.5
         diagonal = lax.broadcasted_iota(jnp.int32, scores.shape, 0) == lax.broadcasted_iota(
             jnp.int32, scores.shape, 1
         )
         coef_ref[...] = jnp.where(diagonal, sig - 1.0, NEG_WEIGHT * sig).astype(BF16)
-        grad_tail = dot_nn(q_ref[0], coef_ref[...])
+        grad_tail = dot_nn(edge_ref[0, 0], coef_ref[...])
         acc_ref[...] += dot_nt(grad_tail.astype(BF16), hot_ref[...])
 
         kinds = live_ids(rid_ref[0], meta_ref, step, steps)
         kind = kind_hot(kinds, rel_ref.shape[0])
         rel = relation_columns(rel_ref, kind)
-        head = head_ref[0].astype(F32)
+        head = edge_ref[0, 1].astype(F32)
         half = head.shape[0] // 2
         h_re, h_im, r_re, r_im = head[:half], head[half:], rel[:half], rel[half:]
         grad_query = dot_nt(tail, coef_ref[...])
@@ -253,20 +269,39 @@
     @pl.when(step == steps - 1)
     def _():
         emit(lanes, meta_ref[1], acc_ref, outs)
-
-
-def pick_kernel(plan_ref, in_ref, out_ref):
-    for b in range(in_ref.shape[0]):
-        out_ref[b] = in_ref[plan_ref[b]]
-
-
-def place_kernel(block, plan_ref, in_ref, out_ref):
-    for b in range(in_ref.shape[0]):
-        out_ref[plan_ref[b]] = in_ref[b]
+        block = acc_ref.shape[0] // lanes
+        for out in outs:
+            if out.shape[1] > block:
+                out[:, block:] = jnp.zeros((out.shape[0], out.shape[1] - block, out.shape[2]), out.dtype)
+
+
+def pick_kernel(plan_ref, in_ref, out_ref, sems):
+    copies = [
+        pltpu.make_async_copy(in_ref.at[plan_ref[b]], out_ref.at[b], sems.at[b])
+        for b in range(in_ref.shape[0])
+    ]
+    for copy in copies:
+        copy.start()
+    for copy in copies:
+        copy.wait()
+
+
+def place_kernel(block, plan_ref, in_ref, out_ref, held_ref, load_sem, sems):
+    load = pltpu.make_async_copy(in_ref, held_ref, load_sem)
+    load.start()
+    load.wait()
     if in_ref.shape[1] > block:
-        total = jnp.sum(in_ref[:, block:].astype(F32), axis=0).astype(BF16)
+        total = jnp.sum(held_ref[:, block:].astype(F32), axis=0).astype(BF16)
         for b in range(in_ref.shape[0]):
-            out_ref[b, block:] = total
+            held_ref[b, block:] = total
+    copies = [
+        pltpu.make_async_copy(held_ref.at[b], out_ref.at[plan_ref[b]], sems.at[b])
+        for b in range(in_ref.shape[0])
+    ]
+    for copy in copies:
+        copy.start()
+    for copy in copies:
+        copy.wait()
 
 
 def adagrad(table, state, grad, axis):
@@ -274,33 +309,59 @@
     return table - grad * (LEARN_RATE / jnp.sqrt(state + mean))
 
 
-def update_kernel(lanes, meta_ref, table_ref, state_ref, *refs):
-    parts, out_ref, grad_ref = refs[:-2], refs[-2], refs[-1]
+def update_kernel(lanes, joined, meta_ref, *refs):
+    count = len(ring_plan(lanes, 2))
+    if joined:
+        table_any, state_ref, rel_ref, rel_state_ref = refs[:4]
+        parts_any, refs = refs[4 : 4 + count], refs[4 + count :]
+        out_any, rel_out_ref, rel_grad_ref = refs[:3]
+        refs = refs[3:]
+    else:
+        table_any, state_ref = refs[:2]
+        parts_any, out_any, refs = refs[2 : 2 + count], refs[2 + count], refs[3 + count :]
+    table_ref, grad_ref, parts, (part_sems, load_sems, store_sems) = refs[0], refs[1], refs[2:-3], refs[-3:]
+    features, rows = table_ref.shape
+    chunk = 256 if rows % 256 == 0 else rows
+    spots = [pl.ds(first, chunk) for first in range(0, rows, chunk)]
+    fetches = [
+        pltpu.make_async_copy(far, near, part_sems.at[k])
+        for k, (far, near) in enumerate(zip(parts_any, parts))
+    ]
+    loads = [
+        pltpu.make_async_copy(table_any.at[:, spot], table_ref.at[:, spot], load_sems.at[k])
+        for k, spot in enumerate(spots)
+    ]
+    stores = [
+        pltpu.make_async_copy(table_ref.at[:, spot], out_any.at[:, spot], store_sems.at[k])
+        for k, spot in enumerate(spots)
+    ]
+    for copy in fetches + loads:
+        copy.start()
+    for copy in fetches:
+        copy.wait()
     assemble(lanes, meta_ref[1], parts, grad_ref)
-    out_ref[...] = adagrad(table_ref[...], state_ref[...], grad_ref[...], 0)
-
-
-def update_both_kernel(lanes, meta_ref, table_ref, state_ref, rel_ref, rel_state_ref, *refs):
-    parts = refs[:-4]
-    out_ref, rel_out_ref, grad_ref, rel_grad_ref = refs[-4:]
-    assemble(lanes, meta_ref[1], parts, grad_ref)
-    out_ref[...] = adagrad(table_ref[...], state_ref[...], grad_ref[...], 0)
-    block = rel_ref.shape[1] // lanes
-    each = parts[0].shape[1] - block
-    plan = ring_plan(lanes, parts[0].shape[0])
-    for at in range(lanes):
-
-        @pl.when(meta_ref[1] == at)
-        def _():
-            for part, (behind, first, count) in zip(parts, plan):
-                col = ((at - behind) % lanes) * block
-                for b in range(count):
-                    row = (first + b) * each
-                    rel_grad_ref[row : row + each, col : col + block] = part[
-                        b, block:, :block
-                    ].astype(F32)
-
-    rel_out_ref[...] = adagrad(rel_ref[...], rel_state_ref[...], rel_grad_ref[...], 1)
+    for spot, load, store in zip(spots, loads, stores):
+        load.wait()
+        table_ref[:, spot] = adagrad(table_ref[:, spot], state_ref[:, spot], grad_ref[:, spot], 0)
+        store.start()
+    if joined:
+        block = features // lanes
+        each = parts[0].shape[1] - block
+        plan = ring_plan(lanes, parts[0].shape[0])
+        for at in range(lanes):
+
+            @pl.when(meta_ref[1] == at)
+            def _():
+                for part, (behind, first, pieces) in zip(parts, plan):
+                    col = ((at - behind) % lanes) * block
+                    for b in range(pieces):
+                        row = (first + b) * each
+                        piece = part[b, block:, :block].astype(F32)
+                        rel_grad_ref[row : row + each, col : col + block] = piece
+
+        rel_out_ref[...] = adagrad(rel_ref[...], rel_state_ref[...], rel_grad_ref[...], 1)
+    for store in stores:
+        store.wait()
 
 
 def whole(shape):
@@ -318,17 +379,6 @@
     return lax.ppermute(x, "span", [(i, (i + by) % count) for i in range(count)])
 
 
-def plain(kernel, out, *operands, smem=1):
-    vmem = pl.BlockSpec(memory_space=pltpu.VMEM)
-    return pl.pallas_call(
-        kernel,
-        out_shape=out,
-        in_specs=[SMEM_SPEC] * smem + [vmem] * (len(operands) - smem),
-        out_specs=vmem,
-        compiler_params=params(),
-    )(*operands)
-
-
 def swap_buckets(x):
     return lax.all_to_all(x, "bucket", split_axis=0, concat_axis=0, tiled=True)
 
@@ -337,17 +387,23 @@
     return lax.optimization_barrier((x, y))[0]
 
 
-def update(kernel, lanes, meta, weights, parts):
+def update(lanes, meta, table, state, parts, relation=None, relation_state=None):
+    joined = relation is not None
     vmem = pl.BlockSpec(memory_space=pltpu.VMEM)
-    tables = weights[::2]
+    dma = pltpu.SemaphoreType.DMA
+    extra = (relation, relation_state) if joined else ()
+    chunks = max(1, table.shape[1] // 256)
     return pl.pallas_call(
-        functools.partial(kernel, lanes),
-        out_shape=[jax.ShapeDtypeStruct(t.shape, F32) for t in tables],
-        in_specs=[SMEM_SPEC] + [vmem] * (len(weights) + len(parts)),
-        out_specs=[vmem] * len(tables),
-        scratch_shapes=[pltpu.VMEM(t.shape, F32) for t in tables],
-        compiler_params=params(),
-    )(meta, *weights, *parts)
+        functools.partial(update_kernel, lanes, joined),
+        out_shape=[jax.ShapeDtypeStruct(t.shape, F32) for t in (table,) + extra[:1]],
+        in_specs=[SMEM_SPEC, ANY_SPEC, vmem] + [vmem] * len(extra) + [ANY_SPEC] * len(parts),
+        out_specs=[ANY_SPEC] + [vmem] * joined,
+        scratch_shapes=[pltpu.VMEM(t.shape, F32) for t in extra[:1]]
+        + [pltpu.VMEM(table.shape, F32)] * 2
+        + [pltpu.VMEM(part.shape, BF16) for part in parts]
+        + [dma((len(parts),)), dma((chunks,)), dma((chunks,))],
+        compiler_params=params(24),
+    )(meta, table, state, *extra, *parts)
 
 
 def sum_all(x):
@@ -392,19 +448,27 @@
 
     owned = target_cols.astype(BF16).reshape(features, buckets, width).transpose(1, 0, 2)
     spread = swap_buckets(owned)
-    chosen = plain(pick_kernel, jax.ShapeDtypeStruct(owned.shape, BF16), plan, spread)
+    dma = pltpu.SemaphoreType.DMA
+    chosen = pl.pallas_call(
+        pick_kernel,
+        out_shape=jax.ShapeDtypeStruct(owned.shape, BF16),
+        in_specs=[SMEM_SPEC, ANY_SPEC],
+        out_specs=ANY_SPEC,
+        scratch_shapes=[dma((buckets,))],
+        compiler_params=params(8),
+    )(plan, spread)
     fetched = swap_buckets(chosen)
     packed = kinds % buckets == 0 and width >= block
     pieces = (buckets, block, width)
-    piece_shape = jax.ShapeDtypeStruct(pieces, BF16)
     bundles = (buckets, block + kinds // buckets, width) if packed else pieces
     bundle_shape = jax.ShapeDtypeStruct(bundles, BF16)
 
     edge_shape = (steps, features, E_CH)
-    query, head = pl.pallas_call(
+    both_shape = (steps, 2) + edge_shape[1:]
+    edges = pl.pallas_call(
         functools.partial(prep_kernel, steps),
         grid=(steps,),
-        out_shape=[jax.ShapeDtypeStruct(edge_shape, BF16)] * 2,
+        out_shape=jax.ShapeDtypeStruct(both_shape, BF16),
         in_specs=[
             SMEM_SPEC,
             per_span(hid.shape),
@@ -412,13 +476,13 @@
             whole(source_cols.shape),
             whole(relation.shape),
         ],
-        out_specs=[per_span(edge_shape)] * 2,
+        out_specs=per_span(both_shape),
         scratch_shapes=[pltpu.VMEM((features, rows), BF16)],
-        compiler_params=params(),
+        compiler_params=params(56),
         cost_estimate=cost(4 * steps * features * rows * E_CH, 8 * features * steps * E_CH),
     )(meta, hid, rid, source_cols, relation)
 
-    bundle_outs, piece_outs = ring_shapes(bundles, lanes), ring_shapes(pieces, lanes)
+    bundle_outs = ring_shapes(bundles, lanes)
     grad_head, rel_part, *target_out = pl.pallas_call(
         functools.partial(main_kernel, steps, lanes, packed),
         grid=(steps,),
@@ -432,9 +496,8 @@
             per_span(tid.shape),
             per_span(rid.shape),
             whole(relation.shape),
-            per_span(edge_shape),
-            per_span(edge_shape),
-            whole(owned.shape),
+            per_span(both_shape),
+            ANY_SPEC,
         ],
         out_specs=[per_span(edge_shape), whole((features, kinds))]
         + [whole(out.shape) for out in bundle_outs],
@@ -443,38 +506,59 @@
             pltpu.VMEM((features, rows), F32),
             pltpu.VMEM((rows, E_CH), BF16),
             pltpu.VMEM((E_CH, E_CH), BF16),
+            pltpu.VMEM(owned.shape if width % 128 else (16, 128), BF16),
+            dma((buckets,)),
         ],
-        compiler_params=params(),
+        compiler_params=params(48),
         cost_estimate=cost(12 * steps * features * rows * E_CH, 8 * features * steps * E_CH),
-    )(meta, tid, rid, relation, query, head, fetched)
+    )(meta, tid, rid, relation, edges, fetched)
 
     source_out = pl.pallas_call(
         functools.partial(source_kernel, steps, lanes),
         grid=(steps,),
-        out_shape=piece_outs,
+        out_shape=bundle_outs,
         in_specs=[SMEM_SPEC, per_span(hid.shape), per_span(edge_shape)],
-        out_specs=[whole(out.shape) for out in piece_outs],
+        out_specs=[whole(out.shape) for out in bundle_outs],
         scratch_shapes=[pltpu.VMEM((features, rows), F32)],
-        compiler_params=params(),
+        compiler_params=params(24),
         cost_estimate=cost(4 * steps * features * rows * E_CH, 8 * features * steps * E_CH),
     )(meta, hid, grad_head)
 
-    target_sum = ring_sum(target_out, [source_out])
+    reach = lanes // 2
+    ahead, behind = ring_payload(target_out, reach)
+    for away in range(reach - 1, 0, -1):
+        ahead, behind = shift_span(ahead, 1), shift_span(behind, -1)
+        ahead, behind = after((ahead, behind), source_out)
+        ahead, behind = ring_payload(target_out, away, ahead, behind)
+    source_ahead, source_behind = ring_payload(source_out, reach)
+    ahead, source_ahead = shift_two(ahead, source_ahead, 1)
+    behind, source_behind = shift_two(behind, source_behind, -1)
+    target_sum = ring_total(target_out, ahead, behind)
     returned = swap_buckets(target_sum)
-    placing = functools.partial(place_kernel, block)
-    sorted_out = plain(placing, bundle_shape, plan, returned)
+    sorted_out = pl.pallas_call(
+        functools.partial(place_kernel, block),
+        out_shape=bundle_shape,
+        in_specs=[SMEM_SPEC, ANY_SPEC],
+        out_specs=ANY_SPEC,
+        scratch_shapes=[pltpu.VMEM(bundles, BF16), dma, dma((buckets,))],
+        compiler_params=params(16),
+    )(plan, returned)
     target_home = swap_buckets(sorted_out)
-    source_sum = ring_sum(source_out, [sorted_out])
+    for away in range(reach - 1, 0, -1):
+        source_ahead, source_behind = after((source_ahead, source_behind), target_sum)
+        source_ahead, source_behind = ring_payload(source_out, away, source_ahead, source_behind)
+        source_ahead, source_behind = shift_span(source_ahead, 1), shift_span(source_behind, -1)
+    source_ahead, source_behind = after((source_ahead, source_behind), returned)
+    source_sum = ring_total(source_out, source_ahead, source_behind)
     source_parts = gather_span(source_sum)
     home_parts = gather_span(target_home)
-    source_weights = (source_cols, source_state.reshape(1, rows))
-    target_weights = (target_cols, target_state.reshape(1, rows))
-    (new_source,) = update(update_kernel, lanes, meta, source_weights, source_parts)
+    (new_source,) = update(lanes, meta, source_cols, source_state.reshape(1, rows), source_parts)
+    target_update = (lanes, meta, target_cols, target_state.reshape(1, rows), home_parts)
     if packed:
-        weights = target_weights + (relation, relation_state.reshape(kinds, 1))
-        new_target, new_relation = update(update_both_kernel, lanes, meta, weights, home_parts)
+        relation_update = (relation, relation_state.reshape(kinds, 1))
+        new_target, new_relation = update(*target_update, *relation_update)
     else:
-        (new_target,) = update(update_kernel, lanes, meta, target_weights, home_parts)
+        (new_target,) = update(*target_update)
         rel_total = sum_all(rel_part).T
         mean = jnp.mean(rel_total * rel_total, axis=1)
         new_relation = relation - LEARN_RATE * rel_total / jnp.sqrt(relation_state + mean)[:, None]

time: 140 us -> 132 us (0.943)
  Pallas kernels: 41.6 us -> 29.8 us
  starting transfers between devices: 33.3 us -> 27 us
  blocking collectives: 27.7 us -> 33.7 us
  waiting for transfers between devices: 28.5 us -> 34.4 us
  local copies, waits for them, and re-layouts: 3.7 us -> 2.17 us
    pallas_call x1, Pallas kernels: 18.1 us -> 11.2 us  [per_device(): pl.pallas_call(functools.partial(main_kernel, steps, lanes, packed), grid...]
    all_to_all x2, blocking collectives: 27.7 us -> 33.7 us  [swap_buckets(): return lax.all_to_all(x, 'bucket', split_axis=0, concat_axis=0, tiled=True)]
    ppermute x16 -> x14, waiting for transfers between devices: 21.1 us -> 26 us  [shift_span(): lax.ppermute(x, 'span', [(i, (i + by) % count) for i in range(count)])]
    ppermute x16 -> x14, starting transfers between devices: 24.8 us -> 20 us  [shift_span(): lax.ppermute(x, 'span', [(i, (i + by) % count) for i in range(count)])]
    pallas_call x1, Pallas kernels: 6.2 us -> 2.6 us  [per_device(): pl.pallas_call(functools.partial(source_kernel, steps, lanes), grid=(step...]
    unnamed x44 -> x22, local copies, waits for them, and re-layouts: 2.92 us -> 0.04 us
    slice x4, local copies, waits for them, and re-layouts: 0.03 us -> 1.95 us  [gather_span(): parts += [shift_span(ahead[:half], 1), shift_span(behind[half:], -1)]]
    all_to_all x2, starting transfers between devices: 8.56 us -> 6.97 us  [swap_buckets(): return lax.all_to_all(x, 'bucket', split_axis=0, concat_axis=0, tiled=True)]
  transfers between devices with their start and end apart: 18 -> 16, of which waited for: 10 -> 10; matrix products, arithmetic and copies ran while one was open for 1% -> 3% of each run, Pallas kernels for 13% -> 10%
where the time goes in v3:
time: 132 us
  waiting for transfers between devices  34.4 us (26%)
  blocking collectives  33.7 us (26%)
  Pallas kernels  29.8 us (23%)
  starting transfers between devices  27 us (20%)
  other arithmetic  3.24 us (2%)
  local copies, waits for them, and re-layouts  2.17 us (2%)
  between operations  1.54 us (1%)
    all_to_all x2, blocking collectives, swap_buckets(): return lax.all_to_all(x, 'bucket', split_axis=0, concat_axis=0, tiled=True)  33.7 us
    ppermute x14, waiting for transfers between devices, shift_span(): lax.ppermute(x, 'span', [(i, (i + by) % count) for i in range(count)])  26 us
    ppermute x14, starting transfers between devices, shift_span(): lax.ppermute(x, 'span', [(i, (i + by) % count) for i in range(count)])  20 us
    pallas_call x1, Pallas kernels, per_device(): pl.pallas_call(functools.partial(main_kernel, steps, lanes, packed), grid...  11.2 us
    all_to_all x2, waiting for transfers between devices, swap_buckets(): return lax.all_to_all(x, 'bucket', split_axis=0, concat_axis=0, tiled=True)  8.37 us
    pallas_call x2, Pallas kernels, update(): pl.pallas_call(functools.partial(update_kernel, lanes, joined), out_shape...  7.37 us
    all_to_all x2, starting transfers between devices, swap_buckets(): return lax.all_to_all(x, 'bucket', split_axis=0, concat_axis=0, tiled=True)  6.97 us
    pallas_call x1, Pallas kernels, per_device(): pl.pallas_call(functools.partial(prep_kernel, steps), grid=(steps,), out_...  5.58 us
  transfers between devices with their start and end apart: 16, of which 10 were waited for; matrix products, arithmetic and copies ran while one was open for 3% of the time, Pallas kernels for 10%

profile of v3, /device:TPU:0, one launch (start us, length us, event | category | flops | bytes accessed | tf_op | source)
XLA Modules:
  0.0 131.8 jit_solution(15498287379848493737)
XLA Ops:
  0.6 1.5 %bitcast_bitcast_fusion = bf16[8,400,128]{2,1,0:T(8,128)(2,1)S(1)} fusion(f32[1024,400]{0,1:T(8,128)} %param.12), kind=kLoop, calls=%fused_computation | loop fusion | flops 409600 | bytes 2457600 | tf_op jit(solution)/shard_map/transpose | solution.py:449
  2.2 17.9 %all_to_all.20.in_ref = bf16[8,400,128]{2,1,0:T(8,128)(2,1)S(1)} all-to-all(bf16[8,400,128]{2,1,0:T(8,128)(2,1)S(1)} %bitcast_bitcast_fusion), channel_id=1, replica_groups=mesh['bucket'=8,'span'=4] {'bucket'}, dimensions={0} | all-to-all | bytes 1638400 | tf_op jit(solution)/shard_map/all_to_all | solution.py:383
  20.1 1.5 %shard_map.131 = bf16[8,400,128]{2,1,0:T(8,128)(2,1)} custom-call(s32[8]{0:T(128)S(1)} %copy-done.5, bf16[8,400,128]{2,1,0:T(8,128)(2,1)S(1)} %all_to_all.20.in_ref), custom_call_target="tpu_custom_call" | custom-call | tf_op jit(solution)/shard_map/pallas_call | solution.py:452
  21.6 3.6 %all-to-all-start.1 = ((bf16[8,400,128]{2,1,0:T(8,128)(2,1)}), bf16[8,400,128]{2,1,0:T(8,128)(2,1)S(1)}, u32[]{:S(2)}, u32[]{:S(2)}) async-start(bf16[8,400,128]{2,1,0:T(8,128)(2,1)} %shard_map.131), calls=%async_computation.1 | async-start | bytes 1638400 | tf_op jit(solution)/shard_map/all_to_all | solution.py:383
  25.8 0.6 pad_add_fusion.meta_ref
  26.4 5.6 %shard_map.130.edge_ref = bf16[4,2,400,640]{3,2,1,0:T(8,128)(2,1)} custom-call(s32[2]{0:T(128)} %pad_add_fusion.meta_ref, s32[4,1,640]{2,1,0:T(1,128)} %bitcast.28, s32[4,1,640]{2,1,0:T(1,128)} %bitcast.26, f32[400,1024]{1,0:T(8,128)} %bitcast.21, f32[16,400]{1,0:T(8,128)} %refs_2_.1), custom_call_target="tpu_custom_call" | custom-call | flops 4194304000 | bytes 8192000 | tf_op jit(solution)/shard_map/pallas_call | solution.py:468
  32.0 6.1 %all-to-all-done.1.parts_ref = bf16[8,400,128]{2,1,0:T(8,128)(2,1)S(1)} async-done(((bf16[8,400,128]{2,1,0:T(8,128)(2,1)}), bf16[8,400,128]{2,1,0:T(8,128)(2,1)S(1)}, u32[]{:S(2)}, u32[]{:S(2)}) %all-to-all-start.1) | async-done | bytes 819232 | tf_op jit(solution)/shard_map/all_to_all | solution.py:383
  38.0 0.0 copy-start.9
  38.0 11.2 %shard_map.132 = (bf16[4,400,640]{2,1,0:T(8,128)(2,1)S(1)}, f32[400,16]{1,0:T(8,128)}, f32[8,102,128]{2,1,0:T(8,128)S(1)}, f32[8,102,128]{2,1,0:T(8,128)S(1)}, f...) custom-call(s32[2]{0:T(128)S(1)} %copy-done.6, ...), custom_call_target="tpu_custom_call" | custom-call | flops 12582912000 | bytes 8192000 | tf_op jit(solution)/shard_map/pallas_call | solution.py:486
  49.2 0.1 collective-permute-start
  49.3 3.8 %collective-permute-start.1 = (bf16[4,102,128]{2,1,0:T(8,128)(2,1)S(1)}, bf16[4,102,128]{2,1,0:T(8,128)(2,1)S(1)}, u32[]{:S(2)}, u32[]{:S(2)}) collective-permute-start(bf16[4,102,128]{2,1,0:T(8,128)(2,1)S(1)} %get-tuple-element.27), channel_id=1, source_target_pairs={{0,3},{1,0},{2,1},{3,2},{4,7},{5,4},{6,5},{7,6},{8,11},{9,8},{10,9... | collective-permute-start | bytes 313352 | tf_op jit(solution)/shard_map/ppermute | solution.py:379
  53.1 2.6 %shard_map.133 = (f32[8,102,128]{2,1,0:T(8,128)S(1)}, f32[8,102,128]{2,1,0:T(8,128)S(1)}, f32[8,102,128]{2,1,0:T(8,128)S(1)}, bf16[4,102,128]{2,1,0:T(8,128)(2,1)S(1)}, bf16[4,102,128]{2,1,0:T(8,128)(2,1)S(1)}) custom-call(s32[2]{0:T(128)S(1)} %copy-done.6, s32[4,1,640]{2,1,0:T(1,128)S(1)} %bitcast.29, bf16[4,400,640]{2,1,0:T(8,128)(2,1)S(1)} %get-tuple-element.22.grad_ref), custom_call_target="tpu_custom_call" | custom-call | flops 4194304000 | bytes 8192000 | tf_op jit(solution)/shard_map/pallas_call | solution.py:516
  55.8 0.7 collective-permute-done
  56.5 3.2 %collective-permute-start.3 = (bf16[12,102,128]{2,1,0:T(8,128)(2,1)S(1)}, bf16[12,102,128]{2,1,0:T(8,128)(2,1)S(1)}, u32[]{:S(2)}, u32[]{:S(2)}) collective-permute-start(bf16[12,102,128]{2,1,0:T(8,128)(2,1)S(1)} %pad_maximum_fusion.1), channel_id=1, source_target_pairs={{0,3},{1,0},{2,1},{3,2},{4,7},{5,4},{6,5},{7,6},{8,11},{9,8},{10,9... | collective-permute-start | bytes 940040 | tf_op jit(solution)/shard_map/ppermute | solution.py:379
  59.8 0.1 collective-permute-start.2
  59.9 7.8 %collective-permute-done.3 = bf16[12,102,128]{2,1,0:T(8,128)(2,1)S(1)} collective-permute-done((bf16[12,102,128]{2,1,0:T(8,128)(2,1)S(1)}, bf16[12,102,128]{2,1,0:T(8,128)(2,1)S(1)}, u32[]{:S(2)}, u32[]{:S(2)}) %collective-permute-start.3) | collective-permute-done | bytes 313376 | tf_op jit(solution)/shard_map/ppermute | solution.py:379
  67.7 4.5 %collective-permute-done.2 = bf16[12,102,128]{2,1,0:T(8,128)(2,1)S(1)} collective-permute-done((bf16[12,102,128]{2,1,0:T(8,128)(2,1)S(1)}, bf16[12,102,128]{2,1,0:T(8,128)(2,1)S(1)}, u32[]{:S(2)}, u32[]{:S(2)}) %collective-permute-start.2) | collective-permute-done | bytes 313376 | tf_op jit(solution)/shard_map/ppermute | solution.py:379
  72.2 0.1 add_convert_fusion.1
  72.4 1.9 %collective-permute-start.5 = (bf16[8,102,128]{2,1,0:T(8,128)(2,1)S(1)}, bf16[8,102,128]{2,1,0:T(8,128)(2,1)S(1)}, u32[]{:S(2)}, u32[]{:S(2)}) collective-permute-start(bf16[8,102,128]{2,1,0:T(8,128)(2,1)S(1)} %pad_maximum_fusion.3), channel_id=1, source_target_pairs={{0,3},{1,0},{2,1},{3,2},{4,7},{5,4},{6,5},{7,6},{8,11},{9,8},{10,9... | collective-permute-start | bytes 626696 | tf_op jit(solution)/shard_map/ppermute | solution.py:379
  74.4 0.7 pad_maximum_fusion.2
  75.1 0.1 collective-permute-start.4
  75.2 15.9 %all_to_all.21.in_ref = bf16[8,102,128]{2,1,0:T(8,128)(2,1)S(1)} all-to-all(bf16[8,102,128]{2,1,0:T(8,128)(2,1)S(1)} %add_convert_fusion.1), channel_id=1, replica_groups=mesh['bucket'=8,'span'=4] {'bucket'}, dimensions={0} | all-to-all | bytes 417792 | tf_op jit(solution)/shard_map/all_to_all | solution.py:383
  91.1 1.6 %shard_map.135 = bf16[8,102,128]{2,1,0:T(8,128)(2,1)} custom-call(s32[8]{0:T(128)S(1)} %copy-done.5, bf16[8,102,128]{2,1,0:T(8,128)(2,1)S(1)} %all_to_all.21.in_ref), custom_call_target="tpu_custom_call" | custom-call | tf_op jit(solution)/shard_map/pallas_call | solution.py:538
  92.7 3.4 %all-to-all-start.3 = ((bf16[8,102,128]{2,1,0:T(8,128)(2,1)}), bf16[8,102,128]{2,1,0:T(8,128)(2,1)S(1)}, u32[]{:S(2)}, u32[]{:S(2)}) async-start(bf16[8,102,128]{2,1,0:T(8,128)(2,1)} %shard_map.135), calls=%async_computation.3 | async-start | bytes 425984 | tf_op jit(solution)/shard_map/all_to_all | solution.py:383
  96.1 0.0 collective-permute-done.5
  96.1 0.1 add_convert_fusion.refs_2_
  96.2 1.6 %collective-permute-start.6 = (bf16[8,102,128]{2,1,0:T(8,128)(2,1)S(1)}, bf16[8,102,128]{2,1,0:T(8,128)(2,1)S(1)}, u32[]{:S(2)}, u32[]{:S(2)}) collective-permute-start(bf16[8,102,128]{2,1,0:T(8,128)(2,1)S(1)} %add_convert_fusion.refs_2_), channel_id=1, source_target_pairs={{0,1},{1,2},{2,3},{3,0},{4,5},{5,6},{6,7},{7,4},{8,9},{9,10},{10,1... | collective-permute-start | bytes 626696 | tf_op jit(solution)/shard_map/ppermute | solution.py:379
  97.8 2.3 %collective-permute-start.7 = (bf16[8,102,128]{2,1,0:T(8,128)(2,1)S(1)}, bf16[8,102,128]{2,1,0:T(8,128)(2,1)S(1)}, u32[]{:S(2)}, u32[]{:S(2)}) collective-permute-start(bf16[8,102,128]{2,1,0:T(8,128)(2,1)S(1)} %add_convert_fusion.refs_2_), channel_id=1, source_target_pairs={{0,3},{1,0},{2,1},{3,2},{4,7},{5,4},{6,5},{7,6},{8,11},{9,8},{10,9... | collective-permute-start | bytes 626696 | tf_op jit(solution)/shard_map/ppermute | solution.py:379
  100.1 2.3 %all-to-all-done.3.refs_4_ = bf16[8,102,128]{2,1,0:T(8,128)(2,1)S(1)} async-done(((bf16[8,102,128]{2,1,0:T(8,128)(2,1)}), bf16[8,102,128]{2,1,0:T(8,128)(2,1)S(1)}, u32[]{:S(2)}, u32[]{:S(2)}) %all-to-all-start.3) | async-done | bytes 208928 | tf_op jit(solution)/shard_map/all_to_all | solution.py:383
  102.4 1.5 %collective-permute-start.10 = (bf16[8,102,128]{2,1,0:T(8,128)(2,1)S(1)}, bf16[8,102,128]{2,1,0:T(8,128)(2,1)S(1)}, u32[]{:S(2)}, u32[]{:S(2)}) collective-permute-start(bf16[8,102,128]{2,1,0:T(8,128)(2,1)S(1)} %all-to-all-done.3.refs_4_), channel_id=1, source_target_pairs={{0,1},{1,2},{2,3},{3,0},{4,5},{5,6},{6,7},{7,4},{8,9},{9,10},{10,1... | collective-permute-start | bytes 626696 | tf_op jit(solution)/shard_map/ppermute | solution.py:379
  103.9 2.3 %collective-permute-start.11 = (bf16[8,102,128]{2,1,0:T(8,128)(2,1)S(1)}, bf16[8,102,128]{2,1,0:T(8,128)(2,1)S(1)}, u32[]{:S(2)}, u32[]{:S(2)}) collective-permute-start(bf16[8,102,128]{2,1,0:T(8,128)(2,1)S(1)} %all-to-all-done.3.refs_4_), channel_id=1, source_target_pairs={{0,3},{1,0},{2,1},{3,2},{4,7},{5,4},{6,5},{7,6},{8,11},{9,8},{10,9... | collective-permute-start | bytes 626696 | tf_op jit(solution)/shard_map/ppermute | solution.py:379
  106.2 0.0 collective-permute-done.6.refs_3_
  106.2 0.1 collective-permute-start.8
  106.3 4.5 %collective-permute-done.7.refs_4_ = bf16[8,102,128]{2,1,0:T(8,128)(2,1)S(1)} collective-permute-done((bf16[8,102,128]{2,1,0:T(8,128)(2,1)S(1)}, bf16[8,102,128]{2,1,0:T(8,128)(2,1)S(1)}, u32[]{:S(2)}, u32[]{:S(2)}) %collective-permute-start.7) | collective-permute-done | bytes 208928 | tf_op jit(solution)/shard_map/ppermute | solution.py:379
  110.8 0.7 slice.77
  111.4 1.5 %collective-permute-start.9 = (bf16[4,102,128]{2,1,0:T(8,128)(2,1)}, bf16[4,102,128]{2,1,0:T(8,128)(2,1)S(1)}, u32[]{:S(2)}, u32[]{:S(2)}) collective-permute-start(bf16[4,102,128]{2,1,0:T(8,128)(2,1)} %slice.77), channel_id=1, source_target_pairs={{0,3},{1,0},{2,1},{3,2},{4,7},{5,4},{6,5},{7,6},{8,11},{9,8},{10,9... | collective-permute-start | bytes 313352 | tf_op jit(solution)/shard_map/ppermute | solution.py:379
  112.9 2.4 %collective-permute-done.10.refs_5_ = bf16[8,102,128]{2,1,0:T(8,128)(2,1)S(1)} collective-permute-done((bf16[8,102,128]{2,1,0:T(8,128)(2,1)S(1)}, bf16[8,102,128]{2,1,0:T(8,128)(2,1)S(1)}, u32[]{:S(2)}, u32[]{:S(2)}) %collective-permute-start.10) | collective-permute-done | bytes 208928 | tf_op jit(solution)/shard_map/ppermute | solution.py:379
  115.3 0.6 slice.78
  116.0 0.0 collective-permute-start.12
  116.0 3.9 %collective-permute-done.11.refs_6_ = bf16[8,102,128]{2,1,0:T(8,128)(2,1)S(1)} collective-permute-done((bf16[8,102,128]{2,1,0:T(8,128)(2,1)S(1)}, bf16[8,102,128]{2,1,0:T(8,128)(2,1)S(1)}, u32[]{:S(2)}, u32[]{:S(2)}) %collective-permute-start.11) | collective-permute-done | bytes 208928 | tf_op jit(solution)/shard_map/ppermute | solution.py:379
  119.9 0.6 slice.79
  120.5 1.5 %collective-permute-start.13 = (bf16[4,102,128]{2,1,0:T(8,128)(2,1)}, bf16[4,102,128]{2,1,0:T(8,128)(2,1)S(1)}, u32[]{:S(2)}, u32[]{:S(2)}) collective-permute-start(bf16[4,102,128]{2,1,0:T(8,128)(2,1)} %slice.79), channel_id=1, source_target_pairs={{0,3},{1,0},{2,1},{3,2},{4,7},{5,4},{6,5},{7,6},{8,11},{9,8},{10,9... | collective-permute-start | bytes 313352 | tf_op jit(solution)/shard_map/ppermute | solution.py:379
  122.1 0.1 copy.15.refs_3_
  122.2 0.1 collective-permute-done.8.refs_5_
  122.2 2.2 %collective-permute-done.9.refs_6_ = bf16[4,102,128]{2,1,0:T(8,128)(2,1)S(1)} collective-permute-done((bf16[4,102,128]{2,1,0:T(8,128)(2,1)}, bf16[4,102,128]{2,1,0:T(8,128)(2,1)S(1)}, u32[]{:S(2)}, u32[]{:S(2)}) %collective-permute-start.9) | collective-permute-done | bytes 104480 | tf_op jit(solution)/shard_map/ppermute | solution.py:379
  124.4 3.4 %shard_map.134 = f32[400,1024]{1,0:T(8,128)} custom-call(s32[2]{0:T(128)S(1)} %copy-done.6, f32[400,1024]{1,0:T(8,128)S(1)} %bitcast.22, f32[1,1024]{1,0:T(1,128)S(1)} %bitcast.23, bf16[8,102,128]{2,1,0:T(8,128)(2,1)S(1)} %add_convert_fusion.refs_2_, bf16[8,102,128]{2,1,0:T(8,128)(2,1)S(1)} %collective-permute-done.6.refs_3_, ...), custom_call_target="tpu_custom_call" | custom-call | tf_op jit(solution)/shard_map/pallas_call | solution.py:396
  127.8 0.0 collective-permute-done.13.refs_8_
  127.9 4.0 %shard_map.136 = (f32[400,1024]{1,0:T(8,128)}, f32[16,400]{1,0:T(8,128)}) custom-call(s32[2]{0:T(128)S(1)} %copy-done.6, f32[400,1024]{1,0:T(8,128)S(1)} %bitcast.20, f32[1,1024]{1,0:T(1,128)S(1)} %bitcast.24, f32[16,400]{1,0:T(8,128)S(1)} %copy-done.2, f32[16,1]{1,0:T(8,128)S(1)} %copy.15.refs_3_, bf16[8,102,128]{2,1,0:T(8,128)(2,1)S(1)} %all-to-all-done.3.refs_4_, ...), custom_call_target="tpu_custom_call" | custom-call | tf_op jit(solution)/shard_map/pallas_call | solution.py:396
  (38 shorter events, 0.4 us)
Async XLA Ops:
  0.6 19.4 %copy-start.5 = (s32[8]{0:T(128)S(1)}, s32[8]{0:T(128)}, u32[]{:S(2)}) copy-start(s32[8]{0:T(128)} %plan_ref.3) | copy-start | bytes 100
  21.6 16.5 %all-to-all-start.1 = ((bf16[8,400,128]{2,1,0:T(8,128)(2,1)}), bf16[8,400,128]{2,1,0:T(8,128)(2,1)S(1)}, u32[]{:S(2)}, u32[]{:S(2)}) async-start(bf16[8,400,128]{2,1,0:T(8,128)(2,1)} %shard_map.131), calls=%async_computation.1 | async-start | bytes 1638400 | tf_op jit(solution)/shard_map/all_to_all | solution.py:383
  26.4 11.6 %copy-start.2 = (f32[16,400]{1,0:T(8,128)S(1)}, f32[16,400]{1,0:T(8,128)}, u32[]{:S(2)}) copy-start(f32[16,400]{1,0:T(8,128)} %refs_2_.1) | copy-start | bytes 76804
  26.4 11.6 %copy-start.6 = (s32[2]{0:T(128)S(1)}, s32[2]{0:T(128)}, u32[]{:S(2)}) copy-start(s32[2]{0:T(128)} %pad_add_fusion.meta_ref) | copy-start | bytes 28
  26.4 11.6 %copy-start.7 = (s32[1,2560]{1,0:T(1,128)S(1)}, s32[1,2560]{1,0:T(1,128)}, u32[]{:S(2)}) copy-start(s32[1,2560]{1,0:T(1,128)} %param.19) | copy-start | bytes 30724
  26.4 11.7 %copy-start.8 = (s32[1,2560]{1,0:T(1,128)S(1)}, s32[1,2560]{1,0:T(1,128)}, u32[]{:S(2)}) copy-start(s32[1,2560]{1,0:T(1,128)} %param.20) | copy-start | bytes 30724
  38.0 15.1 %copy-start.9 = (s32[1,2560]{1,0:T(1,128)S(1)}, s32[1,2560]{1,0:T(1,128)}, u32[]{:S(2)}) copy-start(s32[1,2560]{1,0:T(1,128)} %param.18) | copy-start | bytes 30724
  49.2 7.2 %collective-permute-start = (bf16[4,102,128]{2,1,0:T(8,128)(2,1)S(1)}, bf16[4,102,128]{2,1,0:T(8,128)(2,1)S(1)}, u32[]{:S(2)}, u32[]{:S(2)}) collective-permute-start(bf16[4,102,128]{2,1,0:T(8,128)(2,1)S(1)} %get-tuple-element.26), channel_id=1, source_target_pairs={{0,1},{1,2},{2,3},{3,0},{4,5},{5,6},{6,7},{7,4},{8,9},{9,10},{10,1... | collective-permute-start | bytes 313352 | tf_op jit(solution)/shard_map/ppermute | solution.py:379
  49.3 7.2 %collective-permute-start.1 = (bf16[4,102,128]{2,1,0:T(8,128)(2,1)S(1)}, bf16[4,102,128]{2,1,0:T(8,128)(2,1)S(1)}, u32[]{:S(2)}, u32[]{:S(2)}) collective-permute-start(bf16[4,102,128]{2,1,0:T(8,128)(2,1)S(1)} %get-tuple-element.27), channel_id=1, source_target_pairs={{0,3},{1,0},{2,1},{3,2},{4,7},{5,4},{6,5},{7,6},{8,11},{9,8},{10,9... | collective-permute-start | bytes 313352 | tf_op jit(solution)/shard_map/ppermute | solution.py:379
  56.5 11.2 %collective-permute-start.3 = (bf16[12,102,128]{2,1,0:T(8,128)(2,1)S(1)}, bf16[12,102,128]{2,1,0:T(8,128)(2,1)S(1)}, u32[]{:S(2)}, u32[]{:S(2)}) collective-permute-start(bf16[12,102,128]{2,1,0:T(8,128)(2,1)S(1)} %pad_maximum_fusion.1), channel_id=1, source_target_pairs={{0,3},{1,0},{2,1},{3,2},{4,7},{5,4},{6,5},{7,6},{8,11},{9,8},{10,9... | collective-permute-start | bytes 940040 | tf_op jit(solution)/shard_map/ppermute | solution.py:379
  59.8 12.4 %collective-permute-start.2 = (bf16[12,102,128]{2,1,0:T(8,128)(2,1)S(1)}, bf16[12,102,128]{2,1,0:T(8,128)(2,1)S(1)}, u32[]{:S(2)}, u32[]{:S(2)}) collective-permute-start(bf16[12,102,128]{2,1,0:T(8,128)(2,1)S(1)} %pad_maximum_fusion), channel_id=1, source_target_pairs={{0,1},{1,2},{2,3},{3,0},{4,5},{5,6},{6,7},{7,4},{8,9},{9,10},{10,1... | collective-permute-start | bytes 940040 | tf_op jit(solution)/shard_map/ppermute | solution.py:379
  72.4 23.7 %collective-permute-start.5 = (bf16[8,102,128]{2,1,0:T(8,128)(2,1)S(1)}, bf16[8,102,128]{2,1,0:T(8,128)(2,1)S(1)}, u32[]{:S(2)}, u32[]{:S(2)}) collective-permute-start(bf16[8,102,128]{2,1,0:T(8,128)(2,1)S(1)} %pad_maximum_fusion.3), channel_id=1, source_target_pairs={{0,3},{1,0},{2,1},{3,2},{4,7},{5,4},{6,5},{7,6},{8,11},{9,8},{10,9... | collective-permute-start | bytes 626696 | tf_op jit(solution)/shard_map/ppermute | solution.py:379
  75.1 47.0 %copy-start.10 = (f32[16]{0:T(128)S(1)}, f32[16]{0:T(128)}, u32[]{:S(2)}) copy-start(f32[16]{0:T(128)} %param.16) | copy-start | bytes 196
  75.1 49.3 %copy-start.1 = (f32[1024,400]{0,1:T(8,128)S(1)}, f32[1024,400]{0,1:T(8,128)}, u32[]{:S(2)}) copy-start(f32[1024,400]{0,1:T(8,128)} %param.11) | copy-start | bytes 4915204
  75.1 49.3 %copy-start.3 = (f32[1024]{0:T(1024)S(1)}, f32[1024]{0:T(1024)}, u32[]{:S(2)}) copy-start(f32[1024]{0:T(1024)} %param.13) | copy-start | bytes 12292
  75.1 21.0 %collective-permute-start.4 = (bf16[8,102,128]{2,1,0:T(8,128)(2,1)}, bf16[8,102,128]{2,1,0:T(8,128)(2,1)S(1)}, u32[]{:S(2)}, u32[]{:S(2)}) collective-permute-start(bf16[8,102,128]{2,1,0:T(8,128)(2,1)} %pad_maximum_fusion.2), channel_id=1, source_target_pairs={{0,1},{1,2},{2,3},{3,0},{4,5},{5,6},{6,7},{7,4},{8,9},{9,10},{10,1... | collective-permute-start | bytes 626696 | tf_op jit(solution)/shard_map/ppermute | solution.py:379
  92.7 9.8 %all-to-all-start.3 = ((bf16[8,102,128]{2,1,0:T(8,128)(2,1)}), bf16[8,102,128]{2,1,0:T(8,128)(2,1)S(1)}, u32[]{:S(2)}, u32[]{:S(2)}) async-start(bf16[8,102,128]{2,1,0:T(8,128)(2,1)} %shard_map.135), calls=%async_computation.3 | async-start | bytes 425984 | tf_op jit(solution)/shard_map/all_to_all | solution.py:383
  96.2 10.1 %collective-permute-start.6 = (bf16[8,102,128]{2,1,0:T(8,128)(2,1)S(1)}, bf16[8,102,128]{2,1,0:T(8,128)(2,1)S(1)}, u32[]{:S(2)}, u32[]{:S(2)}) collective-permute-start(bf16[8,102,128]{2,1,0:T(8,128)(2,1)S(1)} %add_convert_fusion.refs_2_), channel_id=1, source_target_pairs={{0,1},{1,2},{2,3},{3,0},{4,5},{5,6},{6,7},{7,4},{8,9},{9,10},{10,1... | collective-permute-start | bytes 626696 | tf_op jit(solution)/shard_map/ppermute | solution.py:379
  97.8 13.0 %collective-permute-start.7 = (bf16[8,102,128]{2,1,0:T(8,128)(2,1)S(1)}, bf16[8,102,128]{2,1,0:T(8,128)(2,1)S(1)}, u32[]{:S(2)}, u32[]{:S(2)}) collective-permute-start(bf16[8,102,128]{2,1,0:T(8,128)(2,1)S(1)} %add_convert_fusion.refs_2_), channel_id=1, source_target_pairs={{0,3},{1,0},{2,1},{3,2},{4,7},{5,4},{6,5},{7,6},{8,11},{9,8},{10,9... | collective-permute-start | bytes 626696 | tf_op jit(solution)/shard_map/ppermute | solution.py:379
  102.4 12.9 %collective-permute-start.10 = (bf16[8,102,128]{2,1,0:T(8,128)(2,1)S(1)}, bf16[8,102,128]{2,1,0:T(8,128)(2,1)S(1)}, u32[]{:S(2)}, u32[]{:S(2)}) collective-permute-start(bf16[8,102,128]{2,1,0:T(8,128)(2,1)S(1)} %all-to-all-done.3.refs_4_), channel_id=1, source_target_pairs={{0,1},{1,2},{2,3},{3,0},{4,5},{5,6},{6,7},{7,4},{8,9},{9,10},{10,1... | collective-permute-start | bytes 626696 | tf_op jit(solution)/shard_map/ppermute | solution.py:379
  103.9 16.0 %collective-permute-start.11 = (bf16[8,102,128]{2,1,0:T(8,128)(2,1)S(1)}, bf16[8,102,128]{2,1,0:T(8,128)(2,1)S(1)}, u32[]{:S(2)}, u32[]{:S(2)}) collective-permute-start(bf16[8,102,128]{2,1,0:T(8,128)(2,1)S(1)} %all-to-all-done.3.refs_4_), channel_id=1, source_target_pairs={{0,3},{1,0},{2,1},{3,2},{4,7},{5,4},{6,5},{7,6},{8,11},{9,8},{10,9... | collective-permute-start | bytes 626696 | tf_op jit(solution)/shard_map/ppermute | solution.py:379
  106.2 16.0 %collective-permute-start.8 = (bf16[4,102,128]{2,1,0:T(8,128)(2,1)S(1)}, bf16[4,102,128]{2,1,0:T(8,128)(2,1)S(1)}, u32[]{:S(2)}, u32[]{:S(2)}) collective-permute-start(bf16[4,102,128]{2,1,0:T(8,128)(2,1)S(1)} %slice.76), channel_id=1, source_target_pairs={{0,1},{1,2},{2,3},{3,0},{4,5},{5,6},{6,7},{7,4},{8,9},{9,10},{10,1... | collective-permute-start | bytes 313352 | tf_op jit(solution)/shard_map/ppermute | solution.py:379
  111.4 13.0 %collective-permute-start.9 = (bf16[4,102,128]{2,1,0:T(8,128)(2,1)}, bf16[4,102,128]{2,1,0:T(8,128)(2,1)S(1)}, u32[]{:S(2)}, u32[]{:S(2)}) collective-permute-start(bf16[4,102,128]{2,1,0:T(8,128)(2,1)} %slice.77), channel_id=1, source_target_pairs={{0,3},{1,0},{2,1},{3,2},{4,7},{5,4},{6,5},{7,6},{8,11},{9,8},{10,9... | collective-permute-start | bytes 313352 | tf_op jit(solution)/shard_map/ppermute | solution.py:379
  116.0 11.8 %collective-permute-start.12 = (bf16[4,102,128]{2,1,0:T(8,128)(2,1)}, bf16[4,102,128]{2,1,0:T(8,128)(2,1)S(1)}, u32[]{:S(2)}, u32[]{:S(2)}) collective-permute-start(bf16[4,102,128]{2,1,0:T(8,128)(2,1)} %slice.78), channel_id=1, source_target_pairs={{0,1},{1,2},{2,3},{3,0},{4,5},{5,6},{6,7},{7,4},{8,9},{9,10},{10,1... | collective-permute-start | bytes 313352 | tf_op jit(solution)/shard_map/ppermute | solution.py:379
  120.5 7.3 %collective-permute-start.13 = (bf16[4,102,128]{2,1,0:T(8,128)(2,1)}, bf16[4,102,128]{2,1,0:T(8,128)(2,1)S(1)}, u32[]{:S(2)}, u32[]{:S(2)}) collective-permute-start(bf16[4,102,128]{2,1,0:T(8,128)(2,1)} %slice.79), channel_id=1, source_target_pairs={{0,3},{1,0},{2,1},{3,2},{4,7},{5,4},{6,5},{7,6},{8,11},{9,8},{10,9... | collective-permute-start | bytes 313352 | tf_op jit(solution)/shard_map/ppermute | solution.py:379
  124.4 3.4 %copy-start = (f32[1024,400]{0,1:T(8,128)S(1)}, f32[1024,400]{0,1:T(8,128)}, u32[]{:S(2)}) copy-start(f32[1024,400]{0,1:T(8,128)} %param.12) | copy-start | bytes 4915204
  124.4 3.4 %copy-start.4 = (f32[1024]{0:T(1024)S(1)}, f32[1024]{0:T(1024)}, u32[]{:S(2)}) copy-start(f32[1024]{0:T(1024)} %param.14) | copy-start | bytes 12292

commit v4 on v3

--- a/solution.py
+++ b/solution.py
@@ -530,11 +530,16 @@
         ahead, behind = shift_span(ahead, 1), shift_span(behind, -1)
         ahead, behind = after((ahead, behind), source_out)
         ahead, behind = ring_payload(target_out, away, ahead, behind)
-    source_ahead, source_behind = ring_payload(source_out, reach)
-    ahead, source_ahead = shift_two(ahead, source_ahead, 1)
-    behind, source_behind = shift_two(behind, source_behind, -1)
+    ahead, behind = shift_span(ahead, 1), shift_span(behind, -1)
     target_sum = ring_total(target_out, ahead, behind)
     returned = swap_buckets(target_sum)
+    ahead, behind = ring_payload(source_out, reach)
+    for away in range(reach - 1, 0, -1):
+        ahead, behind = shift_span(ahead, 1), shift_span(behind, -1)
+        ahead, behind = ring_payload(source_out, away, ahead, behind)
+    ahead, behind = shift_span(ahead, 1), shift_span(behind, -1)
+    source_sum = ring_total(source_out, ahead, behind)
+    returned = after(returned, source_sum)
     sorted_out = pl.pallas_call(
         functools.partial(place_kernel, block),
         out_shape=bundle_shape,
@@ -544,13 +549,8 @@
         compiler_params=params(16),
     )(plan, returned)
     target_home = swap_buckets(sorted_out)
-    for away in range(reach - 1, 0, -1):
-        source_ahead, source_behind = after((source_ahead, source_behind), target_sum)
-        source_ahead, source_behind = ring_payload(source_out, away, source_ahead, source_behind)
-        source_ahead, source_behind = shift_span(source_ahead, 1), shift_span(source_behind, -1)
-    source_ahead, source_behind = after((source_ahead, source_behind), returned)
-    source_sum = ring_total(source_out, source_ahead, source_behind)
     source_parts = gather_span(source_sum)
+    target_home = after(target_home, source_parts)
     home_parts = gather_span(target_home)
     (new_source,) = update(lanes, meta, source_cols, source_state.reshape(1, rows), source_parts)
     target_update = (lanes, meta, target_cols, target_state.reshape(1, rows), home_parts)

time: 132 us -> 130 us (0.985)
  blocking collectives: 33.7 us -> 17.9 us
  starting transfers between devices: 27 us -> 37.8 us
  Pallas kernels: 29.8 us -> 38.6 us
  waiting for transfers between devices: 34.4 us -> 28.4 us
    all_to_all x2 -> x1, blocking collectives: 33.7 us -> 17.9 us  [swap_buckets(): return lax.all_to_all(x, 'bucket', split_axis=0, concat_axis=0, tiled=True)]
    ppermute x14 -> x16, starting transfers between devices: 20 us -> 27.3 us  [shift_span(): lax.ppermute(x, 'span', [(i, (i + by) % count) for i in range(count)])]
    pallas_call x1, Pallas kernels: 11.2 us -> 17.2 us  [per_device(): pl.pallas_call(functools.partial(main_kernel, steps, lanes, packed), grid...]
    ppermute x14 -> x16, waiting for transfers between devices: 26 us -> 21.4 us  [shift_span(): lax.ppermute(x, 'span', [(i, (i + by) % count) for i in range(count)])]
    all_to_all x2 -> x3, starting transfers between devices: 6.97 us -> 10.5 us  [swap_buckets(): return lax.all_to_all(x, 'bucket', split_axis=0, concat_axis=0, tiled=True)]
    pallas_call x1, Pallas kernels: 2.6 us -> 4.29 us  [per_device(): pl.pallas_call(functools.partial(source_kernel, steps, lanes), grid=(step...]
    all_to_all x2 -> x3, waiting for transfers between devices: 8.37 us -> 7 us  [swap_buckets(): return lax.all_to_all(x, 'bucket', split_axis=0, concat_axis=0, tiled=True)]
  transfers between devices with their start and end apart: 16 -> 19, of which waited for: 10 -> 11; matrix products, arithmetic and copies ran while one was open for 3% -> 2% of each run, Pallas kernels for 10% -> 12%
where the time goes in v4:
time: 130 us; the launch traced here: 129 us
  Pallas kernels  38.6 us (30%)
  starting transfers between devices  37.8 us (29%)
  waiting for transfers between devices  28.4 us (22%)
  blocking collectives  17.9 us (14%)
  other arithmetic  3.87 us (3%)
  between operations  1.6 us (1%)
    ppermute x16, starting transfers between devices, shift_span(): lax.ppermute(x, 'span', [(i, (i + by) % count) for i in range(count)])  27.3 us
    ppermute x16, waiting for transfers between devices, shift_span(): lax.ppermute(x, 'span', [(i, (i + by) % count) for i in range(count)])  21.4 us
    all_to_all x1, blocking collectives, swap_buckets(): return lax.all_to_all(x, 'bucket', split_axis=0, concat_axis=0, tiled=True)  17.9 us
    pallas_call x1, Pallas kernels, per_device(): pl.pallas_call(functools.partial(main_kernel, steps, lanes, packed), grid...  17.2 us
    all_to_all x3, starting transfers between devices, swap_buckets(): return lax.all_to_all(x, 'bucket', split_axis=0, concat_axis=0, tiled=True)  10.5 us
    pallas_call x2, Pallas kernels, update(): pl.pallas_call(functools.partial(update_kernel, lanes, joined), out_shape...  7.37 us
    all_to_all x3, waiting for transfers between devices, swap_buckets(): return lax.all_to_all(x, 'bucket', split_axis=0, concat_axis=0, tiled=True)  7 us
    pallas_call x1, Pallas kernels, per_device(): pl.pallas_call(functools.partial(prep_kernel, steps), grid=(steps,), out_...  6.67 us
  transfers between devices with their start and end apart: 19, of which 11 were waited for; matrix products, arithmetic and copies ran while one was open for 2% of the time, Pallas kernels for 12%

profile of v4, /device:TPU:0, one launch (start us, length us, event | category | flops | bytes accessed | tf_op | source)
XLA Modules:
  0.0 129.0 jit_solution(9570073367789114693)
XLA Ops:
  0.6 1.5 %bitcast_bitcast_fusion = bf16[8,400,128]{2,1,0:T(8,128)(2,1)S(1)} fusion(f32[1024,400]{0,1:T(8,128)} %param.12), kind=kLoop, calls=%fused_computation | loop fusion | flops 409600 | bytes 2457600 | tf_op jit(solution)/shard_map/transpose | solution.py:449
  2.2 17.9 %all_to_all.20.in_ref = bf16[8,400,128]{2,1,0:T(8,128)(2,1)S(1)} all-to-all(bf16[8,400,128]{2,1,0:T(8,128)(2,1)S(1)} %bitcast_bitcast_fusion), channel_id=1, replica_groups=mesh['bucket'=8,'span'=4] {'bucket'}, dimensions={0} | all-to-all | bytes 1638400 | tf_op jit(solution)/shard_map/all_to_all | solution.py:383
  20.1 1.5 %shard_map.131 = bf16[8,400,128]{2,1,0:T(8,128)(2,1)} custom-call(s32[8]{0:T(128)S(1)} %copy-done.5, bf16[8,400,128]{2,1,0:T(8,128)(2,1)S(1)} %all_to_all.20.in_ref), custom_call_target="tpu_custom_call" | custom-call | tf_op jit(solution)/shard_map/pallas_call | solution.py:452
  21.6 3.6 %all-to-all-start.1 = ((bf16[8,400,128]{2,1,0:T(8,128)(2,1)}), bf16[8,400,128]{2,1,0:T(8,128)(2,1)S(1)}, u32[]{:S(2)}, u32[]{:S(2)}) async-start(bf16[8,400,128]{2,1,0:T(8,128)(2,1)} %shard_map.131), calls=%async_computation.1 | async-start | bytes 1638400 | tf_op jit(solution)/shard_map/all_to_all | solution.py:383
  25.8 0.6 pad_add_fusion.meta_ref
  26.4 6.7 %shard_map.130.edge_ref = bf16[4,2,400,640]{3,2,1,0:T(8,128)(2,1)} custom-call(s32[2]{0:T(128)} %pad_add_fusion.meta_ref, s32[4,1,640]{2,1,0:T(1,128)} %bitcast.28, s32[4,1,640]{2,1,0:T(1,128)} %bitcast.26, f32[400,1024]{1,0:T(8,128)} %bitcast.21, f32[16,400]{1,0:T(8,128)} %refs_2_.1), custom_call_target="tpu_custom_call" | custom-call | flops 4194304000 | bytes 8192000 | tf_op jit(solution)/shard_map/pallas_call | solution.py:468
  33.1 5.0 %all-to-all-done.1.parts_ref = bf16[8,400,128]{2,1,0:T(8,128)(2,1)S(1)} async-done(((bf16[8,400,128]{2,1,0:T(8,128)(2,1)}), bf16[8,400,128]{2,1,0:T(8,128)(2,1)S(1)}, u32[]{:S(2)}, u32[]{:S(2)}) %all-to-all-start.1) | async-done | bytes 819232 | tf_op jit(solution)/shard_map/all_to_all | solution.py:383
  38.0 0.0 copy-start.9
  38.0 17.2 %shard_map.132 = (bf16[4,400,640]{2,1,0:T(8,128)(2,1)S(1)}, f32[400,16]{1,0:T(8,128)}, f32[8,102,128]{2,1,0:T(8,128)S(1)}, f32[8,102,128]{2,1,0:T(8,128)S(1)}, f...) custom-call(s32[2]{0:T(128)S(1)} %copy-done.6, ...), custom_call_target="tpu_custom_call" | custom-call | flops 12582912000 | bytes 8192000 | tf_op jit(solution)/shard_map/pallas_call | solution.py:486
  55.2 0.1 collective-permute-start.8
  55.3 3.8 %collective-permute-start.9 = (bf16[4,102,128]{2,1,0:T(8,128)(2,1)S(1)}, bf16[4,102,128]{2,1,0:T(8,128)(2,1)S(1)}, u32[]{:S(2)}, u32[]{:S(2)}) collective-permute-start(bf16[4,102,128]{2,1,0:T(8,128)(2,1)S(1)} %get-tuple-element.29), channel_id=1, source_target_pairs={{0,3},{1,0},{2,1},{3,2},{4,7},{5,4},{6,5},{7,6},{8,11},{9,8},{10,9... | collective-permute-start | bytes 313352 | tf_op jit(solution)/shard_map/ppermute | solution.py:379
  59.1 4.3 %shard_map.133 = (f32[8,102,128]{2,1,0:T(8,128)S(1)}, f32[8,102,128]{2,1,0:T(8,128)S(1)}, f32[8,102,128]{2,1,0:T(8,128)S(1)}, bf16[4,102,128]{2,1,0:T(8,128)(2,1)S(1)}, bf16[4,102,128]{2,1,0:T(8,128)(2,1)S(1)}) custom-call(s32[2]{0:T(128)S(1)} %copy-done.6, s32[4,1,640]{2,1,0:T(1,128)S(1)} %bitcast.29, bf16[4,400,640]{2,1,0:T(8,128)(2,1)S(1)} %get-tuple-element.20.grad_ref), custom_call_target="tpu_custom_call" | custom-call | flops 4194304000 | bytes 8192000 | tf_op jit(solution)/shard_map/pallas_call | solution.py:516
  63.4 0.1 collective-permute-start
  63.5 3.9 %collective-permute-start.2 = (bf16[4,102,128]{2,1,0:T(8,128)(2,1)S(1)}, bf16[4,102,128]{2,1,0:T(8,128)(2,1)S(1)}, u32[]{:S(2)}, u32[]{:S(2)}) collective-permute-start(bf16[4,102,128]{2,1,0:T(8,128)(2,1)S(1)} %get-tuple-element.25), channel_id=1, source_target_pairs={{0,3},{1,0},{2,1},{3,2},{4,7},{5,4},{6,5},{7,6},{8,11},{9,8},{10,9... | collective-permute-start | bytes 313352 | tf_op jit(solution)/shard_map/ppermute | solution.py:379
  67.4 0.0 collective-permute-done.8
  67.5 0.1 collective-permute-start.10
  67.6 3.9 %collective-permute-start.11 = (bf16[8,102,128]{2,1,0:T(8,128)(2,1)S(1)}, bf16[8,102,128]{2,1,0:T(8,128)(2,1)S(1)}, u32[]{:S(2)}, u32[]{:S(2)}) collective-permute-start(bf16[8,102,128]{2,1,0:T(8,128)(2,1)S(1)} %pad_maximum_fusion.3), channel_id=1, source_target_pairs={{0,3},{1,0},{2,1},{3,2},{4,7},{5,4},{6,5},{7,6},{8,11},{9,8},{10,9... | collective-permute-start | bytes 626696 | tf_op jit(solution)/shard_map/ppermute | solution.py:379
  71.6 0.1 collective-permute-start.1
  71.6 1.2 collective-permute-done.2
  72.9 0.7 pad_maximum_fusion.1
  73.6 2.6 %collective-permute-start.3 = (bf16[8,102,128]{2,1,0:T(8,128)(2,1)}, bf16[8,102,128]{2,1,0:T(8,128)(2,1)S(1)}, u32[]{:S(2)}, u32[]{:S(2)}) collective-permute-start(bf16[8,102,128]{2,1,0:T(8,128)(2,1)} %pad_maximum_fusion.1), channel_id=1, source_target_pairs={{0,3},{1,0},{2,1},{3,2},{4,7},{5,4},{6,5},{7,6},{8,11},{9,8},{10,9... | collective-permute-start | bytes 626696 | tf_op jit(solution)/shard_map/ppermute | solution.py:379
  76.2 2.0 %collective-permute-done.10 = bf16[8,102,128]{2,1,0:T(8,128)(2,1)S(1)} collective-permute-done((bf16[8,102,128]{2,1,0:T(8,128)(2,1)S(1)}, bf16[8,102,128]{2,1,0:T(8,128)(2,1)S(1)}, u32[]{:S(2)}, u32[]{:S(2)}) %collective-permute-start.10) | collective-permute-done | bytes 208928 | tf_op jit(solution)/shard_map/ppermute | solution.py:379
  78.2 3.8 %collective-permute-done.11 = bf16[8,102,128]{2,1,0:T(8,128)(2,1)S(1)} collective-permute-done((bf16[8,102,128]{2,1,0:T(8,128)(2,1)S(1)}, bf16[8,102,128]{2,1,0:T(8,128)(2,1)S(1)}, u32[]{:S(2)}, u32[]{:S(2)}) %collective-permute-start.11) | collective-permute-done | bytes 208928 | tf_op jit(solution)/shard_map/ppermute | solution.py:379
  82.0 0.8 add_convert_fusion
  82.8 3.5 %all-to-all-start.2 = ((bf16[8,102,128]{2,1,0:T(8,128)(2,1)}), bf16[8,102,128]{2,1,0:T(8,128)(2,1)S(1)}, u32[]{:S(2)}, u32[]{:S(2)}) async-start(bf16[8,102,128]{2,1,0:T(8,128)(2,1)} %add_convert_fusion), calls=%async_computation.2 | async-start | bytes 425984 | tf_op jit(solution)/shard_map/all_to_all | solution.py:383
  86.3 0.3 collective-permute-done.3
  86.6 0.1 add_convert_fusion.1.refs_2_
  86.7 0.1 collective-permute-start.4
  86.8 3.8 %collective-permute-start.5 = (bf16[8,102,128]{2,1,0:T(8,128)(2,1)S(1)}, bf16[8,102,128]{2,1,0:T(8,128)(2,1)S(1)}, u32[]{:S(2)}, u32[]{:S(2)}) collective-permute-start(bf16[8,102,128]{2,1,0:T(8,128)(2,1)S(1)} %add_convert_fusion.1.refs_2_), channel_id=1, source_target_pairs={{0,3},{1,0},{2,1},{3,2},{4,7},{5,4},{6,5},{7,6},{8,11},{9,8},{10,9... | collective-permute-start | bytes 626696 | tf_op jit(solution)/shard_map/ppermute | solution.py:379
  90.6 2.0 %all-to-all-done.2.in_ref = bf16[8,102,128]{2,1,0:T(8,128)(2,1)S(1)} async-done(((bf16[8,102,128]{2,1,0:T(8,128)(2,1)}), bf16[8,102,128]{2,1,0:T(8,128)(2,1)S(1)}, u32[]{:S(2)}, u32[]{:S(2)}) %all-to-all-start.2) | async-done | bytes 208928 | tf_op jit(solution)/shard_map/all_to_all | solution.py:383
  92.6 1.6 %shard_map.135 = bf16[8,102,128]{2,1,0:T(8,128)(2,1)} custom-call(s32[8]{0:T(128)S(1)} %copy-done.5, bf16[8,102,128]{2,1,0:T(8,128)(2,1)S(1)} %all-to-all-done.2.in_ref), custom_call_target="tpu_custom_call" | custom-call | tf_op jit(solution)/shard_map/pallas_call | solution.py:543
  94.2 3.4 %all-to-all-start.3 = ((bf16[8,102,128]{2,1,0:T(8,128)(2,1)}), bf16[8,102,128]{2,1,0:T(8,128)(2,1)S(1)}, u32[]{:S(2)}, u32[]{:S(2)}) async-start(bf16[8,102,128]{2,1,0:T(8,128)(2,1)} %shard_map.135), calls=%async_computation.3 | async-start | bytes 425984 | tf_op jit(solution)/shard_map/all_to_all | solution.py:383
  97.6 0.0 collective-permute-done.4.refs_3_
  97.7 0.1 collective-permute-start.6
  97.7 0.9 collective-permute-done.5.refs_4_
  98.6 3.0 %collective-permute-start.7 = (bf16[4,102,128]{2,1,0:T(8,128)(2,1)S(1)}, bf16[4,102,128]{2,1,0:T(8,128)(2,1)S(1)}, u32[]{:S(2)}, u32[]{:S(2)}) collective-permute-start(bf16[4,102,128]{2,1,0:T(8,128)(2,1)S(1)} %slice.55), channel_id=1, source_target_pairs={{0,3},{1,0},{2,1},{3,2},{4,7},{5,4},{6,5},{7,6},{8,11},{9,8},{10,9... | collective-permute-start | bytes 313352 | tf_op jit(solution)/shard_map/ppermute | solution.py:379
  101.6 3.7 %collective-permute-done.6.refs_5_ = bf16[4,102,128]{2,1,0:T(8,128)(2,1)S(1)} collective-permute-done((bf16[4,102,128]{2,1,0:T(8,128)(2,1)S(1)}, bf16[4,102,128]{2,1,0:T(8,128)(2,1)S(1)}, u32[]{:S(2)}, u32[]{:S(2)}) %collective-permute-start.6) | collective-permute-done | bytes 104480 | tf_op jit(solution)/shard_map/ppermute | solution.py:379
  105.4 0.3 collective-permute-done.7.refs_6_
  105.7 1.2 collective-permute-start.12
  106.9 2.6 %collective-permute-start.13 = (bf16[8,102,128]{2,1,0:T(8,128)(2,1)S(1)}, bf16[8,102,128]{2,1,0:T(8,128)(2,1)S(1)}, u32[]{:S(2)}, u32[]{:S(2)}) collective-permute-start(bf16[8,102,128]{2,1,0:T(8,128)(2,1)S(1)} %all-to-all-done.3.refs_4_), channel_id=1, source_target_pairs={{0,3},{1,0},{2,1},{3,2},{4,7},{5,4},{6,5},{7,6},{8,11},{9,8},{10,9... | collective-permute-start | bytes 626696 | tf_op jit(solution)/shard_map/ppermute | solution.py:379
  109.5 6.2 %collective-permute-done.12.refs_5_ = bf16[8,102,128]{2,1,0:T(8,128)(2,1)S(1)} collective-permute-done((bf16[8,102,128]{2,1,0:T(8,128)(2,1)S(1)}, bf16[8,102,128]{2,1,0:T(8,128)(2,1)S(1)}, u32[]{:S(2)}, u32[]{:S(2)}) %collective-permute-start.12) | collective-permute-done | bytes 208928 | tf_op jit(solution)/shard_map/ppermute | solution.py:379
  115.7 0.1 collective-permute-start.14
  115.8 2.9 %collective-permute-done.13.refs_6_ = bf16[8,102,128]{2,1,0:T(8,128)(2,1)S(1)} collective-permute-done((bf16[8,102,128]{2,1,0:T(8,128)(2,1)S(1)}, bf16[8,102,128]{2,1,0:T(8,128)(2,1)S(1)}, u32[]{:S(2)}, u32[]{:S(2)}) %collective-permute-start.13) | collective-permute-done | bytes 208928 | tf_op jit(solution)/shard_map/ppermute | solution.py:379
  118.7 0.7 slice.59
  119.3 2.2 %collective-permute-start.15 = (bf16[4,102,128]{2,1,0:T(8,128)(2,1)}, bf16[4,102,128]{2,1,0:T(8,128)(2,1)S(1)}, u32[]{:S(2)}, u32[]{:S(2)}) collective-permute-start(bf16[4,102,128]{2,1,0:T(8,128)(2,1)} %slice.59), channel_id=1, source_target_pairs={{0,3},{1,0},{2,1},{3,2},{4,7},{5,4},{6,5},{7,6},{8,11},{9,8},{10,9... | collective-permute-start | bytes 313352 | tf_op jit(solution)/shard_map/ppermute | solution.py:379
  121.5 0.1 copy.15.refs_3_
  121.6 3.4 %shard_map.134 = f32[400,1024]{1,0:T(8,128)} custom-call(s32[2]{0:T(128)S(1)} %copy-done.6, f32[400,1024]{1,0:T(8,128)S(1)} %bitcast.22, f32[1,1024]{1,0:T(1,128)S(1)} %bitcast.23, bf16[8,102,128]{2,1,0:T(8,128)(2,1)S(1)} %add_convert_fusion.1.refs_2_, bf16[8,102,128]{2,1,0:T(8,128)(2,1)S(1)} %collective-permute-done.4.refs_3_, ...), custom_call_target="tpu_custom_call" | custom-call | tf_op jit(solution)/shard_map/pallas_call | solution.py:396
  125.0 4.0 %shard_map.136 = (f32[400,1024]{1,0:T(8,128)}, f32[16,400]{1,0:T(8,128)}) custom-call(s32[2]{0:T(128)S(1)} %copy-done.6, f32[400,1024]{1,0:T(8,128)S(1)} %bitcast.20, f32[1,1024]{1,0:T(1,128)S(1)} %bitcast.24, f32[16,400]{1,0:T(8,128)S(1)} %copy-done.2, f32[16,1]{1,0:T(8,128)S(1)} %copy.15.refs_3_, bf16[8,102,128]{2,1,0:T(8,128)(2,1)S(1)} %all-to-all-done.3.refs_4_, ...), custom_call_target="tpu_custom_call" | custom-call | tf_op jit(solution)/shard_map/pallas_call | solution.py:396
  (41 shorter events, 0.3 us)
Async XLA Ops:
  0.6 19.4 %copy-start.5 = (s32[8]{0:T(128)S(1)}, s32[8]{0:T(128)}, u32[]{:S(2)}) copy-start(s32[8]{0:T(128)} %plan_ref.3) | copy-start | bytes 100
  21.6 16.5 %all-to-all-start.1 = ((bf16[8,400,128]{2,1,0:T(8,128)(2,1)}), bf16[8,400,128]{2,1,0:T(8,128)(2,1)S(1)}, u32[]{:S(2)}, u32[]{:S(2)}) async-start(bf16[8,400,128]{2,1,0:T(8,128)(2,1)} %shard_map.131), calls=%async_computation.1 | async-start | bytes 1638400 | tf_op jit(solution)/shard_map/all_to_all | solution.py:383
  26.4 11.6 %copy-start.2 = (f32[16,400]{1,0:T(8,128)S(1)}, f32[16,400]{1,0:T(8,128)}, u32[]{:S(2)}) copy-start(f32[16,400]{1,0:T(8,128)} %refs_2_.1) | copy-start | bytes 76804
  26.4 11.6 %copy-start.6 = (s32[2]{0:T(128)S(1)}, s32[2]{0:T(128)}, u32[]{:S(2)}) copy-start(s32[2]{0:T(128)} %pad_add_fusion.meta_ref) | copy-start | bytes 28
  26.4 11.6 %copy-start.7 = (s32[1,2560]{1,0:T(1,128)S(1)}, s32[1,2560]{1,0:T(1,128)}, u32[]{:S(2)}) copy-start(s32[1,2560]{1,0:T(1,128)} %param.19) | copy-start | bytes 30724
  26.4 11.7 %copy-start.8 = (s32[1,2560]{1,0:T(1,128)S(1)}, s32[1,2560]{1,0:T(1,128)}, u32[]{:S(2)}) copy-start(s32[1,2560]{1,0:T(1,128)} %param.20) | copy-start | bytes 30724
  38.0 21.1 %copy-start.9 = (s32[1,2560]{1,0:T(1,128)S(1)}, s32[1,2560]{1,0:T(1,128)}, u32[]{:S(2)}) copy-start(s32[1,2560]{1,0:T(1,128)} %param.18) | copy-start | bytes 30724
  55.2 12.2 %collective-permute-start.8 = (bf16[4,102,128]{2,1,0:T(8,128)(2,1)S(1)}, bf16[4,102,128]{2,1,0:T(8,128)(2,1)S(1)}, u32[]{:S(2)}, u32[]{:S(2)}) collective-permute-start(bf16[4,102,128]{2,1,0:T(8,128)(2,1)S(1)} %get-tuple-element.28), channel_id=1, source_target_pairs={{0,1},{1,2},{2,3},{3,0},{4,5},{5,6},{6,7},{7,4},{8,9},{9,10},{10,1... | collective-permute-start | bytes 313352 | tf_op jit(solution)/shard_map/ppermute | solution.py:379
  55.3 12.1 %collective-permute-start.9 = (bf16[4,102,128]{2,1,0:T(8,128)(2,1)S(1)}, bf16[4,102,128]{2,1,0:T(8,128)(2,1)S(1)}, u32[]{:S(2)}, u32[]{:S(2)}) collective-permute-start(bf16[4,102,128]{2,1,0:T(8,128)(2,1)S(1)} %get-tuple-element.29), channel_id=1, source_target_pairs={{0,3},{1,0},{2,1},{3,2},{4,7},{5,4},{6,5},{7,6},{8,11},{9,8},{10,9... | collective-permute-start | bytes 313352 | tf_op jit(solution)/shard_map/ppermute | solution.py:379
  63.4 8.1 %collective-permute-start = (bf16[4,102,128]{2,1,0:T(8,128)(2,1)S(1)}, bf16[4,102,128]{2,1,0:T(8,128)(2,1)S(1)}, u32[]{:S(2)}, u32[]{:S(2)}) collective-permute-start(bf16[4,102,128]{2,1,0:T(8,128)(2,1)S(1)} %get-tuple-element.23), channel_id=1, source_target_pairs={{0,1},{1,2},{2,3},{3,0},{4,5},{5,6},{6,7},{7,4},{8,9},{9,10},{10,1... | collective-permute-start | bytes 313352 | tf_op jit(solution)/shard_map/ppermute | solution.py:379
  63.5 9.3 %collective-permute-start.2 = (bf16[4,102,128]{2,1,0:T(8,128)(2,1)S(1)}, bf16[4,102,128]{2,1,0:T(8,128)(2,1)S(1)}, u32[]{:S(2)}, u32[]{:S(2)}) collective-permute-start(bf16[4,102,128]{2,1,0:T(8,128)(2,1)S(1)} %get-tuple-element.25), channel_id=1, source_target_pairs={{0,3},{1,0},{2,1},{3,2},{4,7},{5,4},{6,5},{7,6},{8,11},{9,8},{10,9... | collective-permute-start | bytes 313352 | tf_op jit(solution)/shard_map/ppermute | solution.py:379
  67.5 10.7 %collective-permute-start.10 = (bf16[8,102,128]{2,1,0:T(8,128)(2,1)S(1)}, bf16[8,102,128]{2,1,0:T(8,128)(2,1)S(1)}, u32[]{:S(2)}, u32[]{:S(2)}) collective-permute-start(bf16[8,102,128]{2,1,0:T(8,128)(2,1)S(1)} %pad_maximum_fusion.2), channel_id=1, source_target_pairs={{0,1},{1,2},{2,3},{3,0},{4,5},{5,6},{6,7},{7,4},{8,9},{9,10},{10,1... | collective-permute-start | bytes 626696 | tf_op jit(solution)/shard_map/ppermute | solution.py:379
  67.6 14.4 %collective-permute-start.11 = (bf16[8,102,128]{2,1,0:T(8,128)(2,1)S(1)}, bf16[8,102,128]{2,1,0:T(8,128)(2,1)S(1)}, u32[]{:S(2)}, u32[]{:S(2)}) collective-permute-start(bf16[8,102,128]{2,1,0:T(8,128)(2,1)S(1)} %pad_maximum_fusion.3), channel_id=1, source_target_pairs={{0,3},{1,0},{2,1},{3,2},{4,7},{5,4},{6,5},{7,6},{8,11},{9,8},{10,9... | collective-permute-start | bytes 626696 | tf_op jit(solution)/shard_map/ppermute | solution.py:379
  71.6 14.7 %collective-permute-start.1 = (bf16[8,102,128]{2,1,0:T(8,128)(2,1)S(1)}, bf16[8,102,128]{2,1,0:T(8,128)(2,1)S(1)}, u32[]{:S(2)}, u32[]{:S(2)}) collective-permute-start(bf16[8,102,128]{2,1,0:T(8,128)(2,1)S(1)} %pad_maximum_fusion), channel_id=1, source_target_pairs={{0,1},{1,2},{2,3},{3,0},{4,5},{5,6},{6,7},{7,4},{8,9},{9,10},{10,1... | collective-permute-start | bytes 626696 | tf_op jit(solution)/shard_map/ppermute | solution.py:379
  73.6 13.0 %collective-permute-start.3 = (bf16[8,102,128]{2,1,0:T(8,128)(2,1)}, bf16[8,102,128]{2,1,0:T(8,128)(2,1)S(1)}, u32[]{:S(2)}, u32[]{:S(2)}) collective-permute-start(bf16[8,102,128]{2,1,0:T(8,128)(2,1)} %pad_maximum_fusion.1), channel_id=1, source_target_pairs={{0,3},{1,0},{2,1},{3,2},{4,7},{5,4},{6,5},{7,6},{8,11},{9,8},{10,9... | collective-permute-start | bytes 626696 | tf_op jit(solution)/shard_map/ppermute | solution.py:379
  82.7 38.8 %copy-start.10 = (f32[16]{0:T(128)S(1)}, f32[16]{0:T(128)}, u32[]{:S(2)}) copy-start(f32[16]{0:T(128)} %param.16) | copy-start | bytes 196
  82.7 38.9 %copy-start.1 = (f32[1024,400]{0,1:T(8,128)S(1)}, f32[1024,400]{0,1:T(8,128)}, u32[]{:S(2)}) copy-start(f32[1024,400]{0,1:T(8,128)} %param.11) | copy-start | bytes 4915204
  82.7 38.9 %copy-start.3 = (f32[1024]{0:T(1024)S(1)}, f32[1024]{0:T(1024)}, u32[]{:S(2)}) copy-start(f32[1024]{0:T(1024)} %param.13) | copy-start | bytes 12292
  82.8 9.9 %all-to-all-start.2 = ((bf16[8,102,128]{2,1,0:T(8,128)(2,1)}), bf16[8,102,128]{2,1,0:T(8,128)(2,1)S(1)}, u32[]{:S(2)}, u32[]{:S(2)}) async-start(bf16[8,102,128]{2,1,0:T(8,128)(2,1)} %add_convert_fusion), calls=%async_computation.2 | async-start | bytes 425984 | tf_op jit(solution)/shard_map/all_to_all | solution.py:383
  86.7 10.9 %collective-permute-start.4 = (bf16[8,102,128]{2,1,0:T(8,128)(2,1)S(1)}, bf16[8,102,128]{2,1,0:T(8,128)(2,1)S(1)}, u32[]{:S(2)}, u32[]{:S(2)}) collective-permute-start(bf16[8,102,128]{2,1,0:T(8,128)(2,1)S(1)} %add_convert_fusion.1.refs_2_), channel_id=1, source_target_pairs={{0,1},{1,2},{2,3},{3,0},{4,5},{5,6},{6,7},{7,4},{8,9},{9,10},{10,1... | collective-permute-start | bytes 626696 | tf_op jit(solution)/shard_map/ppermute | solution.py:379
  86.8 11.8 %collective-permute-start.5 = (bf16[8,102,128]{2,1,0:T(8,128)(2,1)S(1)}, bf16[8,102,128]{2,1,0:T(8,128)(2,1)S(1)}, u32[]{:S(2)}, u32[]{:S(2)}) collective-permute-start(bf16[8,102,128]{2,1,0:T(8,128)(2,1)S(1)} %add_convert_fusion.1.refs_2_), channel_id=1, source_target_pairs={{0,3},{1,0},{2,1},{3,2},{4,7},{5,4},{6,5},{7,6},{8,11},{9,8},{10,9... | collective-permute-start | bytes 626696 | tf_op jit(solution)/shard_map/ppermute | solution.py:379
  94.2 11.5 %all-to-all-start.3 = ((bf16[8,102,128]{2,1,0:T(8,128)(2,1)}), bf16[8,102,128]{2,1,0:T(8,128)(2,1)S(1)}, u32[]{:S(2)}, u32[]{:S(2)}) async-start(bf16[8,102,128]{2,1,0:T(8,128)(2,1)} %shard_map.135), calls=%async_computation.3 | async-start | bytes 425984 | tf_op jit(solution)/shard_map/all_to_all | solution.py:383
  97.7 7.7 %collective-permute-start.6 = (bf16[4,102,128]{2,1,0:T(8,128)(2,1)S(1)}, bf16[4,102,128]{2,1,0:T(8,128)(2,1)S(1)}, u32[]{:S(2)}, u32[]{:S(2)}) collective-permute-start(bf16[4,102,128]{2,1,0:T(8,128)(2,1)S(1)} %slice.54), channel_id=1, source_target_pairs={{0,1},{1,2},{2,3},{3,0},{4,5},{5,6},{6,7},{7,4},{8,9},{9,10},{10,1... | collective-permute-start | bytes 313352 | tf_op jit(solution)/shard_map/ppermute | solution.py:379
  98.6 7.0 %collective-permute-start.7 = (bf16[4,102,128]{2,1,0:T(8,128)(2,1)S(1)}, bf16[4,102,128]{2,1,0:T(8,128)(2,1)S(1)}, u32[]{:S(2)}, u32[]{:S(2)}) collective-permute-start(bf16[4,102,128]{2,1,0:T(8,128)(2,1)S(1)} %slice.55), channel_id=1, source_target_pairs={{0,3},{1,0},{2,1},{3,2},{4,7},{5,4},{6,5},{7,6},{8,11},{9,8},{10,9... | collective-permute-start | bytes 313352 | tf_op jit(solution)/shard_map/ppermute | solution.py:379
  105.7 10.0 %collective-permute-start.12 = (bf16[8,102,128]{2,1,0:T(8,128)(2,1)S(1)}, bf16[8,102,128]{2,1,0:T(8,128)(2,1)S(1)}, u32[]{:S(2)}, u32[]{:S(2)}) collective-permute-start(bf16[8,102,128]{2,1,0:T(8,128)(2,1)S(1)} %all-to-all-done.3.refs_4_), channel_id=1, source_target_pairs={{0,1},{1,2},{2,3},{3,0},{4,5},{5,6},{6,7},{7,4},{8,9},{9,10},{10,1... | collective-permute-start | bytes 626696 | tf_op jit(solution)/shard_map/ppermute | solution.py:379
  106.9 11.8 %collective-permute-start.13 = (bf16[8,102,128]{2,1,0:T(8,128)(2,1)S(1)}, bf16[8,102,128]{2,1,0:T(8,128)(2,1)S(1)}, u32[]{:S(2)}, u32[]{:S(2)}) collective-permute-start(bf16[8,102,128]{2,1,0:T(8,128)(2,1)S(1)} %all-to-all-done.3.refs_4_), channel_id=1, source_target_pairs={{0,3},{1,0},{2,1},{3,2},{4,7},{5,4},{6,5},{7,6},{8,11},{9,8},{10,9... | collective-permute-start | bytes 626696 | tf_op jit(solution)/shard_map/ppermute | solution.py:379
  115.7 9.3 %collective-permute-start.14 = (bf16[4,102,128]{2,1,0:T(8,128)(2,1)S(1)}, bf16[4,102,128]{2,1,0:T(8,128)(2,1)S(1)}, u32[]{:S(2)}, u32[]{:S(2)}) collective-permute-start(bf16[4,102,128]{2,1,0:T(8,128)(2,1)S(1)} %slice.58), channel_id=1, source_target_pairs={{0,1},{1,2},{2,3},{3,0},{4,5},{5,6},{6,7},{7,4},{8,9},{9,10},{10,1... | collective-permute-start | bytes 313352 | tf_op jit(solution)/shard_map/ppermute | solution.py:379
  119.3 5.7 %collective-permute-start.15 = (bf16[4,102,128]{2,1,0:T(8,128)(2,1)}, bf16[4,102,128]{2,1,0:T(8,128)(2,1)S(1)}, u32[]{:S(2)}, u32[]{:S(2)}) collective-permute-start(bf16[4,102,128]{2,1,0:T(8,128)(2,1)} %slice.59), channel_id=1, source_target_pairs={{0,3},{1,0},{2,1},{3,2},{4,7},{5,4},{6,5},{7,6},{8,11},{9,8},{10,9... | collective-permute-start | bytes 313352 | tf_op jit(solution)/shard_map/ppermute | solution.py:379
  121.6 3.4 %copy-start = (f32[1024,400]{0,1:T(8,128)S(1)}, f32[1024,400]{0,1:T(8,128)}, u32[]{:S(2)}) copy-start(f32[1024,400]{0,1:T(8,128)} %param.12) | copy-start | bytes 4915204
  121.6 3.4 %copy-start.4 = (f32[1024]{0:T(1024)S(1)}, f32[1024]{0:T(1024)}, u32[]{:S(2)}) copy-start(f32[1024]{0:T(1024)} %param.14) | copy-start | bytes 12292

commit v5 on v4

--- a/solution.py
+++ b/solution.py
@@ -18,6 +18,7 @@
 
 
 ANY_SPEC = pl.BlockSpec(memory_space=pl.ANY)
+VMEM_SPEC = pl.BlockSpec(memory_space=pltpu.VMEM)
 
 
 def params(mib):
@@ -181,29 +182,17 @@
     steps, lanes, packed, meta_ref, tid_ref, rid_ref, rel_ref, edge_ref, parts_ref, *refs
 ):
     grad_ref, rel_out_ref = refs[:2]
-    outs = refs[2:-6]
-    table_ref, acc_ref, hot_ref, coef_ref, stage_ref, sems = refs[-6:]
+    outs = refs[2:-4]
+    table_ref, acc_ref, hot_ref, coef_ref = refs[-4:]
     step = pl.program_id(0)
 
     @pl.when(step == 0)
     def _():
         pieces, _, width = parts_ref.shape
-        copies = [
-            pltpu.make_async_copy(parts_ref.at[b], there, sems.at[b])
-            for b, there in enumerate(
-                table_ref.at[:, pl.ds(b * width, width)] if width % 128 == 0 else stage_ref.at[b]
-                for b in range(pieces)
-            )
-        ]
-        for copy in copies:
-            copy.start()
+        for b in range(pieces):
+            table_ref[:, b * width : (b + 1) * width] = parts_ref[b]
         acc_ref[...] = jnp.zeros_like(acc_ref)
         rel_out_ref[...] = jnp.zeros_like(rel_out_ref)
-        for copy in copies:
-            copy.wait()
-        if width % 128:
-            for b in range(pieces):
-                table_ref[:, b * width : (b + 1) * width] = stage_ref[b]
 
     @pl.when(is_live(meta_ref, step, steps, tid_ref.shape[2]))
     def _():
@@ -275,33 +264,18 @@
                 out[:, block:] = jnp.zeros((out.shape[0], out.shape[1] - block, out.shape[2]), out.dtype)
 
 
-def pick_kernel(plan_ref, in_ref, out_ref, sems):
-    copies = [
-        pltpu.make_async_copy(in_ref.at[plan_ref[b]], out_ref.at[b], sems.at[b])
-        for b in range(in_ref.shape[0])
-    ]
-    for copy in copies:
-        copy.start()
-    for copy in copies:
-        copy.wait()
-
-
-def place_kernel(block, plan_ref, in_ref, out_ref, held_ref, load_sem, sems):
-    load = pltpu.make_async_copy(in_ref, held_ref, load_sem)
-    load.start()
-    load.wait()
+def pick_kernel(plan_ref, in_ref, out_ref):
+    for b in range(in_ref.shape[0]):
+        out_ref[b] = in_ref[plan_ref[b]]
+
+
+def place_kernel(block, plan_ref, in_ref, out_ref):
+    for b in range(in_ref.shape[0]):
+        out_ref[plan_ref[b]] = in_ref[b]
     if in_ref.shape[1] > block:
-        total = jnp.sum(held_ref[:, block:].astype(F32), axis=0).astype(BF16)
+        total = jnp.sum(in_ref[:, block:].astype(F32), axis=0).astype(BF16)
         for b in range(in_ref.shape[0]):
-            held_ref[b, block:] = total
-    copies = [
-        pltpu.make_async_copy(held_ref.at[b], out_ref.at[plan_ref[b]], sems.at[b])
-        for b in range(in_ref.shape[0])
-    ]
-    for copy in copies:
-        copy.start()
-    for copy in copies:
-        copy.wait()
+            out_ref[b, block:] = total
 
 
 def adagrad(table, state, grad, axis):
@@ -312,37 +286,24 @@
 def update_kernel(lanes, joined, meta_ref, *refs):
     count = len(ring_plan(lanes, 2))
     if joined:
-        table_any, state_ref, rel_ref, rel_state_ref = refs[:4]
-        parts_any, refs = refs[4 : 4 + count], refs[4 + count :]
+        table_ref, state_ref, rel_ref, rel_state_ref = refs[:4]
+        parts, refs = refs[4 : 4 + count], refs[4 + count :]
         out_any, rel_out_ref, rel_grad_ref = refs[:3]
         refs = refs[3:]
     else:
-        table_any, state_ref = refs[:2]
-        parts_any, out_any, refs = refs[2 : 2 + count], refs[2 + count], refs[3 + count :]
-    table_ref, grad_ref, parts, (part_sems, load_sems, store_sems) = refs[0], refs[1], refs[2:-3], refs[-3:]
+        table_ref, state_ref = refs[:2]
+        parts, out_any, refs = refs[2 : 2 + count], refs[2 + count], refs[3 + count :]
+    new_ref, grad_ref, store_sems = refs
     features, rows = table_ref.shape
     chunk = 256 if rows % 256 == 0 else rows
     spots = [pl.ds(first, chunk) for first in range(0, rows, chunk)]
-    fetches = [
-        pltpu.make_async_copy(far, near, part_sems.at[k])
-        for k, (far, near) in enumerate(zip(parts_any, parts))
-    ]
-    loads = [
-        pltpu.make_async_copy(table_any.at[:, spot], table_ref.at[:, spot], load_sems.at[k])
+    stores = [
+        pltpu.make_async_copy(new_ref.at[:, spot], out_any.at[:, spot], store_sems.at[k])
         for k, spot in enumerate(spots)
     ]
-    stores = [
-        pltpu.make_async_copy(table_ref.at[:, spot], out_any.at[:, spot], store_sems.at[k])
-        for k, spot in enumerate(spots)
-    ]
-    for copy in fetches + loads:
-        copy.start()
-    for copy in fetches:
-        copy.wait()
     assemble(lanes, meta_ref[1], parts, grad_ref)
-    for spot, load, store in zip(spots, loads, stores):
-        load.wait()
-        table_ref[:, spot] = adagrad(table_ref[:, spot], state_ref[:, spot], grad_ref[:, spot], 0)
+    for spot, store in zip(spots, stores):
+        new_ref[:, spot] = adagrad(table_ref[:, spot], state_ref[:, spot], grad_ref[:, spot], 0)
         store.start()
     if joined:
         block = features // lanes
@@ -396,12 +357,11 @@
     return pl.pallas_call(
         functools.partial(update_kernel, lanes, joined),
         out_shape=[jax.ShapeDtypeStruct(t.shape, F32) for t in (table,) + extra[:1]],
-        in_specs=[SMEM_SPEC, ANY_SPEC, vmem] + [vmem] * len(extra) + [ANY_SPEC] * len(parts),
+        in_specs=[SMEM_SPEC] + [vmem] * (2 + len(extra) + len(parts)),
         out_specs=[ANY_SPEC] + [vmem] * joined,
         scratch_shapes=[pltpu.VMEM(t.shape, F32) for t in extra[:1]]
         + [pltpu.VMEM(table.shape, F32)] * 2
-        + [pltpu.VMEM(part.shape, BF16) for part in parts]
-        + [dma((len(parts),)), dma((chunks,)), dma((chunks,))],
+        + [dma((chunks,))],
         compiler_params=params(24),
     )(meta, table, state, *extra, *parts)
 
@@ -452,9 +412,8 @@
     chosen = pl.pallas_call(
         pick_kernel,
         out_shape=jax.ShapeDtypeStruct(owned.shape, BF16),
-        in_specs=[SMEM_SPEC, ANY_SPEC],
-        out_specs=ANY_SPEC,
-        scratch_shapes=[dma((buckets,))],
+        in_specs=[SMEM_SPEC, VMEM_SPEC],
+        out_specs=VMEM_SPEC,
         compiler_params=params(8),
     )(plan, spread)
     fetched = swap_buckets(chosen)
@@ -497,7 +456,7 @@
             per_span(rid.shape),
             whole(relation.shape),
             per_span(both_shape),
-            ANY_SPEC,
+            VMEM_SPEC,
         ],
         out_specs=[per_span(edge_shape), whole((features, kinds))]
         + [whole(out.shape) for out in bundle_outs],
@@ -506,8 +465,6 @@
             pltpu.VMEM((features, rows), F32),
             pltpu.VMEM((rows, E_CH), BF16),
             pltpu.VMEM((E_CH, E_CH), BF16),
-            pltpu.VMEM(owned.shape if width % 128 else (16, 128), BF16),
-            dma((buckets,)),
         ],
         compiler_params=params(48),
         cost_estimate=cost(12 * steps * features * rows * E_CH, 8 * features * steps * E_CH),
@@ -543,10 +500,9 @@
     sorted_out = pl.pallas_call(
         functools.partial(place_kernel, block),
         out_shape=bundle_shape,
-        in_specs=[SMEM_SPEC, ANY_SPEC],
-        out_specs=ANY_SPEC,
-        scratch_shapes=[pltpu.VMEM(bundles, BF16), dma, dma((buckets,))],
-        compiler_params=params(16),
+        in_specs=[SMEM_SPEC, VMEM_SPEC],
+        out_specs=VMEM_SPEC,
+        compiler_params=params(8),
     )(plan, returned)
     target_home = swap_buckets(sorted_out)
     source_parts = gather_span(source_sum)

time: 130 us -> 126 us (0.969)
  Pallas kernels: 38.6 us -> 26.7 us
  starting transfers between devices: 37.8 us -> 46.1 us
    all_to_all x3, starting transfers between devices: 10.5 us -> 17.9 us  [swap_buckets(): return lax.all_to_all(x, 'bucket', split_axis=0, concat_axis=0, tiled=True)]
    pallas_call x1, Pallas kernels: 17.2 us -> 11.1 us  [per_device(): pl.pallas_call(functools.partial(main_kernel, steps, lanes, packed), grid...]
    pallas_call x2, Pallas kernels: 7.37 us -> 4.7 us  [update(): pl.pallas_call(functools.partial(update_kernel, lanes, joined), out_shape...]
    pallas_call x1, Pallas kernels: 4.29 us -> 2.6 us  [per_device(): pl.pallas_call(functools.partial(source_kernel, steps, lanes), grid=(step...]
    all_to_all x3, waiting for transfers between devices: 7 us -> 8.49 us  [swap_buckets(): return lax.all_to_all(x, 'bucket', split_axis=0, concat_axis=0, tiled=True)]
  transfers between devices with their start and end apart: 19 -> 19, of which waited for: 11 -> 10; matrix products, arithmetic and copies ran while one was open for 2% -> 3% of each run, Pallas kernels for 12% -> 9%
where the time goes in v5:
time: 126 us
  starting transfers between devices  46.1 us (37%)
  waiting for transfers between devices  28.7 us (23%)
  Pallas kernels  26.7 us (21%)
  blocking collectives  17.9 us (14%)
  other arithmetic  3.88 us (3%)
  between operations  1.53 us (1%)
    ppermute x16, starting transfers between devices, shift_span(): lax.ppermute(x, 'span', [(i, (i + by) % count) for i in range(count)])  28.2 us
    ppermute x16, waiting for transfers between devices, shift_span(): lax.ppermute(x, 'span', [(i, (i + by) % count) for i in range(count)])  20.2 us
    all_to_all x3, starting transfers between devices, swap_buckets(): return lax.all_to_all(x, 'bucket', split_axis=0, concat_axis=0, tiled=True)  17.9 us
    all_to_all x1, blocking collectives, swap_buckets(): return lax.all_to_all(x, 'bucket', split_axis=0, concat_axis=0, tiled=True)  17.9 us
    pallas_call x1, Pallas kernels, per_device(): pl.pallas_call(functools.partial(main_kernel, steps, lanes, packed), grid...  11.1 us
    all_to_all x3, waiting for transfers between devices, swap_buckets(): return lax.all_to_all(x, 'bucket', split_axis=0, concat_axis=0, tiled=True)  8.49 us
    pallas_call x1, Pallas kernels, per_device(): pl.pallas_call(functools.partial(prep_kernel, steps), grid=(steps,), out_...  5.58 us
    pallas_call x2, Pallas kernels, update(): pl.pallas_call(functools.partial(update_kernel, lanes, joined), out_shape...  4.7 us
  transfers between devices with their start and end apart: 19, of which 10 were waited for; matrix products, arithmetic and copies ran while one was open for 3% of the time, Pallas kernels for 9%

profile of v5, /device:TPU:0, one launch (start us, length us, event | category | flops | bytes accessed | tf_op | source)
XLA Modules:
  0.0 125.7 jit_solution(2222054563262380699)
XLA Ops:
  0.6 1.5 %bitcast_bitcast_fusion = bf16[8,400,128]{2,1,0:T(8,128)(2,1)S(1)} fusion(f32[1024,400]{0,1:T(8,128)} %param.12), kind=kLoop, calls=%fused_computation | loop fusion | flops 409600 | bytes 2457600 | tf_op jit(solution)/shard_map/transpose | solution.py:409
  2.2 17.9 %all_to_all.20.in_ref = bf16[8,400,128]{2,1,0:T(8,128)(2,1)S(1)} all-to-all(bf16[8,400,128]{2,1,0:T(8,128)(2,1)S(1)} %bitcast_bitcast_fusion), channel_id=1, replica_groups=mesh['bucket'=8,'span'=4] {'bucket'}, dimensions={0} | all-to-all | bytes 1638400 | tf_op jit(solution)/shard_map/all_to_all | solution.py:344
  20.1 1.5 %shard_map.131 = bf16[8,400,128]{2,1,0:T(8,128)(2,1)} custom-call(s32[8]{0:T(128)S(1)} %copy-done.5, bf16[8,400,128]{2,1,0:T(8,128)(2,1)S(1)} %all_to_all.20.in_ref), custom_call_target="tpu_custom_call" | custom-call | tf_op jit(solution)/shard_map/pallas_call | solution.py:412
  21.6 3.5 %all-to-all-start.1 = ((bf16[8,400,128]{2,1,0:T(8,128)(2,1)}), bf16[8,400,128]{2,1,0:T(8,128)(2,1)S(1)}, u32[]{:S(2)}, u32[]{:S(2)}) async-start(bf16[8,400,128]{2,1,0:T(8,128)(2,1)} %shard_map.131), calls=%async_computation.1 | async-start | bytes 1638400 | tf_op jit(solution)/shard_map/all_to_all | solution.py:344
  25.8 0.6 pad_add_fusion.meta_ref
  26.4 5.6 %shard_map.130.edge_ref = bf16[4,2,400,640]{3,2,1,0:T(8,128)(2,1)} custom-call(s32[2]{0:T(128)} %pad_add_fusion.meta_ref, s32[4,1,640]{2,1,0:T(1,128)} %bitcast.28, s32[4,1,640]{2,1,0:T(1,128)} %bitcast.26, f32[400,1024]{1,0:T(8,128)} %bitcast.21, f32[16,400]{1,0:T(8,128)} %refs_2_.1), custom_call_target="tpu_custom_call" | custom-call | flops 4194304000 | bytes 8192000 | tf_op jit(solution)/shard_map/pallas_call | solution.py:427
  31.9 6.0 %all-to-all-done.1.parts_ref = bf16[8,400,128]{2,1,0:T(8,128)(2,1)S(1)} async-done(((bf16[8,400,128]{2,1,0:T(8,128)(2,1)}), bf16[8,400,128]{2,1,0:T(8,128)(2,1)S(1)}, u32[]{:S(2)}, u32[]{:S(2)}) %all-to-all-start.1) | async-done | bytes 819232 | tf_op jit(solution)/shard_map/all_to_all | solution.py:344
  38.0 0.0 copy-start.9
  38.0 11.1 %shard_map.132 = (bf16[4,400,640]{2,1,0:T(8,128)(2,1)S(1)}, f32[400,16]{1,0:T(8,128)}, f32[8,102,128]{2,1,0:T(8,128)S(1)}, f32[8,102,128]{2,1,0:T(8,128)S(1)}, f...) custom-call(s32[2]{0:T(128)S(1)} %copy-done.6, ...), custom_call_target="tpu_custom_call" | custom-call | flops 12582912000 | bytes 8192000 | tf_op jit(solution)/shard_map/pallas_call | solution.py:445
  49.1 0.0 collective-permute-start.8
  49.1 3.8 %collective-permute-start.9 = (bf16[4,102,128]{2,1,0:T(8,128)(2,1)S(1)}, bf16[4,102,128]{2,1,0:T(8,128)(2,1)S(1)}, u32[]{:S(2)}, u32[]{:S(2)}) collective-permute-start(bf16[4,102,128]{2,1,0:T(8,128)(2,1)S(1)} %get-tuple-element.29), channel_id=1, source_target_pairs={{0,3},{1,0},{2,1},{3,2},{4,7},{5,4},{6,5},{7,6},{8,11},{9,8},{10,9... | collective-permute-start | bytes 313352 | tf_op jit(solution)/shard_map/ppermute | solution.py:340
  52.9 2.6 %shard_map.133 = (f32[8,102,128]{2,1,0:T(8,128)S(1)}, f32[8,102,128]{2,1,0:T(8,128)S(1)}, f32[8,102,128]{2,1,0:T(8,128)S(1)}, bf16[4,102,128]{2,1,0:T(8,128)(2,1)S(1)}, bf16[4,102,128]{2,1,0:T(8,128)(2,1)S(1)}) custom-call(s32[2]{0:T(128)S(1)} %copy-done.6, s32[4,1,640]{2,1,0:T(1,128)S(1)} %bitcast.29, bf16[4,400,640]{2,1,0:T(8,128)(2,1)S(1)} %get-tuple-element.20.grad_ref), custom_call_target="tpu_custom_call" | custom-call | flops 4194304000 | bytes 8192000 | tf_op jit(solution)/shard_map/pallas_call | solution.py:473
  55.6 0.1 collective-permute-start
  55.7 3.9 %collective-permute-start.2 = (bf16[4,102,128]{2,1,0:T(8,128)(2,1)S(1)}, bf16[4,102,128]{2,1,0:T(8,128)(2,1)S(1)}, u32[]{:S(2)}, u32[]{:S(2)}) collective-permute-start(bf16[4,102,128]{2,1,0:T(8,128)(2,1)S(1)} %get-tuple-element.25), channel_id=1, source_target_pairs={{0,3},{1,0},{2,1},{3,2},{4,7},{5,4},{6,5},{7,6},{8,11},{9,8},{10,9... | collective-permute-start | bytes 313352 | tf_op jit(solution)/shard_map/ppermute | solution.py:340
  59.6 0.0 collective-permute-done.8
  59.6 0.0 collective-permute-done.9
  59.6 0.1 collective-permute-start.10
  59.8 3.9 %collective-permute-start.11 = (bf16[8,102,128]{2,1,0:T(8,128)(2,1)S(1)}, bf16[8,102,128]{2,1,0:T(8,128)(2,1)S(1)}, u32[]{:S(2)}, u32[]{:S(2)}) collective-permute-start(bf16[8,102,128]{2,1,0:T(8,128)(2,1)S(1)} %pad_maximum_fusion.3), channel_id=1, source_target_pairs={{0,3},{1,0},{2,1},{3,2},{4,7},{5,4},{6,5},{7,6},{8,11},{9,8},{10,9... | collective-permute-start | bytes 626696 | tf_op jit(solution)/shard_map/ppermute | solution.py:340
  63.6 0.0 collective-permute-done
  63.7 0.1 collective-permute-start.1
  63.8 0.7 pad_maximum_fusion.1
  64.5 3.8 %collective-permute-start.3 = (bf16[8,102,128]{2,1,0:T(8,128)(2,1)}, bf16[8,102,128]{2,1,0:T(8,128)(2,1)S(1)}, u32[]{:S(2)}, u32[]{:S(2)}) collective-permute-start(bf16[8,102,128]{2,1,0:T(8,128)(2,1)} %pad_maximum_fusion.1), channel_id=1, source_target_pairs={{0,3},{1,0},{2,1},{3,2},{4,7},{5,4},{6,5},{7,6},{8,11},{9,8},{10,9... | collective-permute-start | bytes 626696 | tf_op jit(solution)/shard_map/ppermute | solution.py:340
  68.3 1.4 %collective-permute-done.10 = bf16[8,102,128]{2,1,0:T(8,128)(2,1)S(1)} collective-permute-done((bf16[8,102,128]{2,1,0:T(8,128)(2,1)S(1)}, bf16[8,102,128]{2,1,0:T(8,128)(2,1)S(1)}, u32[]{:S(2)}, u32[]{:S(2)}) %collective-permute-start.10) | collective-permute-done | bytes 208928 | tf_op jit(solution)/shard_map/ppermute | solution.py:340
  69.8 3.1 %collective-permute-done.11 = bf16[8,102,128]{2,1,0:T(8,128)(2,1)S(1)} collective-permute-done((bf16[8,102,128]{2,1,0:T(8,128)(2,1)S(1)}, bf16[8,102,128]{2,1,0:T(8,128)(2,1)S(1)}, u32[]{:S(2)}, u32[]{:S(2)}) %collective-permute-start.11) | collective-permute-done | bytes 208928 | tf_op jit(solution)/shard_map/ppermute | solution.py:340
  72.9 0.8 add_convert_fusion
  73.7 10.6 %all-to-all-start.2 = ((bf16[8,102,128]{2,1,0:T(8,128)(2,1)}), bf16[8,102,128]{2,1,0:T(8,128)(2,1)S(1)}, u32[]{:S(2)}, u32[]{:S(2)}) async-start(bf16[8,102,128]{2,1,0:T(8,128)(2,1)} %add_convert_fusion), calls=%async_computation.2 | async-start | bytes 425984 | tf_op jit(solution)/shard_map/all_to_all | solution.py:344
  84.3 0.1 add_convert_fusion.1.refs_2_
  84.4 1.0 collective-permute-start.4
  85.4 2.8 %collective-permute-start.5 = (bf16[8,102,128]{2,1,0:T(8,128)(2,1)S(1)}, bf16[8,102,128]{2,1,0:T(8,128)(2,1)S(1)}, u32[]{:S(2)}, u32[]{:S(2)}) collective-permute-start(bf16[8,102,128]{2,1,0:T(8,128)(2,1)S(1)} %add_convert_fusion.1.refs_2_), channel_id=1, source_target_pairs={{0,3},{1,0},{2,1},{3,2},{4,7},{5,4},{6,5},{7,6},{8,11},{9,8},{10,9... | collective-permute-start | bytes 626696 | tf_op jit(solution)/shard_map/ppermute | solution.py:340
  88.2 2.4 %all-to-all-done.2.in_ref = bf16[8,102,128]{2,1,0:T(8,128)(2,1)S(1)} async-done(((bf16[8,102,128]{2,1,0:T(8,128)(2,1)}), bf16[8,102,128]{2,1,0:T(8,128)(2,1)S(1)}, u32[]{:S(2)}, u32[]{:S(2)}) %all-to-all-start.2) | async-done | bytes 208928 | tf_op jit(solution)/shard_map/all_to_all | solution.py:344
  90.7 1.2 shard_map.135
  91.9 3.8 %all-to-all-start.3 = ((bf16[8,102,128]{2,1,0:T(8,128)(2,1)}), bf16[8,102,128]{2,1,0:T(8,128)(2,1)S(1)}, u32[]{:S(2)}, u32[]{:S(2)}) async-start(bf16[8,102,128]{2,1,0:T(8,128)(2,1)} %shard_map.135), calls=%async_computation.3 | async-start | bytes 425984 | tf_op jit(solution)/shard_map/all_to_all | solution.py:344
  95.7 0.7 collective-permute-start.6
  96.4 0.9 collective-permute-done.5.refs_4_
  97.3 2.3 %collective-permute-start.7 = (bf16[4,102,128]{2,1,0:T(8,128)(2,1)S(1)}, bf16[4,102,128]{2,1,0:T(8,128)(2,1)S(1)}, u32[]{:S(2)}, u32[]{:S(2)}) collective-permute-start(bf16[4,102,128]{2,1,0:T(8,128)(2,1)S(1)} %slice.55), channel_id=1, source_target_pairs={{0,3},{1,0},{2,1},{3,2},{4,7},{5,4},{6,5},{7,6},{8,11},{9,8},{10,9... | collective-permute-start | bytes 313352 | tf_op jit(solution)/shard_map/ppermute | solution.py:340
  99.7 3.7 %collective-permute-done.6.refs_5_ = bf16[4,102,128]{2,1,0:T(8,128)(2,1)S(1)} collective-permute-done((bf16[4,102,128]{2,1,0:T(8,128)(2,1)S(1)}, bf16[4,102,128]{2,1,0:T(8,128)(2,1)S(1)}, u32[]{:S(2)}, u32[]{:S(2)}) %collective-permute-start.6) | collective-permute-done | bytes 104480 | tf_op jit(solution)/shard_map/ppermute | solution.py:340
  103.4 0.8 collective-permute-done.7.refs_6_
  104.2 0.8 collective-permute-start.12
  105.0 3.1 %collective-permute-start.13 = (bf16[8,102,128]{2,1,0:T(8,128)(2,1)S(1)}, bf16[8,102,128]{2,1,0:T(8,128)(2,1)S(1)}, u32[]{:S(2)}, u32[]{:S(2)}) collective-permute-start(bf16[8,102,128]{2,1,0:T(8,128)(2,1)S(1)} %all-to-all-done.3.refs_4_), channel_id=1, source_target_pairs={{0,3},{1,0},{2,1},{3,2},{4,7},{5,4},{6,5},{7,6},{8,11},{9,8},{10,9... | collective-permute-start | bytes 626696 | tf_op jit(solution)/shard_map/ppermute | solution.py:340
  108.0 6.1 %collective-permute-done.12.refs_5_ = bf16[8,102,128]{2,1,0:T(8,128)(2,1)S(1)} collective-permute-done((bf16[8,102,128]{2,1,0:T(8,128)(2,1)S(1)}, bf16[8,102,128]{2,1,0:T(8,128)(2,1)S(1)}, u32[]{:S(2)}, u32[]{:S(2)}) %collective-permute-start.12) | collective-permute-done | bytes 208928 | tf_op jit(solution)/shard_map/ppermute | solution.py:340
  114.1 0.1 collective-permute-start.14
  114.2 2.8 %collective-permute-done.13.refs_6_ = bf16[8,102,128]{2,1,0:T(8,128)(2,1)S(1)} collective-permute-done((bf16[8,102,128]{2,1,0:T(8,128)(2,1)S(1)}, bf16[8,102,128]{2,1,0:T(8,128)(2,1)S(1)}, u32[]{:S(2)}, u32[]{:S(2)}) %collective-permute-start.13) | collective-permute-done | bytes 208928 | tf_op jit(solution)/shard_map/ppermute | solution.py:340
  117.0 0.7 slice.59
  117.6 1.9 %collective-permute-start.15 = (bf16[4,102,128]{2,1,0:T(8,128)(2,1)}, bf16[4,102,128]{2,1,0:T(8,128)(2,1)S(1)}, u32[]{:S(2)}, u32[]{:S(2)}) collective-permute-start(bf16[4,102,128]{2,1,0:T(8,128)(2,1)} %slice.59), channel_id=1, source_target_pairs={{0,3},{1,0},{2,1},{3,2},{4,7},{5,4},{6,5},{7,6},{8,11},{9,8},{10,9... | collective-permute-start | bytes 313352 | tf_op jit(solution)/shard_map/ppermute | solution.py:340
  119.5 0.1 copy.15.refs_3_
  119.6 2.0 %shard_map.134 = f32[400,1024]{1,0:T(8,128)} custom-call(s32[2]{0:T(128)S(1)} %copy-done.6, f32[400,1024]{1,0:T(8,128)S(1)} %bitcast.22, f32[1,1024]{1,0:T(1,128)S(1)} %bitcast.23, bf16[8,102,128]{2,1,0:T(8,128)(2,1)S(1)} %add_convert_fusion.1.refs_2_, bf16[8,102,128]{2,1,0:T(8,128)(2,1)S(1)} %collective-permute-done.4.refs_3_, ...), custom_call_target="tpu_custom_call" | custom-call | tf_op jit(solution)/shard_map/pallas_call | solution.py:357
  121.7 1.4 %collective-permute-done.15.refs_8_ = bf16[4,102,128]{2,1,0:T(8,128)(2,1)S(1)} collective-permute-done((bf16[4,102,128]{2,1,0:T(8,128)(2,1)}, bf16[4,102,128]{2,1,0:T(8,128)(2,1)S(1)}, u32[]{:S(2)}, u32[]{:S(2)}) %collective-permute-start.15) | collective-permute-done | bytes 104480 | tf_op jit(solution)/shard_map/ppermute | solution.py:340
  123.0 2.7 %shard_map.136 = (f32[400,1024]{1,0:T(8,128)}, f32[16,400]{1,0:T(8,128)}) custom-call(s32[2]{0:T(128)S(1)} %copy-done.6, f32[400,1024]{1,0:T(8,128)S(1)} %bitcast.20, f32[1,1024]{1,0:T(1,128)S(1)} %bitcast.24, f32[16,400]{1,0:T(8,128)S(1)} %copy-done.2, f32[16,1]{1,0:T(8,128)S(1)} %copy.15.refs_3_, bf16[8,102,128]{2,1,0:T(8,128)(2,1)S(1)} %all-to-all-done.3.refs_4_, ...), custom_call_target="tpu_custom_call" | custom-call | tf_op jit(solution)/shard_map/pallas_call | solution.py:357
  (41 shorter events, 0.3 us)
Async XLA Ops:
  0.6 19.4 %copy-start.5 = (s32[8]{0:T(128)S(1)}, s32[8]{0:T(128)}, u32[]{:S(2)}) copy-start(s32[8]{0:T(128)} %plan_ref.3) | copy-start | bytes 100
  21.6 16.4 %all-to-all-start.1 = ((bf16[8,400,128]{2,1,0:T(8,128)(2,1)}), bf16[8,400,128]{2,1,0:T(8,128)(2,1)S(1)}, u32[]{:S(2)}, u32[]{:S(2)}) async-start(bf16[8,400,128]{2,1,0:T(8,128)(2,1)} %shard_map.131), calls=%async_computation.1 | async-start | bytes 1638400 | tf_op jit(solution)/shard_map/all_to_all | solution.py:344
  26.3 11.6 %copy-start.2 = (f32[16,400]{1,0:T(8,128)S(1)}, f32[16,400]{1,0:T(8,128)}, u32[]{:S(2)}) copy-start(f32[16,400]{1,0:T(8,128)} %refs_2_.1) | copy-start | bytes 76804
  26.3 11.6 %copy-start.6 = (s32[2]{0:T(128)S(1)}, s32[2]{0:T(128)}, u32[]{:S(2)}) copy-start(s32[2]{0:T(128)} %pad_add_fusion.meta_ref) | copy-start | bytes 28
  26.4 11.6 %copy-start.7 = (s32[1,2560]{1,0:T(1,128)S(1)}, s32[1,2560]{1,0:T(1,128)}, u32[]{:S(2)}) copy-start(s32[1,2560]{1,0:T(1,128)} %param.19) | copy-start | bytes 30724
  26.4 11.7 %copy-start.8 = (s32[1,2560]{1,0:T(1,128)S(1)}, s32[1,2560]{1,0:T(1,128)}, u32[]{:S(2)}) copy-start(s32[1,2560]{1,0:T(1,128)} %param.20) | copy-start | bytes 30724
  38.0 14.9 %copy-start.9 = (s32[1,2560]{1,0:T(1,128)S(1)}, s32[1,2560]{1,0:T(1,128)}, u32[]{:S(2)}) copy-start(s32[1,2560]{1,0:T(1,128)} %param.18) | copy-start | bytes 30724
  49.1 10.5 %collective-permute-start.8 = (bf16[4,102,128]{2,1,0:T(8,128)(2,1)S(1)}, bf16[4,102,128]{2,1,0:T(8,128)(2,1)S(1)}, u32[]{:S(2)}, u32[]{:S(2)}) collective-permute-start(bf16[4,102,128]{2,1,0:T(8,128)(2,1)S(1)} %get-tuple-element.28), channel_id=1, source_target_pairs={{0,1},{1,2},{2,3},{3,0},{4,5},{5,6},{6,7},{7,4},{8,9},{9,10},{10,1... | collective-permute-start | bytes 313352 | tf_op jit(solution)/shard_map/ppermute | solution.py:340
  49.1 10.5 %collective-permute-start.9 = (bf16[4,102,128]{2,1,0:T(8,128)(2,1)S(1)}, bf16[4,102,128]{2,1,0:T(8,128)(2,1)S(1)}, u32[]{:S(2)}, u32[]{:S(2)}) collective-permute-start(bf16[4,102,128]{2,1,0:T(8,128)(2,1)S(1)} %get-tuple-element.29), channel_id=1, source_target_pairs={{0,3},{1,0},{2,1},{3,2},{4,7},{5,4},{6,5},{7,6},{8,11},{9,8},{10,9... | collective-permute-start | bytes 313352 | tf_op jit(solution)/shard_map/ppermute | solution.py:340
  55.6 8.1 %collective-permute-start = (bf16[4,102,128]{2,1,0:T(8,128)(2,1)S(1)}, bf16[4,102,128]{2,1,0:T(8,128)(2,1)S(1)}, u32[]{:S(2)}, u32[]{:S(2)}) collective-permute-start(bf16[4,102,128]{2,1,0:T(8,128)(2,1)S(1)} %get-tuple-element.23), channel_id=1, source_target_pairs={{0,1},{1,2},{2,3},{3,0},{4,5},{5,6},{6,7},{7,4},{8,9},{9,10},{10,1... | collective-permute-start | bytes 313352 | tf_op jit(solution)/shard_map/ppermute | solution.py:340
  55.7 8.1 %collective-permute-start.2 = (bf16[4,102,128]{2,1,0:T(8,128)(2,1)S(1)}, bf16[4,102,128]{2,1,0:T(8,128)(2,1)S(1)}, u32[]{:S(2)}, u32[]{:S(2)}) collective-permute-start(bf16[4,102,128]{2,1,0:T(8,128)(2,1)S(1)} %get-tuple-element.25), channel_id=1, source_target_pairs={{0,3},{1,0},{2,1},{3,2},{4,7},{5,4},{6,5},{7,6},{8,11},{9,8},{10,9... | collective-permute-start | bytes 313352 | tf_op jit(solution)/shard_map/ppermute | solution.py:340
  59.6 10.1 %collective-permute-start.10 = (bf16[8,102,128]{2,1,0:T(8,128)(2,1)S(1)}, bf16[8,102,128]{2,1,0:T(8,128)(2,1)S(1)}, u32[]{:S(2)}, u32[]{:S(2)}) collective-permute-start(bf16[8,102,128]{2,1,0:T(8,128)(2,1)S(1)} %pad_maximum_fusion.2), channel_id=1, source_target_pairs={{0,1},{1,2},{2,3},{3,0},{4,5},{5,6},{6,7},{7,4},{8,9},{9,10},{10,1... | collective-permute-start | bytes 626696 | tf_op jit(solution)/shard_map/ppermute | solution.py:340
  59.8 13.1 %collective-permute-start.11 = (bf16[8,102,128]{2,1,0:T(8,128)(2,1)S(1)}, bf16[8,102,128]{2,1,0:T(8,128)(2,1)S(1)}, u32[]{:S(2)}, u32[]{:S(2)}) collective-permute-start(bf16[8,102,128]{2,1,0:T(8,128)(2,1)S(1)} %pad_maximum_fusion.3), channel_id=1, source_target_pairs={{0,3},{1,0},{2,1},{3,2},{4,7},{5,4},{6,5},{7,6},{8,11},{9,8},{10,9... | collective-permute-start | bytes 626696 | tf_op jit(solution)/shard_map/ppermute | solution.py:340
  63.7 20.6 %collective-permute-start.1 = (bf16[8,102,128]{2,1,0:T(8,128)(2,1)S(1)}, bf16[8,102,128]{2,1,0:T(8,128)(2,1)S(1)}, u32[]{:S(2)}, u32[]{:S(2)}) collective-permute-start(bf16[8,102,128]{2,1,0:T(8,128)(2,1)S(1)} %pad_maximum_fusion), channel_id=1, source_target_pairs={{0,1},{1,2},{2,3},{3,0},{4,5},{5,6},{6,7},{7,4},{8,9},{9,10},{10,1... | collective-permute-start | bytes 626696 | tf_op jit(solution)/shard_map/ppermute | solution.py:340
  64.5 19.7 %collective-permute-start.3 = (bf16[8,102,128]{2,1,0:T(8,128)(2,1)}, bf16[8,102,128]{2,1,0:T(8,128)(2,1)S(1)}, u32[]{:S(2)}, u32[]{:S(2)}) collective-permute-start(bf16[8,102,128]{2,1,0:T(8,128)(2,1)} %pad_maximum_fusion.1), channel_id=1, source_target_pairs={{0,3},{1,0},{2,1},{3,2},{4,7},{5,4},{6,5},{7,6},{8,11},{9,8},{10,9... | collective-permute-start | bytes 626696 | tf_op jit(solution)/shard_map/ppermute | solution.py:340
  73.7 45.8 %copy-start.10 = (f32[16]{0:T(128)S(1)}, f32[16]{0:T(128)}, u32[]{:S(2)}) copy-start(f32[16]{0:T(128)} %param.16) | copy-start | bytes 196
  73.7 45.9 %copy-start.1 = (f32[1024,400]{0,1:T(8,128)S(1)}, f32[1024,400]{0,1:T(8,128)}, u32[]{:S(2)}) copy-start(f32[1024,400]{0,1:T(8,128)} %param.11) | copy-start | bytes 4915204
  73.7 45.9 %copy-start.3 = (f32[1024]{0:T(1024)S(1)}, f32[1024]{0:T(1024)}, u32[]{:S(2)}) copy-start(f32[1024]{0:T(1024)} %param.13) | copy-start | bytes 12292
  73.7 17.0 %all-to-all-start.2 = ((bf16[8,102,128]{2,1,0:T(8,128)(2,1)}), bf16[8,102,128]{2,1,0:T(8,128)(2,1)S(1)}, u32[]{:S(2)}, u32[]{:S(2)}) async-start(bf16[8,102,128]{2,1,0:T(8,128)(2,1)} %add_convert_fusion), calls=%async_computation.2 | async-start | bytes 425984 | tf_op jit(solution)/shard_map/all_to_all | solution.py:344
  84.4 11.3 %collective-permute-start.4 = (bf16[8,102,128]{2,1,0:T(8,128)(2,1)S(1)}, bf16[8,102,128]{2,1,0:T(8,128)(2,1)S(1)}, u32[]{:S(2)}, u32[]{:S(2)}) collective-permute-start(bf16[8,102,128]{2,1,0:T(8,128)(2,1)S(1)} %add_convert_fusion.1.refs_2_), channel_id=1, source_target_pairs={{0,1},{1,2},{2,3},{3,0},{4,5},{5,6},{6,7},{7,4},{8,9},{9,10},{10,1... | collective-permute-start | bytes 626696 | tf_op jit(solution)/shard_map/ppermute | solution.py:340
  85.4 11.9 %collective-permute-start.5 = (bf16[8,102,128]{2,1,0:T(8,128)(2,1)S(1)}, bf16[8,102,128]{2,1,0:T(8,128)(2,1)S(1)}, u32[]{:S(2)}, u32[]{:S(2)}) collective-permute-start(bf16[8,102,128]{2,1,0:T(8,128)(2,1)S(1)} %add_convert_fusion.1.refs_2_), channel_id=1, source_target_pairs={{0,3},{1,0},{2,1},{3,2},{4,7},{5,4},{6,5},{7,6},{8,11},{9,8},{10,9... | collective-permute-start | bytes 626696 | tf_op jit(solution)/shard_map/ppermute | solution.py:340
  91.9 12.3 %all-to-all-start.3 = ((bf16[8,102,128]{2,1,0:T(8,128)(2,1)}), bf16[8,102,128]{2,1,0:T(8,128)(2,1)S(1)}, u32[]{:S(2)}, u32[]{:S(2)}) async-start(bf16[8,102,128]{2,1,0:T(8,128)(2,1)} %shard_map.135), calls=%async_computation.3 | async-start | bytes 425984 | tf_op jit(solution)/shard_map/all_to_all | solution.py:344
  95.7 7.7 %collective-permute-start.6 = (bf16[4,102,128]{2,1,0:T(8,128)(2,1)S(1)}, bf16[4,102,128]{2,1,0:T(8,128)(2,1)S(1)}, u32[]{:S(2)}, u32[]{:S(2)}) collective-permute-start(bf16[4,102,128]{2,1,0:T(8,128)(2,1)S(1)} %slice.54), channel_id=1, source_target_pairs={{0,1},{1,2},{2,3},{3,0},{4,5},{5,6},{6,7},{7,4},{8,9},{9,10},{10,1... | collective-permute-start | bytes 313352 | tf_op jit(solution)/shard_map/ppermute | solution.py:340
  97.3 6.8 %collective-permute-start.7 = (bf16[4,102,128]{2,1,0:T(8,128)(2,1)S(1)}, bf16[4,102,128]{2,1,0:T(8,128)(2,1)S(1)}, u32[]{:S(2)}, u32[]{:S(2)}) collective-permute-start(bf16[4,102,128]{2,1,0:T(8,128)(2,1)S(1)} %slice.55), channel_id=1, source_target_pairs={{0,3},{1,0},{2,1},{3,2},{4,7},{5,4},{6,5},{7,6},{8,11},{9,8},{10,9... | collective-permute-start | bytes 313352 | tf_op jit(solution)/shard_map/ppermute | solution.py:340
  104.2 9.9 %collective-permute-start.12 = (bf16[8,102,128]{2,1,0:T(8,128)(2,1)S(1)}, bf16[8,102,128]{2,1,0:T(8,128)(2,1)S(1)}, u32[]{:S(2)}, u32[]{:S(2)}) collective-permute-start(bf16[8,102,128]{2,1,0:T(8,128)(2,1)S(1)} %all-to-all-done.3.refs_4_), channel_id=1, source_target_pairs={{0,1},{1,2},{2,3},{3,0},{4,5},{5,6},{6,7},{7,4},{8,9},{9,10},{10,1... | collective-permute-start | bytes 626696 | tf_op jit(solution)/shard_map/ppermute | solution.py:340
  105.0 12.0 %collective-permute-start.13 = (bf16[8,102,128]{2,1,0:T(8,128)(2,1)S(1)}, bf16[8,102,128]{2,1,0:T(8,128)(2,1)S(1)}, u32[]{:S(2)}, u32[]{:S(2)}) collective-permute-start(bf16[8,102,128]{2,1,0:T(8,128)(2,1)S(1)} %all-to-all-done.3.refs_4_), channel_id=1, source_target_pairs={{0,3},{1,0},{2,1},{3,2},{4,7},{5,4},{6,5},{7,6},{8,11},{9,8},{10,9... | collective-permute-start | bytes 626696 | tf_op jit(solution)/shard_map/ppermute | solution.py:340
  114.1 7.5 %collective-permute-start.14 = (bf16[4,102,128]{2,1,0:T(8,128)(2,1)S(1)}, bf16[4,102,128]{2,1,0:T(8,128)(2,1)S(1)}, u32[]{:S(2)}, u32[]{:S(2)}) collective-permute-start(bf16[4,102,128]{2,1,0:T(8,128)(2,1)S(1)} %slice.58), channel_id=1, source_target_pairs={{0,1},{1,2},{2,3},{3,0},{4,5},{5,6},{6,7},{7,4},{8,9},{9,10},{10,1... | collective-permute-start | bytes 313352 | tf_op jit(solution)/shard_map/ppermute | solution.py:340
  117.6 5.4 %collective-permute-start.15 = (bf16[4,102,128]{2,1,0:T(8,128)(2,1)}, bf16[4,102,128]{2,1,0:T(8,128)(2,1)S(1)}, u32[]{:S(2)}, u32[]{:S(2)}) collective-permute-start(bf16[4,102,128]{2,1,0:T(8,128)(2,1)} %slice.59), channel_id=1, source_target_pairs={{0,3},{1,0},{2,1},{3,2},{4,7},{5,4},{6,5},{7,6},{8,11},{9,8},{10,9... | collective-permute-start | bytes 313352 | tf_op jit(solution)/shard_map/ppermute | solution.py:340
  119.6 3.4 %copy-start = (f32[1024,400]{0,1:T(8,128)S(1)}, f32[1024,400]{0,1:T(8,128)}, u32[]{:S(2)}) copy-start(f32[1024,400]{0,1:T(8,128)} %param.12) | copy-start | bytes 4915204
  119.6 3.4 %copy-start.4 = (f32[1024]{0:T(1024)S(1)}, f32[1024]{0:T(1024)}, u32[]{:S(2)}) copy-start(f32[1024]{0:T(1024)} %param.14) | copy-start | bytes 12292

commit v6 on v5

--- a/solution.py
+++ b/solution.py
@@ -194,7 +194,13 @@
         acc_ref[...] = jnp.zeros_like(acc_ref)
         rel_out_ref[...] = jnp.zeros_like(rel_out_ref)
 
-    @pl.when(is_live(meta_ref, step, steps, tid_ref.shape[2]))
+    live = is_live(meta_ref, step, steps, tid_ref.shape[2])
+
+    @pl.when(jnp.logical_not(live))
+    def _():
+        grad_ref[...] = jnp.zeros_like(grad_ref)
+
+    @pl.when(live)
     def _():
         ids = live_ids(tid_ref[0], meta_ref, step, steps)
         hot_ref[...] = one_hot(ids, table_ref.shape[1])
@@ -242,26 +248,21 @@
                             ].astype(out.dtype)
 
 
-def source_kernel(steps, lanes, meta_ref, hid_ref, grad_ref, *refs):
+def source_kernel(lanes, meta_ref, hid_ref, grad_ref, *refs):
     outs, acc_ref = refs[:-1], refs[-1]
-    step = pl.program_id(0)
-
-    @pl.when(step == 0)
-    def _():
-        acc_ref[...] = jnp.zeros_like(acc_ref)
-
-    @pl.when(is_live(meta_ref, step, steps, hid_ref.shape[2]))
-    def _():
-        ids = live_ids(hid_ref[0], meta_ref, step, steps)
-        acc_ref[...] += dot_nt(grad_ref[0], one_hot(ids, acc_ref.shape[1]))
-
-    @pl.when(step == steps - 1)
-    def _():
-        emit(lanes, meta_ref[1], acc_ref, outs)
-        block = acc_ref.shape[0] // lanes
-        for out in outs:
-            if out.shape[1] > block:
-                out[:, block:] = jnp.zeros((out.shape[0], out.shape[1] - block, out.shape[2]), out.dtype)
+    steps, rows = grad_ref.shape[0], acc_ref.shape[1]
+    part = 256 if rows % 256 == 0 else rows
+    ids = [live_ids(hid_ref[step], meta_ref, step, steps) for step in range(steps)]
+    for first in range(0, rows, part):
+        total = 0.0
+        for step in range(steps):
+            total += dot_nt(grad_ref[step], one_hot(ids[step] - first, part))
+        acc_ref[:, first : first + part] = total
+    emit(lanes, meta_ref[1], acc_ref, outs)
+    block = acc_ref.shape[0] // lanes
+    for out in outs:
+        if out.shape[1] > block:
+            out[:, block:] = jnp.zeros((out.shape[0], out.shape[1] - block, out.shape[2]), out.dtype)
 
 
 def pick_kernel(plan_ref, in_ref, out_ref):
@@ -471,11 +472,10 @@
     )(meta, tid, rid, relation, edges, fetched)
 
     source_out = pl.pallas_call(
-        functools.partial(source_kernel, steps, lanes),
-        grid=(steps,),
+        functools.partial(source_kernel, lanes),
         out_shape=bundle_outs,
-        in_specs=[SMEM_SPEC, per_span(hid.shape), per_span(edge_shape)],
-        out_specs=[whole(out.shape) for out in bundle_outs],
+        in_specs=[SMEM_SPEC, VMEM_SPEC, VMEM_SPEC],
+        out_specs=[VMEM_SPEC] * len(bundle_outs),
         scratch_shapes=[pltpu.VMEM((features, rows), F32)],
         compiler_params=params(24),
         cost_estimate=cost(4 * steps * features * rows * E_CH, 8 * features * steps * E_CH),

time: 126 us -> 127 us (level)
  starting transfers between devices: 46.1 us -> 37.4 us
  Pallas kernels: 26.7 us -> 34.6 us
    all_to_all x3, starting transfers between devices: 17.9 us -> 10.5 us  [swap_buckets(): return lax.all_to_all(x, 'bucket', split_axis=0, concat_axis=0, tiled=True)]
    pallas_call x1, Pallas kernels: 11.1 us -> 17.1 us  [per_device(): pl.pallas_call(functools.partial(main_kernel, steps, lanes, packed), grid...]
    ppermute x16, waiting for transfers between devices: 20.2 us -> 22.9 us  [shift_span(): lax.ppermute(x, 'span', [(i, (i + by) % count) for i in range(count)])]
    all_to_all x3, waiting for transfers between devices: 8.49 us -> 6.99 us  [swap_buckets(): return lax.all_to_all(x, 'bucket', split_axis=0, concat_axis=0, tiled=True)]
  transfers between devices with their start and end apart: 19 -> 19, of which waited for: 10 -> 12; matrix products, arithmetic and copies ran while one was open for 3% -> 3% of each run, Pallas kernels for 9% -> 11%
where the time goes in v6:
time: 127 us; the launch traced here: 126 us
  starting transfers between devices  37.4 us (29%)
  Pallas kernels  34.6 us (27%)
  waiting for transfers between devices  29.9 us (24%)
  blocking collectives  17.9 us (14%)
  other arithmetic  3.87 us (3%)
  between operations  1.55 us (1%)
    ppermute x16, starting transfers between devices, shift_span(): lax.ppermute(x, 'span', [(i, (i + by) % count) for i in range(count)])  26.9 us
    ppermute x16, waiting for transfers between devices, shift_span(): lax.ppermute(x, 'span', [(i, (i + by) % count) for i in range(count)])  22.9 us
    all_to_all x1, blocking collectives, swap_buckets(): return lax.all_to_all(x, 'bucket', split_axis=0, concat_axis=0, tiled=True)  17.9 us
    pallas_call x1, Pallas kernels, per_device(): pl.pallas_call(functools.partial(main_kernel, steps, lanes, packed), grid...  17.1 us
    all_to_all x3, starting transfers between devices, swap_buckets(): return lax.all_to_all(x, 'bucket', split_axis=0, concat_axis=0, tiled=True)  10.5 us
    all_to_all x3, waiting for transfers between devices, swap_buckets(): return lax.all_to_all(x, 'bucket', split_axis=0, concat_axis=0, tiled=True)  6.99 us
    pallas_call x1, Pallas kernels, per_device(): pl.pallas_call(functools.partial(prep_kernel, steps), grid=(steps,), out_...  6.67 us
    pallas_call x2, Pallas kernels, update(): pl.pallas_call(functools.partial(update_kernel, lanes, joined), out_shape...  4.7 us
  transfers between devices with their start and end apart: 19, of which 12 were waited for; matrix products, arithmetic and copies ran while one was open for 3% of the time, Pallas kernels for 11%

profile of v6, /device:TPU:0, one launch (start us, length us, event | category | flops | bytes accessed | tf_op | source)
XLA Modules:
  0.0 126.0 jit_solution(6862036599279804378)
XLA Ops:
  0.6 1.5 %bitcast_bitcast_fusion = bf16[8,400,128]{2,1,0:T(8,128)(2,1)S(1)} fusion(f32[1024,400]{0,1:T(8,128)} %param.12), kind=kLoop, calls=%fused_computation | loop fusion | flops 409600 | bytes 2457600 | tf_op jit(solution)/shard_map/transpose | solution.py:410
  2.2 17.9 %all_to_all.20.in_ref = bf16[8,400,128]{2,1,0:T(8,128)(2,1)S(1)} all-to-all(bf16[8,400,128]{2,1,0:T(8,128)(2,1)S(1)} %bitcast_bitcast_fusion), channel_id=1, replica_groups=mesh['bucket'=8,'span'=4] {'bucket'}, dimensions={0} | all-to-all | bytes 1638400 | tf_op jit(solution)/shard_map/all_to_all | solution.py:345
  20.1 1.5 %shard_map.131 = bf16[8,400,128]{2,1,0:T(8,128)(2,1)} custom-call(s32[8]{0:T(128)S(1)} %copy-done.5, bf16[8,400,128]{2,1,0:T(8,128)(2,1)S(1)} %all_to_all.20.in_ref), custom_call_target="tpu_custom_call" | custom-call | tf_op jit(solution)/shard_map/pallas_call | solution.py:413
  21.6 3.5 %all-to-all-start.1 = ((bf16[8,400,128]{2,1,0:T(8,128)(2,1)}), bf16[8,400,128]{2,1,0:T(8,128)(2,1)S(1)}, u32[]{:S(2)}, u32[]{:S(2)}) async-start(bf16[8,400,128]{2,1,0:T(8,128)(2,1)} %shard_map.131), calls=%async_computation.1 | async-start | bytes 1638400 | tf_op jit(solution)/shard_map/all_to_all | solution.py:345
  25.8 0.6 pad_add_fusion.meta_ref
  26.4 6.7 %shard_map.130.edge_ref = bf16[4,2,400,640]{3,2,1,0:T(8,128)(2,1)} custom-call(s32[2]{0:T(128)} %pad_add_fusion.meta_ref, s32[4,1,640]{2,1,0:T(1,128)} %bitcast.28, s32[4,1,640]{2,1,0:T(1,128)} %bitcast.26, f32[400,1024]{1,0:T(8,128)} %bitcast.21, f32[16,400]{1,0:T(8,128)} %refs_2_.1), custom_call_target="tpu_custom_call" | custom-call | flops 4194304000 | bytes 8192000 | tf_op jit(solution)/shard_map/pallas_call | solution.py:428
  33.0 5.0 %all-to-all-done.1.parts_ref = bf16[8,400,128]{2,1,0:T(8,128)(2,1)S(1)} async-done(((bf16[8,400,128]{2,1,0:T(8,128)(2,1)}), bf16[8,400,128]{2,1,0:T(8,128)(2,1)S(1)}, u32[]{:S(2)}, u32[]{:S(2)}) %all-to-all-start.1) | async-done | bytes 819232 | tf_op jit(solution)/shard_map/all_to_all | solution.py:345
  38.0 0.0 copy-start.9
  38.0 17.1 %shard_map.132 = (bf16[4,400,640]{2,1,0:T(8,128)(2,1)S(1)}, f32[400,16]{1,0:T(8,128)}, f32[8,102,128]{2,1,0:T(8,128)S(1)}, f32[8,102,128]{2,1,0:T(8,128)S(1)}, f...) custom-call(s32[2]{0:T(128)S(1)} %copy-done.6, ...), custom_call_target="tpu_custom_call" | custom-call | flops 12582912000 | bytes 8192000 | tf_op jit(solution)/shard_map/pallas_call | solution.py:446
  55.1 1.6 %collective-permute-start.8 = (bf16[4,102,128]{2,1,0:T(8,128)(2,1)S(1)}, bf16[4,102,128]{2,1,0:T(8,128)(2,1)S(1)}, u32[]{:S(2)}, u32[]{:S(2)}) collective-permute-start(bf16[4,102,128]{2,1,0:T(8,128)(2,1)S(1)} %get-tuple-element.28), channel_id=1, source_target_pairs={{0,1},{1,2},{2,3},{3,0},{4,5},{5,6},{6,7},{7,4},{8,9},{9,10},{10,1... | collective-permute-start | bytes 313352 | tf_op jit(solution)/shard_map/ppermute | solution.py:341
  56.7 2.2 %collective-permute-start.9 = (bf16[4,102,128]{2,1,0:T(8,128)(2,1)S(1)}, bf16[4,102,128]{2,1,0:T(8,128)(2,1)S(1)}, u32[]{:S(2)}, u32[]{:S(2)}) collective-permute-start(bf16[4,102,128]{2,1,0:T(8,128)(2,1)S(1)} %get-tuple-element.29), channel_id=1, source_target_pairs={{0,3},{1,0},{2,1},{3,2},{4,7},{5,4},{6,5},{7,6},{8,11},{9,8},{10,9... | collective-permute-start | bytes 313352 | tf_op jit(solution)/shard_map/ppermute | solution.py:341
  58.9 3.4 %shard_map.133 = (f32[8,102,128]{2,1,0:T(8,128)S(1)}, f32[8,102,128]{2,1,0:T(8,128)S(1)}, f32[8,102,128]{2,1,0:T(8,128)S(1)}, bf16[4,102,128]{2,1,0:T(8,128)(2,1)S(1)}, bf16[4,102,128]{2,1,0:T(8,128)(2,1)S(1)}) custom-call(s32[2]{0:T(128)S(1)} %copy-done.6, s32[4,1,640]{2,1,0:T(1,128)S(1)} %bitcast.29, bf16[4,400,640]{2,1,0:T(8,128)(2,1)S(1)} %get-tuple-element.20.grad_ref), custom_call_target="tpu_custom_call" | custom-call | flops 4194304000 | bytes 8192000 | tf_op jit(solution)/shard_map/pallas_call | solution.py:474
  62.4 0.1 collective-permute-start
  62.5 3.9 %collective-permute-start.2 = (bf16[4,102,128]{2,1,0:T(8,128)(2,1)S(1)}, bf16[4,102,128]{2,1,0:T(8,128)(2,1)S(1)}, u32[]{:S(2)}, u32[]{:S(2)}) collective-permute-start(bf16[4,102,128]{2,1,0:T(8,128)(2,1)S(1)} %get-tuple-element.25), channel_id=1, source_target_pairs={{0,3},{1,0},{2,1},{3,2},{4,7},{5,4},{6,5},{7,6},{8,11},{9,8},{10,9... | collective-permute-start | bytes 313352 | tf_op jit(solution)/shard_map/ppermute | solution.py:341
  66.3 0.0 collective-permute-done.9
  66.4 0.1 collective-permute-start.10
  66.6 3.9 %collective-permute-start.11 = (bf16[8,102,128]{2,1,0:T(8,128)(2,1)S(1)}, bf16[8,102,128]{2,1,0:T(8,128)(2,1)S(1)}, u32[]{:S(2)}, u32[]{:S(2)}) collective-permute-start(bf16[8,102,128]{2,1,0:T(8,128)(2,1)S(1)} %pad_maximum_fusion.3), channel_id=1, source_target_pairs={{0,3},{1,0},{2,1},{3,2},{4,7},{5,4},{6,5},{7,6},{8,11},{9,8},{10,9... | collective-permute-start | bytes 626696 | tf_op jit(solution)/shard_map/ppermute | solution.py:341
  70.5 0.1 collective-permute-start.1
  70.6 1.2 collective-permute-done.2
  71.8 0.7 pad_maximum_fusion.1
  72.5 2.6 %collective-permute-start.3 = (bf16[8,102,128]{2,1,0:T(8,128)(2,1)}, bf16[8,102,128]{2,1,0:T(8,128)(2,1)S(1)}, u32[]{:S(2)}, u32[]{:S(2)}) collective-permute-start(bf16[8,102,128]{2,1,0:T(8,128)(2,1)} %pad_maximum_fusion.1), channel_id=1, source_target_pairs={{0,3},{1,0},{2,1},{3,2},{4,7},{5,4},{6,5},{7,6},{8,11},{9,8},{10,9... | collective-permute-start | bytes 626696 | tf_op jit(solution)/shard_map/ppermute | solution.py:341
  75.1 2.0 %collective-permute-done.10 = bf16[8,102,128]{2,1,0:T(8,128)(2,1)S(1)} collective-permute-done((bf16[8,102,128]{2,1,0:T(8,128)(2,1)S(1)}, bf16[8,102,128]{2,1,0:T(8,128)(2,1)S(1)}, u32[]{:S(2)}, u32[]{:S(2)}) %collective-permute-start.10) | collective-permute-done | bytes 208928 | tf_op jit(solution)/shard_map/ppermute | solution.py:341
  77.1 3.8 %collective-permute-done.11 = bf16[8,102,128]{2,1,0:T(8,128)(2,1)S(1)} collective-permute-done((bf16[8,102,128]{2,1,0:T(8,128)(2,1)S(1)}, bf16[8,102,128]{2,1,0:T(8,128)(2,1)S(1)}, u32[]{:S(2)}, u32[]{:S(2)}) %collective-permute-start.11) | collective-permute-done | bytes 208928 | tf_op jit(solution)/shard_map/ppermute | solution.py:341
  80.9 0.8 add_convert_fusion
  81.7 3.5 %all-to-all-start.2 = ((bf16[8,102,128]{2,1,0:T(8,128)(2,1)}), bf16[8,102,128]{2,1,0:T(8,128)(2,1)S(1)}, u32[]{:S(2)}, u32[]{:S(2)}) async-start(bf16[8,102,128]{2,1,0:T(8,128)(2,1)} %add_convert_fusion), calls=%async_computation.2 | async-start | bytes 425984 | tf_op jit(solution)/shard_map/all_to_all | solution.py:345
  85.2 0.4 collective-permute-done.3
  85.6 0.1 add_convert_fusion.1.refs_2_
  85.7 0.1 collective-permute-start.4
  85.7 3.8 %collective-permute-start.5 = (bf16[8,102,128]{2,1,0:T(8,128)(2,1)S(1)}, bf16[8,102,128]{2,1,0:T(8,128)(2,1)S(1)}, u32[]{:S(2)}, u32[]{:S(2)}) collective-permute-start(bf16[8,102,128]{2,1,0:T(8,128)(2,1)S(1)} %add_convert_fusion.1.refs_2_), channel_id=1, source_target_pairs={{0,3},{1,0},{2,1},{3,2},{4,7},{5,4},{6,5},{7,6},{8,11},{9,8},{10,9... | collective-permute-start | bytes 626696 | tf_op jit(solution)/shard_map/ppermute | solution.py:341
  89.5 2.0 %all-to-all-done.2.in_ref = bf16[8,102,128]{2,1,0:T(8,128)(2,1)S(1)} async-done(((bf16[8,102,128]{2,1,0:T(8,128)(2,1)}), bf16[8,102,128]{2,1,0:T(8,128)(2,1)S(1)}, u32[]{:S(2)}, u32[]{:S(2)}) %all-to-all-start.2) | async-done | bytes 208928 | tf_op jit(solution)/shard_map/all_to_all | solution.py:345
  91.6 1.2 shard_map.135
  92.8 3.4 %all-to-all-start.3 = ((bf16[8,102,128]{2,1,0:T(8,128)(2,1)}), bf16[8,102,128]{2,1,0:T(8,128)(2,1)S(1)}, u32[]{:S(2)}, u32[]{:S(2)}) async-start(bf16[8,102,128]{2,1,0:T(8,128)(2,1)} %shard_map.135), calls=%async_computation.3 | async-start | bytes 425984 | tf_op jit(solution)/shard_map/all_to_all | solution.py:345
  96.2 0.1 collective-permute-start.6
  96.3 1.2 collective-permute-done.5.refs_4_
  97.6 2.6 %collective-permute-start.7 = (bf16[4,102,128]{2,1,0:T(8,128)(2,1)S(1)}, bf16[4,102,128]{2,1,0:T(8,128)(2,1)S(1)}, u32[]{:S(2)}, u32[]{:S(2)}) collective-permute-start(bf16[4,102,128]{2,1,0:T(8,128)(2,1)S(1)} %slice.55), channel_id=1, source_target_pairs={{0,3},{1,0},{2,1},{3,2},{4,7},{5,4},{6,5},{7,6},{8,11},{9,8},{10,9... | collective-permute-start | bytes 313352 | tf_op jit(solution)/shard_map/ppermute | solution.py:341
  100.2 3.7 %collective-permute-done.6.refs_5_ = bf16[4,102,128]{2,1,0:T(8,128)(2,1)S(1)} collective-permute-done((bf16[4,102,128]{2,1,0:T(8,128)(2,1)S(1)}, bf16[4,102,128]{2,1,0:T(8,128)(2,1)S(1)}, u32[]{:S(2)}, u32[]{:S(2)}) %collective-permute-start.6) | collective-permute-done | bytes 104480 | tf_op jit(solution)/shard_map/ppermute | solution.py:341
  104.0 0.6 collective-permute-done.7.refs_6_
  104.6 0.9 collective-permute-start.12
  105.5 3.0 %collective-permute-start.13 = (bf16[8,102,128]{2,1,0:T(8,128)(2,1)S(1)}, bf16[8,102,128]{2,1,0:T(8,128)(2,1)S(1)}, u32[]{:S(2)}, u32[]{:S(2)}) collective-permute-start(bf16[8,102,128]{2,1,0:T(8,128)(2,1)S(1)} %all-to-all-done.3.refs_4_), channel_id=1, source_target_pairs={{0,3},{1,0},{2,1},{3,2},{4,7},{5,4},{6,5},{7,6},{8,11},{9,8},{10,9... | collective-permute-start | bytes 626696 | tf_op jit(solution)/shard_map/ppermute | solution.py:341
  108.4 6.0 %collective-permute-done.12.refs_5_ = bf16[8,102,128]{2,1,0:T(8,128)(2,1)S(1)} collective-permute-done((bf16[8,102,128]{2,1,0:T(8,128)(2,1)S(1)}, bf16[8,102,128]{2,1,0:T(8,128)(2,1)S(1)}, u32[]{:S(2)}, u32[]{:S(2)}) %collective-permute-start.12) | collective-permute-done | bytes 208928 | tf_op jit(solution)/shard_map/ppermute | solution.py:341
  114.4 0.1 collective-permute-start.14
  114.5 2.8 %collective-permute-done.13.refs_6_ = bf16[8,102,128]{2,1,0:T(8,128)(2,1)S(1)} collective-permute-done((bf16[8,102,128]{2,1,0:T(8,128)(2,1)S(1)}, bf16[8,102,128]{2,1,0:T(8,128)(2,1)S(1)}, u32[]{:S(2)}, u32[]{:S(2)}) %collective-permute-start.13) | collective-permute-done | bytes 208928 | tf_op jit(solution)/shard_map/ppermute | solution.py:341
  117.2 0.7 slice.59
  117.9 2.1 %collective-permute-start.15 = (bf16[4,102,128]{2,1,0:T(8,128)(2,1)}, bf16[4,102,128]{2,1,0:T(8,128)(2,1)S(1)}, u32[]{:S(2)}, u32[]{:S(2)}) collective-permute-start(bf16[4,102,128]{2,1,0:T(8,128)(2,1)} %slice.59), channel_id=1, source_target_pairs={{0,3},{1,0},{2,1},{3,2},{4,7},{5,4},{6,5},{7,6},{8,11},{9,8},{10,9... | collective-permute-start | bytes 313352 | tf_op jit(solution)/shard_map/ppermute | solution.py:341
  120.0 0.1 copy.15.refs_3_
  120.1 2.0 %shard_map.134 = f32[400,1024]{1,0:T(8,128)} custom-call(s32[2]{0:T(128)S(1)} %copy-done.6, f32[400,1024]{1,0:T(8,128)S(1)} %bitcast.22, f32[1,1024]{1,0:T(1,128)S(1)} %bitcast.23, bf16[8,102,128]{2,1,0:T(8,128)(2,1)S(1)} %add_convert_fusion.1.refs_2_, bf16[8,102,128]{2,1,0:T(8,128)(2,1)S(1)} %collective-permute-done.4.refs_3_, ...), custom_call_target="tpu_custom_call" | custom-call | tf_op jit(solution)/shard_map/pallas_call | solution.py:358
  122.2 1.1 collective-permute-done.15.refs_8_
  123.3 2.7 %shard_map.136 = (f32[400,1024]{1,0:T(8,128)}, f32[16,400]{1,0:T(8,128)}) custom-call(s32[2]{0:T(128)S(1)} %copy-done.6, f32[400,1024]{1,0:T(8,128)S(1)} %bitcast.20, f32[1,1024]{1,0:T(1,128)S(1)} %bitcast.24, f32[16,400]{1,0:T(8,128)S(1)} %copy-done.2, f32[16,1]{1,0:T(8,128)S(1)} %copy.15.refs_3_, bf16[8,102,128]{2,1,0:T(8,128)(2,1)S(1)} %all-to-all-done.3.refs_4_, ...), custom_call_target="tpu_custom_call" | custom-call | tf_op jit(solution)/shard_map/pallas_call | solution.py:358
  (41 shorter events, 0.3 us)
Async XLA Ops:
  0.6 19.4 %copy-start.5 = (s32[8]{0:T(128)S(1)}, s32[8]{0:T(128)}, u32[]{:S(2)}) copy-start(s32[8]{0:T(128)} %plan_ref.3) | copy-start | bytes 100
  21.6 16.4 %all-to-all-start.1 = ((bf16[8,400,128]{2,1,0:T(8,128)(2,1)}), bf16[8,400,128]{2,1,0:T(8,128)(2,1)S(1)}, u32[]{:S(2)}, u32[]{:S(2)}) async-start(bf16[8,400,128]{2,1,0:T(8,128)(2,1)} %shard_map.131), calls=%async_computation.1 | async-start | bytes 1638400 | tf_op jit(solution)/shard_map/all_to_all | solution.py:345
  26.3 11.6 %copy-start.2 = (f32[16,400]{1,0:T(8,128)S(1)}, f32[16,400]{1,0:T(8,128)}, u32[]{:S(2)}) copy-start(f32[16,400]{1,0:T(8,128)} %refs_2_.1) | copy-start | bytes 76804
  26.3 11.6 %copy-start.6 = (s32[2]{0:T(128)S(1)}, s32[2]{0:T(128)}, u32[]{:S(2)}) copy-start(s32[2]{0:T(128)} %pad_add_fusion.meta_ref) | copy-start | bytes 28
  26.3 11.6 %copy-start.7 = (s32[1,2560]{1,0:T(1,128)S(1)}, s32[1,2560]{1,0:T(1,128)}, u32[]{:S(2)}) copy-start(s32[1,2560]{1,0:T(1,128)} %param.19) | copy-start | bytes 30724
  26.4 11.7 %copy-start.8 = (s32[1,2560]{1,0:T(1,128)S(1)}, s32[1,2560]{1,0:T(1,128)}, u32[]{:S(2)}) copy-start(s32[1,2560]{1,0:T(1,128)} %param.20) | copy-start | bytes 30724
  38.0 20.9 %copy-start.9 = (s32[1,2560]{1,0:T(1,128)S(1)}, s32[1,2560]{1,0:T(1,128)}, u32[]{:S(2)}) copy-start(s32[1,2560]{1,0:T(1,128)} %param.18) | copy-start | bytes 30724
  55.1 11.2 %collective-permute-start.8 = (bf16[4,102,128]{2,1,0:T(8,128)(2,1)S(1)}, bf16[4,102,128]{2,1,0:T(8,128)(2,1)S(1)}, u32[]{:S(2)}, u32[]{:S(2)}) collective-permute-start(bf16[4,102,128]{2,1,0:T(8,128)(2,1)S(1)} %get-tuple-element.28), channel_id=1, source_target_pairs={{0,1},{1,2},{2,3},{3,0},{4,5},{5,6},{6,7},{7,4},{8,9},{9,10},{10,1... | collective-permute-start | bytes 313352 | tf_op jit(solution)/shard_map/ppermute | solution.py:341
  56.7 9.6 %collective-permute-start.9 = (bf16[4,102,128]{2,1,0:T(8,128)(2,1)S(1)}, bf16[4,102,128]{2,1,0:T(8,128)(2,1)S(1)}, u32[]{:S(2)}, u32[]{:S(2)}) collective-permute-start(bf16[4,102,128]{2,1,0:T(8,128)(2,1)S(1)} %get-tuple-element.29), channel_id=1, source_target_pairs={{0,3},{1,0},{2,1},{3,2},{4,7},{5,4},{6,5},{7,6},{8,11},{9,8},{10,9... | collective-permute-start | bytes 313352 | tf_op jit(solution)/shard_map/ppermute | solution.py:341
  62.4 8.1 %collective-permute-start = (bf16[4,102,128]{2,1,0:T(8,128)(2,1)S(1)}, bf16[4,102,128]{2,1,0:T(8,128)(2,1)S(1)}, u32[]{:S(2)}, u32[]{:S(2)}) collective-permute-start(bf16[4,102,128]{2,1,0:T(8,128)(2,1)S(1)} %get-tuple-element.23), channel_id=1, source_target_pairs={{0,1},{1,2},{2,3},{3,0},{4,5},{5,6},{6,7},{7,4},{8,9},{9,10},{10,1... | collective-permute-start | bytes 313352 | tf_op jit(solution)/shard_map/ppermute | solution.py:341
  62.5 9.3 %collective-permute-start.2 = (bf16[4,102,128]{2,1,0:T(8,128)(2,1)S(1)}, bf16[4,102,128]{2,1,0:T(8,128)(2,1)S(1)}, u32[]{:S(2)}, u32[]{:S(2)}) collective-permute-start(bf16[4,102,128]{2,1,0:T(8,128)(2,1)S(1)} %get-tuple-element.25), channel_id=1, source_target_pairs={{0,3},{1,0},{2,1},{3,2},{4,7},{5,4},{6,5},{7,6},{8,11},{9,8},{10,9... | collective-permute-start | bytes 313352 | tf_op jit(solution)/shard_map/ppermute | solution.py:341
  66.4 10.6 %collective-permute-start.10 = (bf16[8,102,128]{2,1,0:T(8,128)(2,1)S(1)}, bf16[8,102,128]{2,1,0:T(8,128)(2,1)S(1)}, u32[]{:S(2)}, u32[]{:S(2)}) collective-permute-start(bf16[8,102,128]{2,1,0:T(8,128)(2,1)S(1)} %pad_maximum_fusion.2), channel_id=1, source_target_pairs={{0,1},{1,2},{2,3},{3,0},{4,5},{5,6},{6,7},{7,4},{8,9},{9,10},{10,1... | collective-permute-start | bytes 626696 | tf_op jit(solution)/shard_map/ppermute | solution.py:341
  66.6 14.4 %collective-permute-start.11 = (bf16[8,102,128]{2,1,0:T(8,128)(2,1)S(1)}, bf16[8,102,128]{2,1,0:T(8,128)(2,1)S(1)}, u32[]{:S(2)}, u32[]{:S(2)}) collective-permute-start(bf16[8,102,128]{2,1,0:T(8,128)(2,1)S(1)} %pad_maximum_fusion.3), channel_id=1, source_target_pairs={{0,3},{1,0},{2,1},{3,2},{4,7},{5,4},{6,5},{7,6},{8,11},{9,8},{10,9... | collective-permute-start | bytes 626696 | tf_op jit(solution)/shard_map/ppermute | solution.py:341
  70.5 14.7 %collective-permute-start.1 = (bf16[8,102,128]{2,1,0:T(8,128)(2,1)S(1)}, bf16[8,102,128]{2,1,0:T(8,128)(2,1)S(1)}, u32[]{:S(2)}, u32[]{:S(2)}) collective-permute-start(bf16[8,102,128]{2,1,0:T(8,128)(2,1)S(1)} %pad_maximum_fusion), channel_id=1, source_target_pairs={{0,1},{1,2},{2,3},{3,0},{4,5},{5,6},{6,7},{7,4},{8,9},{9,10},{10,1... | collective-permute-start | bytes 626696 | tf_op jit(solution)/shard_map/ppermute | solution.py:341
  72.5 13.1 %collective-permute-start.3 = (bf16[8,102,128]{2,1,0:T(8,128)(2,1)}, bf16[8,102,128]{2,1,0:T(8,128)(2,1)S(1)}, u32[]{:S(2)}, u32[]{:S(2)}) collective-permute-start(bf16[8,102,128]{2,1,0:T(8,128)(2,1)} %pad_maximum_fusion.1), channel_id=1, source_target_pairs={{0,3},{1,0},{2,1},{3,2},{4,7},{5,4},{6,5},{7,6},{8,11},{9,8},{10,9... | collective-permute-start | bytes 626696 | tf_op jit(solution)/shard_map/ppermute | solution.py:341
  81.7 38.3 %copy-start.10 = (f32[16]{0:T(128)S(1)}, f32[16]{0:T(128)}, u32[]{:S(2)}) copy-start(f32[16]{0:T(128)} %param.16) | copy-start | bytes 196
  81.7 38.4 %copy-start.1 = (f32[1024,400]{0,1:T(8,128)S(1)}, f32[1024,400]{0,1:T(8,128)}, u32[]{:S(2)}) copy-start(f32[1024,400]{0,1:T(8,128)} %param.11) | copy-start | bytes 4915204
  81.7 38.4 %copy-start.3 = (f32[1024]{0:T(1024)S(1)}, f32[1024]{0:T(1024)}, u32[]{:S(2)}) copy-start(f32[1024]{0:T(1024)} %param.13) | copy-start | bytes 12292
  81.7 9.9 %all-to-all-start.2 = ((bf16[8,102,128]{2,1,0:T(8,128)(2,1)}), bf16[8,102,128]{2,1,0:T(8,128)(2,1)S(1)}, u32[]{:S(2)}, u32[]{:S(2)}) async-start(bf16[8,102,128]{2,1,0:T(8,128)(2,1)} %add_convert_fusion), calls=%async_computation.2 | async-start | bytes 425984 | tf_op jit(solution)/shard_map/all_to_all | solution.py:345
  85.7 10.6 %collective-permute-start.4 = (bf16[8,102,128]{2,1,0:T(8,128)(2,1)S(1)}, bf16[8,102,128]{2,1,0:T(8,128)(2,1)S(1)}, u32[]{:S(2)}, u32[]{:S(2)}) collective-permute-start(bf16[8,102,128]{2,1,0:T(8,128)(2,1)S(1)} %add_convert_fusion.1.refs_2_), channel_id=1, source_target_pairs={{0,1},{1,2},{2,3},{3,0},{4,5},{5,6},{6,7},{7,4},{8,9},{9,10},{10,1... | collective-permute-start | bytes 626696 | tf_op jit(solution)/shard_map/ppermute | solution.py:341
  85.7 11.8 %collective-permute-start.5 = (bf16[8,102,128]{2,1,0:T(8,128)(2,1)S(1)}, bf16[8,102,128]{2,1,0:T(8,128)(2,1)S(1)}, u32[]{:S(2)}, u32[]{:S(2)}) collective-permute-start(bf16[8,102,128]{2,1,0:T(8,128)(2,1)S(1)} %add_convert_fusion.1.refs_2_), channel_id=1, source_target_pairs={{0,3},{1,0},{2,1},{3,2},{4,7},{5,4},{6,5},{7,6},{8,11},{9,8},{10,9... | collective-permute-start | bytes 626696 | tf_op jit(solution)/shard_map/ppermute | solution.py:341
  92.8 11.8 %all-to-all-start.3 = ((bf16[8,102,128]{2,1,0:T(8,128)(2,1)}), bf16[8,102,128]{2,1,0:T(8,128)(2,1)S(1)}, u32[]{:S(2)}, u32[]{:S(2)}) async-start(bf16[8,102,128]{2,1,0:T(8,128)(2,1)} %shard_map.135), calls=%async_computation.3 | async-start | bytes 425984 | tf_op jit(solution)/shard_map/all_to_all | solution.py:345
  96.2 7.7 %collective-permute-start.6 = (bf16[4,102,128]{2,1,0:T(8,128)(2,1)S(1)}, bf16[4,102,128]{2,1,0:T(8,128)(2,1)S(1)}, u32[]{:S(2)}, u32[]{:S(2)}) collective-permute-start(bf16[4,102,128]{2,1,0:T(8,128)(2,1)S(1)} %slice.54), channel_id=1, source_target_pairs={{0,1},{1,2},{2,3},{3,0},{4,5},{5,6},{6,7},{7,4},{8,9},{9,10},{10,1... | collective-permute-start | bytes 313352 | tf_op jit(solution)/shard_map/ppermute | solution.py:341
  97.6 7.0 %collective-permute-start.7 = (bf16[4,102,128]{2,1,0:T(8,128)(2,1)S(1)}, bf16[4,102,128]{2,1,0:T(8,128)(2,1)S(1)}, u32[]{:S(2)}, u32[]{:S(2)}) collective-permute-start(bf16[4,102,128]{2,1,0:T(8,128)(2,1)S(1)} %slice.55), channel_id=1, source_target_pairs={{0,3},{1,0},{2,1},{3,2},{4,7},{5,4},{6,5},{7,6},{8,11},{9,8},{10,9... | collective-permute-start | bytes 313352 | tf_op jit(solution)/shard_map/ppermute | solution.py:341
  104.6 9.8 %collective-permute-start.12 = (bf16[8,102,128]{2,1,0:T(8,128)(2,1)S(1)}, bf16[8,102,128]{2,1,0:T(8,128)(2,1)S(1)}, u32[]{:S(2)}, u32[]{:S(2)}) collective-permute-start(bf16[8,102,128]{2,1,0:T(8,128)(2,1)S(1)} %all-to-all-done.3.refs_4_), channel_id=1, source_target_pairs={{0,1},{1,2},{2,3},{3,0},{4,5},{5,6},{6,7},{7,4},{8,9},{9,10},{10,1... | collective-permute-start | bytes 626696 | tf_op jit(solution)/shard_map/ppermute | solution.py:341
  105.5 11.8 %collective-permute-start.13 = (bf16[8,102,128]{2,1,0:T(8,128)(2,1)S(1)}, bf16[8,102,128]{2,1,0:T(8,128)(2,1)S(1)}, u32[]{:S(2)}, u32[]{:S(2)}) collective-permute-start(bf16[8,102,128]{2,1,0:T(8,128)(2,1)S(1)} %all-to-all-done.3.refs_4_), channel_id=1, source_target_pairs={{0,3},{1,0},{2,1},{3,2},{4,7},{5,4},{6,5},{7,6},{8,11},{9,8},{10,9... | collective-permute-start | bytes 626696 | tf_op jit(solution)/shard_map/ppermute | solution.py:341
  114.4 7.8 %collective-permute-start.14 = (bf16[4,102,128]{2,1,0:T(8,128)(2,1)S(1)}, bf16[4,102,128]{2,1,0:T(8,128)(2,1)S(1)}, u32[]{:S(2)}, u32[]{:S(2)}) collective-permute-start(bf16[4,102,128]{2,1,0:T(8,128)(2,1)S(1)} %slice.58), channel_id=1, source_target_pairs={{0,1},{1,2},{2,3},{3,0},{4,5},{5,6},{6,7},{7,4},{8,9},{9,10},{10,1... | collective-permute-start | bytes 313352 | tf_op jit(solution)/shard_map/ppermute | solution.py:341
  117.9 5.4 %collective-permute-start.15 = (bf16[4,102,128]{2,1,0:T(8,128)(2,1)}, bf16[4,102,128]{2,1,0:T(8,128)(2,1)S(1)}, u32[]{:S(2)}, u32[]{:S(2)}) collective-permute-start(bf16[4,102,128]{2,1,0:T(8,128)(2,1)} %slice.59), channel_id=1, source_target_pairs={{0,3},{1,0},{2,1},{3,2},{4,7},{5,4},{6,5},{7,6},{8,11},{9,8},{10,9... | collective-permute-start | bytes 313352 | tf_op jit(solution)/shard_map/ppermute | solution.py:341
  120.1 3.2 %copy-start = (f32[1024,400]{0,1:T(8,128)S(1)}, f32[1024,400]{0,1:T(8,128)}, u32[]{:S(2)}) copy-start(f32[1024,400]{0,1:T(8,128)} %param.12) | copy-start | bytes 4915204
  120.1 3.2 %copy-start.4 = (f32[1024]{0:T(1024)S(1)}, f32[1024]{0:T(1024)}, u32[]{:S(2)}) copy-start(f32[1024]{0:T(1024)} %param.14) | copy-start | bytes 12292

commit v7 on v6

--- a/solution.py
+++ b/solution.py
@@ -136,22 +136,28 @@
     ]
 
 
-def gather_span(x):
+def one_way_plan(lanes, pieces):
+    plan = [entry for entry in ring_plan(lanes, pieces) if entry[2] == pieces]
+    return plan + [(lanes // 2, 0, pieces)] * (lanes % 2 == 0)
+
+
+def gather_span(x, halves):
     lanes = lax.axis_size("span")
     parts, ahead, behind = [x], x, x
     for _ in range(1, (lanes + 1) // 2):
         ahead, behind = shift_span(ahead, 1), shift_span(behind, -1)
         parts += [ahead, behind]
-    if lanes % 2 == 0:
+    if lanes % 2 == 0 and halves:
         half = x.shape[0] // 2
         parts += [shift_span(ahead[:half], 1), shift_span(behind[half:], -1)]
+    elif lanes % 2 == 0:
+        parts.append(shift_span(ahead, 1))
     return parts
 
 
-def assemble(lanes, lane, parts, out_ref):
+def assemble(lanes, plan, lane, parts, out_ref):
     width = parts[0].shape[2]
     block = out_ref.shape[0] // lanes
-    plan = ring_plan(lanes, parts[0].shape[0])
     for at in range(lanes):
 
         @pl.when(lane == at)
@@ -285,7 +291,8 @@
 
 
 def update_kernel(lanes, joined, meta_ref, *refs):
-    count = len(ring_plan(lanes, 2))
+    plan_of = one_way_plan if joined else ring_plan
+    count = len(plan_of(lanes, 2))
     if joined:
         table_ref, state_ref, rel_ref, rel_state_ref = refs[:4]
         parts, refs = refs[4 : 4 + count], refs[4 + count :]
@@ -302,14 +309,14 @@
         pltpu.make_async_copy(new_ref.at[:, spot], out_any.at[:, spot], store_sems.at[k])
         for k, spot in enumerate(spots)
     ]
-    assemble(lanes, meta_ref[1], parts, grad_ref)
+    plan = plan_of(lanes, parts[0].shape[0])
+    assemble(lanes, plan, meta_ref[1], parts, grad_ref)
     for spot, store in zip(spots, stores):
         new_ref[:, spot] = adagrad(table_ref[:, spot], state_ref[:, spot], grad_ref[:, spot], 0)
         store.start()
     if joined:
         block = features // lanes
         each = parts[0].shape[1] - block
-        plan = ring_plan(lanes, parts[0].shape[0])
         for at in range(lanes):
 
             @pl.when(meta_ref[1] == at)
@@ -505,9 +512,9 @@
         compiler_params=params(8),
     )(plan, returned)
     target_home = swap_buckets(sorted_out)
-    source_parts = gather_span(source_sum)
-    target_home = after(target_home, source_parts)
-    home_parts = gather_span(target_home)
+    source_parts = gather_span(source_sum, True)
+    target_home = after(target_home, source_parts[:-1])
+    home_parts = gather_span(target_home, not packed)
     (new_source,) = update(lanes, meta, source_cols, source_state.reshape(1, rows), source_parts)
     target_update = (lanes, meta, target_cols, target_state.reshape(1, rows), home_parts)
     if packed:

time: 127 us -> 125 us (0.984)
    ppermute x16 -> x15, starting transfers between devices: 26.9 us -> 25.9 us  [shift_span(): lax.ppermute(x, 'span', [(i, (i + by) % count) for i in range(count)])]
    ppermute x16 -> x15, waiting for transfers between devices: 22.9 us -> 23.4 us  [shift_span(): lax.ppermute(x, 'span', [(i, (i + by) % count) for i in range(count)])]
  transfers between devices with their start and end apart: 19 -> 18, of which waited for: 12 -> 10; matrix products, arithmetic and copies ran while one was open for 3% -> 2% of each run, Pallas kernels for 11% -> 11%
where the time goes in v7:
time: 125 us
  starting transfers between devices  36.4 us (29%)
  Pallas kernels  34.6 us (28%)
  waiting for transfers between devices  30.4 us (24%)
  blocking collectives  17.9 us (14%)
  other arithmetic  3.87 us (3%)
  between operations  1.56 us (1%)
    ppermute x15, starting transfers between devices, shift_span(): lax.ppermute(x, 'span', [(i, (i + by) % count) for i in range(count)])  25.9 us
    ppermute x15, waiting for transfers between devices, shift_span(): lax.ppermute(x, 'span', [(i, (i + by) % count) for i in range(count)])  23.4 us
    all_to_all x1, blocking collectives, swap_buckets(): return lax.all_to_all(x, 'bucket', split_axis=0, concat_axis=0, tiled=True)  17.9 us
    pallas_call x1, Pallas kernels, per_device(): pl.pallas_call(functools.partial(main_kernel, steps, lanes, packed), grid...  17.1 us
    all_to_all x3, starting transfers between devices, swap_buckets(): return lax.all_to_all(x, 'bucket', split_axis=0, concat_axis=0, tiled=True)  10.5 us
    all_to_all x3, waiting for transfers between devices, swap_buckets(): return lax.all_to_all(x, 'bucket', split_axis=0, concat_axis=0, tiled=True)  6.97 us
    pallas_call x1, Pallas kernels, per_device(): pl.pallas_call(functools.partial(prep_kernel, steps), grid=(steps,), out_...  6.69 us
    pallas_call x2, Pallas kernels, update(): pl.pallas_call(functools.partial(update_kernel, lanes, joined), out_shape...  4.7 us
  transfers between devices with their start and end apart: 18, of which 10 were waited for; matrix products, arithmetic and copies ran while one was open for 2% of the time, Pallas kernels for 11%

profile of v7, /device:TPU:0, one launch (start us, length us, event | category | flops | bytes accessed | tf_op | source)
XLA Modules:
  0.0 124.9 jit_solution(10357722460670471213)
XLA Ops:
  0.6 1.5 %bitcast_bitcast_fusion = bf16[8,400,128]{2,1,0:T(8,128)(2,1)S(1)} fusion(f32[1024,400]{0,1:T(8,128)} %param.12), kind=kLoop, calls=%fused_computation | loop fusion | flops 409600 | bytes 2457600 | tf_op jit(solution)/shard_map/transpose | solution.py:417
  2.2 17.9 %all_to_all.20.in_ref = bf16[8,400,128]{2,1,0:T(8,128)(2,1)S(1)} all-to-all(bf16[8,400,128]{2,1,0:T(8,128)(2,1)S(1)} %bitcast_bitcast_fusion), channel_id=1, replica_groups=mesh['bucket'=8,'span'=4] {'bucket'}, dimensions={0} | all-to-all | bytes 1638400 | tf_op jit(solution)/shard_map/all_to_all | solution.py:352
  20.1 1.5 %shard_map.131 = bf16[8,400,128]{2,1,0:T(8,128)(2,1)} custom-call(s32[8]{0:T(128)S(1)} %copy-done.5, bf16[8,400,128]{2,1,0:T(8,128)(2,1)S(1)} %all_to_all.20.in_ref), custom_call_target="tpu_custom_call" | custom-call | tf_op jit(solution)/shard_map/pallas_call | solution.py:420
  21.6 3.5 %all-to-all-start.1 = ((bf16[8,400,128]{2,1,0:T(8,128)(2,1)}), bf16[8,400,128]{2,1,0:T(8,128)(2,1)S(1)}, u32[]{:S(2)}, u32[]{:S(2)}) async-start(bf16[8,400,128]{2,1,0:T(8,128)(2,1)} %shard_map.131), calls=%async_computation.1 | async-start | bytes 1638400 | tf_op jit(solution)/shard_map/all_to_all | solution.py:352
  25.8 0.6 pad_add_fusion.meta_ref
  26.4 6.7 %shard_map.130.edge_ref = bf16[4,2,400,640]{3,2,1,0:T(8,128)(2,1)} custom-call(s32[2]{0:T(128)} %pad_add_fusion.meta_ref, s32[4,1,640]{2,1,0:T(1,128)} %bitcast.28, s32[4,1,640]{2,1,0:T(1,128)} %bitcast.26, f32[400,1024]{1,0:T(8,128)} %bitcast.21, f32[16,400]{1,0:T(8,128)} %refs_2_.1), custom_call_target="tpu_custom_call" | custom-call | flops 4194304000 | bytes 8192000 | tf_op jit(solution)/shard_map/pallas_call | solution.py:435
  33.0 4.9 %all-to-all-done.1.parts_ref = bf16[8,400,128]{2,1,0:T(8,128)(2,1)S(1)} async-done(((bf16[8,400,128]{2,1,0:T(8,128)(2,1)}), bf16[8,400,128]{2,1,0:T(8,128)(2,1)S(1)}, u32[]{:S(2)}, u32[]{:S(2)}) %all-to-all-start.1) | async-done | bytes 819232 | tf_op jit(solution)/shard_map/all_to_all | solution.py:352
  38.0 0.0 copy-start.9
  38.0 17.1 %shard_map.132 = (bf16[4,400,640]{2,1,0:T(8,128)(2,1)S(1)}, f32[400,16]{1,0:T(8,128)}, f32[8,102,128]{2,1,0:T(8,128)S(1)}, f32[8,102,128]{2,1,0:T(8,128)S(1)}, f...) custom-call(s32[2]{0:T(128)S(1)} %copy-done.6, ...), custom_call_target="tpu_custom_call" | custom-call | flops 12582912000 | bytes 8192000 | tf_op jit(solution)/shard_map/pallas_call | solution.py:453
  55.1 0.0 collective-permute-start.8
  55.1 3.8 %collective-permute-start.9 = (bf16[4,102,128]{2,1,0:T(8,128)(2,1)S(1)}, bf16[4,102,128]{2,1,0:T(8,128)(2,1)S(1)}, u32[]{:S(2)}, u32[]{:S(2)}) collective-permute-start(bf16[4,102,128]{2,1,0:T(8,128)(2,1)S(1)} %get-tuple-element.29), channel_id=1, source_target_pairs={{0,3},{1,0},{2,1},{3,2},{4,7},{5,4},{6,5},{7,6},{8,11},{9,8},{10,9... | collective-permute-start | bytes 313352 | tf_op jit(solution)/shard_map/ppermute | solution.py:348
  58.9 3.4 %shard_map.133 = (f32[8,102,128]{2,1,0:T(8,128)S(1)}, f32[8,102,128]{2,1,0:T(8,128)S(1)}, f32[8,102,128]{2,1,0:T(8,128)S(1)}, bf16[4,102,128]{2,1,0:T(8,128)(2,1)S(1)}, bf16[4,102,128]{2,1,0:T(8,128)(2,1)S(1)}) custom-call(s32[2]{0:T(128)S(1)} %copy-done.6, s32[4,1,640]{2,1,0:T(1,128)S(1)} %bitcast.29, bf16[4,400,640]{2,1,0:T(8,128)(2,1)S(1)} %get-tuple-element.20.grad_ref), custom_call_target="tpu_custom_call" | custom-call | flops 4194304000 | bytes 8192000 | tf_op jit(solution)/shard_map/pallas_call | solution.py:481
  62.4 0.1 collective-permute-start
  62.5 3.9 %collective-permute-start.2 = (bf16[4,102,128]{2,1,0:T(8,128)(2,1)S(1)}, bf16[4,102,128]{2,1,0:T(8,128)(2,1)S(1)}, u32[]{:S(2)}, u32[]{:S(2)}) collective-permute-start(bf16[4,102,128]{2,1,0:T(8,128)(2,1)S(1)} %get-tuple-element.25), channel_id=1, source_target_pairs={{0,3},{1,0},{2,1},{3,2},{4,7},{5,4},{6,5},{7,6},{8,11},{9,8},{10,9... | collective-permute-start | bytes 313352 | tf_op jit(solution)/shard_map/ppermute | solution.py:348
  66.3 0.0 collective-permute-done.9
  66.4 0.1 collective-permute-start.10
  66.6 3.9 %collective-permute-start.11 = (bf16[8,102,128]{2,1,0:T(8,128)(2,1)S(1)}, bf16[8,102,128]{2,1,0:T(8,128)(2,1)S(1)}, u32[]{:S(2)}, u32[]{:S(2)}) collective-permute-start(bf16[8,102,128]{2,1,0:T(8,128)(2,1)S(1)} %pad_maximum_fusion.3), channel_id=1, source_target_pairs={{0,3},{1,0},{2,1},{3,2},{4,7},{5,4},{6,5},{7,6},{8,11},{9,8},{10,9... | collective-permute-start | bytes 626696 | tf_op jit(solution)/shard_map/ppermute | solution.py:348
  70.4 0.0 collective-permute-done
  70.5 0.1 collective-permute-start.1
  70.6 1.2 collective-permute-done.2
  71.8 0.7 pad_maximum_fusion.1
  72.5 2.6 %collective-permute-start.3 = (bf16[8,102,128]{2,1,0:T(8,128)(2,1)}, bf16[8,102,128]{2,1,0:T(8,128)(2,1)S(1)}, u32[]{:S(2)}, u32[]{:S(2)}) collective-permute-start(bf16[8,102,128]{2,1,0:T(8,128)(2,1)} %pad_maximum_fusion.1), channel_id=1, source_target_pairs={{0,3},{1,0},{2,1},{3,2},{4,7},{5,4},{6,5},{7,6},{8,11},{9,8},{10,9... | collective-permute-start | bytes 626696 | tf_op jit(solution)/shard_map/ppermute | solution.py:348
  75.1 2.0 %collective-permute-done.10 = bf16[8,102,128]{2,1,0:T(8,128)(2,1)S(1)} collective-permute-done((bf16[8,102,128]{2,1,0:T(8,128)(2,1)S(1)}, bf16[8,102,128]{2,1,0:T(8,128)(2,1)S(1)}, u32[]{:S(2)}, u32[]{:S(2)}) %collective-permute-start.10) | collective-permute-done | bytes 208928 | tf_op jit(solution)/shard_map/ppermute | solution.py:348
  77.1 3.8 %collective-permute-done.11 = bf16[8,102,128]{2,1,0:T(8,128)(2,1)S(1)} collective-permute-done((bf16[8,102,128]{2,1,0:T(8,128)(2,1)S(1)}, bf16[8,102,128]{2,1,0:T(8,128)(2,1)S(1)}, u32[]{:S(2)}, u32[]{:S(2)}) %collective-permute-start.11) | collective-permute-done | bytes 208928 | tf_op jit(solution)/shard_map/ppermute | solution.py:348
  80.9 0.8 add_convert_fusion
  81.7 3.5 %all-to-all-start.2 = ((bf16[8,102,128]{2,1,0:T(8,128)(2,1)}), bf16[8,102,128]{2,1,0:T(8,128)(2,1)S(1)}, u32[]{:S(2)}, u32[]{:S(2)}) async-start(bf16[8,102,128]{2,1,0:T(8,128)(2,1)} %add_convert_fusion), calls=%async_computation.2 | async-start | bytes 425984 | tf_op jit(solution)/shard_map/all_to_all | solution.py:352
  85.2 0.4 collective-permute-done.3
  85.6 0.1 add_convert_fusion.1.refs_2_
  85.7 0.1 collective-permute-start.4
  85.7 3.8 %collective-permute-start.5 = (bf16[8,102,128]{2,1,0:T(8,128)(2,1)S(1)}, bf16[8,102,128]{2,1,0:T(8,128)(2,1)S(1)}, u32[]{:S(2)}, u32[]{:S(2)}) collective-permute-start(bf16[8,102,128]{2,1,0:T(8,128)(2,1)S(1)} %add_convert_fusion.1.refs_2_), channel_id=1, source_target_pairs={{0,3},{1,0},{2,1},{3,2},{4,7},{5,4},{6,5},{7,6},{8,11},{9,8},{10,9... | collective-permute-start | bytes 626696 | tf_op jit(solution)/shard_map/ppermute | solution.py:348
  89.5 2.0 %all-to-all-done.2.in_ref = bf16[8,102,128]{2,1,0:T(8,128)(2,1)S(1)} async-done(((bf16[8,102,128]{2,1,0:T(8,128)(2,1)}), bf16[8,102,128]{2,1,0:T(8,128)(2,1)S(1)}, u32[]{:S(2)}, u32[]{:S(2)}) %all-to-all-start.2) | async-done | bytes 208928 | tf_op jit(solution)/shard_map/all_to_all | solution.py:352
  91.6 1.2 shard_map.135
  92.8 3.4 %all-to-all-start.3 = ((bf16[8,102,128]{2,1,0:T(8,128)(2,1)}), bf16[8,102,128]{2,1,0:T(8,128)(2,1)S(1)}, u32[]{:S(2)}, u32[]{:S(2)}) async-start(bf16[8,102,128]{2,1,0:T(8,128)(2,1)} %shard_map.135), calls=%async_computation.3 | async-start | bytes 425984 | tf_op jit(solution)/shard_map/all_to_all | solution.py:352
  96.2 0.0 collective-permute-done.4.refs_3_
  96.2 0.1 collective-permute-start.6
  96.3 1.2 %collective-permute-done.5.refs_4_ = bf16[8,102,128]{2,1,0:T(8,128)(2,1)S(1)} collective-permute-done((bf16[8,102,128]{2,1,0:T(8,128)(2,1)S(1)}, bf16[8,102,128]{2,1,0:T(8,128)(2,1)S(1)}, u32[]{:S(2)}, u32[]{:S(2)}) %collective-permute-start.5) | collective-permute-done | bytes 208928 | tf_op jit(solution)/shard_map/ppermute | solution.py:348
  97.6 5.8 %collective-permute-done.6.refs_5_ = bf16[4,102,128]{2,1,0:T(8,128)(2,1)S(1)} collective-permute-done((bf16[4,102,128]{2,1,0:T(8,128)(2,1)S(1)}, bf16[4,102,128]{2,1,0:T(8,128)(2,1)S(1)}, u32[]{:S(2)}, u32[]{:S(2)}) %collective-permute-start.6) | collective-permute-done | bytes 104480 | tf_op jit(solution)/shard_map/ppermute | solution.py:348
  103.4 0.0 all-to-all-done.3.refs_4_
  103.4 0.0 collective-permute-start.12
  103.4 3.8 %collective-permute-start.13 = (bf16[8,102,128]{2,1,0:T(8,128)(2,1)S(1)}, bf16[8,102,128]{2,1,0:T(8,128)(2,1)S(1)}, u32[]{:S(2)}, u32[]{:S(2)}) collective-permute-start(bf16[8,102,128]{2,1,0:T(8,128)(2,1)S(1)} %all-to-all-done.3.refs_4_), channel_id=1, source_target_pairs={{0,3},{1,0},{2,1},{3,2},{4,7},{5,4},{6,5},{7,6},{8,11},{9,8},{10,9... | collective-permute-start | bytes 626696 | tf_op jit(solution)/shard_map/ppermute | solution.py:348
  107.2 6.2 %collective-permute-done.12.refs_5_ = bf16[8,102,128]{2,1,0:T(8,128)(2,1)S(1)} collective-permute-done((bf16[8,102,128]{2,1,0:T(8,128)(2,1)S(1)}, bf16[8,102,128]{2,1,0:T(8,128)(2,1)S(1)}, u32[]{:S(2)}, u32[]{:S(2)}) %collective-permute-start.12) | collective-permute-done | bytes 208928 | tf_op jit(solution)/shard_map/ppermute | solution.py:348
  113.4 3.9 %collective-permute-start.7 = (bf16[4,102,128]{2,1,0:T(8,128)(2,1)S(1)}, bf16[4,102,128]{2,1,0:T(8,128)(2,1)S(1)}, u32[]{:S(2)}, u32[]{:S(2)}) collective-permute-start(bf16[4,102,128]{2,1,0:T(8,128)(2,1)S(1)} %slice.47), channel_id=1, source_target_pairs={{0,3},{1,0},{2,1},{3,2},{4,7},{5,4},{6,5},{7,6},{8,11},{9,8},{10,9... | collective-permute-start | bytes 313352 | tf_op jit(solution)/shard_map/ppermute | solution.py:348
  117.2 0.1 copy.15.refs_3_
  117.3 2.8 %collective-permute-done.7.refs_6_ = bf16[4,102,128]{2,1,0:T(8,128)(2,1)S(1)} collective-permute-done((bf16[4,102,128]{2,1,0:T(8,128)(2,1)S(1)}, bf16[4,102,128]{2,1,0:T(8,128)(2,1)S(1)}, u32[]{:S(2)}, u32[]{:S(2)}) %collective-permute-start.7) | collective-permute-done | bytes 104480 | tf_op jit(solution)/shard_map/ppermute | solution.py:348
  120.1 2.0 %shard_map.134 = f32[400,1024]{1,0:T(8,128)} custom-call(s32[2]{0:T(128)S(1)} %copy-done.6, f32[400,1024]{1,0:T(8,128)S(1)} %bitcast.22, f32[1,1024]{1,0:T(1,128)S(1)} %bitcast.23, bf16[8,102,128]{2,1,0:T(8,128)(2,1)S(1)} %add_convert_fusion.1.refs_2_, bf16[8,102,128]{2,1,0:T(8,128)(2,1)S(1)} %collective-permute-done.4.refs_3_, ...), custom_call_target="tpu_custom_call" | custom-call | tf_op jit(solution)/shard_map/pallas_call | solution.py:365
  122.2 0.0 collective-permute-done.13.refs_6_
  122.2 0.0 collective-permute-done.14.refs_7_
  122.2 2.7 %shard_map.136 = (f32[400,1024]{1,0:T(8,128)}, f32[16,400]{1,0:T(8,128)}) custom-call(s32[2]{0:T(128)S(1)} %copy-done.6, f32[400,1024]{1,0:T(8,128)S(1)} %bitcast.20, f32[1,1024]{1,0:T(1,128)S(1)} %bitcast.24, f32[16,400]{1,0:T(8,128)S(1)} %copy-done.2, f32[16,1]{1,0:T(8,128)S(1)} %copy.15.refs_3_, bf16[8,102,128]{2,1,0:T(8,128)(2,1)S(1)} %all-to-all-done.3.refs_4_, ...), custom_call_target="tpu_custom_call" | custom-call | tf_op jit(solution)/shard_map/pallas_call | solution.py:365
  (37 shorter events, 0.3 us)
Async XLA Ops:
  0.6 19.4 %copy-start.5 = (s32[8]{0:T(128)S(1)}, s32[8]{0:T(128)}, u32[]{:S(2)}) copy-start(s32[8]{0:T(128)} %plan_ref.3) | copy-start | bytes 100
  21.6 16.4 %all-to-all-start.1 = ((bf16[8,400,128]{2,1,0:T(8,128)(2,1)}), bf16[8,400,128]{2,1,0:T(8,128)(2,1)S(1)}, u32[]{:S(2)}, u32[]{:S(2)}) async-start(bf16[8,400,128]{2,1,0:T(8,128)(2,1)} %shard_map.131), calls=%async_computation.1 | async-start | bytes 1638400 | tf_op jit(solution)/shard_map/all_to_all | solution.py:352
  26.3 11.6 %copy-start.2 = (f32[16,400]{1,0:T(8,128)S(1)}, f32[16,400]{1,0:T(8,128)}, u32[]{:S(2)}) copy-start(f32[16,400]{1,0:T(8,128)} %refs_2_.1) | copy-start | bytes 76804
  26.3 11.6 %copy-start.6 = (s32[2]{0:T(128)S(1)}, s32[2]{0:T(128)}, u32[]{:S(2)}) copy-start(s32[2]{0:T(128)} %pad_add_fusion.meta_ref) | copy-start | bytes 28
  26.3 11.6 %copy-start.7 = (s32[1,2560]{1,0:T(1,128)S(1)}, s32[1,2560]{1,0:T(1,128)}, u32[]{:S(2)}) copy-start(s32[1,2560]{1,0:T(1,128)} %param.19) | copy-start | bytes 30724
  26.4 11.7 %copy-start.8 = (s32[1,2560]{1,0:T(1,128)S(1)}, s32[1,2560]{1,0:T(1,128)}, u32[]{:S(2)}) copy-start(s32[1,2560]{1,0:T(1,128)} %param.20) | copy-start | bytes 30724
  38.0 20.9 %copy-start.9 = (s32[1,2560]{1,0:T(1,128)S(1)}, s32[1,2560]{1,0:T(1,128)}, u32[]{:S(2)}) copy-start(s32[1,2560]{1,0:T(1,128)} %param.18) | copy-start | bytes 30724
  55.1 11.2 %collective-permute-start.8 = (bf16[4,102,128]{2,1,0:T(8,128)(2,1)S(1)}, bf16[4,102,128]{2,1,0:T(8,128)(2,1)S(1)}, u32[]{:S(2)}, u32[]{:S(2)}) collective-permute-start(bf16[4,102,128]{2,1,0:T(8,128)(2,1)S(1)} %get-tuple-element.28), channel_id=1, source_target_pairs={{0,1},{1,2},{2,3},{3,0},{4,5},{5,6},{6,7},{7,4},{8,9},{9,10},{10,1... | collective-permute-start | bytes 313352 | tf_op jit(solution)/shard_map/ppermute | solution.py:348
  55.1 11.2 %collective-permute-start.9 = (bf16[4,102,128]{2,1,0:T(8,128)(2,1)S(1)}, bf16[4,102,128]{2,1,0:T(8,128)(2,1)S(1)}, u32[]{:S(2)}, u32[]{:S(2)}) collective-permute-start(bf16[4,102,128]{2,1,0:T(8,128)(2,1)S(1)} %get-tuple-element.29), channel_id=1, source_target_pairs={{0,3},{1,0},{2,1},{3,2},{4,7},{5,4},{6,5},{7,6},{8,11},{9,8},{10,9... | collective-permute-start | bytes 313352 | tf_op jit(solution)/shard_map/ppermute | solution.py:348
  62.4 8.1 %collective-permute-start = (bf16[4,102,128]{2,1,0:T(8,128)(2,1)S(1)}, bf16[4,102,128]{2,1,0:T(8,128)(2,1)S(1)}, u32[]{:S(2)}, u32[]{:S(2)}) collective-permute-start(bf16[4,102,128]{2,1,0:T(8,128)(2,1)S(1)} %get-tuple-element.23), channel_id=1, source_target_pairs={{0,1},{1,2},{2,3},{3,0},{4,5},{5,6},{6,7},{7,4},{8,9},{9,10},{10,1... | collective-permute-start | bytes 313352 | tf_op jit(solution)/shard_map/ppermute | solution.py:348
  62.5 9.3 %collective-permute-start.2 = (bf16[4,102,128]{2,1,0:T(8,128)(2,1)S(1)}, bf16[4,102,128]{2,1,0:T(8,128)(2,1)S(1)}, u32[]{:S(2)}, u32[]{:S(2)}) collective-permute-start(bf16[4,102,128]{2,1,0:T(8,128)(2,1)S(1)} %get-tuple-element.25), channel_id=1, source_target_pairs={{0,3},{1,0},{2,1},{3,2},{4,7},{5,4},{6,5},{7,6},{8,11},{9,8},{10,9... | collective-permute-start | bytes 313352 | tf_op jit(solution)/shard_map/ppermute | solution.py:348
  66.4 10.6 %collective-permute-start.10 = (bf16[8,102,128]{2,1,0:T(8,128)(2,1)S(1)}, bf16[8,102,128]{2,1,0:T(8,128)(2,1)S(1)}, u32[]{:S(2)}, u32[]{:S(2)}) collective-permute-start(bf16[8,102,128]{2,1,0:T(8,128)(2,1)S(1)} %pad_maximum_fusion.2), channel_id=1, source_target_pairs={{0,1},{1,2},{2,3},{3,0},{4,5},{5,6},{6,7},{7,4},{8,9},{9,10},{10,1... | collective-permute-start | bytes 626696 | tf_op jit(solution)/shard_map/ppermute | solution.py:348
  66.6 14.4 %collective-permute-start.11 = (bf16[8,102,128]{2,1,0:T(8,128)(2,1)S(1)}, bf16[8,102,128]{2,1,0:T(8,128)(2,1)S(1)}, u32[]{:S(2)}, u32[]{:S(2)}) collective-permute-start(bf16[8,102,128]{2,1,0:T(8,128)(2,1)S(1)} %pad_maximum_fusion.3), channel_id=1, source_target_pairs={{0,3},{1,0},{2,1},{3,2},{4,7},{5,4},{6,5},{7,6},{8,11},{9,8},{10,9... | collective-permute-start | bytes 626696 | tf_op jit(solution)/shard_map/ppermute | solution.py:348
  70.5 14.7 %collective-permute-start.1 = (bf16[8,102,128]{2,1,0:T(8,128)(2,1)S(1)}, bf16[8,102,128]{2,1,0:T(8,128)(2,1)S(1)}, u32[]{:S(2)}, u32[]{:S(2)}) collective-permute-start(bf16[8,102,128]{2,1,0:T(8,128)(2,1)S(1)} %pad_maximum_fusion), channel_id=1, source_target_pairs={{0,1},{1,2},{2,3},{3,0},{4,5},{5,6},{6,7},{7,4},{8,9},{9,10},{10,1... | collective-permute-start | bytes 626696 | tf_op jit(solution)/shard_map/ppermute | solution.py:348
  72.5 13.1 %collective-permute-start.3 = (bf16[8,102,128]{2,1,0:T(8,128)(2,1)}, bf16[8,102,128]{2,1,0:T(8,128)(2,1)S(1)}, u32[]{:S(2)}, u32[]{:S(2)}) collective-permute-start(bf16[8,102,128]{2,1,0:T(8,128)(2,1)} %pad_maximum_fusion.1), channel_id=1, source_target_pairs={{0,3},{1,0},{2,1},{3,2},{4,7},{5,4},{6,5},{7,6},{8,11},{9,8},{10,9... | collective-permute-start | bytes 626696 | tf_op jit(solution)/shard_map/ppermute | solution.py:348
  81.7 35.6 %copy-start.10 = (f32[16]{0:T(128)S(1)}, f32[16]{0:T(128)}, u32[]{:S(2)}) copy-start(f32[16]{0:T(128)} %param.16) | copy-start | bytes 196
  81.7 38.4 %copy-start.1 = (f32[1024,400]{0,1:T(8,128)S(1)}, f32[1024,400]{0,1:T(8,128)}, u32[]{:S(2)}) copy-start(f32[1024,400]{0,1:T(8,128)} %param.11) | copy-start | bytes 4915204
  81.7 38.4 %copy-start.3 = (f32[1024]{0:T(1024)S(1)}, f32[1024]{0:T(1024)}, u32[]{:S(2)}) copy-start(f32[1024]{0:T(1024)} %param.13) | copy-start | bytes 12292
  81.7 9.9 %all-to-all-start.2 = ((bf16[8,102,128]{2,1,0:T(8,128)(2,1)}), bf16[8,102,128]{2,1,0:T(8,128)(2,1)S(1)}, u32[]{:S(2)}, u32[]{:S(2)}) async-start(bf16[8,102,128]{2,1,0:T(8,128)(2,1)} %add_convert_fusion), calls=%async_computation.2 | async-start | bytes 425984 | tf_op jit(solution)/shard_map/all_to_all | solution.py:352
  85.7 10.6 %collective-permute-start.4 = (bf16[8,102,128]{2,1,0:T(8,128)(2,1)S(1)}, bf16[8,102,128]{2,1,0:T(8,128)(2,1)S(1)}, u32[]{:S(2)}, u32[]{:S(2)}) collective-permute-start(bf16[8,102,128]{2,1,0:T(8,128)(2,1)S(1)} %add_convert_fusion.1.refs_2_), channel_id=1, source_target_pairs={{0,1},{1,2},{2,3},{3,0},{4,5},{5,6},{6,7},{7,4},{8,9},{9,10},{10,1... | collective-permute-start | bytes 626696 | tf_op jit(solution)/shard_map/ppermute | solution.py:348
  85.7 11.8 %collective-permute-start.5 = (bf16[8,102,128]{2,1,0:T(8,128)(2,1)S(1)}, bf16[8,102,128]{2,1,0:T(8,128)(2,1)S(1)}, u32[]{:S(2)}, u32[]{:S(2)}) collective-permute-start(bf16[8,102,128]{2,1,0:T(8,128)(2,1)S(1)} %add_convert_fusion.1.refs_2_), channel_id=1, source_target_pairs={{0,3},{1,0},{2,1},{3,2},{4,7},{5,4},{6,5},{7,6},{8,11},{9,8},{10,9... | collective-permute-start | bytes 626696 | tf_op jit(solution)/shard_map/ppermute | solution.py:348
  92.8 10.6 %all-to-all-start.3 = ((bf16[8,102,128]{2,1,0:T(8,128)(2,1)}), bf16[8,102,128]{2,1,0:T(8,128)(2,1)S(1)}, u32[]{:S(2)}, u32[]{:S(2)}) async-start(bf16[8,102,128]{2,1,0:T(8,128)(2,1)} %shard_map.135), calls=%async_computation.3 | async-start | bytes 425984 | tf_op jit(solution)/shard_map/all_to_all | solution.py:352
  96.2 7.1 %collective-permute-start.6 = (bf16[4,102,128]{2,1,0:T(8,128)(2,1)S(1)}, bf16[4,102,128]{2,1,0:T(8,128)(2,1)S(1)}, u32[]{:S(2)}, u32[]{:S(2)}) collective-permute-start(bf16[4,102,128]{2,1,0:T(8,128)(2,1)S(1)} %slice.46), channel_id=1, source_target_pairs={{0,1},{1,2},{2,3},{3,0},{4,5},{5,6},{6,7},{7,4},{8,9},{9,10},{10,1... | collective-permute-start | bytes 313352 | tf_op jit(solution)/shard_map/ppermute | solution.py:348
  103.4 10.0 %collective-permute-start.12 = (bf16[8,102,128]{2,1,0:T(8,128)(2,1)S(1)}, bf16[8,102,128]{2,1,0:T(8,128)(2,1)S(1)}, u32[]{:S(2)}, u32[]{:S(2)}) collective-permute-start(bf16[8,102,128]{2,1,0:T(8,128)(2,1)S(1)} %all-to-all-done.3.refs_4_), channel_id=1, source_target_pairs={{0,1},{1,2},{2,3},{3,0},{4,5},{5,6},{6,7},{7,4},{8,9},{9,10},{10,1... | collective-permute-start | bytes 626696 | tf_op jit(solution)/shard_map/ppermute | solution.py:348
  103.4 18.8 %collective-permute-start.13 = (bf16[8,102,128]{2,1,0:T(8,128)(2,1)S(1)}, bf16[8,102,128]{2,1,0:T(8,128)(2,1)S(1)}, u32[]{:S(2)}, u32[]{:S(2)}) collective-permute-start(bf16[8,102,128]{2,1,0:T(8,128)(2,1)S(1)} %all-to-all-done.3.refs_4_), channel_id=1, source_target_pairs={{0,3},{1,0},{2,1},{3,2},{4,7},{5,4},{6,5},{7,6},{8,11},{9,8},{10,9... | collective-permute-start | bytes 626696 | tf_op jit(solution)/shard_map/ppermute | solution.py:348
  113.3 8.9 %collective-permute-start.14 = (bf16[8,102,128]{2,1,0:T(8,128)(2,1)S(1)}, bf16[8,102,128]{2,1,0:T(8,128)(2,1)S(1)}, u32[]{:S(2)}, u32[]{:S(2)}) collective-permute-start(bf16[8,102,128]{2,1,0:T(8,128)(2,1)S(1)} %collective-permute-done.12.refs_5_), channel_id=1, source_target_pairs={{0,1},{1,2},{2,3},{3,0},{4,5},{5,6},{6,7},{7,4},{8,9},{9,10},{10,1... | collective-permute-start | bytes 626696 | tf_op jit(solution)/shard_map/ppermute | solution.py:348
  113.4 6.8 %collective-permute-start.7 = (bf16[4,102,128]{2,1,0:T(8,128)(2,1)S(1)}, bf16[4,102,128]{2,1,0:T(8,128)(2,1)S(1)}, u32[]{:S(2)}, u32[]{:S(2)}) collective-permute-start(bf16[4,102,128]{2,1,0:T(8,128)(2,1)S(1)} %slice.47), channel_id=1, source_target_pairs={{0,3},{1,0},{2,1},{3,2},{4,7},{5,4},{6,5},{7,6},{8,11},{9,8},{10,9... | collective-permute-start | bytes 313352 | tf_op jit(solution)/shard_map/ppermute | solution.py:348
  120.1 2.1 %copy-start = (f32[1024,400]{0,1:T(8,128)S(1)}, f32[1024,400]{0,1:T(8,128)}, u32[]{:S(2)}) copy-start(f32[1024,400]{0,1:T(8,128)} %param.12) | copy-start | bytes 4915204
  120.1 2.1 %copy-start.4 = (f32[1024]{0:T(1024)S(1)}, f32[1024]{0:T(1024)}, u32[]{:S(2)}) copy-start(f32[1024]{0:T(1024)} %param.14) | copy-start | bytes 12292

commit v8 on v7

--- a/solution.py
+++ b/solution.py
@@ -200,40 +200,65 @@
         acc_ref[...] = jnp.zeros_like(acc_ref)
         rel_out_ref[...] = jnp.zeros_like(rel_out_ref)
 
-    live = is_live(meta_ref, step, steps, tid_ref.shape[2])
-
-    @pl.when(jnp.logical_not(live))
+    group = tid_ref.shape[0]
+    first = step * group
+    last_live = is_live(meta_ref, first + group - 1, steps, tid_ref.shape[2])
+
+    def spans(some):
+        for j in some:
+            ids = live_ids(tid_ref[j], meta_ref, first + j, steps)
+            hot_ref[j] = one_hot(ids, table_ref.shape[1])
+        tails = [dot_nn(table_ref[...], hot_ref[j]).astype(BF16) for j in some]
+        for j, tail in zip(some, tails):
+            scores = dot_tn(edge_ref[j, 0], tail)
+            sig = 0.5 * jnp.tanh(0.5 * scores) + 0.5
+            diagonal = lax.broadcasted_iota(jnp.int32, scores.shape, 0) == lax.broadcasted_iota(
+                jnp.int32, scores.shape, 1
+            )
+            coef_ref[j] = jnp.where(diagonal, sig - 1.0, NEG_WEIGHT * sig).astype(BF16)
+        for j, tail in zip(some, tails):
+            kinds = live_ids(rid_ref[j], meta_ref, first + j, steps)
+            kind = kind_hot(kinds, rel_ref.shape[0])
+            rel = relation_columns(rel_ref, kind)
+            head = edge_ref[j, 1].astype(F32)
+            half = head.shape[0] // 2
+            h_re, h_im, r_re, r_im = head[:half], head[half:], rel[:half], rel[half:]
+            grad_query = dot_nt(tail, coef_ref[j])
+            g_re, g_im = grad_query[:half], grad_query[half:]
+            grad_head = [g_re * r_re + g_im * r_im, g_im * r_re - g_re * r_im]
+            grad_ref[j] = jnp.concatenate(grad_head, axis=0).astype(BF16)
+            grad_rel = [g_re * h_re + g_im * h_im, g_im * h_re - g_re * h_im]
+            grad_rel = jnp.concatenate(grad_rel, axis=0).astype(BF16)
+            rel_out_ref[...] += dot_nt(grad_rel, kind.astype(BF16))
+        total = acc_ref[...]
+        for j in some:
+            grad_tail = dot_nn(edge_ref[j, 0], coef_ref[j])
+            total += dot_nt(grad_tail.astype(BF16), hot_ref[j])
+        acc_ref[...] = total
+
+    @pl.when(last_live)
     def _():
-        grad_ref[...] = jnp.zeros_like(grad_ref)
-
-    @pl.when(live)
+        spans(range(group))
+
+    for j in range(group - 1):
+
+        @pl.when(jnp.logical_not(last_live))
+        def _():
+            live = is_live(meta_ref, first + j, steps, tid_ref.shape[2])
+
+            @pl.when(live)
+            def _():
+                spans([j])
+
+            @pl.when(jnp.logical_not(live))
+            def _():
+                grad_ref[j] = jnp.zeros(grad_ref.shape[1:], BF16)
+
+    @pl.when(jnp.logical_not(last_live))
     def _():
-        ids = live_ids(tid_ref[0], meta_ref, step, steps)
-        hot_ref[...] = one_hot(ids, table_ref.shape[1])
-        tail = dot_nn(table_ref[...], hot_ref[...]).astype(BF16)
-        scores = dot_tn(edge_ref[0, 0], tail)
-        sig = 0.5 * jnp.tanh(0.5 * scores) + 0.5
-        diagonal = lax.broadcasted_iota(jnp.int32, scores.shape, 0) == lax.broadcasted_iota(
-            jnp.int32, scores.shape, 1
-        )
-        coef_ref[...] = jnp.where(diagonal, sig - 1.0, NEG_WEIGHT * sig).astype(BF16)
-        grad_tail = dot_nn(edge_ref[0, 0], coef_ref[...])
-        acc_ref[...] += dot_nt(grad_tail.astype(BF16), hot_ref[...])
-
-        kinds = live_ids(rid_ref[0], meta_ref, step, steps)
-        kind = kind_hot(kinds, rel_ref.shape[0])
-        rel = relation_columns(rel_ref, kind)
-        head = edge_ref[0, 1].astype(F32)
-        half = head.shape[0] // 2
-        h_re, h_im, r_re, r_im = head[:half], head[half:], rel[:half], rel[half:]
-        grad_query = dot_nt(tail, coef_ref[...])
-        g_re, g_im = grad_query[:half], grad_query[half:]
-        grad_head = jnp.concatenate([g_re * r_re + g_im * r_im, g_im * r_re - g_re * r_im], axis=0)
-        grad_ref[0] = grad_head.astype(BF16)
-        grad_rel = jnp.concatenate([g_re * h_re + g_im * h_im, g_im * h_re - g_re * h_im], axis=0)
-        rel_out_ref[...] += dot_nt(grad_rel.astype(BF16), kind.astype(BF16))
-
-    @pl.when(step == steps - 1)
+        grad_ref[group - 1] = jnp.zeros(grad_ref.shape[1:], BF16)
+
+    @pl.when(step == pl.num_programs(0) - 1)
     def _():
         emit(lanes, meta_ref[1], acc_ref, outs)
         if packed:
@@ -338,9 +363,9 @@
     return pl.BlockSpec(tuple(shape), lambda i: zeros)
 
 
-def per_span(shape):
+def per_span(shape, group=1):
     rest = (0,) * (len(shape) - 1)
-    return pl.BlockSpec((1,) + tuple(shape[1:]), lambda i: (i,) + rest)
+    return pl.BlockSpec((group,) + tuple(shape[1:]), lambda i: (i,) + rest)
 
 
 def shift_span(x, by):
@@ -450,9 +475,10 @@
     )(meta, hid, rid, source_cols, relation)
 
     bundle_outs = ring_shapes(bundles, lanes)
+    group = 2 if steps % 2 == 0 else 1
     grad_head, rel_part, *target_out = pl.pallas_call(
         functools.partial(main_kernel, steps, lanes, packed),
-        grid=(steps,),
+        grid=(steps // group,),
         out_shape=[
             jax.ShapeDtypeStruct(edge_shape, BF16),
             jax.ShapeDtypeStruct((features, kinds), F32),
@@ -460,19 +486,19 @@
         + bundle_outs,
         in_specs=[
             SMEM_SPEC,
-            per_span(tid.shape),
-            per_span(rid.shape),
+            per_span(tid.shape, group),
+            per_span(rid.shape, group),
             whole(relation.shape),
-            per_span(both_shape),
+            per_span(both_shape, group),
             VMEM_SPEC,
         ],
-        out_specs=[per_span(edge_shape), whole((features, kinds))]
+        out_specs=[per_span(edge_shape, group), whole((features, kinds))]
         + [whole(out.shape) for out in bundle_outs],
         scratch_shapes=[
             pltpu.VMEM((features, rows), BF16),
             pltpu.VMEM((features, rows), F32),
-            pltpu.VMEM((rows, E_CH), BF16),
-            pltpu.VMEM((E_CH, E_CH), BF16),
+            pltpu.VMEM((group, rows, E_CH), BF16),
+            pltpu.VMEM((group, E_CH, E_CH), BF16),
         ],
         compiler_params=params(48),
         cost_estimate=cost(12 * steps * features * rows * E_CH, 8 * features * steps * E_CH),

time: 125 us -> 126 us (level); the launches traced: 125 us -> 124 us
  starting transfers between devices: 36.4 us -> 44.9 us
  Pallas kernels: 34.6 us -> 26.4 us
  waiting for transfers between devices: 30.4 us -> 28.7 us
    pallas_call x1, Pallas kernels: 17.1 us -> 9.98 us  [per_device(): pl.pallas_call(functools.partial(main_kernel, steps, lanes, packed), grid...]
    all_to_all x3, starting transfers between devices: 10.5 us -> 16.9 us  [swap_buckets(): return lax.all_to_all(x, 'bucket', split_axis=0, concat_axis=0, tiled=True)]
    ppermute x15, waiting for transfers between devices: 23.4 us -> 20.2 us  [shift_span(): lax.ppermute(x, 'span', [(i, (i + by) % count) for i in range(count)])]
    ppermute x15, starting transfers between devices: 25.9 us -> 28 us  [shift_span(): lax.ppermute(x, 'span', [(i, (i + by) % count) for i in range(count)])]
    all_to_all x3, waiting for transfers between devices: 6.97 us -> 8.48 us  [swap_buckets(): return lax.all_to_all(x, 'bucket', split_axis=0, concat_axis=0, tiled=True)]
  transfers between devices with their start and end apart: 18 -> 18, of which waited for: 10 -> 8; matrix products, arithmetic and copies ran while one was open for 2% -> 2% of each run, Pallas kernels for 11% -> 10%
where the time goes in v8:
time: 126 us; the launch traced here: 124 us
  starting transfers between devices  44.9 us (36%)
  waiting for transfers between devices  28.7 us (23%)
  Pallas kernels  26.4 us (21%)
  blocking collectives  17.9 us (14%)
  other arithmetic  3.88 us (3%)
  between operations  1.7 us (1%)
    ppermute x15, starting transfers between devices, shift_span(): lax.ppermute(x, 'span', [(i, (i + by) % count) for i in range(count)])  28 us
    ppermute x15, waiting for transfers between devices, shift_span(): lax.ppermute(x, 'span', [(i, (i + by) % count) for i in range(count)])  20.2 us
    all_to_all x1, blocking collectives, swap_buckets(): return lax.all_to_all(x, 'bucket', split_axis=0, concat_axis=0, tiled=True)  17.9 us
    all_to_all x3, starting transfers between devices, swap_buckets(): return lax.all_to_all(x, 'bucket', split_axis=0, concat_axis=0, tiled=True)  16.9 us
    pallas_call x1, Pallas kernels, per_device(): pl.pallas_call(functools.partial(main_kernel, steps, lanes, packed), grid...  9.98 us
    all_to_all x3, waiting for transfers between devices, swap_buckets(): return lax.all_to_all(x, 'bucket', split_axis=0, concat_axis=0, tiled=True)  8.48 us
    pallas_call x1, Pallas kernels, per_device(): pl.pallas_call(functools.partial(prep_kernel, steps), grid=(steps,), out_...  5.59 us
    pallas_call x2, Pallas kernels, update(): pl.pallas_call(functools.partial(update_kernel, lanes, joined), out_shape...  4.7 us
  transfers between devices with their start and end apart: 18, of which 8 were waited for; matrix products, arithmetic and copies ran while one was open for 2% of the time, Pallas kernels for 10%

profile of v8, /device:TPU:0, one launch (start us, length us, event | category | flops | bytes accessed | tf_op | source)
XLA Modules:
  0.0 123.7 jit_solution(7600239561766677301)
XLA Ops:
  0.6 1.5 %bitcast_bitcast_fusion = bf16[8,400,128]{2,1,0:T(8,128)(2,1)S(1)} fusion(f32[1024,400]{0,1:T(8,128)} %param.12), kind=kLoop, calls=%fused_computation | loop fusion | flops 409600 | bytes 2457600 | tf_op jit(solution)/shard_map/transpose | solution.py:442
  2.2 17.9 %all_to_all.20.in_ref = bf16[8,400,128]{2,1,0:T(8,128)(2,1)S(1)} all-to-all(bf16[8,400,128]{2,1,0:T(8,128)(2,1)S(1)} %bitcast_bitcast_fusion), channel_id=1, replica_groups=mesh['bucket'=8,'span'=4] {'bucket'}, dimensions={0} | all-to-all | bytes 1638400 | tf_op jit(solution)/shard_map/all_to_all | solution.py:377
  20.1 1.5 %shard_map.131 = bf16[8,400,128]{2,1,0:T(8,128)(2,1)} custom-call(s32[8]{0:T(128)S(1)} %copy-done.5, bf16[8,400,128]{2,1,0:T(8,128)(2,1)S(1)} %all_to_all.20.in_ref), custom_call_target="tpu_custom_call" | custom-call | tf_op jit(solution)/shard_map/pallas_call | solution.py:445
  21.6 3.5 %all-to-all-start.1 = ((bf16[8,400,128]{2,1,0:T(8,128)(2,1)}), bf16[8,400,128]{2,1,0:T(8,128)(2,1)S(1)}, u32[]{:S(2)}, u32[]{:S(2)}) async-start(bf16[8,400,128]{2,1,0:T(8,128)(2,1)} %shard_map.131), calls=%async_computation.1 | async-start | bytes 1638400 | tf_op jit(solution)/shard_map/all_to_all | solution.py:377
  25.8 0.6 pad_add_fusion.meta_ref
  26.4 5.6 %shard_map.130.edge_ref = bf16[4,2,400,640]{3,2,1,0:T(8,128)(2,1)} custom-call(s32[2]{0:T(128)} %pad_add_fusion.meta_ref, s32[4,1,640]{2,1,0:T(1,128)} %bitcast.28, s32[4,1,640]{2,1,0:T(1,128)} %bitcast.26, f32[400,1024]{1,0:T(8,128)} %bitcast.21, f32[16,400]{1,0:T(8,128)} %refs_2_.1), custom_call_target="tpu_custom_call" | custom-call | flops 4194304000 | bytes 8192000 | tf_op jit(solution)/shard_map/pallas_call | solution.py:460
  31.9 6.0 %all-to-all-done.1.parts_ref = bf16[8,400,128]{2,1,0:T(8,128)(2,1)S(1)} async-done(((bf16[8,400,128]{2,1,0:T(8,128)(2,1)}), bf16[8,400,128]{2,1,0:T(8,128)(2,1)S(1)}, u32[]{:S(2)}, u32[]{:S(2)}) %all-to-all-start.1) | async-done | bytes 819232 | tf_op jit(solution)/shard_map/all_to_all | solution.py:377
  38.0 0.0 copy-start.9
  38.0 10.0 %shard_map.132 = (bf16[4,400,640]{2,1,0:T(8,128)(2,1)S(1)}, f32[400,16]{1,0:T(8,128)}, f32[8,102,128]{2,1,0:T(8,128)S(1)}, f32[8,102,128]{2,1,0:T(8,128)S(1)}, f...) custom-call(s32[2]{0:T(128)S(1)} %copy-done.6, ...), custom_call_target="tpu_custom_call" | custom-call | flops 12582912000 | bytes 8192000 | tf_op jit(solution)/shard_map/pallas_call | solution.py:479
  48.0 0.0 collective-permute-start.8
  48.0 3.8 %collective-permute-start.9 = (bf16[4,102,128]{2,1,0:T(8,128)(2,1)S(1)}, bf16[4,102,128]{2,1,0:T(8,128)(2,1)S(1)}, u32[]{:S(2)}, u32[]{:S(2)}) collective-permute-start(bf16[4,102,128]{2,1,0:T(8,128)(2,1)S(1)} %get-tuple-element.29), channel_id=1, source_target_pairs={{0,3},{1,0},{2,1},{3,2},{4,7},{5,4},{6,5},{7,6},{8,11},{9,8},{10,9... | collective-permute-start | bytes 313352 | tf_op jit(solution)/shard_map/ppermute | solution.py:373
  51.8 3.4 %shard_map.133 = (f32[8,102,128]{2,1,0:T(8,128)S(1)}, f32[8,102,128]{2,1,0:T(8,128)S(1)}, f32[8,102,128]{2,1,0:T(8,128)S(1)}, bf16[4,102,128]{2,1,0:T(8,128)(2,1)S(1)}, bf16[4,102,128]{2,1,0:T(8,128)(2,1)S(1)}) custom-call(s32[2]{0:T(128)S(1)} %copy-done.6, s32[4,1,640]{2,1,0:T(1,128)S(1)} %bitcast.29, bf16[4,400,640]{2,1,0:T(8,128)(2,1)S(1)} %get-tuple-element.20.grad_ref), custom_call_target="tpu_custom_call" | custom-call | flops 4194304000 | bytes 8192000 | tf_op jit(solution)/shard_map/pallas_call | solution.py:507
  55.3 0.1 collective-permute-start
  55.4 3.9 %collective-permute-start.2 = (bf16[4,102,128]{2,1,0:T(8,128)(2,1)S(1)}, bf16[4,102,128]{2,1,0:T(8,128)(2,1)S(1)}, u32[]{:S(2)}, u32[]{:S(2)}) collective-permute-start(bf16[4,102,128]{2,1,0:T(8,128)(2,1)S(1)} %get-tuple-element.25), channel_id=1, source_target_pairs={{0,3},{1,0},{2,1},{3,2},{4,7},{5,4},{6,5},{7,6},{8,11},{9,8},{10,9... | collective-permute-start | bytes 313352 | tf_op jit(solution)/shard_map/ppermute | solution.py:373
  59.2 0.0 collective-permute-done.8
  59.3 0.0 collective-permute-done.9
  59.3 0.1 collective-permute-start.10
  59.5 3.9 %collective-permute-start.11 = (bf16[8,102,128]{2,1,0:T(8,128)(2,1)S(1)}, bf16[8,102,128]{2,1,0:T(8,128)(2,1)S(1)}, u32[]{:S(2)}, u32[]{:S(2)}) collective-permute-start(bf16[8,102,128]{2,1,0:T(8,128)(2,1)S(1)} %pad_maximum_fusion.3), channel_id=1, source_target_pairs={{0,3},{1,0},{2,1},{3,2},{4,7},{5,4},{6,5},{7,6},{8,11},{9,8},{10,9... | collective-permute-start | bytes 626696 | tf_op jit(solution)/shard_map/ppermute | solution.py:373
  63.4 0.1 collective-permute-start.1
  63.5 0.0 collective-permute-done.2
  63.5 0.7 pad_maximum_fusion.1
  64.2 3.8 %collective-permute-start.3 = (bf16[8,102,128]{2,1,0:T(8,128)(2,1)}, bf16[8,102,128]{2,1,0:T(8,128)(2,1)S(1)}, u32[]{:S(2)}, u32[]{:S(2)}) collective-permute-start(bf16[8,102,128]{2,1,0:T(8,128)(2,1)} %pad_maximum_fusion.1), channel_id=1, source_target_pairs={{0,3},{1,0},{2,1},{3,2},{4,7},{5,4},{6,5},{7,6},{8,11},{9,8},{10,9... | collective-permute-start | bytes 626696 | tf_op jit(solution)/shard_map/ppermute | solution.py:373
  68.0 0.8 collective-permute-done.10
  68.8 3.9 %collective-permute-done.11 = bf16[8,102,128]{2,1,0:T(8,128)(2,1)S(1)} collective-permute-done((bf16[8,102,128]{2,1,0:T(8,128)(2,1)S(1)}, bf16[8,102,128]{2,1,0:T(8,128)(2,1)S(1)}, u32[]{:S(2)}, u32[]{:S(2)}) %collective-permute-start.11) | collective-permute-done | bytes 208928 | tf_op jit(solution)/shard_map/ppermute | solution.py:373
  72.7 0.8 add_convert_fusion
  73.4 9.6 %all-to-all-start.2 = ((bf16[8,102,128]{2,1,0:T(8,128)(2,1)}), bf16[8,102,128]{2,1,0:T(8,128)(2,1)S(1)}, u32[]{:S(2)}, u32[]{:S(2)}) async-start(bf16[8,102,128]{2,1,0:T(8,128)(2,1)} %add_convert_fusion), calls=%async_computation.2 | async-start | bytes 425984 | tf_op jit(solution)/shard_map/all_to_all | solution.py:377
  83.0 0.0 collective-permute-done.1
  83.0 0.0 collective-permute-done.3
  83.1 0.1 add_convert_fusion.1.refs_2_
  83.1 1.2 collective-permute-start.4
  84.4 2.7 %collective-permute-start.5 = (bf16[8,102,128]{2,1,0:T(8,128)(2,1)S(1)}, bf16[8,102,128]{2,1,0:T(8,128)(2,1)S(1)}, u32[]{:S(2)}, u32[]{:S(2)}) collective-permute-start(bf16[8,102,128]{2,1,0:T(8,128)(2,1)S(1)} %add_convert_fusion.1.refs_2_), channel_id=1, source_target_pairs={{0,3},{1,0},{2,1},{3,2},{4,7},{5,4},{6,5},{7,6},{8,11},{9,8},{10,9... | collective-permute-start | bytes 626696 | tf_op jit(solution)/shard_map/ppermute | solution.py:373
  87.0 2.4 %all-to-all-done.2.in_ref = bf16[8,102,128]{2,1,0:T(8,128)(2,1)S(1)} async-done(((bf16[8,102,128]{2,1,0:T(8,128)(2,1)}), bf16[8,102,128]{2,1,0:T(8,128)(2,1)S(1)}, u32[]{:S(2)}, u32[]{:S(2)}) %all-to-all-start.2) | async-done | bytes 208928 | tf_op jit(solution)/shard_map/all_to_all | solution.py:377
  89.4 1.2 %shard_map.135 = bf16[8,102,128]{2,1,0:T(8,128)(2,1)} custom-call(s32[8]{0:T(128)S(1)} %copy-done.5, bf16[8,102,128]{2,1,0:T(8,128)(2,1)S(1)} %all-to-all-done.2.in_ref), custom_call_target="tpu_custom_call" | custom-call | tf_op jit(solution)/shard_map/pallas_call | solution.py:533
  90.7 3.8 %all-to-all-start.3 = ((bf16[8,102,128]{2,1,0:T(8,128)(2,1)}), bf16[8,102,128]{2,1,0:T(8,128)(2,1)S(1)}, u32[]{:S(2)}, u32[]{:S(2)}) async-start(bf16[8,102,128]{2,1,0:T(8,128)(2,1)} %shard_map.135), calls=%async_computation.3 | async-start | bytes 425984 | tf_op jit(solution)/shard_map/all_to_all | solution.py:377
  94.5 0.9 collective-permute-start.6
  95.4 0.9 collective-permute-done.5.refs_4_
  96.3 5.4 %collective-permute-done.6.refs_5_ = bf16[4,102,128]{2,1,0:T(8,128)(2,1)S(1)} collective-permute-done((bf16[4,102,128]{2,1,0:T(8,128)(2,1)S(1)}, bf16[4,102,128]{2,1,0:T(8,128)(2,1)S(1)}, u32[]{:S(2)}, u32[]{:S(2)}) %collective-permute-start.6) | collective-permute-done | bytes 104480 | tf_op jit(solution)/shard_map/ppermute | solution.py:373
  101.7 0.0 all-to-all-done.3.refs_4_
  101.7 0.0 collective-permute-start.12
  101.7 3.8 %collective-permute-start.13 = (bf16[8,102,128]{2,1,0:T(8,128)(2,1)S(1)}, bf16[8,102,128]{2,1,0:T(8,128)(2,1)S(1)}, u32[]{:S(2)}, u32[]{:S(2)}) collective-permute-start(bf16[8,102,128]{2,1,0:T(8,128)(2,1)S(1)} %all-to-all-done.3.refs_4_), channel_id=1, source_target_pairs={{0,3},{1,0},{2,1},{3,2},{4,7},{5,4},{6,5},{7,6},{8,11},{9,8},{10,9... | collective-permute-start | bytes 626696 | tf_op jit(solution)/shard_map/ppermute | solution.py:373
  105.5 6.1 %collective-permute-done.12.refs_5_ = bf16[8,102,128]{2,1,0:T(8,128)(2,1)S(1)} collective-permute-done((bf16[8,102,128]{2,1,0:T(8,128)(2,1)S(1)}, bf16[8,102,128]{2,1,0:T(8,128)(2,1)S(1)}, u32[]{:S(2)}, u32[]{:S(2)}) %collective-permute-start.12) | collective-permute-done | bytes 208928 | tf_op jit(solution)/shard_map/ppermute | solution.py:373
  111.7 0.0 collective-permute-start.14
  111.7 3.9 %collective-permute-start.7 = (bf16[4,102,128]{2,1,0:T(8,128)(2,1)S(1)}, bf16[4,102,128]{2,1,0:T(8,128)(2,1)S(1)}, u32[]{:S(2)}, u32[]{:S(2)}) collective-permute-start(bf16[4,102,128]{2,1,0:T(8,128)(2,1)S(1)} %slice.47), channel_id=1, source_target_pairs={{0,3},{1,0},{2,1},{3,2},{4,7},{5,4},{6,5},{7,6},{8,11},{9,8},{10,9... | collective-permute-start | bytes 313352 | tf_op jit(solution)/shard_map/ppermute | solution.py:373
  115.6 0.1 copy.15.refs_3_
  115.6 3.1 %collective-permute-done.7.refs_6_ = bf16[4,102,128]{2,1,0:T(8,128)(2,1)S(1)} collective-permute-done((bf16[4,102,128]{2,1,0:T(8,128)(2,1)S(1)}, bf16[4,102,128]{2,1,0:T(8,128)(2,1)S(1)}, u32[]{:S(2)}, u32[]{:S(2)}) %collective-permute-start.7) | collective-permute-done | bytes 104480 | tf_op jit(solution)/shard_map/ppermute | solution.py:373
  118.8 2.0 %shard_map.134 = f32[400,1024]{1,0:T(8,128)} custom-call(s32[2]{0:T(128)S(1)} %copy-done.6, f32[400,1024]{1,0:T(8,128)S(1)} %bitcast.22, f32[1,1024]{1,0:T(1,128)S(1)} %bitcast.23, bf16[8,102,128]{2,1,0:T(8,128)(2,1)S(1)} %add_convert_fusion.1.refs_2_, bf16[8,102,128]{2,1,0:T(8,128)(2,1)S(1)} %collective-permute-done.4.refs_3_, ...), custom_call_target="tpu_custom_call" | custom-call | tf_op jit(solution)/shard_map/pallas_call | solution.py:390
  120.8 0.0 collective-permute-done.13.refs_6_
  120.9 2.7 %shard_map.136 = (f32[400,1024]{1,0:T(8,128)}, f32[16,400]{1,0:T(8,128)}) custom-call(s32[2]{0:T(128)S(1)} %copy-done.6, f32[400,1024]{1,0:T(8,128)S(1)} %bitcast.20, f32[1,1024]{1,0:T(1,128)S(1)} %bitcast.24, f32[16,400]{1,0:T(8,128)S(1)} %copy-done.2, f32[16,1]{1,0:T(8,128)S(1)} %copy.15.refs_3_, bf16[8,102,128]{2,1,0:T(8,128)(2,1)S(1)} %all-to-all-done.3.refs_4_, ...), custom_call_target="tpu_custom_call" | custom-call | tf_op jit(solution)/shard_map/pallas_call | solution.py:390
  (37 shorter events, 0.3 us)
Async XLA Ops:
  0.6 19.4 %copy-start.5 = (s32[8]{0:T(128)S(1)}, s32[8]{0:T(128)}, u32[]{:S(2)}) copy-start(s32[8]{0:T(128)} %plan_ref.3) | copy-start | bytes 100
  21.6 16.4 %all-to-all-start.1 = ((bf16[8,400,128]{2,1,0:T(8,128)(2,1)}), bf16[8,400,128]{2,1,0:T(8,128)(2,1)S(1)}, u32[]{:S(2)}, u32[]{:S(2)}) async-start(bf16[8,400,128]{2,1,0:T(8,128)(2,1)} %shard_map.131), calls=%async_computation.1 | async-start | bytes 1638400 | tf_op jit(solution)/shard_map/all_to_all | solution.py:377
  26.3 11.6 %copy-start.2 = (f32[16,400]{1,0:T(8,128)S(1)}, f32[16,400]{1,0:T(8,128)}, u32[]{:S(2)}) copy-start(f32[16,400]{1,0:T(8,128)} %refs_2_.1) | copy-start | bytes 76804
  26.3 11.6 %copy-start.6 = (s32[2]{0:T(128)S(1)}, s32[2]{0:T(128)}, u32[]{:S(2)}) copy-start(s32[2]{0:T(128)} %pad_add_fusion.meta_ref) | copy-start | bytes 28
  26.4 11.6 %copy-start.7 = (s32[1,2560]{1,0:T(1,128)S(1)}, s32[1,2560]{1,0:T(1,128)}, u32[]{:S(2)}) copy-start(s32[1,2560]{1,0:T(1,128)} %param.19) | copy-start | bytes 30724
  26.4 11.7 %copy-start.8 = (s32[1,2560]{1,0:T(1,128)S(1)}, s32[1,2560]{1,0:T(1,128)}, u32[]{:S(2)}) copy-start(s32[1,2560]{1,0:T(1,128)} %param.20) | copy-start | bytes 30724
  38.0 13.8 %copy-start.9 = (s32[1,2560]{1,0:T(1,128)S(1)}, s32[1,2560]{1,0:T(1,128)}, u32[]{:S(2)}) copy-start(s32[1,2560]{1,0:T(1,128)} %param.18) | copy-start | bytes 30724
  48.0 11.2 %collective-permute-start.8 = (bf16[4,102,128]{2,1,0:T(8,128)(2,1)S(1)}, bf16[4,102,128]{2,1,0:T(8,128)(2,1)S(1)}, u32[]{:S(2)}, u32[]{:S(2)}) collective-permute-start(bf16[4,102,128]{2,1,0:T(8,128)(2,1)S(1)} %get-tuple-element.28), channel_id=1, source_target_pairs={{0,1},{1,2},{2,3},{3,0},{4,5},{5,6},{6,7},{7,4},{8,9},{9,10},{10,1... | collective-permute-start | bytes 313352 | tf_op jit(solution)/shard_map/ppermute | solution.py:373
  48.0 11.2 %collective-permute-start.9 = (bf16[4,102,128]{2,1,0:T(8,128)(2,1)S(1)}, bf16[4,102,128]{2,1,0:T(8,128)(2,1)S(1)}, u32[]{:S(2)}, u32[]{:S(2)}) collective-permute-start(bf16[4,102,128]{2,1,0:T(8,128)(2,1)S(1)} %get-tuple-element.29), channel_id=1, source_target_pairs={{0,3},{1,0},{2,1},{3,2},{4,7},{5,4},{6,5},{7,6},{8,11},{9,8},{10,9... | collective-permute-start | bytes 313352 | tf_op jit(solution)/shard_map/ppermute | solution.py:373
  55.3 8.1 %collective-permute-start = (bf16[4,102,128]{2,1,0:T(8,128)(2,1)S(1)}, bf16[4,102,128]{2,1,0:T(8,128)(2,1)S(1)}, u32[]{:S(2)}, u32[]{:S(2)}) collective-permute-start(bf16[4,102,128]{2,1,0:T(8,128)(2,1)S(1)} %get-tuple-element.23), channel_id=1, source_target_pairs={{0,1},{1,2},{2,3},{3,0},{4,5},{5,6},{6,7},{7,4},{8,9},{9,10},{10,1... | collective-permute-start | bytes 313352 | tf_op jit(solution)/shard_map/ppermute | solution.py:373
  55.4 8.1 %collective-permute-start.2 = (bf16[4,102,128]{2,1,0:T(8,128)(2,1)S(1)}, bf16[4,102,128]{2,1,0:T(8,128)(2,1)S(1)}, u32[]{:S(2)}, u32[]{:S(2)}) collective-permute-start(bf16[4,102,128]{2,1,0:T(8,128)(2,1)S(1)} %get-tuple-element.25), channel_id=1, source_target_pairs={{0,3},{1,0},{2,1},{3,2},{4,7},{5,4},{6,5},{7,6},{8,11},{9,8},{10,9... | collective-permute-start | bytes 313352 | tf_op jit(solution)/shard_map/ppermute | solution.py:373
  59.3 9.5 %collective-permute-start.10 = (bf16[8,102,128]{2,1,0:T(8,128)(2,1)S(1)}, bf16[8,102,128]{2,1,0:T(8,128)(2,1)S(1)}, u32[]{:S(2)}, u32[]{:S(2)}) collective-permute-start(bf16[8,102,128]{2,1,0:T(8,128)(2,1)S(1)} %pad_maximum_fusion.2), channel_id=1, source_target_pairs={{0,1},{1,2},{2,3},{3,0},{4,5},{5,6},{6,7},{7,4},{8,9},{9,10},{10,1... | collective-permute-start | bytes 626696 | tf_op jit(solution)/shard_map/ppermute | solution.py:373
  59.5 13.2 %collective-permute-start.11 = (bf16[8,102,128]{2,1,0:T(8,128)(2,1)S(1)}, bf16[8,102,128]{2,1,0:T(8,128)(2,1)S(1)}, u32[]{:S(2)}, u32[]{:S(2)}) collective-permute-start(bf16[8,102,128]{2,1,0:T(8,128)(2,1)S(1)} %pad_maximum_fusion.3), channel_id=1, source_target_pairs={{0,3},{1,0},{2,1},{3,2},{4,7},{5,4},{6,5},{7,6},{8,11},{9,8},{10,9... | collective-permute-start | bytes 626696 | tf_op jit(solution)/shard_map/ppermute | solution.py:373
  63.4 19.6 %collective-permute-start.1 = (bf16[8,102,128]{2,1,0:T(8,128)(2,1)S(1)}, bf16[8,102,128]{2,1,0:T(8,128)(2,1)S(1)}, u32[]{:S(2)}, u32[]{:S(2)}) collective-permute-start(bf16[8,102,128]{2,1,0:T(8,128)(2,1)S(1)} %pad_maximum_fusion), channel_id=1, source_target_pairs={{0,1},{1,2},{2,3},{3,0},{4,5},{5,6},{6,7},{7,4},{8,9},{9,10},{10,1... | collective-permute-start | bytes 626696 | tf_op jit(solution)/shard_map/ppermute | solution.py:373
  64.2 18.8 %collective-permute-start.3 = (bf16[8,102,128]{2,1,0:T(8,128)(2,1)}, bf16[8,102,128]{2,1,0:T(8,128)(2,1)S(1)}, u32[]{:S(2)}, u32[]{:S(2)}) collective-permute-start(bf16[8,102,128]{2,1,0:T(8,128)(2,1)} %pad_maximum_fusion.1), channel_id=1, source_target_pairs={{0,3},{1,0},{2,1},{3,2},{4,7},{5,4},{6,5},{7,6},{8,11},{9,8},{10,9... | collective-permute-start | bytes 626696 | tf_op jit(solution)/shard_map/ppermute | solution.py:373
  73.4 42.1 %copy-start.10 = (f32[16]{0:T(128)S(1)}, f32[16]{0:T(128)}, u32[]{:S(2)}) copy-start(f32[16]{0:T(128)} %param.16) | copy-start | bytes 196
  73.4 45.3 %copy-start.1 = (f32[1024,400]{0,1:T(8,128)S(1)}, f32[1024,400]{0,1:T(8,128)}, u32[]{:S(2)}) copy-start(f32[1024,400]{0,1:T(8,128)} %param.11) | copy-start | bytes 4915204
  73.4 45.3 %copy-start.3 = (f32[1024]{0:T(1024)S(1)}, f32[1024]{0:T(1024)}, u32[]{:S(2)}) copy-start(f32[1024]{0:T(1024)} %param.13) | copy-start | bytes 12292
  73.4 16.0 %all-to-all-start.2 = ((bf16[8,102,128]{2,1,0:T(8,128)(2,1)}), bf16[8,102,128]{2,1,0:T(8,128)(2,1)S(1)}, u32[]{:S(2)}, u32[]{:S(2)}) async-start(bf16[8,102,128]{2,1,0:T(8,128)(2,1)} %add_convert_fusion), calls=%async_computation.2 | async-start | bytes 425984 | tf_op jit(solution)/shard_map/all_to_all | solution.py:377
  83.1 11.3 %collective-permute-start.4 = (bf16[8,102,128]{2,1,0:T(8,128)(2,1)S(1)}, bf16[8,102,128]{2,1,0:T(8,128)(2,1)S(1)}, u32[]{:S(2)}, u32[]{:S(2)}) collective-permute-start(bf16[8,102,128]{2,1,0:T(8,128)(2,1)S(1)} %add_convert_fusion.1.refs_2_), channel_id=1, source_target_pairs={{0,1},{1,2},{2,3},{3,0},{4,5},{5,6},{6,7},{7,4},{8,9},{9,10},{10,1... | collective-permute-start | bytes 626696 | tf_op jit(solution)/shard_map/ppermute | solution.py:373
  84.4 11.9 %collective-permute-start.5 = (bf16[8,102,128]{2,1,0:T(8,128)(2,1)S(1)}, bf16[8,102,128]{2,1,0:T(8,128)(2,1)S(1)}, u32[]{:S(2)}, u32[]{:S(2)}) collective-permute-start(bf16[8,102,128]{2,1,0:T(8,128)(2,1)S(1)} %add_convert_fusion.1.refs_2_), channel_id=1, source_target_pairs={{0,3},{1,0},{2,1},{3,2},{4,7},{5,4},{6,5},{7,6},{8,11},{9,8},{10,9... | collective-permute-start | bytes 626696 | tf_op jit(solution)/shard_map/ppermute | solution.py:373
  90.7 11.0 %all-to-all-start.3 = ((bf16[8,102,128]{2,1,0:T(8,128)(2,1)}), bf16[8,102,128]{2,1,0:T(8,128)(2,1)S(1)}, u32[]{:S(2)}, u32[]{:S(2)}) async-start(bf16[8,102,128]{2,1,0:T(8,128)(2,1)} %shard_map.135), calls=%async_computation.3 | async-start | bytes 425984 | tf_op jit(solution)/shard_map/all_to_all | solution.py:377
  94.5 7.2 %collective-permute-start.6 = (bf16[4,102,128]{2,1,0:T(8,128)(2,1)S(1)}, bf16[4,102,128]{2,1,0:T(8,128)(2,1)S(1)}, u32[]{:S(2)}, u32[]{:S(2)}) collective-permute-start(bf16[4,102,128]{2,1,0:T(8,128)(2,1)S(1)} %slice.46), channel_id=1, source_target_pairs={{0,1},{1,2},{2,3},{3,0},{4,5},{5,6},{6,7},{7,4},{8,9},{9,10},{10,1... | collective-permute-start | bytes 313352 | tf_op jit(solution)/shard_map/ppermute | solution.py:373
  101.7 10.0 %collective-permute-start.12 = (bf16[8,102,128]{2,1,0:T(8,128)(2,1)S(1)}, bf16[8,102,128]{2,1,0:T(8,128)(2,1)S(1)}, u32[]{:S(2)}, u32[]{:S(2)}) collective-permute-start(bf16[8,102,128]{2,1,0:T(8,128)(2,1)S(1)} %all-to-all-done.3.refs_4_), channel_id=1, source_target_pairs={{0,1},{1,2},{2,3},{3,0},{4,5},{5,6},{6,7},{7,4},{8,9},{9,10},{10,1... | collective-permute-start | bytes 626696 | tf_op jit(solution)/shard_map/ppermute | solution.py:373
  101.7 19.1 %collective-permute-start.13 = (bf16[8,102,128]{2,1,0:T(8,128)(2,1)S(1)}, bf16[8,102,128]{2,1,0:T(8,128)(2,1)S(1)}, u32[]{:S(2)}, u32[]{:S(2)}) collective-permute-start(bf16[8,102,128]{2,1,0:T(8,128)(2,1)S(1)} %all-to-all-done.3.refs_4_), channel_id=1, source_target_pairs={{0,3},{1,0},{2,1},{3,2},{4,7},{5,4},{6,5},{7,6},{8,11},{9,8},{10,9... | collective-permute-start | bytes 626696 | tf_op jit(solution)/shard_map/ppermute | solution.py:373
  111.7 9.2 %collective-permute-start.14 = (bf16[8,102,128]{2,1,0:T(8,128)(2,1)S(1)}, bf16[8,102,128]{2,1,0:T(8,128)(2,1)S(1)}, u32[]{:S(2)}, u32[]{:S(2)}) collective-permute-start(bf16[8,102,128]{2,1,0:T(8,128)(2,1)S(1)} %collective-permute-done.12.refs_5_), channel_id=1, source_target_pairs={{0,1},{1,2},{2,3},{3,0},{4,5},{5,6},{6,7},{7,4},{8,9},{9,10},{10,1... | collective-permute-start | bytes 626696 | tf_op jit(solution)/shard_map/ppermute | solution.py:373
  111.7 7.1 %collective-permute-start.7 = (bf16[4,102,128]{2,1,0:T(8,128)(2,1)S(1)}, bf16[4,102,128]{2,1,0:T(8,128)(2,1)S(1)}, u32[]{:S(2)}, u32[]{:S(2)}) collective-permute-start(bf16[4,102,128]{2,1,0:T(8,128)(2,1)S(1)} %slice.47), channel_id=1, source_target_pairs={{0,3},{1,0},{2,1},{3,2},{4,7},{5,4},{6,5},{7,6},{8,11},{9,8},{10,9... | collective-permute-start | bytes 313352 | tf_op jit(solution)/shard_map/ppermute | solution.py:373
  118.8 2.1 %copy-start = (f32[1024,400]{0,1:T(8,128)S(1)}, f32[1024,400]{0,1:T(8,128)}, u32[]{:S(2)}) copy-start(f32[1024,400]{0,1:T(8,128)} %param.12) | copy-start | bytes 4915204
  118.8 2.1 %copy-start.4 = (f32[1024]{0:T(1024)S(1)}, f32[1024]{0:T(1024)}, u32[]{:S(2)}) copy-start(f32[1024]{0:T(1024)} %param.14) | copy-start | bytes 12292

commit v9 on v8

--- a/solution.py
+++ b/solution.py
@@ -207,8 +207,10 @@
     def spans(some):
         for j in some:
             ids = live_ids(tid_ref[j], meta_ref, first + j, steps)
-            hot_ref[j] = one_hot(ids, table_ref.shape[1])
-        tails = [dot_nn(table_ref[...], hot_ref[j]).astype(BF16) for j in some]
+            hot_ref[:, j * E_CH : (j + 1) * E_CH] = one_hot(ids, table_ref.shape[1])
+        here = slice(some[0] * E_CH, (some[-1] + 1) * E_CH)
+        gathered = dot_nn(table_ref[...], hot_ref[:, here]).astype(BF16)
+        tails = [gathered[:, k * E_CH : (k + 1) * E_CH] for k in range(len(some))]
         for j, tail in zip(some, tails):
             scores = dot_tn(edge_ref[j, 0], tail)
             sig = 0.5 * jnp.tanh(0.5 * scores) + 0.5
@@ -230,11 +232,8 @@
             grad_rel = [g_re * h_re + g_im * h_im, g_im * h_re - g_re * h_im]
             grad_rel = jnp.concatenate(grad_rel, axis=0).astype(BF16)
             rel_out_ref[...] += dot_nt(grad_rel, kind.astype(BF16))
-        total = acc_ref[...]
-        for j in some:
-            grad_tail = dot_nn(edge_ref[j, 0], coef_ref[j])
-            total += dot_nt(grad_tail.astype(BF16), hot_ref[j])
-        acc_ref[...] = total
+        grad_tails = [dot_nn(edge_ref[j, 0], coef_ref[j]).astype(BF16) for j in some]
+        acc_ref[...] += dot_nt(jnp.concatenate(grad_tails, axis=1), hot_ref[:, here])
 
     @pl.when(last_live)
     def _():
@@ -497,7 +496,7 @@
         scratch_shapes=[
             pltpu.VMEM((features, rows), BF16),
             pltpu.VMEM((features, rows), F32),
-            pltpu.VMEM((group, rows, E_CH), BF16),
+            pltpu.VMEM((rows, group * E_CH), BF16),
             pltpu.VMEM((group, E_CH, E_CH), BF16),
         ],
         compiler_params=params(48),

time: 126 us -> 125 us (level)
  Pallas kernels: 26.4 us -> 33.4 us
  starting transfers between devices: 44.9 us -> 39.4 us
  waiting for transfers between devices: 28.7 us -> 26.5 us
    pallas_call x1, Pallas kernels: 9.98 us -> 15.9 us  [per_device(): pl.pallas_call(functools.partial(main_kernel, steps, lanes, packed), grid...]
    all_to_all x3, starting transfers between devices: 16.9 us -> 13 us  [swap_buckets(): return lax.all_to_all(x, 'bucket', split_axis=0, concat_axis=0, tiled=True)]
    ppermute x15, starting transfers between devices: 28 us -> 26.4 us  [shift_span(): lax.ppermute(x, 'span', [(i, (i + by) % count) for i in range(count)])]
  transfers between devices with their start and end apart: 18 -> 18, of which waited for: 8 -> 9; matrix products, arithmetic and copies ran while one was open for 2% -> 2% of each run, Pallas kernels for 10% -> 11%
where the time goes in v9:
time: 125 us; the launch traced here: 123 us
  starting transfers between devices  39.4 us (32%)
  Pallas kernels  33.4 us (27%)
  waiting for transfers between devices  26.5 us (21%)
  blocking collectives  17.9 us (14%)
  other arithmetic  3.87 us (3%)
  between operations  1.7 us (1%)
    ppermute x15, starting transfers between devices, shift_span(): lax.ppermute(x, 'span', [(i, (i + by) % count) for i in range(count)])  26.4 us
    ppermute x15, waiting for transfers between devices, shift_span(): lax.ppermute(x, 'span', [(i, (i + by) % count) for i in range(count)])  19.1 us
    all_to_all x1, blocking collectives, swap_buckets(): return lax.all_to_all(x, 'bucket', split_axis=0, concat_axis=0, tiled=True)  17.9 us
    pallas_call x1, Pallas kernels, per_device(): pl.pallas_call(functools.partial(main_kernel, steps, lanes, packed), grid...  15.9 us
    all_to_all x3, starting transfers between devices, swap_buckets(): return lax.all_to_all(x, 'bucket', split_axis=0, concat_axis=0, tiled=True)  13 us
    all_to_all x3, waiting for transfers between devices, swap_buckets(): return lax.all_to_all(x, 'bucket', split_axis=0, concat_axis=0, tiled=True)  7.38 us
    pallas_call x1, Pallas kernels, per_device(): pl.pallas_call(functools.partial(prep_kernel, steps), grid=(steps,), out_...  6.69 us
    pallas_call x2, Pallas kernels, update(): pl.pallas_call(functools.partial(update_kernel, lanes, joined), out_shape...  4.7 us
  transfers between devices with their start and end apart: 18, of which 9 were waited for; matrix products, arithmetic and copies ran while one was open for 2% of the time, Pallas kernels for 11%

profile of v9, /device:TPU:0, one launch (start us, length us, event | category | flops | bytes accessed | tf_op | source)
XLA Modules:
  0.0 122.9 jit_solution(17624189331423906066)
XLA Ops:
  0.6 1.5 %bitcast_bitcast_fusion = bf16[8,400,128]{2,1,0:T(8,128)(2,1)S(1)} fusion(f32[1024,400]{0,1:T(8,128)} %param.12), kind=kLoop, calls=%fused_computation | loop fusion | flops 409600 | bytes 2457600 | tf_op jit(solution)/shard_map/transpose | solution.py:441
  2.2 17.9 %all_to_all.20.in_ref = bf16[8,400,128]{2,1,0:T(8,128)(2,1)S(1)} all-to-all(bf16[8,400,128]{2,1,0:T(8,128)(2,1)S(1)} %bitcast_bitcast_fusion), channel_id=1, replica_groups=mesh['bucket'=8,'span'=4] {'bucket'}, dimensions={0} | all-to-all | bytes 1638400 | tf_op jit(solution)/shard_map/all_to_all | solution.py:376
  20.1 1.5 %shard_map.131 = bf16[8,400,128]{2,1,0:T(8,128)(2,1)} custom-call(s32[8]{0:T(128)S(1)} %copy-done.5, bf16[8,400,128]{2,1,0:T(8,128)(2,1)S(1)} %all_to_all.20.in_ref), custom_call_target="tpu_custom_call" | custom-call | tf_op jit(solution)/shard_map/pallas_call | solution.py:444
  21.6 3.5 %all-to-all-start.1 = ((bf16[8,400,128]{2,1,0:T(8,128)(2,1)}), bf16[8,400,128]{2,1,0:T(8,128)(2,1)S(1)}, u32[]{:S(2)}, u32[]{:S(2)}) async-start(bf16[8,400,128]{2,1,0:T(8,128)(2,1)} %shard_map.131), calls=%async_computation.1 | async-start | bytes 1638400 | tf_op jit(solution)/shard_map/all_to_all | solution.py:376
  25.8 0.6 pad_add_fusion.meta_ref
  26.4 6.7 %shard_map.130.edge_ref = bf16[4,2,400,640]{3,2,1,0:T(8,128)(2,1)} custom-call(s32[2]{0:T(128)} %pad_add_fusion.meta_ref, s32[4,1,640]{2,1,0:T(1,128)} %bitcast.28, s32[4,1,640]{2,1,0:T(1,128)} %bitcast.26, f32[400,1024]{1,0:T(8,128)} %bitcast.21, f32[16,400]{1,0:T(8,128)} %refs_2_.1), custom_call_target="tpu_custom_call" | custom-call | flops 4194304000 | bytes 8192000 | tf_op jit(solution)/shard_map/pallas_call | solution.py:459
  33.0 4.9 %all-to-all-done.1.parts_ref = bf16[8,400,128]{2,1,0:T(8,128)(2,1)S(1)} async-done(((bf16[8,400,128]{2,1,0:T(8,128)(2,1)}), bf16[8,400,128]{2,1,0:T(8,128)(2,1)S(1)}, u32[]{:S(2)}, u32[]{:S(2)}) %all-to-all-start.1) | async-done | bytes 819232 | tf_op jit(solution)/shard_map/all_to_all | solution.py:376
  38.0 0.0 copy-start.9
  38.0 15.9 %shard_map.132 = (bf16[4,400,640]{2,1,0:T(8,128)(2,1)S(1)}, f32[400,16]{1,0:T(8,128)}, f32[8,102,128]{2,1,0:T(8,128)S(1)}, f32[8,102,128]{2,1,0:T(8,128)S(1)}, f...) custom-call(s32[2]{0:T(128)S(1)} %copy-done.6, ...), custom_call_target="tpu_custom_call" | custom-call | flops 12582912000 | bytes 8192000 | tf_op jit(solution)/shard_map/pallas_call | solution.py:478
  54.0 1.6 %collective-permute-start.8 = (bf16[4,102,128]{2,1,0:T(8,128)(2,1)S(1)}, bf16[4,102,128]{2,1,0:T(8,128)(2,1)S(1)}, u32[]{:S(2)}, u32[]{:S(2)}) collective-permute-start(bf16[4,102,128]{2,1,0:T(8,128)(2,1)S(1)} %get-tuple-element.28), channel_id=1, source_target_pairs={{0,1},{1,2},{2,3},{3,0},{4,5},{5,6},{6,7},{7,4},{8,9},{9,10},{10,1... | collective-permute-start | bytes 313352 | tf_op jit(solution)/shard_map/ppermute | solution.py:372
  55.6 2.2 %collective-permute-start.9 = (bf16[4,102,128]{2,1,0:T(8,128)(2,1)S(1)}, bf16[4,102,128]{2,1,0:T(8,128)(2,1)S(1)}, u32[]{:S(2)}, u32[]{:S(2)}) collective-permute-start(bf16[4,102,128]{2,1,0:T(8,128)(2,1)S(1)} %get-tuple-element.29), channel_id=1, source_target_pairs={{0,3},{1,0},{2,1},{3,2},{4,7},{5,4},{6,5},{7,6},{8,11},{9,8},{10,9... | collective-permute-start | bytes 313352 | tf_op jit(solution)/shard_map/ppermute | solution.py:372
  57.8 3.4 %shard_map.133 = (f32[8,102,128]{2,1,0:T(8,128)S(1)}, f32[8,102,128]{2,1,0:T(8,128)S(1)}, f32[8,102,128]{2,1,0:T(8,128)S(1)}, bf16[4,102,128]{2,1,0:T(8,128)(2,1)S(1)}, bf16[4,102,128]{2,1,0:T(8,128)(2,1)S(1)}) custom-call(s32[2]{0:T(128)S(1)} %copy-done.6, s32[4,1,640]{2,1,0:T(1,128)S(1)} %bitcast.29, bf16[4,400,640]{2,1,0:T(8,128)(2,1)S(1)} %get-tuple-element.20.grad_ref), custom_call_target="tpu_custom_call" | custom-call | flops 4194304000 | bytes 8192000 | tf_op jit(solution)/shard_map/pallas_call | solution.py:506
  61.2 0.1 collective-permute-start
  61.3 3.9 %collective-permute-start.2 = (bf16[4,102,128]{2,1,0:T(8,128)(2,1)S(1)}, bf16[4,102,128]{2,1,0:T(8,128)(2,1)S(1)}, u32[]{:S(2)}, u32[]{:S(2)}) collective-permute-start(bf16[4,102,128]{2,1,0:T(8,128)(2,1)S(1)} %get-tuple-element.25), channel_id=1, source_target_pairs={{0,3},{1,0},{2,1},{3,2},{4,7},{5,4},{6,5},{7,6},{8,11},{9,8},{10,9... | collective-permute-start | bytes 313352 | tf_op jit(solution)/shard_map/ppermute | solution.py:372
  65.2 0.0 collective-permute-done.8
  65.2 0.0 collective-permute-done.9
  65.3 0.1 collective-permute-start.10
  65.4 3.9 %collective-permute-start.11 = (bf16[8,102,128]{2,1,0:T(8,128)(2,1)S(1)}, bf16[8,102,128]{2,1,0:T(8,128)(2,1)S(1)}, u32[]{:S(2)}, u32[]{:S(2)}) collective-permute-start(bf16[8,102,128]{2,1,0:T(8,128)(2,1)S(1)} %pad_maximum_fusion.3), channel_id=1, source_target_pairs={{0,3},{1,0},{2,1},{3,2},{4,7},{5,4},{6,5},{7,6},{8,11},{9,8},{10,9... | collective-permute-start | bytes 626696 | tf_op jit(solution)/shard_map/ppermute | solution.py:372
  69.3 0.0 collective-permute-done
  69.3 0.1 collective-permute-start.1
  69.4 1.3 %collective-permute-done.2 = bf16[4,102,128]{2,1,0:T(8,128)(2,1)S(1)} collective-permute-done((bf16[4,102,128]{2,1,0:T(8,128)(2,1)S(1)}, bf16[4,102,128]{2,1,0:T(8,128)(2,1)S(1)}, u32[]{:S(2)}, u32[]{:S(2)}) %collective-permute-start.2) | collective-permute-done | bytes 104480 | tf_op jit(solution)/shard_map/ppermute | solution.py:372
  70.7 0.7 pad_maximum_fusion.1
  71.4 2.5 %collective-permute-start.3 = (bf16[8,102,128]{2,1,0:T(8,128)(2,1)}, bf16[8,102,128]{2,1,0:T(8,128)(2,1)S(1)}, u32[]{:S(2)}, u32[]{:S(2)}) collective-permute-start(bf16[8,102,128]{2,1,0:T(8,128)(2,1)} %pad_maximum_fusion.1), channel_id=1, source_target_pairs={{0,3},{1,0},{2,1},{3,2},{4,7},{5,4},{6,5},{7,6},{8,11},{9,8},{10,9... | collective-permute-start | bytes 626696 | tf_op jit(solution)/shard_map/ppermute | solution.py:372
  74.0 1.5 %collective-permute-done.10 = bf16[8,102,128]{2,1,0:T(8,128)(2,1)S(1)} collective-permute-done((bf16[8,102,128]{2,1,0:T(8,128)(2,1)S(1)}, bf16[8,102,128]{2,1,0:T(8,128)(2,1)S(1)}, u32[]{:S(2)}, u32[]{:S(2)}) %collective-permute-start.10) | collective-permute-done | bytes 208928 | tf_op jit(solution)/shard_map/ppermute | solution.py:372
  75.4 0.4 collective-permute-done.11
  75.8 0.8 add_convert_fusion
  76.6 4.6 %all-to-all-start.2 = ((bf16[8,102,128]{2,1,0:T(8,128)(2,1)}), bf16[8,102,128]{2,1,0:T(8,128)(2,1)S(1)}, u32[]{:S(2)}, u32[]{:S(2)}) async-start(bf16[8,102,128]{2,1,0:T(8,128)(2,1)} %add_convert_fusion), calls=%async_computation.2 | async-start | bytes 425984 | tf_op jit(solution)/shard_map/all_to_all | solution.py:376
  81.2 0.0 collective-permute-done.1
  81.2 0.0 collective-permute-done.3
  81.2 0.1 add_convert_fusion.1.refs_2_
  81.3 2.0 %collective-permute-start.4 = (bf16[8,102,128]{2,1,0:T(8,128)(2,1)S(1)}, bf16[8,102,128]{2,1,0:T(8,128)(2,1)S(1)}, u32[]{:S(2)}, u32[]{:S(2)}) collective-permute-start(bf16[8,102,128]{2,1,0:T(8,128)(2,1)S(1)} %add_convert_fusion.1.refs_2_), channel_id=1, source_target_pairs={{0,1},{1,2},{2,3},{3,0},{4,5},{5,6},{6,7},{7,4},{8,9},{9,10},{10,1... | collective-permute-start | bytes 626696 | tf_op jit(solution)/shard_map/ppermute | solution.py:372
  83.2 1.9 %collective-permute-start.5 = (bf16[8,102,128]{2,1,0:T(8,128)(2,1)S(1)}, bf16[8,102,128]{2,1,0:T(8,128)(2,1)S(1)}, u32[]{:S(2)}, u32[]{:S(2)}) collective-permute-start(bf16[8,102,128]{2,1,0:T(8,128)(2,1)S(1)} %add_convert_fusion.1.refs_2_), channel_id=1, source_target_pairs={{0,3},{1,0},{2,1},{3,2},{4,7},{5,4},{6,5},{7,6},{8,11},{9,8},{10,9... | collective-permute-start | bytes 626696 | tf_op jit(solution)/shard_map/ppermute | solution.py:372
  85.1 2.4 %all-to-all-done.2.in_ref = bf16[8,102,128]{2,1,0:T(8,128)(2,1)S(1)} async-done(((bf16[8,102,128]{2,1,0:T(8,128)(2,1)}), bf16[8,102,128]{2,1,0:T(8,128)(2,1)S(1)}, u32[]{:S(2)}, u32[]{:S(2)}) %all-to-all-start.2) | async-done | bytes 208928 | tf_op jit(solution)/shard_map/all_to_all | solution.py:376
  87.6 1.2 %shard_map.135 = bf16[8,102,128]{2,1,0:T(8,128)(2,1)} custom-call(s32[8]{0:T(128)S(1)} %copy-done.5, bf16[8,102,128]{2,1,0:T(8,128)(2,1)S(1)} %all-to-all-done.2.in_ref), custom_call_target="tpu_custom_call" | custom-call | tf_op jit(solution)/shard_map/pallas_call | solution.py:532
  88.8 4.8 %all-to-all-start.3 = ((bf16[8,102,128]{2,1,0:T(8,128)(2,1)}), bf16[8,102,128]{2,1,0:T(8,128)(2,1)S(1)}, u32[]{:S(2)}, u32[]{:S(2)}) async-start(bf16[8,102,128]{2,1,0:T(8,128)(2,1)} %shard_map.135), calls=%async_computation.3 | async-start | bytes 425984 | tf_op jit(solution)/shard_map/all_to_all | solution.py:376
  93.7 0.0 collective-permute-done.4.refs_3_
  93.7 0.6 collective-permute-start.6
  94.3 0.9 collective-permute-done.5.refs_4_
  95.2 5.7 %collective-permute-done.6.refs_5_ = bf16[4,102,128]{2,1,0:T(8,128)(2,1)S(1)} collective-permute-done((bf16[4,102,128]{2,1,0:T(8,128)(2,1)S(1)}, bf16[4,102,128]{2,1,0:T(8,128)(2,1)S(1)}, u32[]{:S(2)}, u32[]{:S(2)}) %collective-permute-start.6) | collective-permute-done | bytes 104480 | tf_op jit(solution)/shard_map/ppermute | solution.py:372
  100.9 3.8 %collective-permute-start.13 = (bf16[8,102,128]{2,1,0:T(8,128)(2,1)S(1)}, bf16[8,102,128]{2,1,0:T(8,128)(2,1)S(1)}, u32[]{:S(2)}, u32[]{:S(2)}) collective-permute-start(bf16[8,102,128]{2,1,0:T(8,128)(2,1)S(1)} %all-to-all-done.3.refs_4_), channel_id=1, source_target_pairs={{0,3},{1,0},{2,1},{3,2},{4,7},{5,4},{6,5},{7,6},{8,11},{9,8},{10,9... | collective-permute-start | bytes 626696 | tf_op jit(solution)/shard_map/ppermute | solution.py:372
  104.7 6.1 %collective-permute-done.12.refs_5_ = bf16[8,102,128]{2,1,0:T(8,128)(2,1)S(1)} collective-permute-done((bf16[8,102,128]{2,1,0:T(8,128)(2,1)S(1)}, bf16[8,102,128]{2,1,0:T(8,128)(2,1)S(1)}, u32[]{:S(2)}, u32[]{:S(2)}) %collective-permute-start.12) | collective-permute-done | bytes 208928 | tf_op jit(solution)/shard_map/ppermute | solution.py:372
  110.9 0.0 collective-permute-start.14
  110.9 3.9 %collective-permute-start.7 = (bf16[4,102,128]{2,1,0:T(8,128)(2,1)S(1)}, bf16[4,102,128]{2,1,0:T(8,128)(2,1)S(1)}, u32[]{:S(2)}, u32[]{:S(2)}) collective-permute-start(bf16[4,102,128]{2,1,0:T(8,128)(2,1)S(1)} %slice.47), channel_id=1, source_target_pairs={{0,3},{1,0},{2,1},{3,2},{4,7},{5,4},{6,5},{7,6},{8,11},{9,8},{10,9... | collective-permute-start | bytes 313352 | tf_op jit(solution)/shard_map/ppermute | solution.py:372
  114.8 0.1 copy.15.refs_3_
  114.8 3.2 %collective-permute-done.7.refs_6_ = bf16[4,102,128]{2,1,0:T(8,128)(2,1)S(1)} collective-permute-done((bf16[4,102,128]{2,1,0:T(8,128)(2,1)S(1)}, bf16[4,102,128]{2,1,0:T(8,128)(2,1)S(1)}, u32[]{:S(2)}, u32[]{:S(2)}) %collective-permute-start.7) | collective-permute-done | bytes 104480 | tf_op jit(solution)/shard_map/ppermute | solution.py:372
  118.0 2.0 %shard_map.134 = f32[400,1024]{1,0:T(8,128)} custom-call(s32[2]{0:T(128)S(1)} %copy-done.6, f32[400,1024]{1,0:T(8,128)S(1)} %bitcast.22, f32[1,1024]{1,0:T(1,128)S(1)} %bitcast.23, bf16[8,102,128]{2,1,0:T(8,128)(2,1)S(1)} %add_convert_fusion.1.refs_2_, bf16[8,102,128]{2,1,0:T(8,128)(2,1)S(1)} %collective-permute-done.4.refs_3_, ...), custom_call_target="tpu_custom_call" | custom-call | tf_op jit(solution)/shard_map/pallas_call | solution.py:389
  120.1 0.0 collective-permute-done.14.refs_7_
  120.1 2.7 %shard_map.136 = (f32[400,1024]{1,0:T(8,128)}, f32[16,400]{1,0:T(8,128)}) custom-call(s32[2]{0:T(128)S(1)} %copy-done.6, f32[400,1024]{1,0:T(8,128)S(1)} %bitcast.20, f32[1,1024]{1,0:T(1,128)S(1)} %bitcast.24, f32[16,400]{1,0:T(8,128)S(1)} %copy-done.2, f32[16,1]{1,0:T(8,128)S(1)} %copy.15.refs_3_, bf16[8,102,128]{2,1,0:T(8,128)(2,1)S(1)} %all-to-all-done.3.refs_4_, ...), custom_call_target="tpu_custom_call" | custom-call | tf_op jit(solution)/shard_map/pallas_call | solution.py:389
  (37 shorter events, 0.3 us)
Async XLA Ops:
  0.6 19.4 %copy-start.5 = (s32[8]{0:T(128)S(1)}, s32[8]{0:T(128)}, u32[]{:S(2)}) copy-start(s32[8]{0:T(128)} %plan_ref.3) | copy-start | bytes 100
  21.6 16.4 %all-to-all-start.1 = ((bf16[8,400,128]{2,1,0:T(8,128)(2,1)}), bf16[8,400,128]{2,1,0:T(8,128)(2,1)S(1)}, u32[]{:S(2)}, u32[]{:S(2)}) async-start(bf16[8,400,128]{2,1,0:T(8,128)(2,1)} %shard_map.131), calls=%async_computation.1 | async-start | bytes 1638400 | tf_op jit(solution)/shard_map/all_to_all | solution.py:376
  26.3 11.6 %copy-start.2 = (f32[16,400]{1,0:T(8,128)S(1)}, f32[16,400]{1,0:T(8,128)}, u32[]{:S(2)}) copy-start(f32[16,400]{1,0:T(8,128)} %refs_2_.1) | copy-start | bytes 76804
  26.3 11.6 %copy-start.6 = (s32[2]{0:T(128)S(1)}, s32[2]{0:T(128)}, u32[]{:S(2)}) copy-start(s32[2]{0:T(128)} %pad_add_fusion.meta_ref) | copy-start | bytes 28
  26.3 11.6 %copy-start.7 = (s32[1,2560]{1,0:T(1,128)S(1)}, s32[1,2560]{1,0:T(1,128)}, u32[]{:S(2)}) copy-start(s32[1,2560]{1,0:T(1,128)} %param.19) | copy-start | bytes 30724
  26.4 11.7 %copy-start.8 = (s32[1,2560]{1,0:T(1,128)S(1)}, s32[1,2560]{1,0:T(1,128)}, u32[]{:S(2)}) copy-start(s32[1,2560]{1,0:T(1,128)} %param.20) | copy-start | bytes 30724
  38.0 19.8 %copy-start.9 = (s32[1,2560]{1,0:T(1,128)S(1)}, s32[1,2560]{1,0:T(1,128)}, u32[]{:S(2)}) copy-start(s32[1,2560]{1,0:T(1,128)} %param.18) | copy-start | bytes 30724
  54.0 11.2 %collective-permute-start.8 = (bf16[4,102,128]{2,1,0:T(8,128)(2,1)S(1)}, bf16[4,102,128]{2,1,0:T(8,128)(2,1)S(1)}, u32[]{:S(2)}, u32[]{:S(2)}) collective-permute-start(bf16[4,102,128]{2,1,0:T(8,128)(2,1)S(1)} %get-tuple-element.28), channel_id=1, source_target_pairs={{0,1},{1,2},{2,3},{3,0},{4,5},{5,6},{6,7},{7,4},{8,9},{9,10},{10,1... | collective-permute-start | bytes 313352 | tf_op jit(solution)/shard_map/ppermute | solution.py:372
  55.6 9.6 %collective-permute-start.9 = (bf16[4,102,128]{2,1,0:T(8,128)(2,1)S(1)}, bf16[4,102,128]{2,1,0:T(8,128)(2,1)S(1)}, u32[]{:S(2)}, u32[]{:S(2)}) collective-permute-start(bf16[4,102,128]{2,1,0:T(8,128)(2,1)S(1)} %get-tuple-element.29), channel_id=1, source_target_pairs={{0,3},{1,0},{2,1},{3,2},{4,7},{5,4},{6,5},{7,6},{8,11},{9,8},{10,9... | collective-permute-start | bytes 313352 | tf_op jit(solution)/shard_map/ppermute | solution.py:372
  61.2 8.1 %collective-permute-start = (bf16[4,102,128]{2,1,0:T(8,128)(2,1)S(1)}, bf16[4,102,128]{2,1,0:T(8,128)(2,1)S(1)}, u32[]{:S(2)}, u32[]{:S(2)}) collective-permute-start(bf16[4,102,128]{2,1,0:T(8,128)(2,1)S(1)} %get-tuple-element.23), channel_id=1, source_target_pairs={{0,1},{1,2},{2,3},{3,0},{4,5},{5,6},{6,7},{7,4},{8,9},{9,10},{10,1... | collective-permute-start | bytes 313352 | tf_op jit(solution)/shard_map/ppermute | solution.py:372
  61.3 9.4 %collective-permute-start.2 = (bf16[4,102,128]{2,1,0:T(8,128)(2,1)S(1)}, bf16[4,102,128]{2,1,0:T(8,128)(2,1)S(1)}, u32[]{:S(2)}, u32[]{:S(2)}) collective-permute-start(bf16[4,102,128]{2,1,0:T(8,128)(2,1)S(1)} %get-tuple-element.25), channel_id=1, source_target_pairs={{0,3},{1,0},{2,1},{3,2},{4,7},{5,4},{6,5},{7,6},{8,11},{9,8},{10,9... | collective-permute-start | bytes 313352 | tf_op jit(solution)/shard_map/ppermute | solution.py:372
  65.3 10.2 %collective-permute-start.10 = (bf16[8,102,128]{2,1,0:T(8,128)(2,1)S(1)}, bf16[8,102,128]{2,1,0:T(8,128)(2,1)S(1)}, u32[]{:S(2)}, u32[]{:S(2)}) collective-permute-start(bf16[8,102,128]{2,1,0:T(8,128)(2,1)S(1)} %pad_maximum_fusion.2), channel_id=1, source_target_pairs={{0,1},{1,2},{2,3},{3,0},{4,5},{5,6},{6,7},{7,4},{8,9},{9,10},{10,1... | collective-permute-start | bytes 626696 | tf_op jit(solution)/shard_map/ppermute | solution.py:372
  65.4 10.4 %collective-permute-start.11 = (bf16[8,102,128]{2,1,0:T(8,128)(2,1)S(1)}, bf16[8,102,128]{2,1,0:T(8,128)(2,1)S(1)}, u32[]{:S(2)}, u32[]{:S(2)}) collective-permute-start(bf16[8,102,128]{2,1,0:T(8,128)(2,1)S(1)} %pad_maximum_fusion.3), channel_id=1, source_target_pairs={{0,3},{1,0},{2,1},{3,2},{4,7},{5,4},{6,5},{7,6},{8,11},{9,8},{10,9... | collective-permute-start | bytes 626696 | tf_op jit(solution)/shard_map/ppermute | solution.py:372
  69.3 11.8 %collective-permute-start.1 = (bf16[8,102,128]{2,1,0:T(8,128)(2,1)S(1)}, bf16[8,102,128]{2,1,0:T(8,128)(2,1)S(1)}, u32[]{:S(2)}, u32[]{:S(2)}) collective-permute-start(bf16[8,102,128]{2,1,0:T(8,128)(2,1)S(1)} %pad_maximum_fusion), channel_id=1, source_target_pairs={{0,1},{1,2},{2,3},{3,0},{4,5},{5,6},{6,7},{7,4},{8,9},{9,10},{10,1... | collective-permute-start | bytes 626696 | tf_op jit(solution)/shard_map/ppermute | solution.py:372
  71.4 9.7 %collective-permute-start.3 = (bf16[8,102,128]{2,1,0:T(8,128)(2,1)}, bf16[8,102,128]{2,1,0:T(8,128)(2,1)S(1)}, u32[]{:S(2)}, u32[]{:S(2)}) collective-permute-start(bf16[8,102,128]{2,1,0:T(8,128)(2,1)} %pad_maximum_fusion.1), channel_id=1, source_target_pairs={{0,3},{1,0},{2,1},{3,2},{4,7},{5,4},{6,5},{7,6},{8,11},{9,8},{10,9... | collective-permute-start | bytes 626696 | tf_op jit(solution)/shard_map/ppermute | solution.py:372
  76.6 38.2 %copy-start.10 = (f32[16]{0:T(128)S(1)}, f32[16]{0:T(128)}, u32[]{:S(2)}) copy-start(f32[16]{0:T(128)} %param.16) | copy-start | bytes 196
  76.6 41.4 %copy-start.1 = (f32[1024,400]{0,1:T(8,128)S(1)}, f32[1024,400]{0,1:T(8,128)}, u32[]{:S(2)}) copy-start(f32[1024,400]{0,1:T(8,128)} %param.11) | copy-start | bytes 4915204
  76.6 41.4 %copy-start.3 = (f32[1024]{0:T(1024)S(1)}, f32[1024]{0:T(1024)}, u32[]{:S(2)}) copy-start(f32[1024]{0:T(1024)} %param.13) | copy-start | bytes 12292
  76.6 11.0 %all-to-all-start.2 = ((bf16[8,102,128]{2,1,0:T(8,128)(2,1)}), bf16[8,102,128]{2,1,0:T(8,128)(2,1)S(1)}, u32[]{:S(2)}, u32[]{:S(2)}) async-start(bf16[8,102,128]{2,1,0:T(8,128)(2,1)} %add_convert_fusion), calls=%async_computation.2 | async-start | bytes 425984 | tf_op jit(solution)/shard_map/all_to_all | solution.py:376
  81.3 12.4 %collective-permute-start.4 = (bf16[8,102,128]{2,1,0:T(8,128)(2,1)S(1)}, bf16[8,102,128]{2,1,0:T(8,128)(2,1)S(1)}, u32[]{:S(2)}, u32[]{:S(2)}) collective-permute-start(bf16[8,102,128]{2,1,0:T(8,128)(2,1)S(1)} %add_convert_fusion.1.refs_2_), channel_id=1, source_target_pairs={{0,1},{1,2},{2,3},{3,0},{4,5},{5,6},{6,7},{7,4},{8,9},{9,10},{10,1... | collective-permute-start | bytes 626696 | tf_op jit(solution)/shard_map/ppermute | solution.py:372
  83.2 11.9 %collective-permute-start.5 = (bf16[8,102,128]{2,1,0:T(8,128)(2,1)S(1)}, bf16[8,102,128]{2,1,0:T(8,128)(2,1)S(1)}, u32[]{:S(2)}, u32[]{:S(2)}) collective-permute-start(bf16[8,102,128]{2,1,0:T(8,128)(2,1)S(1)} %add_convert_fusion.1.refs_2_), channel_id=1, source_target_pairs={{0,3},{1,0},{2,1},{3,2},{4,7},{5,4},{6,5},{7,6},{8,11},{9,8},{10,9... | collective-permute-start | bytes 626696 | tf_op jit(solution)/shard_map/ppermute | solution.py:372
  88.8 12.1 %all-to-all-start.3 = ((bf16[8,102,128]{2,1,0:T(8,128)(2,1)}), bf16[8,102,128]{2,1,0:T(8,128)(2,1)S(1)}, u32[]{:S(2)}, u32[]{:S(2)}) async-start(bf16[8,102,128]{2,1,0:T(8,128)(2,1)} %shard_map.135), calls=%async_computation.3 | async-start | bytes 425984 | tf_op jit(solution)/shard_map/all_to_all | solution.py:376
  93.7 7.2 %collective-permute-start.6 = (bf16[4,102,128]{2,1,0:T(8,128)(2,1)S(1)}, bf16[4,102,128]{2,1,0:T(8,128)(2,1)S(1)}, u32[]{:S(2)}, u32[]{:S(2)}) collective-permute-start(bf16[4,102,128]{2,1,0:T(8,128)(2,1)S(1)} %slice.46), channel_id=1, source_target_pairs={{0,1},{1,2},{2,3},{3,0},{4,5},{5,6},{6,7},{7,4},{8,9},{9,10},{10,1... | collective-permute-start | bytes 313352 | tf_op jit(solution)/shard_map/ppermute | solution.py:372
  100.9 10.0 %collective-permute-start.12 = (bf16[8,102,128]{2,1,0:T(8,128)(2,1)S(1)}, bf16[8,102,128]{2,1,0:T(8,128)(2,1)S(1)}, u32[]{:S(2)}, u32[]{:S(2)}) collective-permute-start(bf16[8,102,128]{2,1,0:T(8,128)(2,1)S(1)} %all-to-all-done.3.refs_4_), channel_id=1, source_target_pairs={{0,1},{1,2},{2,3},{3,0},{4,5},{5,6},{6,7},{7,4},{8,9},{9,10},{10,1... | collective-permute-start | bytes 626696 | tf_op jit(solution)/shard_map/ppermute | solution.py:372
  100.9 19.2 %collective-permute-start.13 = (bf16[8,102,128]{2,1,0:T(8,128)(2,1)S(1)}, bf16[8,102,128]{2,1,0:T(8,128)(2,1)S(1)}, u32[]{:S(2)}, u32[]{:S(2)}) collective-permute-start(bf16[8,102,128]{2,1,0:T(8,128)(2,1)S(1)} %all-to-all-done.3.refs_4_), channel_id=1, source_target_pairs={{0,3},{1,0},{2,1},{3,2},{4,7},{5,4},{6,5},{7,6},{8,11},{9,8},{10,9... | collective-permute-start | bytes 626696 | tf_op jit(solution)/shard_map/ppermute | solution.py:372
  110.9 9.2 %collective-permute-start.14 = (bf16[8,102,128]{2,1,0:T(8,128)(2,1)S(1)}, bf16[8,102,128]{2,1,0:T(8,128)(2,1)S(1)}, u32[]{:S(2)}, u32[]{:S(2)}) collective-permute-start(bf16[8,102,128]{2,1,0:T(8,128)(2,1)S(1)} %collective-permute-done.12.refs_5_), channel_id=1, source_target_pairs={{0,1},{1,2},{2,3},{3,0},{4,5},{5,6},{6,7},{7,4},{8,9},{9,10},{10,1... | collective-permute-start | bytes 626696 | tf_op jit(solution)/shard_map/ppermute | solution.py:372
  110.9 7.1 %collective-permute-start.7 = (bf16[4,102,128]{2,1,0:T(8,128)(2,1)S(1)}, bf16[4,102,128]{2,1,0:T(8,128)(2,1)S(1)}, u32[]{:S(2)}, u32[]{:S(2)}) collective-permute-start(bf16[4,102,128]{2,1,0:T(8,128)(2,1)S(1)} %slice.47), channel_id=1, source_target_pairs={{0,3},{1,0},{2,1},{3,2},{4,7},{5,4},{6,5},{7,6},{8,11},{9,8},{10,9... | collective-permute-start | bytes 313352 | tf_op jit(solution)/shard_map/ppermute | solution.py:372
  118.0 2.1 %copy-start = (f32[1024,400]{0,1:T(8,128)S(1)}, f32[1024,400]{0,1:T(8,128)}, u32[]{:S(2)}) copy-start(f32[1024,400]{0,1:T(8,128)} %param.12) | copy-start | bytes 4915204
  118.0 2.1 %copy-start.4 = (f32[1024]{0:T(1024)S(1)}, f32[1024]{0:T(1024)}, u32[]{:S(2)}) copy-start(f32[1024]{0:T(1024)} %param.14) | copy-start | bytes 12292
